TPU v7x, 32 devices: a whole 2x2x4 slice. The times are simulated.
32 devices in a mesh: ctx: 4 (over y, x), fsdp: 8 (over z, core).
Axes of the slice: x: 2, y: 2, z: 4, core: 2. Of those that a mesh axis runs over, the one named last changes fastest.
Arguments:
- inputs: bfloat16 [8, 512, 2048], P('fsdp', 'ctx'), may hold values from -6 to 6
- lengths: int32 [8], P('fsdp'), may hold values from 128 to 512, as said below
- w_query: bfloat16 [2048, 2048], P('fsdp'), may hold values from -0.0625 to 0.0625
- w_key: bfloat16 [2048, 2048], P('fsdp'), may hold values from -0.0625 to 0.0625
- w_value: bfloat16 [2048, 2048], P('fsdp'), may hold values from -0.125 to 0.125
- w_out: bfloat16 [2048, 2048], P('fsdp'), may hold values from -0.5 to 0.5
- w_gate: bfloat16 [2048, 5120], P('fsdp'), may hold values from -0.125 to 0.125
- w_up: bfloat16 [2048, 5120], P('fsdp'), may hold values from -0.125 to 0.125
- w_down: bfloat16 [5120, 2048], P('fsdp'), may hold values from -0.125 to 0.125
- norm_attn: bfloat16 [2048], P('fsdp'), may hold values from 0.5 to 1.5
- norm_ffn: bfloat16 [2048], P('fsdp'), may hold values from 0.5 to 1.5
- relative_bias_table: bfloat16 [32, 32], P('fsdp'), may hold values from -6 to 6
- cotangent: bfloat16 [8, 512, 2048], P('fsdp', 'ctx'), may hold values from -6 to 6
Outputs:
- result: bfloat16 [8, 512, 2048], P('fsdp', 'ctx')
- input_grad: bfloat16 [8, 512, 2048], P('fsdp', 'ctx')
- grad_query: float32 [2048, 2048], P('fsdp')
- grad_key: float32 [2048, 2048], P('fsdp')
- grad_value: float32 [2048, 2048], P('fsdp')
- grad_out: float32 [2048, 2048], P('fsdp')
- grad_gate: float32 [2048, 5120], P('fsdp')
- grad_up: float32 [2048, 5120], P('fsdp')
- grad_down: float32 [5120, 2048], P('fsdp')
- grad_norm_attn: float32 [2048], P('fsdp')
- grad_norm_ffn: float32 [2048], P('fsdp')
- grad_table: float32 [32, 32], P('fsdp')
Inputs may be any that keep to these rules, and one draw needn't show every extreme that they name: `lengths`: one sequence, drawn from the seed, has all 512 slots live; the others have 512 // 4 to 512.
All inputs are finite; a program needn't handle non-finite values.
Results may differ from a plain program's by a relative error of at most 0.024.
Values may be sent and summed in bfloat16 or wider, within the bound.
No kernel may reach another device: no remote copies, remote signals or barrier semaphores. Data moves between devices by JAX's collectives and lax.ppermute only.
A program may use at most 448 MiB of HBM per device.

v0:
```python
import jax
import jax.numpy as jnp
from jax import lax
from jax.sharding import PartitionSpec as P

bucket_edges = (12, 16, 23, 32, 46, 64, 91)
epsilon = 1e-06
masked_score = -1e30


def shifted(block, axis, distance):
    devices = range(lax.axis_size(axis))
    route = [((i - distance) % len(devices), i) for i in devices]
    return lax.ppermute(block, axis, route)


def buckets_of(offset):
    distance = jnp.abs(offset)
    bucket = jnp.minimum(distance, 8)
    for edge_value in bucket_edges:
        bucket = bucket + (distance >= edge_value).astype(jnp.int32)
    return bucket + 16 * (offset > 0).astype(jnp.int32)


def bucket_onehot(query_slots, key_slots, bucket_total):
    bucket = buckets_of(key_slots[None, :] - query_slots[:, None])
    return (bucket[None] == jnp.arange(bucket_total, dtype=jnp.int32)[:, None, None]).astype(
        jnp.bfloat16
    )


def block_scores(queries, key_heads, gathered_bias_table, bucket_indicator, open_keys):
    raw_scores = jnp.einsum("qhd,khd->hqk", queries, key_heads, preferred_element_type=jnp.float32)
    position_bias_terms = jnp.einsum(
        "pzj,ps->szj", bucket_indicator, gathered_bias_table, preferred_element_type=jnp.float32
    )
    return jnp.where(open_keys[None, None, :], raw_scores + position_bias_terms, masked_score)


def norm_scale(values):
    return lax.rsqrt(jnp.mean(values * values, axis=-1, keepdims=True) + epsilon)


def norm_back(values, scale, gain_row, grad_normed):
    weighted = grad_normed * gain_row
    grad_values = scale * weighted - values * scale**3 * jnp.mean(
        weighted * values, axis=-1, keepdims=True
    )
    grad_gain = jnp.sum(grad_normed * values * scale, axis=0)
    return (grad_values, grad_gain)


def pass_keys(stacked):
    return shifted(stacked, "ctx", 1)


def pass_again(stacked):
    return shifted(stacked, "ctx", 1)


def pass_grads(stacked):
    return shifted(stacked.astype(jnp.bfloat16), "ctx", 1).astype(stacked.dtype)


def on_device(
    inputs,
    lengths,
    w_query,
    w_key,
    w_value,
    w_out,
    w_gate,
    w_up,
    w_down,
    norm_attn,
    norm_ffn,
    relative_bias_table,
    cotangent,
):
    cycle_size = lax.axis_size("ctx")
    position = lax.axis_index("ctx")
    row_count = inputs.shape[1]
    width = inputs.shape[2]
    head_count = relative_bias_table.shape[1]
    head_width = width // head_count
    seq_length = lengths[0]
    seq_inputs = inputs[0].astype(jnp.float32)
    slot_offset = jnp.arange(row_count, dtype=jnp.int32)
    query_slots = position * row_count + slot_offset
    live_rows = (query_slots < seq_length).astype(jnp.float32)[:, None]
    grad_result = cotangent[0].astype(jnp.float32) * live_rows
    full_query, full_key, full_value, full_out, gain_attn, gathered_bias_table = (
        lax.all_gather(w_query, "fsdp", axis=0, tiled=True),
        lax.all_gather(w_key, "fsdp", axis=0, tiled=True),
        lax.all_gather(w_value, "fsdp", axis=0, tiled=True),
        lax.all_gather(w_out, "fsdp", axis=0, tiled=True),
        lax.all_gather(norm_attn, "fsdp", axis=0, tiled=True),
        lax.all_gather(relative_bias_table, "fsdp", axis=0, tiled=True),
    )
    bucket_total = gathered_bias_table.shape[0]
    scale_attn = norm_scale(seq_inputs)
    normed = (seq_inputs * scale_attn * gain_attn.astype(jnp.float32)).astype(jnp.bfloat16)
    queries = (
        jnp.dot(normed, full_query, preferred_element_type=jnp.float32)
        .astype(jnp.bfloat16)
        .reshape(row_count, head_count, head_width)
    )
    key_heads = (
        jnp.dot(normed, full_key, preferred_element_type=jnp.float32)
        .astype(jnp.bfloat16)
        .reshape(row_count, head_count, head_width)
    )
    value_heads = (
        jnp.dot(normed, full_value, preferred_element_type=jnp.float32)
        .astype(jnp.bfloat16)
        .reshape(row_count, head_count, head_width)
    )
    own_pair = jnp.stack([key_heads, value_heads])
    running_top = jnp.full((head_count, row_count, 1), masked_score, jnp.float32)
    running_total = jnp.zeros((head_count, row_count, 1), jnp.float32)
    running_sum = jnp.zeros((head_count, row_count, head_width), jnp.float32)
    stored = []
    current = own_pair
    for turn in range(cycle_size):
        if turn > 0:
            current = pass_keys(current)
        stored.append(current)
        source = (position - turn) % cycle_size
        key_slots = source * row_count + slot_offset
        open_keys = key_slots < seq_length
        bucket_indicator = bucket_onehot(query_slots, key_slots, bucket_total)
        scores = block_scores(queries, current[0], gathered_bias_table, bucket_indicator, open_keys)
        new_top = jnp.maximum(running_top, jnp.max(scores, axis=-1, keepdims=True))
        fading = jnp.exp(running_top - new_top)
        weights = jnp.where(open_keys[None, None, :], jnp.exp(scores - new_top), 0.0)
        running_total = running_total * fading + jnp.sum(weights, axis=-1, keepdims=True)
        running_sum = running_sum * fading + jnp.einsum(
            "hqk,khd->hqd",
            weights.astype(jnp.bfloat16),
            current[1],
            preferred_element_type=jnp.float32,
        )
        running_top = new_top
    attended_exact = jnp.transpose(running_sum / running_total, (1, 0, 2))
    log_total = running_top + jnp.log(running_total)
    attended = attended_exact.reshape(row_count, width).astype(jnp.bfloat16)
    hidden = seq_inputs + jnp.dot(attended, full_out, preferred_element_type=jnp.float32)
    gathered_gate_weight, full_up, full_down, gain_ffn = (
        lax.all_gather(w_gate, "fsdp", axis=0, tiled=True),
        lax.all_gather(w_up, "fsdp", axis=0, tiled=True),
        lax.all_gather(w_down, "fsdp", axis=0, tiled=True),
        lax.all_gather(norm_ffn, "fsdp", axis=0, tiled=True),
    )
    scale_ffn = norm_scale(hidden)
    normed_ffn = (hidden * scale_ffn * gain_ffn.astype(jnp.float32)).astype(jnp.bfloat16)
    gate_proj = jnp.dot(normed_ffn, gathered_gate_weight, preferred_element_type=jnp.float32)
    up_proj = jnp.dot(normed_ffn, full_up, preferred_element_type=jnp.float32)
    activated, gelu_pull = jax.vjp(lambda inner: jax.nn.gelu(inner, approximate=True), gate_proj)
    mixed_units = (activated * up_proj).astype(jnp.bfloat16)
    result = hidden + jnp.dot(mixed_units, full_down, preferred_element_type=jnp.float32)
    gathered_gate_weight, full_up, full_down, gain_ffn = (
        lax.all_gather(w_gate, "fsdp", axis=0, tiled=True),
        lax.all_gather(w_up, "fsdp", axis=0, tiled=True),
        lax.all_gather(w_down, "fsdp", axis=0, tiled=True),
        lax.all_gather(norm_ffn, "fsdp", axis=0, tiled=True),
    )
    gradient_reduced_precision = grad_result.astype(jnp.bfloat16)
    grad_down = jnp.einsum(
        "tf,td->fd", mixed_units, gradient_reduced_precision, preferred_element_type=jnp.float32
    )
    grad_mixed = jnp.einsum(
        "td,fd->tf", gradient_reduced_precision, full_down, preferred_element_type=jnp.float32
    )
    grad_gate_proj = gelu_pull(grad_mixed * up_proj)[0].astype(jnp.bfloat16)
    grad_up_proj = (grad_mixed * activated).astype(jnp.bfloat16)
    grad_gate = jnp.einsum(
        "tc,tf->cf", normed_ffn, grad_gate_proj, preferred_element_type=jnp.float32
    )
    grad_up = jnp.einsum("tc,tf->cf", normed_ffn, grad_up_proj, preferred_element_type=jnp.float32)
    grad_normed_ffn = jnp.einsum(
        "tf,cf->tc", grad_gate_proj, gathered_gate_weight, preferred_element_type=jnp.float32
    )
    grad_normed_ffn = grad_normed_ffn + jnp.einsum(
        "tf,cf->tc", grad_up_proj, full_up, preferred_element_type=jnp.float32
    )
    grad_hidden_norm, grad_gain_ffn = norm_back(
        hidden, scale_ffn, gain_ffn.astype(jnp.float32), grad_normed_ffn
    )
    grad_hidden = grad_result + grad_hidden_norm
    share_gate, share_up, share_down, share_gain_ffn = (
        lax.psum_scatter(
            grad_gate.astype(jnp.bfloat16), "fsdp", scatter_dimension=0, tiled=True
        ).astype(jnp.float32),
        lax.psum_scatter(
            grad_up.astype(jnp.bfloat16), "fsdp", scatter_dimension=0, tiled=True
        ).astype(jnp.float32),
        lax.psum_scatter(
            grad_down.astype(jnp.bfloat16), "fsdp", scatter_dimension=0, tiled=True
        ).astype(jnp.float32),
        lax.psum_scatter(
            grad_gain_ffn.astype(jnp.bfloat16), "fsdp", scatter_dimension=0, tiled=True
        ).astype(jnp.float32),
    )
    full_query, full_key, full_value, full_out, gain_attn, gathered_bias_table = (
        lax.all_gather(w_query, "fsdp", axis=0, tiled=True),
        lax.all_gather(w_key, "fsdp", axis=0, tiled=True),
        lax.all_gather(w_value, "fsdp", axis=0, tiled=True),
        lax.all_gather(w_out, "fsdp", axis=0, tiled=True),
        lax.all_gather(norm_attn, "fsdp", axis=0, tiled=True),
        lax.all_gather(relative_bias_table, "fsdp", axis=0, tiled=True),
    )
    grad_attn_low = grad_hidden.astype(jnp.bfloat16)
    grad_out = jnp.einsum("tc,td->cd", attended, grad_attn_low, preferred_element_type=jnp.float32)
    grad_attended = (
        jnp.einsum("td,cd->tc", grad_attn_low, full_out, preferred_element_type=jnp.float32)
        .astype(jnp.bfloat16)
        .reshape(row_count, head_count, head_width)
    )
    row_delta = jnp.einsum("qhd,qhd->hq", grad_attended.astype(jnp.float32), attended_exact)[
        :, :, None
    ]
    grad_queries = jnp.zeros((row_count, head_count, head_width), jnp.float32)
    grad_table = jnp.zeros((bucket_total, head_count), jnp.float32)
    travelling = jnp.zeros((2, row_count, head_count, head_width), jnp.float32)
    current = own_pair
    for turn in range(cycle_size):
        if turn > 0:
            current = pass_again(current)
        source = (position - turn) % cycle_size
        key_slots = source * row_count + slot_offset
        open_keys = key_slots < seq_length
        bucket_indicator = bucket_onehot(query_slots, key_slots, bucket_total)
        scores = block_scores(queries, current[0], gathered_bias_table, bucket_indicator, open_keys)
        probabilities = jnp.where(open_keys[None, None, :], jnp.exp(scores - log_total), 0.0)
        grad_values_part = jnp.einsum(
            "hqk,qhd->khd",
            probabilities.astype(jnp.bfloat16),
            grad_attended,
            preferred_element_type=jnp.float32,
        )
        grad_probs = jnp.einsum(
            "qhd,khd->hqk", grad_attended, current[1], preferred_element_type=jnp.float32
        )
        score_gradient_matrix = (probabilities * (grad_probs - row_delta)).astype(jnp.bfloat16)
        grad_queries = grad_queries + jnp.einsum(
            "hqk,khd->qhd", score_gradient_matrix, current[0], preferred_element_type=jnp.float32
        )
        grad_keys_part = jnp.einsum(
            "hqk,qhd->khd", score_gradient_matrix, queries, preferred_element_type=jnp.float32
        )
        grad_table = grad_table + jnp.einsum(
            "csp,usp->uc",
            score_gradient_matrix,
            bucket_indicator,
            preferred_element_type=jnp.float32,
        )
        travelling = pass_grads(travelling + jnp.stack([grad_keys_part, grad_values_part]))
    grad_query_rows = grad_queries.reshape(row_count, width).astype(jnp.bfloat16)
    grad_key_rows = travelling[0].reshape(row_count, width).astype(jnp.bfloat16)
    grad_value_rows = travelling[1].reshape(row_count, width).astype(jnp.bfloat16)
    grad_query = jnp.einsum(
        "tc,td->cd", normed, grad_query_rows, preferred_element_type=jnp.float32
    )
    grad_key = jnp.einsum("tc,td->cd", normed, grad_key_rows, preferred_element_type=jnp.float32)
    grad_value = jnp.einsum(
        "tc,td->cd", normed, grad_value_rows, preferred_element_type=jnp.float32
    )
    grad_normed = jnp.einsum(
        "td,cd->tc", grad_query_rows, full_query, preferred_element_type=jnp.float32
    )
    grad_normed = grad_normed + jnp.einsum(
        "td,cd->tc", grad_key_rows, full_key, preferred_element_type=jnp.float32
    )
    grad_normed = grad_normed + jnp.einsum(
        "td,cd->tc", grad_value_rows, full_value, preferred_element_type=jnp.float32
    )
    grad_input_norm, grad_gain_attn = norm_back(
        seq_inputs, scale_attn, gain_attn.astype(jnp.float32), grad_normed
    )
    input_grad = (grad_hidden + grad_input_norm).astype(jnp.bfloat16)[None]
    share_query, share_key, share_value, share_out, share_gain_attn, share_table = (
        lax.psum_scatter(
            grad_query.astype(jnp.bfloat16), "fsdp", scatter_dimension=0, tiled=True
        ).astype(jnp.float32),
        lax.psum_scatter(
            grad_key.astype(jnp.bfloat16), "fsdp", scatter_dimension=0, tiled=True
        ).astype(jnp.float32),
        lax.psum_scatter(
            grad_value.astype(jnp.bfloat16), "fsdp", scatter_dimension=0, tiled=True
        ).astype(jnp.float32),
        lax.psum_scatter(
            grad_out.astype(jnp.bfloat16), "fsdp", scatter_dimension=0, tiled=True
        ).astype(jnp.float32),
        lax.psum_scatter(
            grad_gain_attn.astype(jnp.bfloat16), "fsdp", scatter_dimension=0, tiled=True
        ).astype(jnp.float32),
        lax.psum_scatter(
            grad_table.astype(jnp.bfloat16), "fsdp", scatter_dimension=0, tiled=True
        ).astype(jnp.float32),
    )
    totals = (
        lax.psum(share_query.astype(jnp.bfloat16), "ctx").astype(jnp.float32),
        lax.psum(share_key.astype(jnp.bfloat16), "ctx").astype(jnp.float32),
        lax.psum(share_value.astype(jnp.bfloat16), "ctx").astype(jnp.float32),
        lax.psum(share_out.astype(jnp.bfloat16), "ctx").astype(jnp.float32),
        lax.psum(share_gate.astype(jnp.bfloat16), "ctx").astype(jnp.float32),
        lax.psum(share_up.astype(jnp.bfloat16), "ctx").astype(jnp.float32),
        lax.psum(share_down.astype(jnp.bfloat16), "ctx").astype(jnp.float32),
        lax.psum(share_gain_attn.astype(jnp.bfloat16), "ctx").astype(jnp.float32),
        lax.psum(share_gain_ffn.astype(jnp.bfloat16), "ctx").astype(jnp.float32),
        lax.psum(share_table.astype(jnp.bfloat16), "ctx").astype(jnp.float32),
    )
    return (
        result.astype(jnp.bfloat16)[None],
        input_grad,
        totals[0],
        totals[1],
        totals[2],
        totals[3],
        totals[4],
        totals[5],
        totals[6],
        totals[7],
        totals[8],
        totals[9],
    )


def solution(mesh):
    in_specs = (
        P("fsdp", "ctx", None),
        P("fsdp"),
        P("fsdp", None),
        P("fsdp", None),
        P("fsdp", None),
        P("fsdp", None),
        P("fsdp", None),
        P("fsdp", None),
        P("fsdp", None),
        P("fsdp"),
        P("fsdp"),
        P("fsdp", None),
        P("fsdp", "ctx", None),
    )
    out_specs = (
        P("fsdp", "ctx", None),
        P("fsdp", "ctx", None),
        P("fsdp", None),
        P("fsdp", None),
        P("fsdp", None),
        P("fsdp", None),
        P("fsdp", None),
        P("fsdp", None),
        P("fsdp", None),
        P("fsdp"),
        P("fsdp"),
        P("fsdp", None),
    )
    return jax.shard_map(
        on_device, mesh=mesh, in_specs=in_specs, out_specs=out_specs, check_vma=False
    )
```

profile of v0, /device:TPU:0, one launch (start us, length us, event | category | flops | bytes accessed | tf_op | source)
XLA Modules:
  0.0 2188.8 jit_solution(5084074569234909751)
XLA Ops:
  12.7 13.5 all-gather
  27.1 67.4 %all-gather.13.cloned.1.call-done = bf16[2048,2048]{1,0:T(8,128)(2,1)} async-done(((bf16[256,2048]{1,0:T(8,128)(2,1)}), bf16[2048,2048]{1,0:T(8,128)(2,1)}) %all-gather.13.cloned.1.call-update) | async-done | bytes 8388624 | tf_op jit(solution)/shard_map/all_gather | solution.py:94
  99.4 77.2 %all-gather.15.cloned.1.call-done = bf16[2048,2048]{1,0:T(8,128)(2,1)} async-done(((bf16[256,2048]{1,0:T(8,128)(2,1)}), bf16[2048,2048]{1,0:T(8,128)(2,1)}) %all-gather.15.cloned.1.call-update) | async-done | bytes 8388624 | tf_op jit(solution)/shard_map/all_gather | solution.py:95
  183.3 9.2 all-gather.2
  192.5 11.3 all-gather.1
  212.3 46.6 %all-gather.11.cloned.1.call-done = bf16[2048,2048]{1,0:T(8,128)(2,1)} async-done(((bf16[256,2048]{1,0:T(8,128)(2,1)}), bf16[2048,2048]{1,0:T(8,128)(2,1)}) %all-gather.11.cloned.1.call-update) | async-done | bytes 8388624 | tf_op jit(solution)/shard_map/all_gather | solution.py:93
  274.3 16.3 collective-permute-done.2
  298.5 42.4 %all-gather.17.cloned.1.call-done = bf16[2048,2048]{1,0:T(8,128)(2,1)} async-done(((bf16[256,2048]{1,0:T(8,128)(2,1)}), bf16[2048,2048]{1,0:T(8,128)(2,1)}) %all-gather.17.cloned.1.call-update) | async-done | bytes 8388624 | tf_op jit(solution)/shard_map/all_gather | solution.py:96
  347.9 178.6 %all-gather.19.cloned.1.call-done = bf16[2048,5120]{1,0:T(8,128)(2,1)} async-done(((bf16[256,5120]{1,0:T(8,128)(2,1)}), bf16[2048,5120]{1,0:T(8,128)(2,1)}) %all-gather.19.cloned.1.call-update) | async-done | bytes 20971536 | tf_op jit(solution)/shard_map/all_gather | solution.py:149
  526.5 23.6 %fusion.221 = f32[128,5120]{1,0:T(8,128)} fusion(bf16[128,2048]{1,0:T(8,128)(2,1)} %multiply_convert_fusion.6, bf16[2048,5120]{1,0:T(8,128)(2,1)} %all-gather.19.cloned.1.call-done), kind=kOutput, calls=%fused_computation.317 | convolution fusion | flops 2684354560 | bytes 24117248 | tf_op jit(solution)/shard_map/dot_general | solution.py:156
  550.1 161.6 %all-gather.21.cloned.1.call-done = bf16[2048,5120]{1,0:T(8,128)(2,1)} async-done(((bf16[256,5120]{1,0:T(8,128)(2,1)}), bf16[2048,5120]{1,0:T(8,128)(2,1)}) %all-gather.21.cloned.1.call-update) | async-done | bytes 20971536 | tf_op jit(solution)/shard_map/all_gather | solution.py:150
  711.7 11.9 fusion.222
  723.7 173.4 %all-gather.23.cloned.1.call-done = bf16[5120,2048]{1,0:T(8,128)(2,1)} async-done(((bf16[640,2048]{1,0:T(8,128)(2,1)}), bf16[5120,2048]{1,0:T(8,128)(2,1)}) %all-gather.23.cloned.1.call-update) | async-done | bytes 20971536 | tf_op jit(solution)/shard_map/all_gather | solution.py:151
  897.1 14.9 multiply_convert_fusion
  912.0 11.6 fusion.223
  923.7 11.6 multiply_reduce_fusion
  979.9 23.0 %collective-permute-done.3 = bf16[2,128,32,64]{1,3,2,0:T(8,128)(2,1)S(1)} collective-permute-done((bf16[2,128,32,64]{1,3,2,0:T(8,128)(2,1)S(1)}, bf16[2,128,32,64]{1,3,2,0:T(8,128)(2,1)S(1)}, u32[]{:S(2)}, u32[]{:S(2)}) %collective-permute-start.3) | collective-permute-done | bytes 1048608 | tf_op jit(solution)/shard_map/ppermute | solution.py:14
  1005.7 23.2 %collective-permute-done.4 = bf16[2,128,32,64]{1,3,2,0:T(8,128)(2,1)S(1)} collective-permute-done((bf16[2,128,32,64]{1,3,2,0:T(8,128)(2,1)S(1)}, bf16[2,128,32,64]{1,3,2,0:T(8,128)(2,1)S(1)}, u32[]{:S(2)}, u32[]{:S(2)}) %collective-permute-start.4) | collective-permute-done | bytes 1048608 | tf_op jit(solution)/shard_map/ppermute | solution.py:14
  1031.8 22.2 %collective-permute-done.5 = bf16[2,128,32,64]{1,3,2,0:T(8,128)(2,1)S(1)} collective-permute-done((bf16[2,128,32,64]{1,3,2,0:T(8,128)(2,1)S(1)}, bf16[2,128,32,64]{1,3,2,0:T(8,128)(2,1)S(1)}, u32[]{:S(2)}, u32[]{:S(2)}) %collective-permute-start.5) | collective-permute-done | bytes 1048608 | tf_op jit(solution)/shard_map/ppermute | solution.py:14
  1054.4 23.8 %collective-permute-done.6 = bf16[2,128,32,64]{1,3,2,0:T(8,128)(2,1)S(1)} collective-permute-done((bf16[2,128,32,64]{1,3,2,0:T(8,128)(2,1)S(1)}, bf16[2,128,32,64]{1,3,2,0:T(8,128)(2,1)S(1)}, u32[]{:S(2)}, u32[]{:S(2)}) %collective-permute-start.6) | collective-permute-done | bytes 1048608 | tf_op jit(solution)/shard_map/ppermute | solution.py:14
  1092.2 10.1 convolution_convert_fusion.2
  1103.6 10.0 convolution_convert_fusion.1
  1115.1 10.1 convolution_convert_fusion
  1125.5 85.3 %reduce-scatter.10.cloned.1.call-done = bf16[256,2048]{1,0:T(8,128)(2,1)} async-done(((bf16[2048,2048]{1,0:T(8,128)(2,1)}), bf16[256,2048]{1,0:T(8,128)(2,1)}) %reduce-scatter.10.cloned.1.call-update) | async-done | bytes 1048592 | tf_op jit(solution)/shard_map/reduce_scatter | solution.py:285
  1210.7 90.3 %reduce-scatter.12.cloned.1.call-done = bf16[256,2048]{1,0:T(8,128)(2,1)} async-done(((bf16[2048,2048]{1,0:T(8,128)(2,1)}), bf16[256,2048]{1,0:T(8,128)(2,1)}) %reduce-scatter.12.cloned.1.call-update) | async-done | bytes 1048592 | tf_op jit(solution)/shard_map/reduce_scatter | solution.py:288
  1301.0 208.3 %reduce-scatter.16.cloned.1.call-done = bf16[256,5120]{1,0:T(8,128)(2,1)} async-done(((bf16[2048,5120]{1,0:T(8,128)(2,1)}), bf16[256,5120]{1,0:T(8,128)(2,1)}) %reduce-scatter.16.cloned.1.call-update) | async-done | bytes 2621456 | tf_op jit(solution)/shard_map/reduce_scatter | solution.py:191
  1509.3 208.4 %reduce-scatter.18.cloned.1.call-done = bf16[256,5120]{1,0:T(8,128)(2,1)} async-done(((bf16[2048,5120]{1,0:T(8,128)(2,1)}), bf16[256,5120]{1,0:T(8,128)(2,1)}) %reduce-scatter.18.cloned.1.call-update) | async-done | bytes 2621456 | tf_op jit(solution)/shard_map/reduce_scatter | solution.py:194
  1717.8 208.3 %reduce-scatter.20.cloned.1.call-done = bf16[640,2048]{1,0:T(8,128)(2,1)} async-done(((bf16[5120,2048]{1,0:T(8,128)(2,1)}), bf16[640,2048]{1,0:T(8,128)(2,1)}) %reduce-scatter.20.cloned.1.call-update) | async-done | bytes 2621456 | tf_op jit(solution)/shard_map/reduce_scatter | solution.py:197
  1941.4 11.6 fusion.8
  1959.2 25.9 %all-reduce.3 = (bf16[2048]{0:T(1024)(128)(2,1)S(1)}, bf16[2048]{0:T(1024)(128)(2,1)S(1)}, bf16[32,32]{1,0:T(8,128)(2,1)S(1)}) all-reduce(bf16[2048]{0:T(1024)(128)(2,1)S(1)} %get-tuple-element.14, bf16[2048]{0:T(1024)(128)(2,1)S(1)} %get-tuple-element.12, ...), channel_id=9, replica_groups=mesh['ctx'=4,'fsdp'=8] {'fsdp'}, use_global_device_ids=true, to_apply=%region_27.28.clone | all-reduce | flops 5120 | bytes 20480
  1985.3 10.0 all-reduce.4
  1998.3 166.4 %all-reduce.8.cloned.1.call-done = (bf16[256,2048]{1,0:T(8,128)(2,1)}, bf16[256,2048]{1,0:T(8,128)(2,1)}, bf16[256,2048]{1,0:T(8,128)(2,1)}, bf16[256,2048]{1,0:...) async-done(((bf16[256,2048]{1,0:T(8,128)(2,1)}, bf16[256,2048]{1,0:T(8,128)(2,1)}, bf16[256,2048]{1,0:T(8,128)(2,1)}, ...) | async-done | bytes 12058640 | tf_op jit(solution)/shard_map/psum | solution.py:302
  (282 shorter events, 163.0 us)
Async XLA Ops:
  7.2 87.2 %all-gather.13.cloned.1.call-start = ((), (), s32[]{:S(2)}) async-start(), calls=%async_computation.8 | async-start | bytes 9437184 | tf_op jit(solution)/shard_map/all_gather | solution.py:94
  7.9 168.7 %all-gather.15.cloned.1.call-start = ((), (), s32[]{:S(2)}) async-start(), calls=%async_computation.9 | async-start | bytes 9437184 | tf_op jit(solution)/shard_map/all_gather | solution.py:95
  8.7 250.3 %all-gather.11.cloned.1.call-start = ((), (), s32[]{:S(2)}) async-start(), calls=%async_computation.7 | async-start | bytes 9437184 | tf_op jit(solution)/shard_map/all_gather | solution.py:93
  9.4 331.6 %all-gather.17.cloned.1.call-start = ((), (), s32[]{:S(2)}) async-start(), calls=%async_computation.10 | async-start | bytes 9437184 | tf_op jit(solution)/shard_map/all_gather | solution.py:96
  10.0 516.5 %all-gather.19.cloned.1.call-start = ((), (), s32[]{:S(2)}) async-start(), calls=%async_computation.11 | async-start | bytes 23592960 | tf_op jit(solution)/shard_map/all_gather | solution.py:149
  10.6 701.1 %all-gather.21.cloned.1.call-start = ((), (), s32[]{:S(2)}) async-start(), calls=%async_computation.12 | async-start | bytes 23592960 | tf_op jit(solution)/shard_map/all_gather | solution.py:150
  11.2 885.9 %all-gather.23.cloned.1.call-start = ((), (), s32[]{:S(2)}) async-start(), calls=%async_computation.13 | async-start | bytes 23592960 | tf_op jit(solution)/shard_map/all_gather | solution.py:151
  11.9 1113.5 %reduce-scatter.14.cloned.1.call-start = ((), (), s32[]{:S(2)}) async-start(), calls=%async_computation.17 | async-start | bytes 9437184 | tf_op jit(solution)/shard_map/reduce_scatter | solution.py:291
  99.4 82.3 %copy-start.29 = (bf16[128,2048]{0,1:T(8,128)(2,1)}, bf16[128,2048]{0,1:T(8,128)(2,1)S(1)}, u32[]{:S(2)}) copy-start(bf16[128,2048]{0,1:T(8,128)(2,1)S(1)} %copy.123) | copy-start | bytes 1572868
  181.6 24.4 %copy-start.27 = (bf16[128,2048]{0,1:T(8,128)(2,1)}, bf16[128,2048]{0,1:T(8,128)(2,1)S(1)}, u32[]{:S(2)}) copy-start(bf16[128,2048]{0,1:T(8,128)(2,1)S(1)} %copy.126) | copy-start | bytes 1572868
  181.8 26.3 %collective-permute-start = (bf16[2,128,32,64]{1,3,2,0:T(8,128)(2,1)S(1)}, bf16[2,128,32,64]{1,3,2,0:T(8,128)(2,1)S(1)}, u32[]{:S(2)}, u32[]{:S(2)}) collective-permute-start(bf16[2,128,32,64]{1,3,2,0:T(8,128)(2,1)S(1)} %pad_maximum_fusion), channel_id=1, source_target_pairs={{24,0},{0,8},{8,16},{16,24},{25,1},{1,9},{9,17},{17,25},{26,2},{2,... | collective-permute-start | bytes 3145736 | tf_op jit(solution)/shard_map/ppermute | solution.py:14
  208.0 55.9 %collective-permute-start.1 = (bf16[2,128,32,64]{1,3,2,0:T(8,128)(2,1)S(1)}, bf16[2,128,32,64]{1,3,2,0:T(8,128)(2,1)}, u32[]{:S(2)}, u32[]{:S(2)}) collective-permute-start(bf16[2,128,32,64]{1,3,2,0:T(8,128)(2,1)S(1)} %collective-permute-done), channel_id=1, source_target_pairs={{24,0},{0,8},{8,16},{16,24},{25,1},{1,9},{9,17},{17,25},{26,2},{2,... | collective-permute-start | bytes 3145736 | tf_op jit(solution)/shard_map/ppermute | solution.py:14
  263.9 26.7 %collective-permute-start.2 = (bf16[2,128,32,64]{1,3,2,0:T(8,128)(2,1)}, bf16[2,128,32,64]{1,3,2,0:T(8,128)(2,1)S(1)}, u32[]{:S(2)}, u32[]{:S(2)}) collective-permute-start(bf16[2,128,32,64]{1,3,2,0:T(8,128)(2,1)} %collective-permute-done.1), channel_id=1, source_target_pairs={{24,0},{0,8},{8,16},{16,24},{25,1},{1,9},{9,17},{17,25},{26,2},{2,... | collective-permute-start | bytes 3145736 | tf_op jit(solution)/shard_map/ppermute | solution.py:14
  271.1 23.6 %copy-start.4 = (f32[32,128,128]{1,2,0:T(8,128)}, f32[32,128,128]{1,2,0:T(8,128)S(1)}, u32[]{:S(2)}) copy-start(f32[32,128,128]{1,2,0:T(8,128)S(1)} %get-tuple-element.56) | copy-start | bytes 6291460
  271.1 19.5 copy-start.24
  274.3 20.9 copy-start.1
  942.4 183.1 %reduce-scatter.8.cloned.1.call-start = ((), (), s32[]{:S(2)}) async-start(), calls=%async_computation.14 | async-start | bytes 9437184 | tf_op jit(solution)/shard_map/reduce_scatter | solution.py:282
  973.4 237.4 %reduce-scatter.10.cloned.1.call-start = ((), (), s32[]{:S(2)}) async-start(), calls=%async_computation.15 | async-start | bytes 9437184 | tf_op jit(solution)/shard_map/reduce_scatter | solution.py:285
  976.6 26.3 %collective-permute-start.3 = (bf16[2,128,32,64]{1,3,2,0:T(8,128)(2,1)S(1)}, bf16[2,128,32,64]{1,3,2,0:T(8,128)(2,1)S(1)}, u32[]{:S(2)}, u32[]{:S(2)}) collective-permute-start(bf16[2,128,32,64]{1,3,2,0:T(8,128)(2,1)S(1)} %pad_maximum_fusion.1), channel_id=1, source_target_pairs={{24,0},{0,8},{8,16},{16,24},{25,1},{1,9},{9,17},{17,25},{26,2},{2,... | collective-permute-start | bytes 3145736 | tf_op jit(solution)/shard_map/ppermute | solution.py:14
  979.9 24.1 %copy-start.39 = (bf16[32,128,128]{1,2,0:T(8,128)(2,1)S(1)}, bf16[32,128,128]{1,2,0:T(8,128)(2,1)}, u32[]{:S(2)}) copy-start(bf16[32,128,128]{1,2,0:T(8,128)(2,1)} %copy-done.38) | copy-start | bytes 3145732
  1003.2 25.7 %collective-permute-start.4 = (bf16[2,128,32,64]{1,3,2,0:T(8,128)(2,1)S(1)}, bf16[2,128,32,64]{1,3,2,0:T(8,128)(2,1)S(1)}, u32[]{:S(2)}, u32[]{:S(2)}) collective-permute-start(bf16[2,128,32,64]{1,3,2,0:T(8,128)(2,1)S(1)} %fusion.9), channel_id=1, source_target_pairs={{24,0},{0,8},{8,16},{16,24},{25,1},{1,9},{9,17},{17,25},{26,2},{2,... | collective-permute-start | bytes 3145736 | tf_op jit(solution)/shard_map/ppermute | solution.py:14
  1005.7 23.6 %copy-start.42 = (bf16[32,128,128]{1,2,0:T(8,128)(2,1)S(1)}, bf16[32,128,128]{1,2,0:T(8,128)(2,1)}, u32[]{:S(2)}) copy-start(bf16[32,128,128]{1,2,0:T(8,128)(2,1)} %copy-done.41) | copy-start | bytes 3145732
  1029.3 24.7 %collective-permute-start.5 = (bf16[2,128,32,64]{1,3,2,0:T(8,128)(2,1)S(1)}, bf16[2,128,32,64]{1,3,2,0:T(8,128)(2,1)S(1)}, u32[]{:S(2)}, u32[]{:S(2)}) collective-permute-start(bf16[2,128,32,64]{1,3,2,0:T(8,128)(2,1)S(1)} %fusion.10), channel_id=1, source_target_pairs={{24,0},{0,8},{8,16},{16,24},{25,1},{1,9},{9,17},{17,25},{26,2},{2,... | collective-permute-start | bytes 3145736 | tf_op jit(solution)/shard_map/ppermute | solution.py:14
  1054.4 23.9 %collective-permute-start.6 = (bf16[2,128,32,64]{1,3,2,0:T(8,128)(2,1)S(1)}, bf16[2,128,32,64]{1,3,2,0:T(8,128)(2,1)S(1)}, u32[]{:S(2)}, u32[]{:S(2)}) collective-permute-start(bf16[2,128,32,64]{1,3,2,0:T(8,128)(2,1)S(1)} %fusion.11), channel_id=1, source_target_pairs={{24,0},{0,8},{8,16},{16,24},{25,1},{1,9},{9,17},{17,25},{26,2},{2,... | collective-permute-start | bytes 3145736 | tf_op jit(solution)/shard_map/ppermute | solution.py:14
  1084.8 216.2 %reduce-scatter.12.cloned.1.call-start = ((), (), s32[]{:S(2)}) async-start(), calls=%async_computation.16 | async-start | bytes 9437184 | tf_op jit(solution)/shard_map/reduce_scatter | solution.py:288
  1090.7 418.6 %reduce-scatter.16.cloned.1.call-start = ((), (), s32[]{:S(2)}) async-start(), calls=%async_computation.18 | async-start | bytes 23592960 | tf_op jit(solution)/shard_map/reduce_scatter | solution.py:191
  1102.3 615.5 %reduce-scatter.18.cloned.1.call-start = ((), (), s32[]{:S(2)}) async-start(), calls=%async_computation.19 | async-start | bytes 23592960 | tf_op jit(solution)/shard_map/reduce_scatter | solution.py:194
  1113.7 812.4 %reduce-scatter.20.cloned.1.call-start = ((), (), s32[]{:S(2)}) async-start(), calls=%async_computation.20 | async-start | bytes 23592960 | tf_op jit(solution)/shard_map/reduce_scatter | solution.py:197
  1125.2 1039.5 %all-reduce.8.cloned.1.call-start = ((), (), s32[]{:S(2)}) async-start(), calls=%async_computation.21 | async-start | bytes 24117248 | tf_op jit(solution)/shard_map/psum | solution.py:302
  1934.6 21.3 slice-start.2
  1955.9 41.2 %copy-start.16 = (f32[128,2048]{1,0:T(8,128)S(1)}, f32[128,2048]{1,0:T(8,128)}, u32[]{:S(2)}) copy-start(f32[128,2048]{1,0:T(8,128)} %copy-done.15) | copy-start | bytes 3145732
  1955.9 41.2 %copy-start.65 = (f32[128]{0:T(128)S(1)}, f32[128]{0:T(128)}, u32[]{:S(2)}) copy-start(f32[128]{0:T(128)} %get-tuple-element.43) | copy-start | bytes 1540
  (62 other events, 261.8 us)
Sparse Core Ops, SparseCore 0:
  9.6 84.7 all-gather.12
  96.0 80.5 all-gather.14
  178.2 80.6 all-gather.10
  260.4 80.5 all-gather.16
  342.5 184.0 all-gather.18
  528.0 183.6 all-gather.20
  713.4 183.6 all-gather.22
  942.5 87.7 reduce-scatter.13
  1032.6 87.9 reduce-scatter.7
  1122.8 87.9 reduce-scatter.9
  1213.0 87.9 reduce-scatter.11
  1303.2 206.0 reduce-scatter.15
  1511.7 206.0 reduce-scatter.17
  1720.0 206.0 reduce-scatter.19
  1930.7 233.8 all-reduce.7
where the time goes:
time: 2200 us; the launch traced here: 2190 us
  waiting for transfers between devices  1830 us (83%)
  matrix products  222 us (10%)
  blocking collectives  70 us (3%)
  other arithmetic  27.2 us (1%)
    reduce_scatter x1, waiting for transfers between devices, on_device(): lax.psum_scatter(grad_up.astype(jnp.bfloat16), 'fsdp', scatter_dimension=...  208 us
    reduce_scatter x1, waiting for transfers between devices, on_device(): lax.psum_scatter(grad_down.astype(jnp.bfloat16), 'fsdp', scatter_dimensio...  208 us
    reduce_scatter x1, waiting for transfers between devices, on_device(): lax.psum_scatter(grad_gate.astype(jnp.bfloat16), 'fsdp', scatter_dimensio...  208 us
    all_gather x1, waiting for transfers between devices, on_device(): lax.all_gather(w_gate, 'fsdp', axis=0, tiled=True)  179 us
    all_gather x1, waiting for transfers between devices, on_device(): lax.all_gather(w_down, 'fsdp', axis=0, tiled=True)  173 us
    psum x1, waiting for transfers between devices, on_device(): lax.psum(share_query.astype(jnp.bfloat16), 'ctx').astype(jnp.float32)  166 us
    all_gather x1, waiting for transfers between devices, on_device(): lax.all_gather(w_up, 'fsdp', axis=0, tiled=True)  162 us
    ppermute x7, waiting for transfers between devices, shifted(): return lax.ppermute(block, axis, route)  109 us
  transfers between devices with their start and end apart: 22, of which 19 were waited for; matrix products, arithmetic and copies ran while one was open for 9% of the time, Pallas kernels for 0%

commit v1 on v0

v1 whole, which is shorter than its diff:
```python
import functools

import jax
import jax.numpy as jnp
from jax import lax
from jax.experimental import pallas as pl
from jax.experimental.pallas import tpu as pltpu
from jax.sharding import PartitionSpec as P

bucket_edges = (12, 16, 23, 32, 46, 64, 91)
epsilon = 1e-06
masked_score = -1e30
f32 = jnp.float32
bf16 = jnp.bfloat16
vmem_limit = 48 * 1024 * 1024


def dot(a, b, ca=1, cb=0):
    return lax.dot_general(a, b, (((ca,), (cb,)), ((), ())), preferred_element_type=f32)


def buckets_of(offset):
    distance = jnp.abs(offset)
    bucket = jnp.minimum(distance, 8)
    for edge_value in bucket_edges:
        bucket = bucket + (distance >= edge_value).astype(jnp.int32)
    return bucket + 16 * (offset > 0).astype(jnp.int32)


def core_swap(a):
    size = lax.axis_size("fsdp")
    return lax.ppermute(a, "fsdp", [(r, r ^ 1) for r in range(size)])


def chip_send(a, pairs):
    return lax.ppermute(a, "fsdp", [(2 * s + k, 2 * d + k) for s, d in pairs for k in range(2)])


def ctx_send(a, distance):
    size = lax.axis_size("ctx")
    return lax.ppermute(a, "ctx", [(i, i ^ distance) for i in range(size)])


def chip_gather(own, chip):
    chips = lax.axis_size("fsdp") // 2
    if chips == 4:
        above = chip_send(own, [(1, 0), (2, 1), (3, 2), (0, 3)])
        below = chip_send(own, [(0, 1), (1, 2), (2, 3), (3, 0)])
        middle = jnp.where(chip == 1, above, jnp.where(chip == 2, below, own))
        far = chip_send(middle, [(3, 1), (0, 2), (1, 0), (2, 3)])
        return [own, above, far, below]
    return [own] + [
        chip_send(own, [((z + t) % chips, z) for z in range(chips)]) for t in range(1, chips)
    ]


def chip_reduce(slots, chip):
    chips = lax.axis_size("fsdp") // 2
    if chips == 4:
        far = chip_send(slots[2], [(0, 1), (3, 2), (1, 3), (2, 0)]).astype(f32)
        zero = jnp.zeros((), f32)
        up = (slots[1].astype(f32) + jnp.where(chip == 1, far, zero)).astype(bf16)
        down = (slots[3].astype(f32) + jnp.where(chip == 2, far, zero)).astype(bf16)
        ends = jnp.where((chip == 0) | (chip == 3), far, zero)
        from_below = chip_send(up, [(0, 1), (1, 2), (2, 3), (3, 0)])
        from_above = chip_send(down, [(1, 0), (2, 1), (3, 2), (0, 3)])
        return slots[0].astype(f32) + ends + from_below.astype(f32) + from_above.astype(f32)
    total = slots[0].astype(f32)
    for t in range(1, chips):
        total = total + chip_send(slots[t], [(z, (z + t) % chips) for z in range(chips)]).astype(f32)
    return total


def weight_gather(own, chip):
    slots = chip_gather(own, chip)
    return slots + [core_swap(s) for s in slots]


def weight_reduce(mine, other, chip):
    total = (mine.astype(f32) + core_swap(other).astype(f32)).astype(bf16)
    return chip_reduce([total[t] for t in range(total.shape[0])], chip).astype(bf16)


def ctx_gather(a):
    return [a] + [ctx_send(a, t) for t in range(1, lax.axis_size("ctx"))]


def ctx_reduce(partial, rows):
    total = partial[:rows].astype(f32)
    for t in range(1, lax.axis_size("ctx")):
        total = total + ctx_send(partial[t * rows : (t + 1) * rows], t).astype(f32)
    return total


def take_blocks(a, axis, starts, size):
    return jnp.concatenate([lax.dynamic_slice_in_dim(a, s, size, axis) for s in starts], axis)


def forward_kernel(rows, blocks, scal_ref, qkv_ref, bias_ref, att_ref, prob_ref, toeplitz_ref):
    position, length = scal_ref[0], scal_ref[1]
    width = 2 * blocks * rows
    lane = lax.broadcasted_iota(jnp.int32, (1, rows), 1)
    open_keys = jnp.concatenate(
        [((position ^ t) * rows + lane) < length for t in range(blocks)], axis=1
    )
    for j in range(2):
        row = jnp.broadcast_to(bias_ref[0, j : j + 1, :], (rows, width))
        toeplitz_ref[j] = pltpu.roll(row, width - rows, 1, stride=1, stride_axis=0)
    for t in range(blocks):
        halves = []
        at = slice(t * rows, (t + 1) * rows)
        for j in range(2):
            q = qkv_ref[at, 64 * j : 64 * j + 64]
            k = qkv_ref[:, 128 + 64 * j : 192 + 64 * j]
            v = qkv_ref[:, 256 + 64 * j : 320 + 64 * j]
            bias = jnp.concatenate(
                [
                    toeplitz_ref[
                        j,
                        :,
                        pl.ds(
                            pl.multiple_of(
                                (blocks - 1 + (position ^ s) - (position ^ t)) * rows, rows
                            ),
                            rows,
                        ),
                    ]
                    for s in range(blocks)
                ],
                axis=1,
            )
            scores = jnp.where(open_keys, dot(q, k, 1, 1) + bias, masked_score)
            top = jnp.max(scores, axis=1, keepdims=True)
            e = jnp.exp(scores - top)
            probs = (e * (1.0 / jnp.sum(e, axis=1, keepdims=True))).astype(bf16)
            prob_ref[j, at, :] = probs
            halves.append(dot(probs, v))
        att_ref[at, :] = jnp.concatenate(halves, axis=1).astype(bf16)


def backward_kernel(
    rows, blocks, scal_ref, qkv_ref, prob_ref, gatt_ref, out_ref, diag_ref, fold_ref
):
    position = scal_ref[0]
    width = 2 * blocks * rows
    results = [[], [], []]
    for j in range(2):
        fold_ref[...] = jnp.zeros_like(fold_ref)
        k = qkv_ref[:, 128 + 64 * j : 192 + 64 * j]
        v = qkv_ref[:, 256 + 64 * j : 320 + 64 * j]
        grad_q, grad_k, grad_v = [], None, None
        for t in range(blocks):
            at = slice(t * rows, (t + 1) * rows)
            q = qkv_ref[at, 64 * j : 64 * j + 64]
            g = gatt_ref[at, 64 * j : 64 * j + 64]
            probs = prob_ref[j, at, :]
            p = probs.astype(f32)
            gp = dot(g, v, 1, 1)
            pg = p * gp
            delta = jnp.sum(pg, axis=1, keepdims=True)
            ds = (pg - p * delta).astype(bf16)
            grad_q.append(dot(ds, k))
            gk = dot(ds, q, 0, 0)
            gv = dot(probs, g, 0, 0)
            grad_k = gk if grad_k is None else grad_k + gk
            grad_v = gv if grad_v is None else grad_v + gv
            ds32 = ds.astype(f32)
            for s in range(blocks):
                lanes = pl.ds(
                    pl.multiple_of((blocks - 1 + (position ^ s) - (position ^ t)) * rows, rows),
                    rows,
                )
                fold_ref[:, lanes] += ds32[:, s * rows : (s + 1) * rows]
        results[0].append(jnp.concatenate(grad_q, axis=0))
        results[1].append(grad_k)
        results[2].append(grad_v)
        a = fold_ref[...]
        half = rows // 2
        while half >= 8:
            a = a[:half] + pltpu.roll(a[half:], width - half, 1)
            half //= 2
        row = lax.broadcasted_iota(jnp.int32, a.shape, 0)
        for bit in (1, 2, 4):
            a = jnp.where((row & bit) != 0, pltpu.roll(a, width - bit, 1), a)
        diag_ref[0, j : j + 1, :] = jnp.sum(a, axis=0, keepdims=True)
    for n in range(3):
        out_ref[:, 128 * n : 128 * n + 128] = jnp.concatenate(results[n], axis=1).astype(bf16)


def attention_forward(scal, qkv, bias, rows, blocks):
    tokens = rows * blocks
    pairs = bias.shape[0]
    return pl.pallas_call(
        functools.partial(forward_kernel, rows, blocks),
        grid=(pairs,),
        in_specs=[
            pl.BlockSpec(memory_space=pltpu.SMEM),
            pl.BlockSpec((tokens, 384), lambda p: (0, p)),
            pl.BlockSpec((1, 2, 2 * tokens), lambda p: (p, 0, 0)),
        ],
        out_specs=[
            pl.BlockSpec((tokens, 128), lambda p: (0, p)),
            pl.BlockSpec((2, tokens, tokens), lambda p: (p, 0, 0)),
        ],
        out_shape=[
            jax.ShapeDtypeStruct((tokens, 128 * pairs), bf16),
            jax.ShapeDtypeStruct((2 * pairs, tokens, tokens), bf16),
        ],
        scratch_shapes=[pltpu.VMEM((2, rows, 2 * tokens), f32)],
        compiler_params=pltpu.CompilerParams(vmem_limit_bytes=vmem_limit),
        cost_estimate=pl.CostEstimate(
            flops=8 * pairs * tokens * tokens * 64,
            bytes_accessed=4 * pairs * tokens * tokens,
            transcendentals=2 * pairs * tokens * tokens,
        ),
    )(scal, qkv, bias)


def attention_backward(scal, qkv, probs, grad_att, rows, blocks):
    tokens = rows * blocks
    pairs = probs.shape[0] // 2
    return pl.pallas_call(
        functools.partial(backward_kernel, rows, blocks),
        grid=(pairs,),
        in_specs=[
            pl.BlockSpec(memory_space=pltpu.SMEM),
            pl.BlockSpec((tokens, 384), lambda p: (0, p)),
            pl.BlockSpec((2, tokens, tokens), lambda p: (p, 0, 0)),
            pl.BlockSpec((tokens, 128), lambda p: (0, p)),
        ],
        out_specs=[
            pl.BlockSpec((tokens, 384), lambda p: (0, p)),
            pl.BlockSpec((1, 2, 2 * tokens), lambda p: (p, 0, 0)),
        ],
        out_shape=[
            jax.ShapeDtypeStruct((tokens, 384 * pairs), bf16),
            jax.ShapeDtypeStruct((pairs, 2, 2 * tokens), f32),
        ],
        scratch_shapes=[pltpu.VMEM((rows, 2 * tokens), f32)],
        compiler_params=pltpu.CompilerParams(vmem_limit_bytes=vmem_limit),
        cost_estimate=pl.CostEstimate(
            flops=16 * pairs * tokens * tokens * 64,
            bytes_accessed=4 * pairs * tokens * tokens,
            transcendentals=0,
        ),
    )(scal, qkv, probs, grad_att)


def norm_scale(values):
    return lax.rsqrt(jnp.mean(values * values, axis=-1, keepdims=True) + epsilon)


def norm_back(values, scale, gain_row, grad_normed):
    weighted = grad_normed * gain_row
    grad_values = scale * weighted - values * scale**3 * jnp.mean(
        weighted * values, axis=-1, keepdims=True
    )
    grad_gain = jnp.sum(grad_normed * values * scale, axis=0)
    return grad_values, grad_gain


def on_device(
    inputs,
    lengths,
    w_query,
    w_key,
    w_value,
    w_out,
    w_gate,
    w_up,
    w_down,
    norm_attn,
    norm_ffn,
    relative_bias_table,
    cotangent,
):
    blocks = lax.axis_size("ctx")
    shards = lax.axis_size("fsdp")
    chips = shards // 2
    position = lax.axis_index("ctx")
    shard = lax.axis_index("fsdp")
    chip, core = shard // 2, shard % 2
    rows, width = inputs.shape[1], inputs.shape[2]
    tokens = rows * blocks
    heads = relative_bias_table.shape[1]
    head_width = width // heads
    my_heads = heads // blocks
    pairs = my_heads // 2
    strided = (heads // shards) % blocks == 0
    units = w_gate.shape[1] // blocks
    shard_rows = width // shards
    unit_rows = w_down.shape[0] // blocks
    length = lengths[0]
    scal = jnp.stack([position, length]).astype(jnp.int32)

    order = [2 * ((chip + t) % chips) + (core ^ p) for p in range(2) for t in range(chips)]
    place = [((r & 1) ^ core) * chips + ((r >> 1) - chip) % chips for r in range(shards)]

    if strided:
        each = heads // shards // blocks
        local = jnp.arange(my_heads, dtype=jnp.int32)
        my_head_ids = (local // each) * (heads // shards) + position * each + local % each
    else:
        my_head_ids = position * my_heads + jnp.arange(my_heads, dtype=jnp.int32)
    head_columns = (
        my_head_ids[:, None] * head_width + jnp.arange(head_width, dtype=jnp.int32)
    ).reshape(-1)
    per_shard = w_down.shape[0]
    local = jnp.arange(units, dtype=jnp.int32)
    unit_columns = (local // unit_rows) * per_shard + position * unit_rows + local % unit_rows

    def select(stacked, columns):
        chosen = jnp.arange(stacked.shape[-1], dtype=jnp.int32)[:, None] == columns[None, :]
        flat = stacked.reshape(-1, stacked.shape[-1])
        picked = jnp.dot(flat, chosen.astype(bf16), preferred_element_type=f32).astype(bf16)
        return picked.reshape(*stacked.shape[:-1], columns.shape[0])

    picked = select(jnp.stack([w_query, w_key, w_value]), head_columns)
    own_qkv = jnp.transpose(picked.reshape(3, shard_rows, pairs, 128), (1, 2, 0, 3)).reshape(
        shard_rows, pairs * 384
    )
    small = jnp.concatenate([norm_attn, norm_ffn, relative_bias_table.reshape(-1)])[None]

    own_x = take_blocks(inputs[0], 1, [o * shard_rows for o in order], shard_rows)
    all_x = jnp.concatenate(ctx_gather(own_x), axis=0)
    query_slots = position * rows + jnp.arange(rows, dtype=jnp.int32)
    live_rows = (query_slots < length).astype(f32)[:, None]
    own_dy = (cotangent[0].astype(f32) * live_rows).astype(bf16)
    all_dy = jnp.concatenate(ctx_gather(own_dy), axis=0)

    all_small = jnp.concatenate(weight_gather(small, chip), axis=0)
    full_qkv = jnp.concatenate(weight_gather(own_qkv, chip), axis=0)
    if strided:
        head_rows = w_out.shape[0] // blocks
        own_out = lax.dynamic_slice_in_dim(w_out, position * head_rows, head_rows, 0)
        full_out = take_blocks(
            jnp.concatenate(weight_gather(own_out, chip), axis=0),
            0,
            [p * head_rows for p in place],
            head_rows,
        )
    else:
        full_out = lax.dynamic_slice_in_dim(
            lax.all_gather(w_out, "fsdp", axis=0, tiled=True),
            position * my_heads * head_width,
            my_heads * head_width,
            0,
        )
    picked = select(jnp.stack([w_gate, w_up]), unit_columns)
    own_gate_up = jnp.concatenate([picked[0], picked[1]], axis=1)
    full_gate_up = jnp.concatenate(weight_gather(own_gate_up, chip), axis=0)
    own_down = lax.dynamic_slice_in_dim(w_down, position * unit_rows, unit_rows, 0)
    full_down = take_blocks(
        jnp.concatenate(weight_gather(own_down, chip), axis=0),
        0,
        [p * unit_rows for p in place],
        unit_rows,
    )

    gain_local = all_small[:, :shard_rows].astype(f32).reshape(1, width)
    natural = jnp.concatenate(
        [lax.dynamic_slice_in_dim(all_small, p, 1, 0) for p in place], axis=0
    )
    gain_ffn = natural[:, shard_rows : 2 * shard_rows].astype(f32).reshape(1, width)
    table = natural[:, 2 * shard_rows :].reshape(-1, heads)
    bucket_total = table.shape[0]

    chosen_heads = (jnp.arange(heads, dtype=jnp.int32)[:, None] == my_head_ids[None, :]).astype(bf16)
    my_table = jnp.dot(table, chosen_heads, preferred_element_type=f32)
    offset = jnp.arange(2 * tokens, dtype=jnp.int32) - tokens
    bucket_ids = jnp.arange(bucket_total, dtype=jnp.int32)
    of_offset = (buckets_of(offset)[None, :] == bucket_ids[:, None]).astype(f32)
    bias = jnp.einsum(
        "bh,bo->ho", my_table, of_offset, precision=lax.Precision.HIGHEST
    ).reshape(pairs, 2, 2 * tokens)

    all_x32 = all_x.astype(f32)
    scale_all = norm_scale(all_x32)
    normed = (all_x32 * scale_all * gain_local).astype(bf16)
    qkv = dot(normed, full_qkv).astype(bf16)
    attended, probs = attention_forward(scal, qkv, bias, rows, blocks)
    hidden = inputs[0].astype(f32) + ctx_reduce(dot(attended, full_out).astype(bf16), rows)

    scale_ffn = norm_scale(hidden)
    own_nffn = (hidden * scale_ffn * gain_ffn).astype(bf16)
    own_nffn = take_blocks(own_nffn, 1, [o * shard_rows for o in order], shard_rows)
    normed_ffn = jnp.concatenate(ctx_gather(own_nffn), axis=0)
    gate_up = dot(normed_ffn, full_gate_up)
    gate_proj, up_proj = gate_up[:, :units], gate_up[:, units:]
    activated, gelu_pull = jax.vjp(lambda inner: jax.nn.gelu(inner, approximate=True), gate_proj)
    mixed_units = (activated * up_proj).astype(bf16)

    def by_shard(a):
        blocked = a.reshape(shards, -1, a.shape[-1])
        size = blocked.shape[1]
        mine = take_blocks(a, 0, [o * size for o in order[:chips]], size)
        other = take_blocks(a, 0, [o * size for o in order[chips:]], size)
        return (
            mine.reshape(chips, size, -1),
            other.reshape(chips, size, -1),
        )

    grad_down = dot(mixed_units, all_dy, 0, 0).astype(bf16)
    share_down = weight_reduce(*by_shard(grad_down), chip)
    result = hidden + ctx_reduce(dot(mixed_units, full_down).astype(bf16), rows)
    grad_mixed = dot(all_dy, full_down, 1, 1)
    grad_gate_proj = gelu_pull(grad_mixed * up_proj)[0].astype(bf16)
    grad_up_proj = (grad_mixed * activated).astype(bf16)
    grad_gate_up = jnp.concatenate([grad_gate_proj, grad_up_proj], axis=1)
    grad_nffn = ctx_reduce(dot(grad_gate_up, full_gate_up, 1, 1).astype(bf16), rows)
    grad_nffn = take_blocks(grad_nffn, 1, [p * shard_rows for p in place], shard_rows)
    grad_w = dot(normed_ffn, grad_gate_up, 0, 0).astype(bf16).reshape(2, chips, shard_rows, -1)
    share_gate_up = weight_reduce(grad_w[0], grad_w[1], chip)
    grad_hidden_norm, grad_gain_ffn = norm_back(hidden, scale_ffn, gain_ffn, grad_nffn)
    grad_hidden = cotangent[0].astype(f32) * live_rows + grad_hidden_norm

    grad_low = jnp.concatenate(ctx_gather(grad_hidden.astype(bf16)), axis=0)
    grad_att = dot(grad_low, full_out, 1, 1).astype(bf16)
    grad_qkv, diagonals = attention_backward(scal, qkv, probs, grad_att, rows, blocks)
    grad_out = dot(attended, grad_low, 0, 0).astype(bf16)
    if strided:
        share_out = weight_reduce(*by_shard(grad_out), chip)
    grad_w = dot(normed, grad_qkv, 0, 0).astype(bf16).reshape(2, chips, shard_rows, -1)
    share_qkv = weight_reduce(grad_w[0], grad_w[1], chip)
    grad_normed = ctx_reduce(dot(grad_qkv, full_qkv, 1, 1).astype(bf16), rows)
    grad_norm, grad_gain_attn = norm_back(
        own_x.astype(f32), scale_all[:rows], gain_local, grad_normed
    )
    grad_norm = take_blocks(grad_norm, 1, [p * shard_rows for p in place], shard_rows)
    input_grad = (grad_hidden + grad_norm).astype(bf16)[None]

    grad_gain_attn = take_blocks(
        grad_gain_attn[None], 1, [p * shard_rows for p in place], shard_rows
    )[0]
    aligned = jnp.arange(2 * tokens, dtype=jnp.int32)
    aligned = jnp.where(aligned < 2 * tokens - rows, aligned, aligned - 2 * tokens)
    aligned = aligned - (blocks - 1) * rows
    of_aligned = (buckets_of(aligned)[:, None] == bucket_ids[None, :]).astype(f32)
    my_grad_table = jnp.dot(
        diagonals.reshape(my_heads, 2 * tokens), of_aligned, precision=lax.Precision.HIGHEST
    )
    grad_table = jnp.einsum(
        "gb,hg->bh",
        my_grad_table,
        (jnp.arange(heads, dtype=jnp.int32)[:, None] == my_head_ids[None, :]).astype(f32),
        precision=lax.Precision.HIGHEST,
    )
    packed = jnp.concatenate([grad_gain_attn, grad_gain_ffn, grad_table.reshape(-1)])
    packed = lax.psum(packed, ("ctx", "fsdp"))
    g_attn = lax.dynamic_slice_in_dim(packed, shard * shard_rows, shard_rows)
    g_ffn = lax.dynamic_slice_in_dim(packed, width + shard * shard_rows, shard_rows)
    table_rows = relative_bias_table.shape[0]
    g_table = lax.dynamic_slice_in_dim(
        packed[2 * width :].reshape(bucket_total, heads), shard * table_rows, table_rows, 0
    )

    def by_position(share):
        pieces = jnp.stack(ctx_gather(share))
        return jnp.concatenate(
            [lax.dynamic_slice_in_dim(pieces, position ^ c, 1, 0) for c in range(blocks)]
        )

    def spread(pieces, groups):
        n, r, _ = pieces.shape
        return jnp.transpose(pieces.reshape(n, r, groups, -1), (1, 2, 0, 3)).reshape(r, -1).astype(f32)

    qkv_pieces = by_position(share_qkv).reshape(blocks, shard_rows, pairs, 3, 128)
    head_groups = shards if strided else 1
    outs_qkv = [
        spread(qkv_pieces[:, :, :, n].reshape(blocks, shard_rows, -1), head_groups) for n in range(3)
    ]
    if strided:
        g_out = by_position(share_out).reshape(-1, width).astype(f32)
    else:
        spot = jnp.zeros((width, width), bf16)
        spot = lax.dynamic_update_slice_in_dim(
            spot, grad_out, position * my_heads * head_width, 0
        )
        g_out = lax.psum_scatter(spot, "fsdp", scatter_dimension=0, tiled=True)
        g_out = lax.psum(g_out, "ctx").astype(f32)
    gate_up_pieces = by_position(share_gate_up)
    g_gate = spread(gate_up_pieces[:, :, :units], shards)
    g_up = spread(gate_up_pieces[:, :, units:], shards)
    g_down = by_position(share_down).reshape(-1, width).astype(f32)
    return (
        result.astype(bf16)[None],
        input_grad,
        *outs_qkv,
        g_out,
        g_gate,
        g_up,
        g_down,
        g_attn,
        g_ffn,
        g_table,
    )


def solution(mesh):
    rows = P("fsdp", None)
    tokens = P("fsdp", "ctx", None)
    in_specs = (tokens, P("fsdp")) + (rows,) * 7 + (P("fsdp"), P("fsdp"), rows, tokens)
    out_specs = (tokens, tokens) + (rows,) * 7 + (P("fsdp"), P("fsdp"), rows)
    return jax.shard_map(
        on_device, mesh=mesh, in_specs=in_specs, out_specs=out_specs, check_vma=False
    )
```

time: 2200 us -> 832 us (0.38)
  waiting for transfers between devices: 1830 us -> 399 us
  matrix products: 222 us -> 74.8 us
  starting transfers between devices: 7.59 us -> 100 us
  local copies, waits for them, and re-layouts: 17.5 us -> 104 us
  other arithmetic: 27.2 us -> 69.6 us
  Pallas kernels: 0 us -> 33.2 us
  blocking collectives: 70 us -> 37.3 us
    reduce_scatter x7 -> x0, waiting for transfers between devices: 801 us -> none  [the longest x1 208 us: on_device(): lax.psum_scatter(grad_up.astype(jnp.bfloat16), 'fsdp', scatter_dimension=...]
    all_gather x7 -> x0, waiting for transfers between devices: 747 us -> none  [the longest x1 179 us: on_device(): lax.all_gather(w_gate, 'fsdp', axis=0, tiled=True)]
    ppermute x7 -> x87, waiting for transfers between devices: 109 us -> 399 us  [the longest x27 255 us: chip_send(): lax.ppermute(a, 'fsdp', [(2 * s + k, 2 * d + k) for s, d in pairs for k i...]
    psum x1 -> x0, waiting for transfers between devices: 166 us -> none  [on_device(): lax.psum(share_query.astype(jnp.bfloat16), 'ctx').astype(jnp.float32)]
    dot_general x53 -> x18, matrix products: 222 us -> 74.8 us  [the longest x12 65 us: dot(): lax.dot_general(a, b, (((ca,), (cb,)), ((), ())), preferred_element_type=...]
    ppermute x7 -> x87, starting transfers between devices: 6.37 us -> 100 us  [the longest x27 53.1 us: chip_send(): lax.ppermute(a, 'fsdp', [(2 * s + k, 2 * d + k) for s, d in pairs for k i...]
    all_gather x3 -> x0, blocking collectives: 34 us -> none  [the longest x1 13.5 us: on_device(): lax.all_gather(norm_attn, 'fsdp', axis=0, tiled=True)]
    unnamed x150 -> x178, local copies, waits for them, and re-layouts: 14.6 us -> 47.9 us
  transfers between devices with their start and end apart: 22 -> 87, of which waited for: 19 -> 36; matrix products, arithmetic and copies ran while one was open for 9% -> 23% of each run, Pallas kernels for 0% -> 4%
where the time goes in v1:
time: 832 us; the launch traced here: 822 us
  waiting for transfers between devices  399 us (48%)
  local copies, waits for them, and re-layouts  104 us (12%)
  starting transfers between devices  100 us (12%)
  matrix products  74.8 us (9%)
  other arithmetic  69.6 us (8%)
  blocking collectives  37.3 us (4%)
  Pallas kernels  33.2 us (4%)
    ppermute x27, waiting for transfers between devices, chip_send(): lax.ppermute(a, 'fsdp', [(2 * s + k, 2 * d + k) for s, d in pairs for k i...  255 us
    ppermute x36, waiting for transfers between devices, ctx_send(): return lax.ppermute(a, 'ctx', [(i, i ^ distance) for i in range(size)])  140 us
    dot_general x12, matrix products, dot(): lax.dot_general(a, b, (((ca,), (cb,)), ((), ())), preferred_element_type=...  65 us
    ppermute x27, starting transfers between devices, chip_send(): lax.ppermute(a, 'fsdp', [(2 * s + k, 2 * d + k) for s, d in pairs for k i...  53.1 us
    unnamed x178, local copies, waits for them, and re-layouts  47.9 us
    ppermute x36, starting transfers between devices, ctx_send(): return lax.ppermute(a, 'ctx', [(i, i ^ distance) for i in range(size)])  45.1 us
    psum x1, blocking collectives, on_device(): packed = lax.psum(packed, ('ctx', 'fsdp'))  37.3 us
    convert_element_type x7, local copies, waits for them, and re-layouts, spread(): jnp.transpose(pieces.reshape(n, r, groups, -1), (1, 2, 0, 3)).reshape(r, -1)  22.9 us
  transfers between devices with their start and end apart: 87, of which 36 were waited for; matrix products, arithmetic and copies ran while one was open for 23% of the time, Pallas kernels for 4%

profile of v1, /device:TPU:0, one launch (start us, length us, event | category | flops | bytes accessed | tf_op | source)
XLA Modules:
  0.0 821.5 jit_solution(18376869385825531153)
XLA Ops:
  19.5 7.1 fusion.8
  58.2 16.7 %collective-permute-done.19 = bf16[64,2048]{1,0:T(8,128)(2,1)} collective-permute-done((bf16[64,2048]{1,0:T(8,128)(2,1)}, bf16[64,2048]{1,0:T(8,128)(2,1)}, u32[]{:S(2)}, u32[]{:S(2)}) %collective-permute-start.19) | collective-permute-done | bytes 262176 | tf_op jit(solution)/shard_map/ppermute | solution.py:36
  88.0 21.4 %collective-permute-done.37 = bf16[160,2048]{1,0:T(8,128)(2,1)S(1)} collective-permute-done((bf16[160,2048]{1,0:T(8,128)(2,1)S(1)}, bf16[160,2048]{1,0:T(8,128)(2,1)S(1)}, u32[]{:S(2)}, u32[]{:S(2)}) %collective-permute-start.37) | collective-permute-done | bytes 655392 | tf_op jit(solution)/shard_map/ppermute | solution.py:36
  113.6 12.6 %collective-permute-done.10 = bf16[256,1536]{0,1:T(8,128)(2,1)S(1)} collective-permute-done((bf16[256,1536]{0,1:T(8,128)(2,1)S(1)}, bf16[256,1536]{0,1:T(8,128)(2,1)S(1)}, u32[]{:S(2)}, u32[]{:S(2)}) %collective-permute-start.10) | collective-permute-done | bytes 786464 | tf_op jit(solution)/shard_map/ppermute | solution.py:36
  127.5 54.5 %collective-permute-done.30 = bf16[256,2560]{1,0:T(8,128)(2,1)S(1)} collective-permute-done((bf16[256,2560]{1,0:T(8,128)(2,1)S(1)}, bf16[256,2560]{1,0:T(8,128)(2,1)S(1)}, u32[]{:S(2)}, u32[]{:S(2)}) %collective-permute-start.30) | collective-permute-done | bytes 1310752 | tf_op jit(solution)/shard_map/ppermute | solution.py:36
  190.6 10.2 %collective-permute-done.39 = bf16[160,2048]{1,0:T(8,128)(2,1)S(1)} collective-permute-done((bf16[160,2048]{1,0:T(8,128)(2,1)S(1)}, bf16[160,2048]{1,0:T(8,128)(2,1)S(1)}, u32[]{:S(2)}, u32[]{:S(2)}) %collective-permute-start.39) | collective-permute-done | bytes 655392 | tf_op jit(solution)/shard_map/ppermute | solution.py:36
  206.5 8.0 collective-permute-done.12
  229.1 16.2 %shard_map.220 = (bf16[512,512]{1,0:T(8,128)(2,1)S(1)}, bf16[8,512,512]{2,1,0:T(8,128)(2,1)}) custom-call(s32[2]{0:T(128)S(1)} %pad_add_fusion.scal_ref, bf16[512,1536]{1,0:T(8,128)(2,1)S(1)} %convolution_convert_fusion.7.qkv_ref, f32[4,2,1024]{2,1,0:T(2,128)S(1)} %reshape.340.bias_ref), custom_call_target="tpu_custom_call" | custom-call | flops 536870912 | bytes 4194304 | tf_op jit(solution)/shard_map/pallas_call | solution.py:193
  256.8 6.5 collective-permute-done.24
  263.3 12.1 %collective-permute-done.25 = bf16[128,2048]{1,0:T(8,128)(2,1)S(1)} collective-permute-done((bf16[128,2048]{1,0:T(8,128)(2,1)S(1)}, bf16[128,2048]{1,0:T(8,128)(2,1)S(1)}, u32[]{:S(2)}, u32[]{:S(2)}) %collective-permute-start.25) | collective-permute-done | bytes 524320 | tf_op jit(solution)/shard_map/ppermute | solution.py:41
  283.7 7.5 collective-permute-done.27
  292.7 22.2 %collective-permute-done.28 = bf16[128,2048]{1,0:T(8,128)(2,1)S(1)} collective-permute-done((bf16[128,2048]{1,0:T(8,128)(2,1)S(1)}, bf16[128,2048]{1,0:T(8,128)(2,1)S(1)}, u32[]{:S(2)}, u32[]{:S(2)}) %collective-permute-start.28) | collective-permute-done | bytes 524320 | tf_op jit(solution)/shard_map/ppermute | solution.py:41
  314.9 8.3 %fusion.64 = f32[512,2560]{1,0:T(8,128)S(1)} fusion(bf16[2048,2560]{1,0:T(8,128)(2,1)} %constant_dynamic-update-slice_fusion.32, bf16[128,2048]{1,0:T(8,128)(2,1)S(1)} %collective-permute-done.29, bf16[128,2048]{1,0:T(8,128)(2,1)S(1)} %collective-permute-done.28, bf16[128,2048]{1,0:T(8,128)(2,1)S(1)} %collective-permute-done.27, ...), kind=kOutput, calls=%fused_computation.161 | convolution fusion | flops 5377097728 | bytes 17825792 | tf_op jit(solution)/shard_map/dot_general | solution.py:19
  324.6 8.1 fusion.15
  338.1 8.7 %convolution_convert_fusion.8 = bf16[512,2048]{1,0:T(8,128)(2,1)S(1)} fusion(bf16[2048,2560]{1,0:T(8,128)(2,1)} %constant_dynamic-update-slice_fusion.32, bf16[512,1280]{1,0:T(8,128)(2,1)S(1)} %copy-done.36, bf16[512,1280]{1,0:T(8,128)(2,1)S(1)} %get-tuple-element.46), kind=kOutput, calls=%fused_computation.35 | convolution fusion | flops 5375000576 | bytes 15204352 | tf_op jit(solution)/shard_map/dot_general | solution.py:19
  354.5 9.9 %convolution_convert_fusion = bf16[2048,2560]{1,0:T(8,128)(2,1)} fusion(bf16[512,1280]{1,0:T(8,128)(2,1)} %get-tuple-element.47, bf16[512,1280]{1,0:T(8,128)(2,1)} %copy-done.35, bf16[128,2048]{1,0:T(8,128)(2,1)S(1)} %collective-permute-done.29, bf16[128,2048]{1,0:T(8,128)(2,1)S(1)} %collective-permute-done.28, ...), kind=kOutput, calls=%fused_computation.3 | convolution fusion | flops 5387583488 | bytes 15204352 | tf_op jit(solution)/shard_map/dot_general | solution.py:19
  368.9 13.2 %collective-permute-done.51 = bf16[128,2048]{1,0:T(8,128)(2,1)S(1)} collective-permute-done((bf16[128,2048]{1,0:T(8,128)(2,1)S(1)}, bf16[128,2048]{1,0:T(8,128)(2,1)S(1)}, u32[]{:S(2)}, u32[]{:S(2)}) %collective-permute-start.51) | collective-permute-done | bytes 524320 | tf_op jit(solution)/shard_map/ppermute | solution.py:41
  389.1 8.8 %fusion.111 = (bf16[1024,2560]{1,0:T(8,128)(2,1)}, bf16[1024,2560]{1,0:T(8,128)(2,1)}) fusion(bf16[2048,2560]{1,0:T(8,128)(2,1)} %convolution_convert_fusion), kind=kLoop, calls=%fused_computation.362 | loop fusion | bytes 20971520 | tf_op jit(solution)/shard_map/slice | solution.py:413
  400.7 12.2 %collective-permute-done.54 = bf16[128,2048]{1,0:T(8,128)(2,1)} collective-permute-done((bf16[128,2048]{1,0:T(8,128)(2,1)}, bf16[128,2048]{1,0:T(8,128)(2,1)}, u32[]{:S(2)}, u32[]{:S(2)}) %collective-permute-start.54) | collective-permute-done | bytes 524320 | tf_op jit(solution)/shard_map/ppermute | solution.py:41
  416.4 17.0 %shard_map.221 = (bf16[512,1536]{1,0:T(8,128)(2,1)S(1)}, f32[4,2,1024]{2,1,0:T(2,128)S(1)}) custom-call(s32[2]{0:T(128)S(1)} %pad_add_fusion.scal_ref, bf16[512,1536]{1,0:T(8,128)(2,1)S(1)} %convolution_convert_fusion.7.qkv_ref, bf16[8,512,512]{2,1,0:T(8,128)(2,1)} %get-tuple-element.17.prob_ref, bf16[512,512]{1,0:T(8,128)(2,1)S(1)} %convolution_convert_fusion.9.gatt_ref), custom_call_target="tpu_custom_call" | custom-call | flops 1073741824 | bytes 4194304 | tf_op jit(solution)/shard_map/pallas_call | solution.py:222
  472.9 7.1 collective-permute-done.67
  484.7 37.3 %psum.7 = f32[5120]{0:T(1024)S(1)} all-reduce(f32[5120]{0:T(1024)S(1)} %pad_maximum_fusion.28), channel_id=1, replica_groups=mesh['ctx'=4,'fsdp'=8] {'ctx','fsdp'}, use_global_device_ids=true, to_apply=%region_6.7 | all-reduce | flops 5120 | bytes 40960 | tf_op jit(solution)/shard_map/psum | solution.py:449
  539.9 8.7 %collective-permute-done.81 = bf16[160,2048]{1,0:T(8,128)(2,1)S(1)} collective-permute-done((bf16[160,2048]{1,0:T(8,128)(2,1)S(1)}, bf16[160,2048]{1,0:T(8,128)(2,1)S(1)}, u32[]{:S(2)}, u32[]{:S(2)}) %collective-permute-start.81) | collective-permute-done | bytes 655392 | tf_op jit(solution)/shard_map/ppermute | solution.py:36
  558.0 10.6 %collective-permute-done.82 = bf16[160,2048]{1,0:T(8,128)(2,1)S(1)} collective-permute-done((bf16[160,2048]{1,0:T(8,128)(2,1)S(1)}, bf16[160,2048]{1,0:T(8,128)(2,1)S(1)}, u32[]{:S(2)}, u32[]{:S(2)}) %collective-permute-start.82) | collective-permute-done | bytes 655392 | tf_op jit(solution)/shard_map/ppermute | solution.py:36
  568.5 12.3 %collective-permute-done.83 = bf16[160,2048]{1,0:T(8,128)(2,1)S(1)} collective-permute-done((bf16[160,2048]{1,0:T(8,128)(2,1)S(1)}, bf16[160,2048]{1,0:T(8,128)(2,1)S(1)}, u32[]{:S(2)}, u32[]{:S(2)}) %collective-permute-start.83) | collective-permute-done | bytes 655392 | tf_op jit(solution)/shard_map/ppermute | solution.py:36
  586.9 7.2 collective-permute-done.60
  618.2 41.4 %collective-permute-done.62 = bf16[256,1536]{0,1:T(8,128)(2,1)} collective-permute-done((bf16[256,1536]{0,1:T(8,128)(2,1)}, bf16[256,1536]{0,1:T(8,128)(2,1)}, u32[]{:S(2)}, u32[]{:S(2)}) %collective-permute-start.62) | collective-permute-done | bytes 786464 | tf_op jit(solution)/shard_map/ppermute | solution.py:36
  673.5 8.8 %collective-permute-done.64 = bf16[256,1536]{0,1:T(8,128)(2,1)S(1)} collective-permute-done((bf16[256,1536]{0,1:T(8,128)(2,1)S(1)}, bf16[256,1536]{0,1:T(8,128)(2,1)S(1)}, u32[]{:S(2)}, u32[]{:S(2)}) %collective-permute-start.64) | collective-permute-done | bytes 786464 | tf_op jit(solution)/shard_map/ppermute | solution.py:41
  683.0 16.3 %collective-permute-done.75 = bf16[256,2560]{1,0:T(8,128)(2,1)S(1)} collective-permute-done((bf16[256,2560]{1,0:T(8,128)(2,1)S(1)}, bf16[256,2560]{1,0:T(8,128)(2,1)S(1)}, u32[]{:S(2)}, u32[]{:S(2)}) %collective-permute-start.75) | collective-permute-done | bytes 1310752 | tf_op jit(solution)/shard_map/ppermute | solution.py:36
  699.3 18.3 %collective-permute-done.76 = bf16[256,2560]{1,0:T(8,128)(2,1)S(1)} collective-permute-done((bf16[256,2560]{1,0:T(8,128)(2,1)S(1)}, bf16[256,2560]{1,0:T(8,128)(2,1)S(1)}, u32[]{:S(2)}, u32[]{:S(2)}) %collective-permute-start.76) | collective-permute-done | bytes 1310752 | tf_op jit(solution)/shard_map/ppermute | solution.py:36
  733.1 17.1 %collective-permute-done.77 = bf16[256,2560]{1,0:T(8,128)(2,1)} collective-permute-done((bf16[256,2560]{1,0:T(8,128)(2,1)S(1)}, bf16[256,2560]{1,0:T(8,128)(2,1)}, u32[]{:S(2)}, u32[]{:S(2)}) %collective-permute-start.77) | collective-permute-done | bytes 1310752 | tf_op jit(solution)/shard_map/ppermute | solution.py:41
  750.3 27.1 %collective-permute-done.79 = bf16[256,2560]{1,0:T(8,128)(2,1)} collective-permute-done((bf16[256,2560]{1,0:T(8,128)(2,1)S(1)}, bf16[256,2560]{1,0:T(8,128)(2,1)}, u32[]{:S(2)}, u32[]{:S(2)}) %collective-permute-start.79) | collective-permute-done | bytes 1310752 | tf_op jit(solution)/shard_map/ppermute | solution.py:41
  (467 shorter events, 324.6 us)
Async XLA Ops:
  2.1 35.6 %collective-permute-start.3 = (bf16[1,640]{1,0:T(2,128)(2,1)S(1)}, bf16[1,640]{1,0:T(2,128)(2,1)S(1)}, u32[]{:S(2)}, u32[]{:S(2)}) collective-permute-start(bf16[1,640]{1,0:T(2,128)(2,1)S(1)} %broadcast_in_dim.52), channel_id=1, source_target_pairs={{2,0},{3,1},{4,2},{5,3},{6,4},{7,5},{0,6},{1,7},{10,8},{11,9},{12,... | collective-permute-start | bytes 3848 | tf_op jit(solution)/shard_map/ppermute | solution.py:36
  7.2 36.3 %collective-permute-start.6 = (bf16[1,640]{1,0:T(2,128)(2,1)S(1)}, bf16[1,640]{1,0:T(2,128)(2,1)S(1)}, u32[]{:S(2)}, u32[]{:S(2)}) collective-permute-start(bf16[1,640]{1,0:T(2,128)(2,1)S(1)} %broadcast_in_dim.52), channel_id=1, source_target_pairs={{0,1},{1,0},{2,3},{3,2},{4,5},{5,4},{6,7},{7,6},{8,9},{9,8},{10,11... | collective-permute-start | bytes 3848 | tf_op jit(solution)/shard_map/ppermute | solution.py:32
  9.0 40.4 %collective-permute-start.18 = (bf16[64,2048]{1,0:T(8,128)(2,1)}, bf16[64,2048]{1,0:T(8,128)(2,1)}, u32[]{:S(2)}, u32[]{:S(2)}) collective-permute-start(bf16[64,2048]{1,0:T(8,128)(2,1)} %get-tuple-element.43), channel_id=1, source_target_pairs={{0,2},{1,3},{2,4},{3,5},{4,6},{5,7},{6,0},{7,1},{8,10},{9,11},{10,... | collective-permute-start | bytes 786440 | tf_op jit(solution)/shard_map/ppermute | solution.py:36
  45.4 33.8 %collective-permute-start = (bf16[128,2048]{1,0:T(8,128)(2,1)S(1)}, bf16[128,2048]{1,0:T(8,128)(2,1)}, u32[]{:S(2)}, u32[]{:S(2)}) collective-permute-start(bf16[128,2048]{1,0:T(8,128)(2,1)S(1)} %constant_dynamic-update-slice_fusion), channel_id=1, source_target_pairs={{0,8},{8,0},{16,24},{24,16},{1,9},{9,1},{17,25},{25,17},{2,10},{10... | collective-permute-start | bytes 1572872 | tf_op jit(solution)/shard_map/ppermute | solution.py:41
  49.4 38.5 %collective-permute-start.38 = (bf16[160,2048]{1,0:T(8,128)(2,1)S(1)}, bf16[160,2048]{1,0:T(8,128)(2,1)}, u32[]{:S(2)}, u32[]{:S(2)}) collective-permute-start(bf16[160,2048]{1,0:T(8,128)(2,1)S(1)} %get-tuple-element.39), channel_id=1, source_target_pairs={{0,2},{1,3},{2,4},{3,5},{4,6},{5,7},{6,0},{7,1},{8,10},{9,11},{10,... | collective-permute-start | bytes 1966088 | tf_op jit(solution)/shard_map/ppermute | solution.py:36
  74.9 34.4 %collective-permute-start.37 = (bf16[160,2048]{1,0:T(8,128)(2,1)S(1)}, bf16[160,2048]{1,0:T(8,128)(2,1)S(1)}, u32[]{:S(2)}, u32[]{:S(2)}) collective-permute-start(bf16[160,2048]{1,0:T(8,128)(2,1)S(1)} %get-tuple-element.39), channel_id=1, source_target_pairs={{2,0},{3,1},{4,2},{5,3},{6,4},{7,5},{0,6},{1,7},{10,8},{11,9},{12,... | collective-permute-start | bytes 1966088 | tf_op jit(solution)/shard_map/ppermute | solution.py:36
  79.2 125.6 %collective-permute-start.40 = (bf16[160,2048]{1,0:T(8,128)(2,1)S(1)}, bf16[160,2048]{1,0:T(8,128)(2,1)S(1)}, u32[]{:S(2)}, u32[]{:S(2)}) collective-permute-start(bf16[160,2048]{1,0:T(8,128)(2,1)S(1)} %get-tuple-element.39), channel_id=1, source_target_pairs={{0,1},{1,0},{2,3},{3,2},{4,5},{5,4},{6,7},{7,6},{8,9},{9,8},{10,11... | collective-permute-start | bytes 1966088 | tf_op jit(solution)/shard_map/ppermute | solution.py:32
  84.5 41.7 %collective-permute-start.10 = (bf16[256,1536]{0,1:T(8,128)(2,1)S(1)}, bf16[256,1536]{0,1:T(8,128)(2,1)S(1)}, u32[]{:S(2)}, u32[]{:S(2)}) collective-permute-start(bf16[256,1536]{0,1:T(8,128)(2,1)S(1)} %bitcast.226), channel_id=1, source_target_pairs={{2,0},{3,1},{4,2},{5,3},{6,4},{7,5},{0,6},{1,7},{10,8},{11,9},{12,... | collective-permute-start | bytes 2359304 | tf_op jit(solution)/shard_map/ppermute | solution.py:36
  111.1 71.0 %collective-permute-start.30 = (bf16[256,2560]{1,0:T(8,128)(2,1)S(1)}, bf16[256,2560]{1,0:T(8,128)(2,1)S(1)}, u32[]{:S(2)}, u32[]{:S(2)}) collective-permute-start(bf16[256,2560]{1,0:T(8,128)(2,1)S(1)} %copy-done.14), channel_id=1, source_target_pairs={{2,0},{3,1},{4,2},{5,3},{6,4},{7,5},{0,6},{1,7},{10,8},{11,9},{12,... | collective-permute-start | bytes 3932168 | tf_op jit(solution)/shard_map/ppermute | solution.py:36
  111.2 76.6 %collective-permute-start.31 = (bf16[256,2560]{1,0:T(8,128)(2,1)S(1)}, bf16[256,2560]{1,0:T(8,128)(2,1)S(1)}, u32[]{:S(2)}, u32[]{:S(2)}) collective-permute-start(bf16[256,2560]{1,0:T(8,128)(2,1)S(1)} %copy-done.14), channel_id=1, source_target_pairs={{0,2},{1,3},{2,4},{3,5},{4,6},{5,7},{6,0},{7,1},{8,10},{9,11},{10,... | collective-permute-start | bytes 3932168 | tf_op jit(solution)/shard_map/ppermute | solution.py:36
  113.6 101.2 %collective-permute-start.13 = (bf16[256,1536]{0,1:T(8,128)(2,1)S(1)}, bf16[256,1536]{0,1:T(8,128)(2,1)S(1)}, u32[]{:S(2)}, u32[]{:S(2)}) collective-permute-start(bf16[256,1536]{0,1:T(8,128)(2,1)S(1)} %bitcast.227), channel_id=1, source_target_pairs={{0,1},{1,0},{2,3},{3,2},{4,5},{5,4},{6,7},{7,6},{8,9},{9,8},{10,11... | collective-permute-start | bytes 2359304 | tf_op jit(solution)/shard_map/ppermute | solution.py:32
  126.2 127.7 %collective-permute-start.33 = (bf16[256,2560]{1,0:T(8,128)(2,1)S(1)}, bf16[256,2560]{1,0:T(8,128)(2,1)S(1)}, u32[]{:S(2)}, u32[]{:S(2)}) collective-permute-start(bf16[256,2560]{1,0:T(8,128)(2,1)S(1)} %copy-done.14), channel_id=1, source_target_pairs={{0,1},{1,0},{2,3},{3,2},{4,5},{5,4},{6,7},{7,6},{8,9},{9,8},{10,11... | collective-permute-start | bytes 3932168 | tf_op jit(solution)/shard_map/ppermute | solution.py:32
  204.8 118.5 %collective-permute-start.47 = (bf16[128,2048]{1,0:T(8,128)(2,1)}, bf16[128,2048]{1,0:T(8,128)(2,1)S(1)}, u32[]{:S(2)}, u32[]{:S(2)}) collective-permute-start(bf16[128,2048]{1,0:T(8,128)(2,1)} %fusion.49), channel_id=1, source_target_pairs={{0,8},{8,0},{16,24},{24,16},{1,9},{9,1},{17,25},{25,17},{2,10},{10... | collective-permute-start | bytes 1572872 | tf_op jit(solution)/shard_map/ppermute | solution.py:41
  216.6 33.5 %collective-permute-start.32 = (bf16[256,2560]{1,0:T(8,128)(2,1)S(1)}, bf16[256,2560]{1,0:T(8,128)(2,1)S(1)}, u32[]{:S(2)}, u32[]{:S(2)}) collective-permute-start(bf16[256,2560]{1,0:T(8,128)(2,1)S(1)} %get-tuple-element.104), channel_id=1, source_target_pairs={{6,2},{7,3},{0,4},{1,5},{2,0},{3,1},{4,6},{5,7},{14,10},{15,11},{8... | collective-permute-start | bytes 3932168 | tf_op jit(solution)/shard_map/ppermute | solution.py:36
  221.0 34.7 %collective-permute-start.34 = (bf16[256,2560]{1,0:T(8,128)(2,1)S(1)}, bf16[256,2560]{1,0:T(8,128)(2,1)S(1)}, u32[]{:S(2)}, u32[]{:S(2)}) collective-permute-start(bf16[256,2560]{1,0:T(8,128)(2,1)S(1)} %collective-permute-done.30), channel_id=1, source_target_pairs={{0,1},{1,0},{2,3},{3,2},{4,5},{5,4},{6,7},{7,6},{8,9},{9,8},{10,11... | collective-permute-start | bytes 3932168 | tf_op jit(solution)/shard_map/ppermute | solution.py:32
  277.6 37.3 %collective-permute-start.28 = (bf16[128,2048]{1,0:T(8,128)(2,1)S(1)}, bf16[128,2048]{1,0:T(8,128)(2,1)S(1)}, u32[]{:S(2)}, u32[]{:S(2)}) collective-permute-start(bf16[128,2048]{1,0:T(8,128)(2,1)S(1)} %constant_dynamic-update-slice_fusion.24), channel_id=1, source_target_pairs={{0,16},{8,24},{16,0},{24,8},{1,17},{9,25},{17,1},{25,9},{2,18},{10... | collective-permute-start | bytes 1572872 | tf_op jit(solution)/shard_map/ppermute | solution.py:41
  278.4 36.5 %collective-permute-start.29 = (bf16[128,2048]{1,0:T(8,128)(2,1)S(1)}, bf16[128,2048]{1,0:T(8,128)(2,1)S(1)}, u32[]{:S(2)}, u32[]{:S(2)}) collective-permute-start(bf16[128,2048]{1,0:T(8,128)(2,1)S(1)} %constant_dynamic-update-slice_fusion.24), channel_id=1, source_target_pairs={{0,24},{8,16},{16,8},{24,0},{1,25},{9,17},{17,9},{25,1},{2,26},{10... | collective-permute-start | bytes 1572872 | tf_op jit(solution)/shard_map/ppermute | solution.py:41
  281.0 43.5 %collective-permute-start.48 = (bf16[128,2048]{1,0:T(8,128)(2,1)}, bf16[128,2048]{1,0:T(8,128)(2,1)S(1)}, u32[]{:S(2)}, u32[]{:S(2)}) collective-permute-start(bf16[128,2048]{1,0:T(8,128)(2,1)} %fusion.49), channel_id=1, source_target_pairs={{0,16},{8,24},{16,0},{24,8},{1,17},{9,25},{17,1},{25,9},{2,18},{10... | collective-permute-start | bytes 1572872 | tf_op jit(solution)/shard_map/ppermute | solution.py:41
  336.0 47.6 %collective-permute-start.44 = (bf16[128,2048]{1,0:T(8,128)(2,1)S(1)}, bf16[128,2048]{1,0:T(8,128)(2,1)S(1)}, u32[]{:S(2)}, u32[]{:S(2)}) collective-permute-start(bf16[128,2048]{1,0:T(8,128)(2,1)S(1)} %get-tuple-element.96), channel_id=1, source_target_pairs={{0,8},{8,0},{16,24},{24,16},{1,9},{9,1},{17,25},{25,17},{2,10},{10... | collective-permute-start | bytes 1572872 | tf_op jit(solution)/shard_map/ppermute | solution.py:41
  336.6 47.0 %collective-permute-start.45 = (bf16[128,2048]{1,0:T(8,128)(2,1)S(1)}, bf16[128,2048]{1,0:T(8,128)(2,1)S(1)}, u32[]{:S(2)}, u32[]{:S(2)}) collective-permute-start(bf16[128,2048]{1,0:T(8,128)(2,1)S(1)} %get-tuple-element.98), channel_id=1, source_target_pairs={{0,16},{8,24},{16,0},{24,8},{1,17},{9,25},{17,1},{25,9},{2,18},{10... | collective-permute-start | bytes 1572872 | tf_op jit(solution)/shard_map/ppermute | solution.py:41
  347.6 34.6 %collective-permute-start.51 = (bf16[128,2048]{1,0:T(8,128)(2,1)S(1)}, bf16[128,2048]{1,0:T(8,128)(2,1)S(1)}, u32[]{:S(2)}, u32[]{:S(2)}) collective-permute-start(bf16[128,2048]{1,0:T(8,128)(2,1)S(1)} %get-tuple-element.95), channel_id=1, source_target_pairs={{0,16},{8,24},{16,0},{24,8},{1,17},{9,25},{17,1},{25,9},{2,18},{10... | collective-permute-start | bytes 1572872 | tf_op jit(solution)/shard_map/ppermute | solution.py:41
  382.2 146.2 %collective-permute-start.80 = (bf16[4,160,2048]{2,1,0:T(8,128)(2,1)}, bf16[4,160,2048]{2,1,0:T(8,128)(2,1)}, u32[]{:S(2)}, u32[]{:S(2)}) collective-permute-start(bf16[4,160,2048]{2,1,0:T(8,128)(2,1)} %bitcast.74), channel_id=1, source_target_pairs={{0,1},{1,0},{2,3},{3,2},{4,5},{5,4},{6,7},{7,6},{8,9},{9,8},{10,11... | collective-permute-start | bytes 7864328 | tf_op jit(solution)/shard_map/ppermute | solution.py:32
  397.9 198.9 %collective-permute-start.73 = (bf16[4,256,2560]{2,1,0:T(8,128)(2,1)}, bf16[4,256,2560]{2,1,0:T(8,128)(2,1)}, u32[]{:S(2)}, u32[]{:S(2)}) collective-permute-start(bf16[4,256,2560]{2,1,0:T(8,128)(2,1)} %bitcast.230), channel_id=1, source_target_pairs={{0,1},{1,0},{2,3},{3,2},{4,5},{5,4},{6,7},{7,6},{8,9},{9,8},{10,11... | collective-permute-start | bytes 15728648 | tf_op jit(solution)/shard_map/ppermute | solution.py:32
  464.6 88.3 %collective-permute-start.59 = (bf16[4,256,1536]{1,2,0:T(8,128)(2,1)}, bf16[4,256,1536]{1,2,0:T(8,128)(2,1)}, u32[]{:S(2)}, u32[]{:S(2)}) collective-permute-start(bf16[4,256,1536]{1,2,0:T(8,128)(2,1)} %copy.28), channel_id=1, source_target_pairs={{0,1},{1,0},{2,3},{3,2},{4,5},{5,4},{6,7},{7,6},{8,9},{9,8},{10,11... | collective-permute-start | bytes 9437192 | tf_op jit(solution)/shard_map/ppermute | solution.py:32
  480.9 42.4 %collective-permute-start.68 = (bf16[64,2048]{1,0:T(8,128)(2,1)}, bf16[64,2048]{1,0:T(8,128)(2,1)S(1)}, u32[]{:S(2)}, u32[]{:S(2)}) collective-permute-start(bf16[64,2048]{1,0:T(8,128)(2,1)} %get-tuple-element.102), channel_id=1, source_target_pairs={{0,2},{1,3},{2,4},{3,5},{4,6},{5,7},{6,0},{7,1},{8,10},{9,11},{10,... | collective-permute-start | bytes 786440 | tf_op jit(solution)/shard_map/ppermute | solution.py:36
  481.7 41.6 %collective-permute-start.69 = (bf16[64,2048]{1,0:T(8,128)(2,1)}, bf16[64,2048]{1,0:T(8,128)(2,1)S(1)}, u32[]{:S(2)}, u32[]{:S(2)}) collective-permute-start(bf16[64,2048]{1,0:T(8,128)(2,1)} %get-tuple-element.103), channel_id=1, source_target_pairs={{2,0},{3,1},{4,2},{5,3},{6,4},{7,5},{0,6},{1,7},{10,8},{11,9},{12,... | collective-permute-start | bytes 786440 | tf_op jit(solution)/shard_map/ppermute | solution.py:36
  555.8 38.2 %collective-permute-start.60 = (bf16[256,1536]{0,1:T(8,128)(2,1)S(1)}, bf16[256,1536]{0,1:T(8,128)(2,1)S(1)}, u32[]{:S(2)}, u32[]{:S(2)}) collective-permute-start(bf16[256,1536]{0,1:T(8,128)(2,1)S(1)} %slice_bitcast_fusion.6), channel_id=1, source_target_pairs={{0,2},{1,3},{6,4},{7,5},{2,6},{3,7},{4,0},{5,1},{8,10},{9,11},{14,... | collective-permute-start | bytes 2359304 | tf_op jit(solution)/shard_map/ppermute | solution.py:36
  596.8 62.9 %collective-permute-start.62 = (bf16[256,1536]{0,1:T(8,128)(2,1)}, bf16[256,1536]{0,1:T(8,128)(2,1)}, u32[]{:S(2)}, u32[]{:S(2)}) collective-permute-start(bf16[256,1536]{0,1:T(8,128)(2,1)} %get-tuple-element.68), channel_id=1, source_target_pairs={{2,0},{3,1},{4,2},{5,3},{6,4},{7,5},{0,6},{1,7},{10,8},{11,9},{12,... | collective-permute-start | bytes 2359304 | tf_op jit(solution)/shard_map/ppermute | solution.py:36
  603.5 61.6 %collective-permute-start.74 = (bf16[256,2560]{1,0:T(8,128)(2,1)S(1)}, bf16[256,2560]{1,0:T(8,128)(2,1)S(1)}, u32[]{:S(2)}, u32[]{:S(2)}) collective-permute-start(bf16[256,2560]{1,0:T(8,128)(2,1)S(1)} %slice_bitcast_fusion.2), channel_id=1, source_target_pairs={{0,2},{1,3},{6,4},{7,5},{2,6},{3,7},{4,0},{5,1},{8,10},{9,11},{14,... | collective-permute-start | bytes 3932168 | tf_op jit(solution)/shard_map/ppermute | solution.py:36
  665.8 33.6 %collective-permute-start.75 = (bf16[256,2560]{1,0:T(8,128)(2,1)S(1)}, bf16[256,2560]{1,0:T(8,128)(2,1)S(1)}, u32[]{:S(2)}, u32[]{:S(2)}) collective-permute-start(bf16[256,2560]{1,0:T(8,128)(2,1)S(1)} %get-tuple-element.48), channel_id=1, source_target_pairs={{0,2},{1,3},{2,4},{3,5},{4,6},{5,7},{6,0},{7,1},{8,10},{9,11},{10,... | collective-permute-start | bytes 3932168 | tf_op jit(solution)/shard_map/ppermute | solution.py:36
  665.8 51.8 %collective-permute-start.76 = (bf16[256,2560]{1,0:T(8,128)(2,1)S(1)}, bf16[256,2560]{1,0:T(8,128)(2,1)S(1)}, u32[]{:S(2)}, u32[]{:S(2)}) collective-permute-start(bf16[256,2560]{1,0:T(8,128)(2,1)S(1)} %get-tuple-element.49), channel_id=1, source_target_pairs={{2,0},{3,1},{4,2},{5,3},{6,4},{7,5},{0,6},{1,7},{10,8},{11,9},{12,... | collective-permute-start | bytes 3932168 | tf_op jit(solution)/shard_map/ppermute | solution.py:36
  719.1 58.2 %collective-permute-start.79 = (bf16[256,2560]{1,0:T(8,128)(2,1)S(1)}, bf16[256,2560]{1,0:T(8,128)(2,1)}, u32[]{:S(2)}, u32[]{:S(2)}) collective-permute-start(bf16[256,2560]{1,0:T(8,128)(2,1)S(1)} %fusion.19), channel_id=1, source_target_pairs={{0,24},{8,16},{16,8},{24,0},{1,25},{9,17},{17,9},{25,1},{2,26},{10... | collective-permute-start | bytes 3932168 | tf_op jit(solution)/shard_map/ppermute | solution.py:41
  (104 other events, 2077.5 us)

commit v2 on v1

v2 whole, which is shorter than its diff:
```python
import functools

import jax
import jax.numpy as jnp
import numpy as np
from jax import lax
from jax.experimental import pallas as pl
from jax.experimental.pallas import tpu as pltpu
from jax.sharding import PartitionSpec as P

bucket_total = 32
bucket_total = 32
bucket_edges = (12, 16, 23, 32, 46, 64, 91)
epsilon = 1e-06
masked_score = -1e30
f32 = jnp.float32
bf16 = jnp.bfloat16
i32 = jnp.int32
vmem_limit = 52 * 1024 * 1024
extra = 16
ANY = pl.ANY


def dot(a, b, ca=1, cb=0):
    return lax.dot_general(a, b, (((ca,), (cb,)), ((), ())), preferred_element_type=f32)


def buckets_of(offset):
    distance = jnp.abs(offset)
    bucket = jnp.minimum(distance, 8)
    for edge_value in bucket_edges:
        bucket = bucket + (distance >= edge_value).astype(i32)
    return bucket + 16 * (offset > 0).astype(i32)


def after(value, *earlier):
    return lax.optimization_barrier((value, *earlier))[0]


def together(values, *earlier):
    return lax.optimization_barrier((*values, *earlier))[: len(values)]


def core_swap(a):
    size = lax.axis_size("fsdp")
    return lax.ppermute(a, "fsdp", [(r, r ^ 1) for r in range(size)])


def chip_send(a, pairs):
    return lax.ppermute(a, "fsdp", [(2 * s + k, 2 * d + k) for s, d in pairs for k in range(2)])


def ctx_send(a, distance):
    size = lax.axis_size("ctx")
    return lax.ppermute(a, "ctx", [(i, i ^ distance) for i in range(size)])


def near_slots(chips):
    return [0, 1, 3] if chips == 4 else list(range(chips))


def far_slots(chips):
    return [2] if chips == 4 else []


def gather_near(own):
    chips = lax.axis_size("fsdp") // 2
    if chips == 4:
        above = chip_send(own, [(1, 0), (2, 1), (3, 2), (0, 3)])
        below = chip_send(own, [(0, 1), (1, 2), (2, 3), (3, 0)])
        return [own, above, below]
    return [own] + [
        chip_send(own, [((z + t) % chips, z) for z in range(chips)]) for t in range(1, chips)
    ]


def gather_far(near, chip):
    if lax.axis_size("fsdp") // 2 != 4:
        return []
    own, above, below = near
    middle = jnp.where(chip == 1, above, jnp.where(chip == 2, below, own))
    return [chip_send(middle, [(3, 1), (0, 2), (1, 0), (2, 3)])]


def with_other_core(slots):
    if not slots:
        return []
    half = jnp.concatenate(slots, axis=0) if len(slots) > 1 else slots[0]
    return [half, core_swap(half)]


def add_low(a, b):
    return (a.astype(f32) + b.astype(f32)).astype(bf16)


def core_sum(mine, other):
    chips = lax.axis_size("fsdp") // 2
    swapped = core_swap(other)
    if chips != 4:
        return [add_low(mine, swapped)]
    near = mine.shape[0] // 4 * 3
    return [add_low(mine[near:], swapped[near:]), add_low(mine[:near], swapped[:near])]


def reduce_far(far):
    return chip_send(far, [(0, 1), (3, 2), (1, 3), (2, 0)])


def reduce_near(near, far, chip):
    chips = lax.axis_size("fsdp") // 2
    size = near.shape[0] // len(near_slots(chips))
    near = near.astype(f32)
    if chips == 4:
        far = far.astype(f32)
        zero = jnp.zeros((), f32)
        ends = near[:size] + jnp.where((chip == 0) | (chip == 3), far, zero)
        up = (near[size : 2 * size] + jnp.where(chip == 1, far, zero)).astype(bf16)
        down = (near[2 * size :] + jnp.where(chip == 2, far, zero)).astype(bf16)
        from_below = chip_send(up, [(0, 1), (1, 2), (2, 3), (3, 0)])
        from_above = chip_send(down, [(1, 0), (2, 1), (3, 2), (0, 3)])
        return (ends + from_below.astype(f32) + from_above.astype(f32)).astype(bf16)
    total = near[:size]
    for t in range(1, chips):
        part = near[t * size : (t + 1) * size].astype(bf16)
        total = total + chip_send(part, [(z, (z + t) % chips) for z in range(chips)]).astype(f32)
    return total.astype(bf16)


def ctx_gather(a):
    return [a] + [ctx_send(a, t) for t in range(1, lax.axis_size("ctx"))]


def ctx_exchange(parts):
    return [parts[0]] + [ctx_send(parts[t], t) for t in range(1, len(parts))]


smem = pl.BlockSpec(memory_space=pltpu.SMEM)


def whole(a):
    return pl.BlockSpec(a.shape, lambda *_: (0,) * len(a.shape))


def struct(shape, dtype):
    return jax.ShapeDtypeStruct(shape, dtype)


def call(kernel, grid, in_specs, out_specs, out_shape, args, scratch=(), flops=0, moved=None, exps=0):
    if moved is None:
        moved = sum(a.size * a.dtype.itemsize for a in args) + sum(
            int(np.prod(o.shape)) * jnp.dtype(o.dtype).itemsize for o in out_shape
        )
    return pl.pallas_call(
        kernel,
        grid=grid,
        in_specs=in_specs,
        out_specs=out_specs,
        out_shape=out_shape,
        scratch_shapes=scratch,
        compiler_params=pltpu.CompilerParams(vmem_limit_bytes=vmem_limit),
        cost_estimate=pl.CostEstimate(flops=flops, bytes_accessed=moved, transcendentals=exps),
    )(*args)


def shard_places(refs, stride):
    return [(ref, s * stride) for ref in refs for s in range(ref.shape[0] // stride)]


def tile_of(size, most):
    tile = most
    while size % tile:
        tile //= 2
    return tile


def start_and_wait(copies):
    for c in copies:
        c.start()
    for c in copies:
        c.wait()


def at_step(n):
    return pl.when(pl.program_id(0) == n)


def choose_attention_kernel(head_ids, head_width, with_out, scal, q, k, v, wo, na, nf, table, out):
    position = scal[0]
    rows = q.shape[0]
    wide = out.shape[1]
    for c, ids in enumerate(head_ids):

        @pl.when(position == c)
        def _():
            for n, ref in enumerate((q, k, v)):
                for pair in range(len(ids) // 2):
                    halves = [
                        ref[:, h * head_width : (h + 1) * head_width]
                        for h in ids[2 * pair : 2 * pair + 2]
                    ]
                    out[n * rows : (n + 1) * rows, pair * 128 : pair * 128 + 128] = (
                        jnp.concatenate(halves, axis=1)
                    )
            if with_out:
                blocks = len(head_ids)
                size = rows // blocks
                for b in range(blocks):
                    out[3 * rows + b * size : 3 * rows + (b + 1) * size, :] = wo[
                        c * size : (c + 1) * size, b * wide : (b + 1) * wide
                    ]

    row = lax.broadcasted_iota(i32, (extra, rows), 0)
    gains = jnp.where(row == 0, na[...].astype(f32), jnp.where(row == 1, nf[...].astype(f32), 0.0))
    buckets, heads = table.shape
    low = jnp.concatenate(
        [
            jnp.zeros((2, heads), f32),
            table[...].astype(f32),
            jnp.zeros((extra - 2 - buckets, heads), f32),
        ],
        axis=0,
    )
    low = jnp.concatenate([low, jnp.zeros((extra, rows - heads), f32)], axis=1)
    last = out.shape[0] - extra
    out[last:, :] = jnp.zeros((extra, wide), bf16)
    out[last:, :rows] = (gains + low).astype(bf16)


def choose_units_kernel(shards, scal, gate, up, out):
    position = scal[0]
    units = out.shape[1] // 2
    size = units // shards
    group = gate.shape[1] // shards
    for c in range(gate.shape[1] // units):

        @pl.when(position == c)
        def _():
            for n, ref in enumerate((gate, up)):
                out[:, n * units : (n + 1) * units] = jnp.concatenate(
                    [
                        ref[:, r * group + c * size : r * group + (c + 1) * size]
                        for r in range(shards)
                    ],
                    axis=1,
                )


def tokens_kernel(shards, scal, x, cotangent, out):
    rows, width = x.shape
    size = width // shards
    for l in range(shards):
        start = pl.multiple_of(scal[2 + l] * size, size)
        out[:rows, l * size : (l + 1) * size] = x[:, pl.ds(start, size)]
    row = lax.broadcasted_iota(i32, (rows, width), 0) + scal[0] * rows
    out[rows:, :] = jnp.where(row < scal[1], cotangent[...].astype(f32), 0.0).astype(bf16)


def head_choice(each, shards, position, my_heads, heads):
    h = lax.broadcasted_iota(i32, (my_heads, heads), 0)
    if each:
        shift = each.bit_length() - 1
        head_id = (h >> shift) * (heads // shards) + position * each + (h & (each - 1))
    else:
        head_id = position * my_heads + h
    return (lax.broadcasted_iota(i32, (my_heads, heads), 1) == head_id).astype(f32).astype(bf16)


def bucket_rows(scal, shards, offset):
    row = lax.broadcasted_iota(i32, (bucket_total, offset.shape[1]), 0)
    buckets = bucket_total // shards
    shift = buckets.bit_length() - 1
    bucket_id = jnp.zeros_like(row)
    for l in range(shards):
        bucket_id = jnp.where(
            (row >> shift) == l, scal[2 + l] * buckets + (row & (buckets - 1)), bucket_id
        )
    return (buckets_of(offset) == bucket_id).astype(f32).astype(bf16)


def qkv_kernel(blocks, parts, shards, each, scal, *refs):
    tokens_refs, weights = refs[:blocks], refs[blocks : blocks + parts]
    normed, qkv, bias, gains, scales, joined, small, sems, small_sems = refs[blocks + parts :]
    rows = tokens_refs[0].shape[0]
    tokens, width = normed.shape
    size = width // shards
    stride = sum(w.shape[0] for w in weights) // shards
    places = shard_places(weights, stride)
    step = pl.program_id(0)

    def copy(n, l):
        ref, at = places[l]
        return pltpu.make_async_copy(
            ref.at[pl.ds(at + n * size, size), :],
            joined.at[n, pl.ds(l * size, size), :],
            sems.at[n, l],
        )

    def small_copy(l):
        ref, at = places[l]
        return pltpu.make_async_copy(
            ref.at[pl.ds(at + stride - extra, extra), :], small.at[l], small_sems.at[l]
        )

    @at_step(0)
    def _():
        for l in range(shards):
            small_copy(l).start()
        for n in range(3):
            for l in range(shards):
                copy(n, l).start()
        for l in range(shards):
            small_copy(l).wait()
        my_heads = 2 * bias.shape[0]
        heads = my_heads * blocks
        buckets = bucket_total // shards
        tables = []
        for l in range(shards):
            value = small[l, :, :size].astype(f32)
            gains[:, l * size : (l + 1) * size] = value[:2]
            tables.append(value[2 : 2 + buckets, :heads])
        table = jnp.concatenate(tables, axis=0).astype(bf16)
        chosen = head_choice(each, shards, scal[0], my_heads, heads)
        mine = dot(chosen, table, 1, 1).astype(bf16)
        offset = tokens - lax.broadcasted_iota(i32, (1, 2 * tokens), 1)
        value = dot(mine, bucket_rows(scal, shards, offset))
        for pair in range(bias.shape[0]):
            bias[pair] = value[2 * pair : 2 * pair + 2]
        for t in range(blocks):
            at = slice(t * rows, (t + 1) * rows)
            x = tokens_refs[t][...].astype(f32)
            scale = lax.rsqrt(jnp.mean(x * x, axis=1, keepdims=True) + epsilon)
            normed[at, :] = (x * scale * gains[0:1, :]).astype(bf16)
            scales[at, :] = jnp.broadcast_to(scale, (rows, 128))

    for n in range(3):

        @at_step(n)
        def _():
            for l in range(shards):
                copy(n, l).wait()

    qkv[...] = dot(normed[...], joined[step]).astype(bf16)


def project(scal, tokens_all, weights, shards, each, pairs):
    rows, width = tokens_all[0].shape[0] // 2, tokens_all[0].shape[1]
    blocks = len(tokens_all)
    tokens = rows * blocks
    wide = 128 * pairs
    return call(
        functools.partial(qkv_kernel, blocks, len(weights), shards, each),
        (3,),
        [smem]
        + [pl.BlockSpec((rows, width), lambda n: (0, 0))] * blocks
        + [pl.BlockSpec(memory_space=ANY)] * len(weights),
        [
            pl.BlockSpec((tokens, width), lambda n: (0, 0)),
            pl.BlockSpec((tokens, wide), lambda n: (0, n)),
            pl.BlockSpec((pairs, 2, 2 * tokens), lambda n: (0, 0, 0)),
            pl.BlockSpec((2, width), lambda n: (0, 0)),
            pl.BlockSpec((tokens, 128), lambda n: (0, 0)),
        ],
        [
            struct((tokens, width), bf16),
            struct((tokens, 3 * wide), bf16),
            struct((pairs, 2, 2 * tokens), f32),
            struct((2, width), f32),
            struct((tokens, 128), f32),
        ],
        (scal, *tokens_all, *weights),
        [
            pltpu.VMEM((3, width, wide), bf16),
            pltpu.VMEM((shards, extra, wide), bf16),
            pltpu.SemaphoreType.DMA((3, shards)),
            pltpu.SemaphoreType.DMA((shards,)),
        ],
        flops=6 * tokens * width * wide,
    )


def lanes_of(position, blocks, rows, query, key):
    start = (blocks - 1 + (position ^ query) - (position ^ key)) * rows
    return pl.ds(pl.multiple_of(start, rows), rows)


def forward_kernel(rows, blocks, scal, q_ref, k_ref, v_ref, bias_ref, att, prob, toeplitz):
    position, length = scal[0], scal[1]
    width = 2 * blocks * rows
    slot = lax.broadcasted_iota(i32, (rows, rows), 0)
    for j in range(2):
        row = jnp.broadcast_to(bias_ref[0, j : j + 1, :], (rows, width))
        toeplitz[j] = pltpu.roll(row, width - rows, 1, stride=1, stride_axis=0)
    values = [v_ref[:, 64 * j : 64 * j + 64].astype(f32).T.astype(bf16) for j in range(2)]
    for t in range(blocks):
        at = slice(t * rows, (t + 1) * rows)
        halves = []
        for j in range(2):
            q = q_ref[at, 64 * j : 64 * j + 64]
            k = k_ref[:, 64 * j : 64 * j + 64]
            scores = dot(k, q, 1, 1)
            pieces = []
            for s in range(blocks):
                piece = (
                    scores[s * rows : (s + 1) * rows]
                    + toeplitz[j, :, lanes_of(position, blocks, rows, t, s)]
                )
                live = slot + (position ^ s) * rows < length
                pieces.append(jnp.where(live, piece, masked_score))
            scores = jnp.concatenate(pieces, axis=0)
            top = jnp.max(scores, axis=0, keepdims=True)
            e = jnp.exp(scores - top)
            probs = (e * (1.0 / jnp.sum(e, axis=0, keepdims=True))).astype(bf16)
            prob[j, :, at] = probs
            halves.append(dot(values[j], probs))
        att[at, :] = jnp.concatenate(halves, axis=0).T.astype(bf16)


def backward_kernel(
    rows, blocks, scal, q_ref, k_ref, v_ref, prob, gatt, gq, gk, gv, diag_ref, fold, ds_all
):
    position = scal[0]
    width = 2 * blocks * rows
    grads = [[], [], []]
    for j in range(2):
        columns = slice(64 * j, 64 * j + 64)
        k, v = k_ref[:, columns], v_ref[:, columns]
        fold[...] = jnp.zeros_like(fold)
        for t in range(blocks):
            at = slice(t * rows, (t + 1) * rows)
            gp = dot(v, gatt[at, columns], 1, 1)
            p = prob[j, :, at].astype(f32)
            pg = p * gp
            delta = jnp.sum(pg, axis=0, keepdims=True)
            ds = (pg - p * delta).astype(bf16)
            ds_all[:, at] = ds
            ds = ds.astype(f32)
            for s in range(blocks):
                fold[:, lanes_of(position, blocks, rows, t, s)] += ds[s * rows : (s + 1) * rows]
        grads[0].append(dot(k.astype(f32).T.astype(bf16), ds_all[...]))
        grads[1].append(dot(ds_all[...], q_ref[:, columns]))
        grads[2].append(dot(prob[j], gatt[:, columns]))
        a = fold[...]
        half = rows // 2
        while half >= 8:
            a = a[:half] + pltpu.roll(a[half:], width - half, 1)
            half //= 2
        row = lax.broadcasted_iota(i32, a.shape, 0)
        for bit in (1, 2, 4):
            a = jnp.where((row & bit) != 0, pltpu.roll(a, width - bit, 1), a)
        diag_ref[0, j : j + 1, :] = jnp.sum(a, axis=0, keepdims=True)
    gq[...] = jnp.concatenate(grads[0], axis=0).T.astype(bf16)
    gk[...] = jnp.concatenate(grads[1], axis=1).astype(bf16)
    gv[...] = jnp.concatenate(grads[2], axis=1).astype(bf16)


def attention_forward(scal, qkv, bias, rows, blocks):
    tokens = rows * blocks
    pairs = bias.shape[0]
    return call(
        functools.partial(forward_kernel, rows, blocks),
        (pairs,),
        [smem]
        + [pl.BlockSpec((tokens, 128), lambda p, n=n: (0, n * pairs + p)) for n in range(3)]
        + [pl.BlockSpec((1, 2, 2 * tokens), lambda p: (p, 0, 0))],
        [
            pl.BlockSpec((tokens, 128), lambda p: (0, p)),
            pl.BlockSpec((2, tokens, tokens), lambda p: (p, 0, 0)),
        ],
        [struct((tokens, 128 * pairs), bf16), struct((2 * pairs, tokens, tokens), bf16)],
        (scal, qkv, qkv, qkv, bias),
        [pltpu.VMEM((2, rows, 2 * tokens), f32)],
        flops=8 * pairs * tokens * tokens * 64,
        exps=2 * pairs * tokens * tokens,
    )


def attention_backward(scal, qkv, probs, grad_att, rows, blocks):
    tokens = rows * blocks
    pairs = probs.shape[0] // 2
    block = pl.BlockSpec((tokens, 128), lambda p: (0, p))
    return call(
        functools.partial(backward_kernel, rows, blocks),
        (pairs,),
        [smem]
        + [pl.BlockSpec((tokens, 128), lambda p, n=n: (0, n * pairs + p)) for n in range(3)]
        + [pl.BlockSpec((2, tokens, tokens), lambda p: (p, 0, 0)), block],
        [block, block, block, pl.BlockSpec((1, 2, 2 * tokens), lambda p: (p, 0, 0))],
        [struct((tokens, 128 * pairs), bf16)] * 3 + [struct((pairs, 2, 2 * tokens), f32)],
        (scal, qkv, qkv, qkv, probs, grad_att),
        [pltpu.VMEM((rows, 2 * tokens), f32), pltpu.VMEM((tokens, tokens), bf16)],
        flops=16 * pairs * tokens * tokens * 64,
    )


def out_copies(shards, scal, weights, joined, sems):
    blocks, depth, _ = joined.shape
    size = depth // shards
    stride = sum(w.shape[0] for w in weights) // shards
    first = stride - extra - blocks * size
    copies = []
    for b in range(blocks):
        for l, (ref, at) in enumerate(shard_places(weights, stride)):
            start = pl.multiple_of(scal[2 + l] * size, size)
            copies.append(
                pltpu.make_async_copy(
                    ref.at[pl.ds(at + first + b * size, size), :],
                    joined.at[b, pl.ds(start, size), :],
                    sems.at[b, l],
                )
            )
    return copies


def out_kernel(blocks, parts, shards, scal, att, *refs):
    weights, outs, joined, sems = refs[:parts], refs[parts:-2], refs[-2], refs[-1]
    start_and_wait(out_copies(shards, scal, weights, joined, sems))
    rows = outs[0].shape[0]
    wide = joined.shape[2]
    for b in range(joined.shape[0]):
        total = dot(att[...], joined[b]).astype(bf16)
        for t in range(blocks):
            outs[t][:, b * wide : (b + 1) * wide] = total[t * rows : (t + 1) * rows]


def multiply_out(scal, att, weights, shards, blocks):
    tokens, wide = att.shape
    rows, width = tokens // blocks, wide * blocks
    return call(
        functools.partial(out_kernel, blocks, len(weights), shards),
        (1,),
        [smem, whole(att)] + [pl.BlockSpec(memory_space=ANY)] * len(weights),
        [pl.BlockSpec((rows, width), lambda i: (0, 0))] * blocks,
        [struct((rows, width), bf16)] * blocks,
        (scal, att, *weights),
        [pltpu.VMEM((blocks, wide, wide), bf16), pltpu.SemaphoreType.DMA((blocks, shards))],
        flops=2 * tokens * wide * width,
    )


def grad_attended_kernel(blocks, parts, shards, scal, *refs):
    low, weights = refs[:blocks], refs[blocks : blocks + parts]
    out, joined, sems = refs[blocks + parts :]
    start_and_wait(out_copies(shards, scal, weights, joined, sems))
    wide = joined.shape[2]
    for t, ref in enumerate(low):
        rows = ref.shape[0]
        total = None
        for b in range(joined.shape[0]):
            term = dot(ref[:, b * wide : (b + 1) * wide], joined[b], 1, 1)
            total = term if total is None else total + term
        out[t * rows : (t + 1) * rows, :] = total.astype(bf16)


def make_grad_attended(scal, low_all, weights, shards):
    blocks = len(low_all)
    rows, width = low_all[0].shape
    tokens, wide = rows * blocks, width // blocks
    return call(
        functools.partial(grad_attended_kernel, blocks, len(weights), shards),
        (1,),
        [smem] + [whole(a) for a in low_all] + [pl.BlockSpec(memory_space=ANY)] * len(weights),
        [pl.BlockSpec((tokens, wide), lambda i: (0, 0))],
        [struct((tokens, wide), bf16)],
        (scal, *low_all, *weights),
        [pltpu.VMEM((blocks, wide, wide), bf16), pltpu.SemaphoreType.DMA((blocks, shards))],
        flops=2 * tokens * wide * width,
    )[0]


def hidden_kernel(blocks, shards, scal, x, gains, *refs):
    parts, hidden, nffn = refs[:blocks], refs[blocks], refs[blocks + 1]
    total = x[...].astype(f32)
    for part in parts:
        total = total + part[...].astype(f32)
    hidden[...] = total
    scale = lax.rsqrt(jnp.mean(total * total, axis=1, keepdims=True) + epsilon)
    size = total.shape[1] // shards
    for l in range(shards):
        at = slice(l * size, (l + 1) * size)
        start = pl.multiple_of(scal[2 + l] * size, size)
        nffn[:, at] = (hidden[:, pl.ds(start, size)] * scale * gains[1:2, at]).astype(bf16)


def make_hidden(scal, x, gains, parts, shards):
    rows, width = x.shape
    args = (scal, x, gains, *parts)
    return call(
        functools.partial(hidden_kernel, len(parts), shards),
        (1,),
        [smem] + [whole(a) for a in args[1:]],
        [pl.BlockSpec((rows, width), lambda i: (0, 0))] * 2,
        [struct((rows, width), f32), struct((rows, width), bf16)],
        args,
    )


def gelu_tanh(g):
    return jnp.tanh(0.7978845608028654 * (g + 0.044715 * (g * g * g)))


def units_kernel(blocks, parts, tile, *refs):
    tokens_refs, weights = refs[:blocks], refs[blocks : blocks + parts]
    normed, gate, up, mixed, joined, sems = refs[blocks + parts :]
    rows = tokens_refs[0].shape[0]
    units = weights[0].shape[1] // 2
    step = pl.program_id(0)

    def copies(i):
        result, at = [], 0
        for w, ref in enumerate(weights):
            for n in range(2):
                result.append(
                    pltpu.make_async_copy(
                        ref.at[:, pl.ds(n * units + i * tile, tile)],
                        joined.at[i, pl.ds(at, ref.shape[0]), pl.ds(n * tile, tile)],
                        sems.at[i, 2 * w + n],
                    )
                )
            at += ref.shape[0]
        return result

    @at_step(0)
    def _():
        for i in range(units // tile):
            for c in copies(i):
                c.start()
        for t in range(blocks):
            normed[t * rows : (t + 1) * rows, :] = tokens_refs[t][...]

    for i in range(units // tile):

        @at_step(i)
        def _():
            for c in copies(i):
                c.wait()

    both = dot(normed[...], joined[step])
    g, u = both[:, :tile], both[:, tile:]
    gate[...] = g
    up[...] = u
    mixed[...] = (0.5 * g * (1.0 + gelu_tanh(g)) * u).astype(bf16)


def make_units(tokens_all, weights):
    rows, width = tokens_all[0].shape
    blocks = len(tokens_all)
    tokens = rows * blocks
    units = weights[0].shape[1] // 2
    tile = tile_of(units, 256)
    steps = units // tile
    out = pl.BlockSpec((tokens, tile), lambda i: (0, i))
    return call(
        functools.partial(units_kernel, blocks, len(weights), tile),
        (steps,),
        [whole(a) for a in tokens_all] + [pl.BlockSpec(memory_space=ANY)] * len(weights),
        [pl.BlockSpec((tokens, width), lambda i: (0, 0)), out, out, out],
        [
            struct((tokens, width), bf16),
            struct((tokens, units), f32),
            struct((tokens, units), f32),
            struct((tokens, units), bf16),
        ],
        (*tokens_all, *weights),
        [
            pltpu.VMEM((steps, width, 2 * tile), bf16),
            pltpu.SemaphoreType.DMA((steps, 2 * len(weights))),
        ],
        flops=4 * tokens * width * units,
    )


def grad_down_kernel(blocks, shards, scal, mixed, *refs):
    dy, outs, turned, low = refs[:blocks], refs[blocks:-2], refs[-2], refs[-1]

    @at_step(0)
    def _():
        turned[...] = mixed[...].T

    low[...] = dot(turned[...], jnp.concatenate([r[...] for r in dy], axis=0)).astype(bf16)
    size = low.shape[0] // shards
    each = shards // len(outs)
    for l in range(shards):
        start = pl.multiple_of(scal[2 + l] * size, size)
        outs[side_of(shards)[l][0]][pl.ds(side_of(shards)[l][1] * size, size), :] = low[
            pl.ds(start, size), :
        ]


def side_of(shards):
    chips = shards // 2
    sides, counts = [], [0, 0]
    for slots in (near_slots(chips), far_slots(chips)):
        for p in range(2):
            for _ in slots:
                sides.append((p, counts[p]))
                counts[p] += 1
    return sides


def make_grad_down(scal, mixed, tokens_all, shards):
    blocks = len(tokens_all)
    tokens, units = mixed.shape
    rows, width = tokens // blocks, tokens_all[0].shape[1]
    tile = tile_of(width, 512)
    return call(
        functools.partial(grad_down_kernel, blocks, shards),
        (width // tile,),
        [smem, whole(mixed)] + [pl.BlockSpec((rows, tile), lambda i: (1, i))] * blocks,
        [pl.BlockSpec((units // 2, tile), lambda i: (0, i))] * 2,
        [struct((units // 2, width), bf16)] * 2,
        (scal, mixed, *tokens_all),
        [pltpu.VMEM((units, tokens), bf16), pltpu.VMEM((units, tile), bf16)],
        flops=2 * tokens * units * width,
    )


def down_copies(shards, scal, weights, joined, sems):
    size = joined.shape[0] // shards
    copies = []
    for l, (ref, at) in enumerate(shard_places(weights, size)):
        start = pl.multiple_of(scal[2 + l] * size, size) if shards > 1 else 0
        copies.append(
            pltpu.make_async_copy(
                ref.at[pl.ds(at, size), :], joined.at[pl.ds(start, size), :], sems.at[l]
            )
        )
    return copies


def units_back_kernel(blocks, parts, shards, tile, scal, gate, up, *refs):
    dy, weights = refs[:blocks], refs[blocks : blocks + parts]
    out, joined, grads, sems = refs[blocks + parts :]
    step = pl.program_id(0)
    rows = dy[0].shape[0]
    units = joined.shape[0]

    @at_step(0)
    def _():
        copies = down_copies(shards, scal, weights, joined, sems)
        for c in copies:
            c.start()
        for t in range(blocks):
            grads[t * rows : (t + 1) * rows, :] = dy[t][...]
        for c in copies:
            c.wait()

    weight = joined[pl.ds(pl.multiple_of(step * tile, tile), tile), :]
    grad = dot(grads[...], weight, 1, 1)
    g, u = gate[...], up[...]
    t = gelu_tanh(g)
    slope = 0.5 * (1.0 + t) + 0.5 * g * (1.0 - t * t) * (
        0.7978845608028654 * (1.0 + 3 * 0.044715 * (g * g))
    )
    out[:, pl.ds(pl.multiple_of(step * tile, tile), tile)] = (grad * u * slope).astype(bf16)
    out[:, pl.ds(pl.multiple_of(units + step * tile, tile), tile)] = (
        grad * (0.5 * g * (1.0 + t))
    ).astype(bf16)


def units_back(scal, gate, up, tokens_all, weights, shards):
    blocks = len(tokens_all)
    tokens, units = gate.shape
    rows, width = tokens // blocks, tokens_all[0].shape[1]
    tile = tile_of(units, 256)
    block = pl.BlockSpec((tokens, tile), lambda i: (0, i))
    return call(
        functools.partial(units_back_kernel, blocks, len(weights), shards, tile),
        (units // tile,),
        [smem, block, block]
        + [pl.BlockSpec((rows, width), lambda i: (1, 0))] * blocks
        + [pl.BlockSpec(memory_space=ANY)] * len(weights),
        [pl.BlockSpec((tokens, 2 * units), lambda i: (0, 0))],
        [struct((tokens, 2 * units), bf16)],
        (scal, gate, up, *tokens_all, *weights),
        [
            pltpu.VMEM((units, width), bf16),
            pltpu.VMEM((tokens, width), bf16),
            pltpu.SemaphoreType.DMA((shards,)),
        ],
        flops=2 * tokens * units * width,
    )[0]


def result_kernel(blocks, parts, shards, tile, scal, mixed, *refs):
    weights, outs, joined, sems = refs[:parts], refs[parts:-2], refs[-2], refs[-1]
    start_and_wait(down_copies(shards, scal, weights, joined, sems))
    rows, width = outs[0].shape
    for i in range(width // tile):
        at = slice(i * tile, (i + 1) * tile)
        total = dot(mixed[...], joined[:, at]).astype(bf16)
        for t in range(blocks):
            outs[t][:, at] = total[t * rows : (t + 1) * rows]


def multiply_down(scal, mixed, weights, shards, blocks):
    tokens, units = mixed.shape
    width = weights[0].shape[1]
    rows = tokens // blocks
    return call(
        functools.partial(result_kernel, blocks, len(weights), shards, tile_of(width, 512)),
        (1,),
        [smem, whole(mixed)] + [pl.BlockSpec(memory_space=ANY)] * len(weights),
        [pl.BlockSpec((rows, width), lambda i: (0, 0))] * blocks,
        [struct((rows, width), bf16)] * blocks,
        (scal, mixed, *weights),
        [pltpu.VMEM((units, width), bf16), pltpu.SemaphoreType.DMA((shards,))],
        flops=2 * tokens * units * width,
    )


def shard_specs(weights, rows):
    specs, ranges, first = [], [], 0
    for w in weights:
        count = w.shape[0] // rows
        specs.append(
            pl.BlockSpec(
                (rows, w.shape[1]), lambda l, f=first, n=count: (jnp.clip(l - f, 0, n - 1), 0)
            )
        )
        ranges.append((first, first + count))
        first += count
    return specs, ranges


def within(bounds):
    l = pl.program_id(0)
    return pl.when((l >= bounds[0]) & (l < bounds[1]))


def ffn_transposed_kernel(ranges, g, *refs):
    weights, outs = refs[: len(ranges)], refs[len(ranges) :]
    rows = outs[0].shape[0]
    for ref, bounds in zip(weights, ranges):

        @within(bounds)
        def _():
            total = dot(g[...], ref[...], 1, 1).astype(bf16)
            for t, out in enumerate(outs):
                out[...] = total[t * rows : (t + 1) * rows]


def ffn_transposed(g, weights, size, shards, blocks):
    tokens, depth = g.shape
    rows, width = tokens // blocks, size * shards
    specs, ranges = shard_specs(weights, size)
    return call(
        functools.partial(ffn_transposed_kernel, ranges),
        (shards,),
        [whole(g)] + specs,
        [pl.BlockSpec((rows, size), lambda l: (0, l))] * blocks,
        [struct((rows, width), bf16)] * blocks,
        (g, *weights),
        flops=2 * tokens * depth * width,
    )


def units_grad_kernel(shards, normed, g, *refs):
    outs, turned = refs[:-1], refs[-1]

    @at_step(0)
    def _():
        turned[...] = normed[...].T

    total = dot(turned[...], g[...]).astype(bf16)
    at = 0
    for out in outs:
        n = out.shape[0]
        out[...] = total[at : at + n]
        at += n


def units_grad(normed, g, shards):
    tokens, depth = normed.shape
    width = g.shape[1]
    tile = tile_of(width, 512)
    sizes = []
    for slots in (near_slots(shards // 2), far_slots(shards // 2)):
        if slots:
            sizes += [len(slots) * (depth // shards)] * 2
    return call(
        functools.partial(units_grad_kernel, shards),
        (width // tile,),
        [whole(normed), pl.BlockSpec((tokens, tile), lambda i: (0, i))],
        [pl.BlockSpec((n, tile), lambda i: (0, i)) for n in sizes],
        [struct((n, width), bf16) for n in sizes],
        (normed, g),
        [pltpu.VMEM((depth, tokens), bf16)],
        flops=2 * tokens * depth * width,
    )


def attn_transposed_kernel(blocks, ranges, size, scales, gq, gk, gv, *refs):
    tokens_refs, weights = refs[:blocks], refs[blocks : blocks + len(ranges)]
    outs, gain = refs[blocks + len(ranges) : -1], refs[-1]
    rows = outs[0].shape[0]
    for ref, bounds in zip(weights, ranges):

        @within(bounds)
        def _():
            total = None
            for n, g in enumerate((gq, gk, gv)):
                term = dot(g[...], ref[n * size : (n + 1) * size, :], 1, 1)
                total = term if total is None else total + term
            summed = jnp.zeros((1, size), f32)
            for t, out in enumerate(outs):
                at = slice(t * rows, (t + 1) * rows)
                out[...] = total[at].astype(bf16)
                unit = tokens_refs[t][...].astype(f32) * scales[at, 0:1]
                summed = summed + jnp.sum(total[at] * unit, axis=0, keepdims=True)
            gain[...] = summed


def attn_transposed(scales, grads, tokens_all, weights, size, shards, blocks):
    tokens, wide = grads[0].shape
    rows, width = tokens // blocks, size * shards
    stride = sum(w.shape[0] for w in weights) // shards
    specs, ranges = shard_specs(weights, stride)
    tile = pl.BlockSpec((rows, size), lambda l: (0, l))
    results = call(
        functools.partial(attn_transposed_kernel, blocks, ranges, size),
        (shards,),
        [whole(scales)] + [whole(g) for g in grads] + [tile] * blocks + specs,
        [tile] * blocks + [pl.BlockSpec((1, size), lambda l: (0, l))],
        [struct((rows, width), bf16)] * blocks + [struct((1, width), f32)],
        (scales, *grads, *tokens_all, *weights),
        flops=6 * tokens * wide * width,
    )
    return results[:-1], results[-1]


def split_low(a):
    high = a.astype(bf16)
    return high, (a - high.astype(f32)).astype(bf16)


def attn_grad_kernel(
    blocks, shards, each, with_out, scal, normed, att, gq, gk, gv, diag, gain_attn, gain_ffn, *refs
):
    low = refs[:blocks]
    mine, other, joined, turned, table = refs[blocks:]
    tokens, width = normed.shape
    wide = att.shape[1]
    size = width // shards
    head_rows = wide // shards
    rows = tokens // blocks
    my_heads = 2 * diag.shape[0]
    heads = my_heads * blocks

    @at_step(0)
    def _():
        for n, g in enumerate((gq, gk, gv)):
            joined[:, n * wide : (n + 1) * wide] = g[...]
        if with_out:
            turned[...] = dot(
                att[...].T, jnp.concatenate([r[...] for r in low], axis=0)
            ).astype(bf16)
        lane = lax.broadcasted_iota(i32, (1, 2 * tokens), 1)
        lane = jnp.where(lane < 2 * tokens - rows, lane, lane - 2 * tokens)
        of_offset = bucket_rows(scal, shards, (blocks - 1) * rows - lane)
        sums = jnp.concatenate([diag[p] for p in range(diag.shape[0])], axis=0)
        total = None
        for part in split_low(sums):
            term = dot(of_offset, part, 1, 1)
            total = term if total is None else total + term
        chosen = head_choice(each, shards, scal[0], my_heads, heads)
        value = None
        for part in split_low(total):
            term = dot(part, chosen)
            value = term if value is None else value + term
        table[...] = value

    buckets = bucket_total // shards
    for l, (side, at) in enumerate(side_of(shards)):

        @at_step(l)
        def _():
            out = other if side else mine
            total = dot(normed[:, l * size : (l + 1) * size], joined[...], 0, 0).astype(bf16)
            for n in range(3):
                out[n * size : (n + 1) * size, :] = total[:, n * wide : (n + 1) * wide]
            if with_out:
                start = pl.multiple_of(scal[2 + l] * head_rows, head_rows)
                for b in range(blocks):
                    out[3 * size + b * head_rows : 3 * size + (b + 1) * head_rows, :] = turned[
                        pl.ds(start, head_rows), b * wide : (b + 1) * wide
                    ]
            part = jnp.concatenate(
                [
                    jnp.zeros((2, heads), f32),
                    table[l * buckets : (l + 1) * buckets, :],
                    jnp.zeros((extra - 2 - buckets, heads), f32),
                ],
                axis=0,
            )
            part = jnp.concatenate([part, jnp.zeros((extra, size - heads), f32)], axis=1)
            row = lax.broadcasted_iota(i32, (extra, size), 0)
            columns = slice(l * size, (l + 1) * size)
            part = part + jnp.where(
                row == 0,
                gain_attn[:, columns],
                jnp.where(row == 1, gain_ffn[:, columns], 0.0),
            )
            last = out.shape[0] - extra
            out[last:, :] = jnp.zeros((extra, wide), bf16)
            out[last:, :size] = part.astype(bf16)


def attn_grad(scal, normed, att, grads, diag, gain_attn, gain_ffn, low_all, shards, each, stride):
    tokens, width = normed.shape
    wide = att.shape[1]
    blocks = len(low_all)
    sides = side_of(shards)
    half = shards // 2

    def index(side):
        steps = [l for l in range(shards) if sides[l][0] == side]

        def at(l):
            place = 0
            for s in steps[1:]:
                place = place + (l >= s).astype(i32)
            return (place, 0)

        return at

    args = (scal, normed, att, *grads, diag, gain_attn, gain_ffn, *low_all)
    return call(
        functools.partial(attn_grad_kernel, blocks, shards, each, bool(each)),
        (shards,),
        [smem] + [whole(a) for a in args[1:]],
        [pl.BlockSpec((stride, wide), index(0)), pl.BlockSpec((stride, wide), index(1))],
        [struct((half * stride, wide), bf16)] * 2,
        args,
        [
            pltpu.VMEM((tokens, 3 * wide), bf16),
            pltpu.VMEM((wide, width), bf16),
            pltpu.VMEM((bucket_total, 2 * diag.shape[0] * blocks), f32),
        ],
        flops=8 * tokens * wide * width,
    )


def ffn_norm_back_kernel(blocks, shards, scal, hidden, gains, own, *refs):
    parts = refs[:blocks]
    grad_hidden, low, grad_gain, g, gain = refs[blocks:]
    size = hidden.shape[1] // shards
    for l in range(shards):
        at = slice(l * size, (l + 1) * size)
        start = pl.multiple_of(scal[2 + l] * size, size)
        total = parts[0][:, at].astype(f32)
        for part in parts[1:]:
            total = total + part[:, at].astype(f32)
        g[:, pl.ds(start, size)] = total
        gain[:, pl.ds(start, size)] = gains[1:2, at]
    h = hidden[...]
    scale = lax.rsqrt(jnp.mean(h * h, axis=1, keepdims=True) + epsilon)
    weighted = g[...] * gain[...]
    inner = jnp.mean(weighted * h, axis=1, keepdims=True)
    value = own[...].astype(f32) + scale * weighted - h * (scale * scale * scale) * inner
    grad_hidden[...] = value
    low[...] = value.astype(bf16)
    g[...] = g[...] * h * scale
    for l in range(shards):
        start = pl.multiple_of(scal[2 + l] * size, size)
        grad_gain[:, l * size : (l + 1) * size] = jnp.sum(
            g[:, pl.ds(start, size)], axis=0, keepdims=True
        )


def ffn_norm_back(scal, hidden, gains, own, parts, shards):
    rows, width = hidden.shape
    block = pl.BlockSpec((rows, width), lambda i: (0, 0))
    return call(
        functools.partial(ffn_norm_back_kernel, len(parts), shards),
        (1,),
        [smem, block, whole(gains), pl.BlockSpec((rows, width), lambda i: (1, 0))]
        + [block] * len(parts),
        [block, block, pl.BlockSpec((1, width), lambda i: (0, 0))],
        [struct((rows, width), f32), struct((rows, width), bf16), struct((1, width), f32)],
        (scal, hidden, gains, own, *parts),
        [pltpu.VMEM((rows, width), f32), pltpu.VMEM((1, width), f32)],
    )


def attn_norm_back_kernel(blocks, shards, scal, grad_hidden, gains, own, *refs):
    parts = refs[:blocks]
    grad, value = refs[blocks:]
    x = own[...].astype(f32)
    g = parts[0][...].astype(f32)
    for part in parts[1:]:
        g = g + part[...].astype(f32)
    scale = lax.rsqrt(jnp.mean(x * x, axis=1, keepdims=True) + epsilon)
    weighted = g * gains[0:1, :]
    inner = jnp.mean(weighted * x, axis=1, keepdims=True)
    value[...] = scale * weighted - x * (scale * scale * scale) * inner
    size = x.shape[1] // shards
    for l in range(shards):
        at = slice(l * size, (l + 1) * size)
        where = pl.ds(pl.multiple_of(scal[2 + l] * size, size), size)
        grad[:, where] = (grad_hidden[:, where] + value[:, at]).astype(bf16)


def attn_norm_back(scal, grad_hidden, gains, own, parts, shards):
    rows, width = grad_hidden.shape
    block = pl.BlockSpec((rows, width), lambda i: (0, 0))
    return call(
        functools.partial(attn_norm_back_kernel, len(parts), shards),
        (1,),
        [smem, block, whole(gains), block] + [block] * len(parts),
        [block],
        [struct((rows, width), bf16)],
        (scal, grad_hidden, gains, own, *parts),
        [pltpu.VMEM((rows, width), f32)],
    )[0]


def by_position(scal, blocks, body):
    for p in range(blocks):

        @pl.when(scal[0] == p)
        def _():
            body([p ^ c for c in range(blocks)])


def columns_kernel(groups, scal, *refs):
    pieces, outs = refs[:-2], refs[-2:]
    blocks = len(pieces)
    units = pieces[0].shape[1] // 2
    size = units // groups
    wide = blocks * size

    def body(order):
        for n, out in enumerate(outs):
            for g in range(groups):
                at = n * units + g * size
                out[:, g * wide : (g + 1) * wide] = jnp.concatenate(
                    [pieces[t][:, at : at + size] for t in order], axis=1
                ).astype(f32)

    by_position(scal, blocks, body)


def assemble_units(scal, pieces, groups):
    rows, columns = pieces[0].shape
    tile = min(rows, 32)
    wide = len(pieces) * columns // 2
    return call(
        functools.partial(columns_kernel, groups),
        (rows // tile,),
        [smem] + [pl.BlockSpec((tile, columns), lambda i: (i, 0))] * len(pieces),
        [pl.BlockSpec((tile, wide), lambda i: (i, 0))] * 2,
        [struct((rows, wide), f32)] * 2,
        (scal, *pieces),
    )


def rows_kernel(size, scal, *refs):
    position = scal[0]
    for t, piece in enumerate(refs[:-1]):
        start = pl.multiple_of((position ^ t) * size, 8)
        refs[-1][pl.ds(start, size), :] = piece[...].astype(f32)


def assemble_rows(scal, pieces):
    rows, columns = pieces[0].shape
    tile = tile_of(columns, 512)
    return call(
        functools.partial(rows_kernel, rows),
        (columns // tile,),
        [smem] + [pl.BlockSpec((rows, tile), lambda i: (0, i))] * len(pieces),
        [pl.BlockSpec((rows * len(pieces), tile), lambda i: (0, i))],
        [struct((rows * len(pieces), columns), f32)],
        (scal, *pieces),
    )[0]


def attention_outputs_kernel(each, groups, head_width, scal, *refs):
    blocks = groups
    columns = refs[: 3 * blocks]
    rest = refs[3 * blocks :]
    with_out = bool(each)
    out_blocks = rest[:blocks] if with_out else ()
    rest = rest[blocks:] if with_out else rest
    small, outs = rest[:blocks], rest[blocks:]
    wide = columns[0].shape[1]
    step = pl.program_id(0)

    def body(order):
        for n in range(3):
            pieces = [columns[3 * t + n] for t in order]
            if each:
                size = each * head_width
                for g in range(wide // size):
                    outs[n][:, g * blocks * size : (g + 1) * blocks * size] = jnp.concatenate(
                        [ref[:, g * size : (g + 1) * size] for ref in pieces], axis=1
                    ).astype(f32)
            else:
                for c, ref in enumerate(pieces):
                    outs[n][:, c * wide : (c + 1) * wide] = ref[...].astype(f32)

        @at_step(0)
        def _():
            total = small[order[0]][...].astype(f32)
            for t in order[1:]:
                total = total + small[t][...].astype(f32)
            outs[-1][...] = total

    by_position(scal, blocks, body)
    if with_out:
        for t in range(blocks):

            @pl.when((step ^ scal[0]) == t)
            def _():
                size = outs[3].shape[0]
                for b in range(blocks):
                    outs[3][:, b * wide : (b + 1) * wide] = out_blocks[t][
                        b * size : (b + 1) * size, :
                    ].astype(f32)


def attention_outputs(scal, pieces, rows, each, head_width):
    stride, wide = pieces[0].shape
    blocks = len(pieces)
    tile = rows // blocks
    width = wide * blocks
    per = rows // tile
    specs, args = [], []
    for a in pieces:
        for n in range(3):
            specs.append(pl.BlockSpec((tile, wide), lambda i, n=n: (n * per + i, 0)))
            args.append(a)
    if each:
        specs += [pl.BlockSpec((rows, wide), lambda i: (3, 0))] * blocks
        args += pieces
    specs += [pl.BlockSpec((extra, wide), lambda i: (stride // extra - 1, 0))] * blocks
    args += pieces
    block = pl.BlockSpec((tile, width), lambda i: (i, 0))
    count = 4 if each else 3
    return call(
        functools.partial(attention_outputs_kernel, each, blocks, head_width),
        (blocks,),
        [smem] + specs,
        [block] * count + [pl.BlockSpec((extra, wide), lambda i: (0, 0))],
        [struct((rows, width), f32)] * count + [struct((extra, wide), f32)],
        (scal, *args),
    )


def take_blocks(a, starts, size):
    return jnp.concatenate([lax.dynamic_slice_in_dim(a, s, size, 0) for s in starts], 0)


def on_device(
    inputs,
    lengths,
    w_query,
    w_key,
    w_value,
    w_out,
    w_gate,
    w_up,
    w_down,
    norm_attn,
    norm_ffn,
    relative_bias_table,
    cotangent,
):
    blocks = lax.axis_size("ctx")
    shards = lax.axis_size("fsdp")
    chips = shards // 2
    position = lax.axis_index("ctx")
    shard = lax.axis_index("fsdp")
    chip, core = shard // 2, shard % 2
    rows, width = inputs.shape[1], inputs.shape[2]
    tokens = rows * blocks
    heads = relative_bias_table.shape[1]
    head_width = width // heads
    my_heads = heads // blocks
    pairs = my_heads // 2
    each = heads // shards // blocks if (heads // shards) % blocks == 0 else 0
    strided = each in (1, 2)
    each = each if strided else 0
    units = w_gate.shape[1] // blocks
    shard_rows = width // shards
    unit_rows = w_down.shape[0] // blocks

    slot_of, parity_of = [], []
    for slots in (near_slots(chips), far_slots(chips)):
        for p in range(2):
            slot_of += slots
            parity_of += [p] * len(slots)
    pad = [0, 0]
    order = 2 * ((chip + jnp.array(pad + slot_of, i32)) % chips) + (
        core ^ jnp.array(pad + parity_of, i32)
    )
    index = jnp.arange(shards + 2, dtype=i32)
    scal = jnp.where(index == 0, position, jnp.where(index == 1, lengths[0], order)).astype(i32)

    def heads_of(c):
        if strided:
            return [
                (h // each) * (heads // shards) + c * each + h % each for h in range(my_heads)
            ]
        return [c * my_heads + h for h in range(my_heads)]

    own_tokens = call(
        functools.partial(tokens_kernel, shards),
        (1,),
        [smem] + [pl.BlockSpec((rows, width), lambda i: (0, 0))] * 2,
        [pl.BlockSpec((2 * rows, width), lambda i: (0, 0))],
        [struct((2 * rows, width), bf16)],
        (scal, inputs[0], cotangent[0]),
    )[0]
    all_tokens = ctx_gather(own_tokens)
    args = (
        after(scal, own_tokens),
        w_query,
        w_key,
        w_value,
        w_out,
        norm_attn.reshape(1, -1),
        norm_ffn.reshape(1, -1),
        relative_bias_table,
    )
    stride = (4 if strided else 3) * shard_rows + extra
    own_attn = call(
        functools.partial(
            choose_attention_kernel, [heads_of(c) for c in range(blocks)], head_width, strided
        ),
        (1,),
        [smem] + [whole(a) for a in args[1:]],
        [pl.BlockSpec((stride, 128 * pairs), lambda i: (0, 0))],
        [struct((stride, 128 * pairs), bf16)],
        args,
    )[0]
    near_attn = gather_near(own_attn)
    tile = tile_of(shard_rows, 64)
    own_gate_up = call(
        functools.partial(choose_units_kernel, shards),
        (shard_rows // tile,),
        [smem] + [pl.BlockSpec((tile, w_gate.shape[1]), lambda i: (i, 0))] * 2,
        [pl.BlockSpec((tile, 2 * units), lambda i: (i, 0))],
        [struct((shard_rows, 2 * units), bf16)],
        (after(scal, own_attn), w_gate, w_up),
    )[0]
    joint = together([*near_attn, *all_tokens], own_gate_up)
    near_attn, all_tokens = joint[: len(near_attn)], joint[len(near_attn) :]
    far_attn = gather_far(near_attn, chip)
    joint = together(with_other_core(near_attn) + far_attn)
    weights_attn, far_attn = list(joint[:2]), joint[2:]
    near_gate_up = gather_near(after(own_gate_up, *far_attn))
    weights_attn += with_other_core(far_attn)
    if not strided:
        gathered = lax.all_gather(w_out, "fsdp", axis=0, tiled=True)
        size = my_heads * head_width
        full_out = lax.dynamic_slice_in_dim(gathered, position * size, size, 0)

    normed, qkv, bias, gains, scales = project(
        scal, all_tokens, weights_attn, shards, each, pairs
    )
    attended, probs = attention_forward(scal, qkv, bias, rows, blocks)
    if strided:
        parts = multiply_out(scal, attended, weights_attn, shards, blocks)
    else:
        whole_part = dot(attended, full_out).astype(bf16)
        parts = [whole_part[t * rows : (t + 1) * rows] for t in range(blocks)]
    parts = ctx_exchange(parts)
    hidden, own_nffn = make_hidden(scal, inputs[0], gains, parts, shards)

    near_gate_up = together(near_gate_up, own_nffn)
    far_gate_up = gather_far(near_gate_up, chip)
    joint = together(with_other_core(near_gate_up) + ctx_gather(own_nffn) + far_gate_up)
    weights_gate_up = list(joint[:2])
    all_nffn, far_gate_up = joint[2 : 2 + blocks], joint[2 + blocks :]
    own_down = lax.dynamic_slice_in_dim(w_down, position * unit_rows, unit_rows, 0)
    near_down = gather_near(after(own_down, all_nffn[0]))
    weights_gate_up += with_other_core(far_gate_up)
    normed_ffn, gate, up, mixed_units = make_units(all_nffn, weights_gate_up)

    aligned = unit_rows % 16 == 0
    if aligned:
        grads_down = make_grad_down(scal, mixed_units, all_tokens, shards)
    else:
        all_dy = jnp.concatenate([a[rows:] for a in all_tokens], axis=0)
        grad_down = dot(mixed_units, all_dy, 0, 0).astype(bf16)
        grads_down = [
            take_blocks(
                grad_down,
                [order[2 + l] * unit_rows for l in range(shards) if parity_of[l] == side],
                unit_rows,
            )
            for side in range(2)
        ]
    sums_down = core_sum(*grads_down)
    near_down = together(near_down, *sums_down)
    far_down = gather_far(near_down, chip)
    joint = together(with_other_core(near_down) + far_down)
    down_parts, far_down = list(joint[:2]), joint[2:]
    down_parts, down_shards = down_parts + with_other_core(far_down), shards
    if not aligned:
        joined = jnp.concatenate(down_parts, axis=0)
        place = jnp.argsort(order[2:])
        down_parts = [take_blocks(joined, [place[r] * unit_rows for r in range(shards)], unit_rows)]
        down_shards = 1

    far_sum = None
    if len(sums_down) == 2:
        far_sum = reduce_far(after(sums_down[0], *far_down))
    grad_units = units_back(scal, gate, up, all_tokens, down_parts, down_shards)
    parts = ffn_transposed(grad_units, weights_gate_up, shard_rows, shards, blocks)
    if far_sum is not None:
        *parts, far_sum = together([*parts, far_sum])
    parts = list(parts)
    share_down = reduce_near(after(sums_down[-1], *parts), far_sum, chip)
    parts = ctx_exchange(parts)
    grads_gate_up = units_grad(normed_ffn, after(grad_units, parts[0]), shards)
    result_parts = multiply_down(
        scal, after(mixed_units, *grads_gate_up), down_parts, down_shards, blocks
    )
    parts = together(parts, *grads_gate_up, *result_parts)
    grad_hidden, low, grad_gain_ffn = ffn_norm_back(
        scal, hidden, gains, own_tokens, parts, shards
    )

    all_low = ctx_gather(low)
    far_sum = None
    if len(grads_gate_up) == 4:
        swapped = core_swap(after(grads_gate_up[3], share_down, low))
        far_sum = reduce_far(add_low(grads_gate_up[2], swapped))
        swapped = core_swap(after(grads_gate_up[1], swapped))
    else:
        swapped = core_swap(after(grads_gate_up[1], share_down, low))
    near_sum = add_low(grads_gate_up[0], swapped)
    joint = together([*all_low, near_sum])
    all_low, near_sum = joint[:-1], joint[-1]
    pieces_down = ctx_gather(after(share_down, *all_low))
    if strided:
        grad_att = make_grad_attended(scal, all_low, weights_attn, shards)
    else:
        grad_att = dot(jnp.concatenate(all_low, axis=0), full_out, 1, 1).astype(bf16)
    *grads, diagonals = attention_backward(scal, qkv, probs, grad_att, rows, blocks)
    parts, grad_gain_attn = attn_transposed(
        scales, grads, all_tokens, weights_attn, shard_rows, shards, blocks
    )
    joint = together([*parts, *pieces_down, near_sum] + ([] if far_sum is None else [far_sum]))
    parts, pieces_down = list(joint[:blocks]), joint[blocks : 2 * blocks]
    near_sum = joint[2 * blocks]
    far_sum = None if far_sum is None else joint[-1]
    share_gate_up = reduce_near(near_sum, far_sum, chip)
    parts = ctx_exchange(parts)
    grads_attn = attn_grad(
        scal,
        normed,
        attended,
        [after(grads[0], parts[0]), *grads[1:]],
        diagonals,
        grad_gain_attn,
        grad_gain_ffn,
        all_low,
        shards,
        each,
        stride,
    )
    parts = together(parts, *grads_attn)
    input_grad = attn_norm_back(scal, grad_hidden, gains, own_tokens, parts, shards)
    sums_attn = core_sum(grads_attn[0], after(grads_attn[1], input_grad))
    result_parts = ctx_exchange(together(result_parts, *sums_attn))
    result = hidden
    for part in result_parts:
        result = result + part.astype(f32)
    result = result.astype(bf16)
    share_gate_up, result = together([share_gate_up, result])
    far_sum = None
    if len(sums_attn) == 2:
        far_sum = reduce_far(after(sums_attn[0], share_gate_up))
    share_attn = reduce_near(after(sums_attn[-1], share_gate_up), far_sum, chip)
    joint = together([*ctx_gather(share_gate_up), share_attn])
    pieces_gate_up, share_attn = joint[:-1], joint[-1]
    pieces_attn = ctx_gather(share_attn)

    g_down = assemble_rows(scal, pieces_down)
    if blocks * unit_rows % 128 == 0:
        g_gate, g_up = assemble_units(scal, pieces_gate_up, shards)
    else:
        stacked = jnp.stack(pieces_gate_up)
        stacked = [
            lax.dynamic_slice_in_dim(stacked, position ^ c, 1, 0)[0] for c in range(blocks)
        ]
        g_gate, g_up = [
            jnp.concatenate(
                [
                    stacked[c][:, n * units + r * unit_rows : n * units + (r + 1) * unit_rows]
                    for r in range(shards)
                    for c in range(blocks)
                ],
                axis=1,
            ).astype(f32)
            for n in range(2)
        ]
    *outs_attn, small = attention_outputs(scal, pieces_attn, shard_rows, each, head_width)
    if not strided:
        spot = jnp.zeros((width, width), bf16)
        spot = lax.dynamic_update_slice_in_dim(
            spot,
            dot(attended, jnp.concatenate(all_low, axis=0), 0, 0).astype(bf16),
            position * my_heads * head_width,
            0,
        )
        g_out = lax.psum_scatter(spot, "fsdp", scatter_dimension=0, tiled=True)
        outs_attn.append(lax.psum(g_out, "ctx").astype(f32))
    buckets = relative_bias_table.shape[0]
    return (
        result[None],
        input_grad[None],
        *outs_attn,
        g_gate,
        g_up,
        g_down,
        small[0, :shard_rows],
        small[1, :shard_rows],
        small[2 : 2 + buckets, :heads],
    )


def solution(mesh):
    rows = P("fsdp", None)
    tokens = P("fsdp", "ctx", None)
    in_specs = (tokens, P("fsdp")) + (rows,) * 7 + (P("fsdp"), P("fsdp"), rows, tokens)
    out_specs = (tokens, tokens) + (rows,) * 7 + (P("fsdp"), P("fsdp"), rows)
    return jax.shard_map(
        on_device, mesh=mesh, in_specs=in_specs, out_specs=out_specs, check_vma=False
    )
```

time: 832 us -> 647 us (0.78)
  Pallas kernels: 33.2 us -> 164 us
  local copies, waits for them, and re-layouts: 104 us -> 25.3 us
  matrix products: 74.8 us -> 0 us
  waiting for transfers between devices: 399 us -> 351 us
  other arithmetic: 69.6 us -> 23.5 us
  blocking collectives: 37.3 us -> 0 us
  starting transfers between devices: 100 us -> 70.9 us
    pallas_call x2 -> x22, Pallas kernels: 33.2 us -> 164 us  [call(): pl.pallas_call(kernel, grid=grid, in_specs=in_specs, out_specs=out_specs,...]
    ppermute x27 -> x18, waiting for transfers between devices: 255 us -> 180 us  [chip_send(): lax.ppermute(a, 'fsdp', [(2 * s + k, 2 * d + k) for s, d in pairs for k i...]
    dot_general x18 -> x0, matrix products: 74.8 us -> none  [the longest x12 65 us: dot(): lax.dot_general(a, b, (((ca,), (cb,)), ((), ())), preferred_element_type=...]
    psum x1 -> x0, blocking collectives: 37.3 us -> none  [on_device(): packed = lax.psum(packed, ('ctx', 'fsdp'))]
    convert_element_type x8 -> x0, local copies, waits for them, and re-layouts: 28.7 us -> none  [the longest x7 22.9 us: spread(): jnp.transpose(pieces.reshape(n, r, groups, -1), (1, 2, 0, 3)).reshape(r, -1)]
    unnamed x178 -> x113, local copies, waits for them, and re-layouts: 47.9 us -> 20 us
    ppermute x36 -> x30, waiting for transfers between devices: 140 us -> 160 us  [ctx_send(): return lax.ppermute(a, 'ctx', [(i, i ^ distance) for i in range(size)])]
    ppermute x27 -> x18, starting transfers between devices: 53.1 us -> 35.1 us  [chip_send(): lax.ppermute(a, 'fsdp', [(2 * s + k, 2 * d + k) for s, d in pairs for k i...]
  transfers between devices with their start and end apart: 87 -> 58, of which waited for: 36 -> 32; matrix products, arithmetic and copies ran while one was open for 23% -> 3% of each run, Pallas kernels for 4% -> 21%
where the time goes in v2:
time: 647 us; the launch traced here: 637 us
  waiting for transfers between devices  351 us (54%)
  Pallas kernels  164 us (25%)
  starting transfers between devices  70.9 us (11%)
  local copies, waits for them, and re-layouts  25.3 us (4%)
  other arithmetic  23.5 us (4%)
    ppermute x18, waiting for transfers between devices, chip_send(): lax.ppermute(a, 'fsdp', [(2 * s + k, 2 * d + k) for s, d in pairs for k i...  180 us
    pallas_call x22, Pallas kernels, call(): pl.pallas_call(kernel, grid=grid, in_specs=in_specs, out_specs=out_specs,...  164 us
    ppermute x30, waiting for transfers between devices, ctx_send(): return lax.ppermute(a, 'ctx', [(i, i ^ distance) for i in range(size)])  160 us
    ppermute x30, starting transfers between devices, ctx_send(): return lax.ppermute(a, 'ctx', [(i, i ^ distance) for i in range(size)])  35.2 us
    ppermute x18, starting transfers between devices, chip_send(): lax.ppermute(a, 'fsdp', [(2 * s + k, 2 * d + k) for s, d in pairs for k i...  35.1 us
    unnamed x113, local copies, waits for them, and re-layouts  20 us
  transfers between devices with their start and end apart: 58, of which 32 were waited for; matrix products, arithmetic and copies ran while one was open for 3% of the time, Pallas kernels for 21%

profile of v2, /device:TPU:0, one launch (start us, length us, event | category | flops | bytes accessed | tf_op | source)
XLA Modules:
  0.0 637.1 jit_solution(3513062191201083429)
XLA Ops:
  22.6 20.3 %collective-permute-done.4.refs_3_ = bf16[256,2048]{1,0:T(8,128)(2,1)} collective-permute-done((bf16[256,2048]{1,0:T(8,128)(2,1)}, bf16[256,2048]{1,0:T(8,128)(2,1)}, u32[]{:S(2)}, u32[]{:S(2)}) %collective-permute-start.4) | collective-permute-done | bytes 1048608 | tf_op jit(solution)/shard_map/ppermute | solution.py:55
  42.9 21.0 %collective-permute-done.3.refs_2_ = bf16[256,2048]{1,0:T(8,128)(2,1)} collective-permute-done((bf16[256,2048]{1,0:T(8,128)(2,1)}, bf16[256,2048]{1,0:T(8,128)(2,1)}, u32[]{:S(2)}, u32[]{:S(2)}) %collective-permute-start.3) | collective-permute-done | bytes 1048608 | tf_op jit(solution)/shard_map/ppermute | solution.py:55
  69.3 23.9 %collective-permute-done.6.refs_6_.refs_2_ = bf16[1040,512]{1,0:T(8,128)(2,1)S(1)} collective-permute-done((bf16[1040,512]{1,0:T(8,128)(2,1)S(1)}, bf16[1040,512]{1,0:T(8,128)(2,1)S(1)}, u32[]{:S(2)}, u32[]{:S(2)}) %collective-permute-start.6) | collective-permute-done | bytes 1064992 | tf_op jit(solution)/shard_map/ppermute | solution.py:50
  98.1 10.0 %shard_map.241 = (bf16[512,2048]{1,0:T(8,128)(2,1)}, bf16[512,1536]{1,0:T(8,128)(2,1)}, f32[4,2,1024]{2,1,0:T(2,128)S(1)}, f32[2,2048]{1,0:T(2,128)S(1)}, f32[512,128]{1,0:T(8,128)S(1)}) custom-call(s32[10]{0:T(128)S(1)} %compare_select_fusion.3.scal, bf16[256,2048]{1,0:T(8,128)(2,1)} %shard_map.238.refs_0_.own, ...), custom_call_target="tpu_custom_call" | custom-call | flops 3221225472 | bytes 16695336 | tf_op jit(solution)/shard_map/pallas_call | solution.py:153
  108.1 12.0 %shard_map.242 = (bf16[512,512]{1,0:T(8,128)(2,1)S(1)}, bf16[8,512,512]{2,1,0:T(8,128)(2,1)}) custom-call(s32[10]{0:T(128)S(1)} %compare_select_fusion.3.scal, bf16[512,1536]{1,0:T(8,128)(2,1)} %get-tuple-element.157.q_ref.k_ref.v_ref, bf16[512,1536]{1,0:T(8,128)(2,1)} %get-tuple-element.157.q_ref.k_ref.v_ref, ...), custom_call_target="tpu_custom_call" | custom-call | flops 536870912 | bytes 9469992 | tf_op jit(solution)/shard_map/pallas_call | solution.py:153
  129.5 11.3 %collective-permute-done.8.refs_1_ = bf16[128,2048]{1,0:T(8,128)(2,1)S(1)} collective-permute-done((bf16[128,2048]{1,0:T(8,128)(2,1)S(1)}, bf16[128,2048]{1,0:T(8,128)(2,1)S(1)}, u32[]{:S(2)}, u32[]{:S(2)}) %collective-permute-start.8) | collective-permute-done | bytes 524320 | tf_op jit(solution)/shard_map/ppermute | solution.py:55
  140.8 11.3 %collective-permute-done.9.refs_2_ = bf16[128,2048]{1,0:T(8,128)(2,1)S(1)} collective-permute-done((bf16[128,2048]{1,0:T(8,128)(2,1)S(1)}, bf16[128,2048]{1,0:T(8,128)(2,1)S(1)}, u32[]{:S(2)}, u32[]{:S(2)}) %collective-permute-start.9) | collective-permute-done | bytes 524320 | tf_op jit(solution)/shard_map/ppermute | solution.py:55
  166.5 12.2 %collective-permute-done.16.refs_3_ = bf16[128,2048]{1,0:T(8,128)(2,1)S(1)} collective-permute-done((bf16[128,2048]{1,0:T(8,128)(2,1)S(1)}, bf16[128,2048]{1,0:T(8,128)(2,1)S(1)}, u32[]{:S(2)}, u32[]{:S(2)}) %collective-permute-start.16) | collective-permute-done | bytes 524320 | tf_op jit(solution)/shard_map/ppermute | solution.py:55
  178.7 10.4 %collective-permute-done.15.refs_2_ = bf16[128,2048]{1,0:T(8,128)(2,1)S(1)} collective-permute-done((bf16[128,2048]{1,0:T(8,128)(2,1)S(1)}, bf16[128,2048]{1,0:T(8,128)(2,1)S(1)}, u32[]{:S(2)}, u32[]{:S(2)}) %collective-permute-start.15) | collective-permute-done | bytes 524320 | tf_op jit(solution)/shard_map/ppermute | solution.py:55
  197.7 10.9 %shard_map.245 = (bf16[512,2048]{1,0:T(8,128)(2,1)}, f32[512,1280]{1,0:T(8,128)}, f32[512,1280]{1,0:T(8,128)}, bf16[512,1280]{1,0:T(8,128)(2,1)}) custom-call(bf16[128,2048]{1,0:T(8,128)(2,1)S(1)} %get-tuple-element.172.refs_0_, bf16[128,2048]{1,0:T(8,128)(2,1)S(1)} %collective-permute-done.14.refs_1_, ...), custom_call_target="tpu_custom_call" | custom-call | flops 5368709120 | bytes 21233664 | tf_op jit(solution)/shard_map/pallas_call | solution.py:153
  208.6 7.5 %shard_map.246 = (bf16[640,2048]{1,0:T(8,128)(2,1)}, bf16[640,2048]{1,0:T(8,128)(2,1)}) custom-call(s32[10]{0:T(128)S(1)} %compare_select_fusion.3.scal, bf16[512,1280]{1,0:T(8,128)(2,1)} %get-tuple-element.206.mixed, bf16[256,2048]{1,0:T(8,128)(2,1)} %shard_map.238.refs_0_.own, bf16[256,2048]{1,0:T(8,128)(2,1)} %collective-permute-done.2.refs_1_, ...), custom_call_target="tpu_custom_call" | custom-call | flops 2684354560 | bytes 10747944 | tf_op jit(solution)/shard_map/pallas_call | solution.py:153
  226.3 9.4 %collective-permute-done.20 = bf16[160,2048]{1,0:T(8,128)(2,1)S(1)} collective-permute-done((bf16[160,2048]{1,0:T(8,128)(2,1)S(1)}, bf16[160,2048]{1,0:T(8,128)(2,1)S(1)}, u32[]{:S(2)}, u32[]{:S(2)}) %collective-permute-start.20) | collective-permute-done | bytes 655392 | tf_op jit(solution)/shard_map/ppermute | solution.py:50
  235.7 13.5 %collective-permute-done.19 = bf16[160,2048]{1,0:T(8,128)(2,1)S(1)} collective-permute-done((bf16[160,2048]{1,0:T(8,128)(2,1)S(1)}, bf16[160,2048]{1,0:T(8,128)(2,1)S(1)}, u32[]{:S(2)}, u32[]{:S(2)}) %collective-permute-start.19) | collective-permute-done | bytes 655392 | tf_op jit(solution)/shard_map/ppermute | solution.py:50
  251.4 15.5 %collective-permute-done.23.refs_6_.refs_2_ = bf16[160,2048]{1,0:T(8,128)(2,1)S(1)} collective-permute-done((bf16[160,2048]{1,0:T(8,128)(2,1)S(1)}, bf16[160,2048]{1,0:T(8,128)(2,1)S(1)}, u32[]{:S(2)}, u32[]{:S(2)}) %collective-permute-start.23) | collective-permute-done | bytes 655392 | tf_op jit(solution)/shard_map/ppermute | solution.py:50
  270.3 11.2 %shard_map.247.g = bf16[512,2560]{1,0:T(8,128)(2,1)} custom-call(s32[10]{0:T(128)S(1)} %compare_select_fusion.3.scal, f32[512,1280]{1,0:T(8,128)} %get-tuple-element.179.gate, f32[512,1280]{1,0:T(8,128)} %get-tuple-element.180.up, bf16[256,2048]{1,0:T(8,128)(2,1)} %shard_map.238.refs_0_.own, bf16[256,2048]{1,0:T(8,128)(2,1)} %collective-permute-done.2.refs_1_, ...), custom_call_target="tpu_custom_call" | custom-call | flops 2684354560 | bytes 17301544 | tf_op jit(solution)/shard_map/pallas_call | solution.py:153
  281.5 12.6 %shard_map.248 = (bf16[128,2048]{1,0:T(8,128)(2,1)S(1)}, bf16[128,2048]{1,0:T(8,128)(2,1)S(1)}, bf16[128,2048]{1,0:T(8,128)(2,1)S(1)}, bf16[128,2048]{1,0:T(8,128)(2,1)}) custom-call(bf16[512,2560]{1,0:T(8,128)(2,1)} %shard_map.247.g, bf16[768,2560]{1,0:T(8,128)(2,1)} %copy-done.48, bf16[768,2560]{1,0:T(8,128)(2,1)} %copy-done.49, ...), custom_call_target="tpu_custom_call" | custom-call | flops 5368709120 | bytes 15204352 | tf_op jit(solution)/shard_map/pallas_call | solution.py:153
  302.7 9.7 %shard_map.249 = (bf16[768,2560]{1,0:T(8,128)(2,1)}, bf16[768,2560]{1,0:T(8,128)(2,1)}, bf16[256,2560]{1,0:T(8,128)(2,1)S(1)}, bf16[256,2560]{1,0:T(8,128)(2,1)}) custom-call(bf16[512,2048]{1,0:T(8,128)(2,1)} %get-tuple-element.200.normed, bf16[512,2560]{1,0:T(8,128)(2,1)} %shard_map.247.g), custom_call_target="tpu_custom_call" | custom-call | flops 5368709120 | bytes 15204352 | tf_op jit(solution)/shard_map/pallas_call | solution.py:153
  312.4 7.5 %shard_map.250 = (bf16[128,2048]{1,0:T(8,128)(2,1)S(1)}, bf16[128,2048]{1,0:T(8,128)(2,1)S(1)}, bf16[128,2048]{1,0:T(8,128)(2,1)S(1)}, bf16[128,2048]{1,0:T(8,128)(2,1)}) custom-call(s32[10]{0:T(128)S(1)} %compare_select_fusion.3.scal, bf16[512,1280]{1,0:T(8,128)(2,1)} %get-tuple-element.206.mixed, bf16[480,2048]{1,0:T(8,128)(2,1)} %copy-done.34, ...), custom_call_target="tpu_custom_call" | custom-call | flops 2684354560 | bytes 8650792 | tf_op jit(solution)/shard_map/pallas_call | solution.py:153
  351.0 10.6 %collective-permute-done.30.refs_2_ = bf16[128,2048]{1,0:T(8,128)(2,1)S(1)} collective-permute-done((bf16[128,2048]{1,0:T(8,128)(2,1)S(1)}, bf16[128,2048]{1,0:T(8,128)(2,1)S(1)}, u32[]{:S(2)}, u32[]{:S(2)}) %collective-permute-start.30) | collective-permute-done | bytes 524320 | tf_op jit(solution)/shard_map/ppermute | solution.py:55
  371.9 11.7 %shard_map.253 = (bf16[512,512]{1,0:T(8,128)(2,1)S(1)}, bf16[512,512]{1,0:T(8,128)(2,1)S(1)}, bf16[512,512]{1,0:T(8,128)(2,1)S(1)}, f32[4,2,1024]{2,1,0:T(2,128)S(1)}) custom-call(s32[10]{0:T(128)S(1)} %compare_select_fusion.3.scal, bf16[512,1536]{1,0:T(8,128)(2,1)} %get-tuple-element.157.q_ref.k_ref.v_ref, ...), custom_call_target="tpu_custom_call" | custom-call | flops 1073741824 | bytes 11042856 | tf_op jit(solution)/shard_map/pallas_call | solution.py:153
  386.1 10.8 %shard_map.254 = (bf16[128,2048]{1,0:T(8,128)(2,1)S(1)}, bf16[128,2048]{1,0:T(8,128)(2,1)S(1)}, bf16[128,2048]{1,0:T(8,128)(2,1)S(1)}, bf16[128,2048]{1,0:T(8,128)(2,1)}, f32[1,2048]{1,0:T(1,128)S(1)}) custom-call(f32[512,128]{1,0:T(8,128)S(1)} %get-tuple-element.156.scales, bf16[512,512]{1,0:T(8,128)(2,1)} %copy-done.8, bf16[512,512]{1,0:T(8,128)(2,1)} %copy-done.10, ...), custom_call_target="tpu_custom_call" | custom-call | flops 3221225472 | bytes 16654336 | tf_op jit(solution)/shard_map/pallas_call | solution.py:153
  401.5 11.3 %shard_map.255 = (bf16[4160,512]{1,0:T(8,128)(2,1)}, bf16[4160,512]{1,0:T(8,128)(2,1)}) custom-call(s32[10]{0:T(128)S(1)} %compare_select_fusion.3.scal, bf16[512,2048]{1,0:T(8,128)(2,1)} %get-tuple-element.235.normed, bf16[512,512]{1,0:T(8,128)(2,1)S(1)} %copy-done.15, bf16[512,512]{1,0:T(8,128)(2,1)S(1)} %copy-done.9, bf16[512,512]{1,0:T(8,128)(2,1)S(1)} %copy-done.11, ...), custom_call_target="tpu_custom_call" | custom-call | flops 4294967296 | bytes 14860328 | tf_op jit(solution)/shard_map/pallas_call | solution.py:153
  412.9 9.7 %collective-permute-done.43.refs_2_ = bf16[128,2048]{1,0:T(8,128)(2,1)S(1)} collective-permute-done((bf16[128,2048]{1,0:T(8,128)(2,1)S(1)}, bf16[128,2048]{1,0:T(8,128)(2,1)S(1)}, u32[]{:S(2)}, u32[]{:S(2)}) %collective-permute-start.43) | collective-permute-done | bytes 524320 | tf_op jit(solution)/shard_map/ppermute | solution.py:55
  442.2 20.1 %collective-permute-done.40 = bf16[256,2560]{1,0:T(8,128)(2,1)S(1)} collective-permute-done((bf16[256,2560]{1,0:T(8,128)(2,1)S(1)}, bf16[256,2560]{1,0:T(8,128)(2,1)S(1)}, u32[]{:S(2)}, u32[]{:S(2)}) %collective-permute-start.40) | collective-permute-done | bytes 1310752 | tf_op jit(solution)/shard_map/ppermute | solution.py:50
  462.2 26.3 %collective-permute-done.41 = bf16[256,2560]{1,0:T(8,128)(2,1)S(1)} collective-permute-done((bf16[256,2560]{1,0:T(8,128)(2,1)S(1)}, bf16[256,2560]{1,0:T(8,128)(2,1)S(1)}, u32[]{:S(2)}, u32[]{:S(2)}) %collective-permute-start.41) | collective-permute-done | bytes 1310752 | tf_op jit(solution)/shard_map/ppermute | solution.py:50
  492.2 23.8 %collective-permute-done.52 = bf16[1040,512]{1,0:T(8,128)(2,1)S(1)} collective-permute-done((bf16[1040,512]{1,0:T(8,128)(2,1)S(1)}, bf16[1040,512]{1,0:T(8,128)(2,1)S(1)}, u32[]{:S(2)}, u32[]{:S(2)}) %collective-permute-start.52) | collective-permute-done | bytes 1064992 | tf_op jit(solution)/shard_map/ppermute | solution.py:50
  524.1 20.9 %collective-permute-done.53 = bf16[1040,512]{1,0:T(8,128)(2,1)S(1)} collective-permute-done((bf16[1040,512]{1,0:T(8,128)(2,1)S(1)}, bf16[1040,512]{1,0:T(8,128)(2,1)S(1)}, u32[]{:S(2)}, u32[]{:S(2)}) %collective-permute-start.53) | collective-permute-done | bytes 1064992 | tf_op jit(solution)/shard_map/ppermute | solution.py:50
  545.0 18.3 %collective-permute-done.54 = bf16[1040,512]{1,0:T(8,128)(2,1)S(1)} collective-permute-done((bf16[1040,512]{1,0:T(8,128)(2,1)S(1)}, bf16[1040,512]{1,0:T(8,128)(2,1)S(1)}, u32[]{:S(2)}, u32[]{:S(2)}) %collective-permute-start.54) | collective-permute-done | bytes 1064992 | tf_op jit(solution)/shard_map/ppermute | solution.py:50
  564.0 13.9 %collective-permute-done.50.refs_2_ = bf16[256,2560]{1,0:T(8,128)(2,1)S(1)} collective-permute-done((bf16[256,2560]{1,0:T(8,128)(2,1)S(1)}, bf16[256,2560]{1,0:T(8,128)(2,1)S(1)}, u32[]{:S(2)}, u32[]{:S(2)}) %collective-permute-start.50) | collective-permute-done | bytes 1310752 | tf_op jit(solution)/shard_map/ppermute | solution.py:55
  585.8 8.8 %shard_map.258 = (f32[256,5120]{1,0:T(8,128)}, f32[256,5120]{1,0:T(8,128)}) custom-call(s32[10]{0:T(128)S(1)} %compare_select_fusion.3.scal, bf16[256,2560]{1,0:T(8,128)(2,1)S(1)} %fusion.3.refs_0_, bf16[256,2560]{1,0:T(8,128)(2,1)} %collective-permute-done.49.refs_1_, bf16[256,2560]{1,0:T(8,128)(2,1)} %copy-done.40, bf16[256,2560]{1,0:T(8,128)(2,1)} %copy-done.39), custom_call_target="tpu_custom_call" | custom-call | bytes 15728680 | tf_op jit(solution)/shard_map/pallas_call | solution.py:153
  594.6 10.8 %collective-permute-done.57.refs_9_.refs_10_.refs_11_.refs_15_.refs_19_ = bf16[1040,512]{1,0:T(8,128)(2,1)S(1)} collective-permute-done((bf16[1040,512]{1,0:T(8,128)(2,1)S(1)}, bf16[1040,512]{1,0:T(8,128)(2,1)S(1)}, u32[]{:S(2)}, u32[]{:S(2)}) %collective-permute-start.57) | collective-permute-done | bytes 1064992 | tf_op jit(solution)/shard_map/ppermute | solution.py:55
  605.4 21.8 %collective-permute-done.56.refs_6_.refs_7_.refs_8_.refs_14_.refs_18_ = bf16[1040,512]{1,0:T(8,128)(2,1)S(1)} collective-permute-done((bf16[1040,512]{1,0:T(8,128)(2,1)S(1)}, bf16[1040,512]{1,0:T(8,128)(2,1)S(1)}, u32[]{:S(2)}, u32[]{:S(2)}) %collective-permute-start.56) | collective-permute-done | bytes 1064992 | tf_op jit(solution)/shard_map/ppermute | solution.py:55
  (247 shorter events, 185.6 us)
Async XLA Ops:
  10.5 53.5 %collective-permute-start.1 = (bf16[1040,512]{1,0:T(8,128)(2,1)}, bf16[1040,512]{1,0:T(8,128)(2,1)}, u32[]{:S(2)}, u32[]{:S(2)}) collective-permute-start(bf16[1040,512]{1,0:T(8,128)(2,1)} %shard_map.239), channel_id=1, source_target_pairs={{0,2},{1,3},{2,4},{3,5},{4,6},{5,7},{6,0},{7,1},{8,10},{9,11},{10,... | collective-permute-start | bytes 3194888 | tf_op jit(solution)/shard_map/ppermute | solution.py:50
  13.5 50.4 %collective-permute-start = (bf16[1040,512]{1,0:T(8,128)(2,1)}, bf16[1040,512]{1,0:T(8,128)(2,1)}, u32[]{:S(2)}, u32[]{:S(2)}) collective-permute-start(bf16[1040,512]{1,0:T(8,128)(2,1)} %shard_map.239), channel_id=1, source_target_pairs={{2,0},{3,1},{4,2},{5,3},{6,4},{7,5},{0,6},{1,7},{10,8},{11,9},{12,... | collective-permute-start | bytes 3194888 | tf_op jit(solution)/shard_map/ppermute | solution.py:50
  15.5 27.3 %collective-permute-start.4 = (bf16[256,2048]{1,0:T(8,128)(2,1)}, bf16[256,2048]{1,0:T(8,128)(2,1)}, u32[]{:S(2)}, u32[]{:S(2)}) collective-permute-start(bf16[256,2048]{1,0:T(8,128)(2,1)} %shard_map.238.refs_0_.own), channel_id=1, source_target_pairs={{0,24},{8,16},{16,8},{24,0},{1,25},{9,17},{17,9},{25,1},{2,26},{10... | collective-permute-start | bytes 3145736 | tf_op jit(solution)/shard_map/ppermute | solution.py:55
  18.2 45.6 %collective-permute-start.3 = (bf16[256,2048]{1,0:T(8,128)(2,1)}, bf16[256,2048]{1,0:T(8,128)(2,1)}, u32[]{:S(2)}, u32[]{:S(2)}) collective-permute-start(bf16[256,2048]{1,0:T(8,128)(2,1)} %shard_map.238.refs_0_.own), channel_id=1, source_target_pairs={{0,16},{8,24},{16,0},{24,8},{1,17},{9,25},{17,1},{25,9},{2,18},{10... | collective-permute-start | bytes 3145736 | tf_op jit(solution)/shard_map/ppermute | solution.py:55
  18.7 45.2 %collective-permute-start.2 = (bf16[256,2048]{1,0:T(8,128)(2,1)}, bf16[256,2048]{1,0:T(8,128)(2,1)}, u32[]{:S(2)}, u32[]{:S(2)}) collective-permute-start(bf16[256,2048]{1,0:T(8,128)(2,1)} %shard_map.238.refs_0_.own), channel_id=1, source_target_pairs={{0,8},{8,0},{16,24},{24,16},{1,9},{9,1},{17,25},{25,17},{2,10},{10... | collective-permute-start | bytes 3145736 | tf_op jit(solution)/shard_map/ppermute | solution.py:55
  67.2 26.0 %collective-permute-start.5 = (bf16[3120,512]{1,0:T(8,128)(2,1)S(1)}, bf16[3120,512]{1,0:T(8,128)(2,1)S(1)}, u32[]{:S(2)}, u32[]{:S(2)}) collective-permute-start(bf16[3120,512]{1,0:T(8,128)(2,1)S(1)} %constant_dynamic-update-slice_fusion.refs_4_.refs_0_), channel_id=1, source_target_pairs={{0,1},{1,0},{2,3},{3,2},{4,5},{5,4},{6,7},{7,6},{8,9},{9,8},{10,11... | collective-permute-start | bytes 9584648 | tf_op jit(solution)/shard_map/ppermute | solution.py:46
  67.3 25.9 %collective-permute-start.6 = (bf16[1040,512]{1,0:T(8,128)(2,1)S(1)}, bf16[1040,512]{1,0:T(8,128)(2,1)S(1)}, u32[]{:S(2)}, u32[]{:S(2)}) collective-permute-start(bf16[1040,512]{1,0:T(8,128)(2,1)S(1)} %get-tuple-element.284), channel_id=1, source_target_pairs={{6,2},{7,3},{0,4},{1,5},{2,0},{3,1},{4,6},{5,7},{14,10},{15,11},{8... | collective-permute-start | bytes 3194888 | tf_op jit(solution)/shard_map/ppermute | solution.py:50
  93.3 62.6 %collective-permute-start.12 = (bf16[256,2560]{1,0:T(8,128)(2,1)S(1)}, bf16[256,2560]{1,0:T(8,128)(2,1)}, u32[]{:S(2)}, u32[]{:S(2)}) collective-permute-start(bf16[256,2560]{1,0:T(8,128)(2,1)S(1)} %shard_map.240), channel_id=1, source_target_pairs={{0,2},{1,3},{2,4},{3,5},{4,6},{5,7},{6,0},{7,1},{8,10},{9,11},{10,... | collective-permute-start | bytes 3932168 | tf_op jit(solution)/shard_map/ppermute | solution.py:50
  95.2 60.7 %collective-permute-start.11 = (bf16[256,2560]{1,0:T(8,128)(2,1)S(1)}, bf16[256,2560]{1,0:T(8,128)(2,1)}, u32[]{:S(2)}, u32[]{:S(2)}) collective-permute-start(bf16[256,2560]{1,0:T(8,128)(2,1)S(1)} %shard_map.240), channel_id=1, source_target_pairs={{2,0},{3,1},{4,2},{5,3},{6,4},{7,5},{0,6},{1,7},{10,8},{11,9},{12,... | collective-permute-start | bytes 3932168 | tf_op jit(solution)/shard_map/ppermute | solution.py:50
  159.4 32.2 %collective-permute-start.13 = (bf16[768,2560]{1,0:T(8,128)(2,1)S(1)}, bf16[768,2560]{1,0:T(8,128)(2,1)S(1)}, u32[]{:S(2)}, u32[]{:S(2)}) collective-permute-start(bf16[768,2560]{1,0:T(8,128)(2,1)S(1)} %constant_dynamic-update-slice_fusion.3.refs_4_.refs_0_), channel_id=1, source_target_pairs={{0,1},{1,0},{2,3},{3,2},{4,5},{5,4},{6,7},{7,6},{8,9},{9,8},{10,11... | collective-permute-start | bytes 11796488 | tf_op jit(solution)/shard_map/ppermute | solution.py:46
  159.5 32.1 %collective-permute-start.17 = (bf16[256,2560]{1,0:T(8,128)(2,1)S(1)}, bf16[256,2560]{1,0:T(8,128)(2,1)S(1)}, u32[]{:S(2)}, u32[]{:S(2)}) collective-permute-start(bf16[256,2560]{1,0:T(8,128)(2,1)S(1)} %get-tuple-element.282), channel_id=1, source_target_pairs={{6,2},{7,3},{0,4},{1,5},{2,0},{3,1},{4,6},{5,7},{14,10},{15,11},{8... | collective-permute-start | bytes 3932168 | tf_op jit(solution)/shard_map/ppermute | solution.py:50
  218.7 30.5 %collective-permute-start.19 = (bf16[160,2048]{1,0:T(8,128)(2,1)S(1)}, bf16[160,2048]{1,0:T(8,128)(2,1)S(1)}, u32[]{:S(2)}, u32[]{:S(2)}) collective-permute-start(bf16[160,2048]{1,0:T(8,128)(2,1)S(1)} %constant_dynamic-slice_fusion), channel_id=1, source_target_pairs={{2,0},{3,1},{4,2},{5,3},{6,4},{7,5},{0,6},{1,7},{10,8},{11,9},{12,... | collective-permute-start | bytes 1966088 | tf_op jit(solution)/shard_map/ppermute | solution.py:50
  294.1 25.9 %collective-permute-start.26 = (bf16[128,2048]{1,0:T(8,128)(2,1)S(1)}, bf16[128,2048]{1,0:T(8,128)(2,1)S(1)}, u32[]{:S(2)}, u32[]{:S(2)}) collective-permute-start(bf16[128,2048]{1,0:T(8,128)(2,1)S(1)} %get-tuple-element.197), channel_id=1, source_target_pairs={{0,8},{8,0},{16,24},{24,16},{1,9},{9,1},{17,25},{25,17},{2,10},{10... | collective-permute-start | bytes 1572872 | tf_op jit(solution)/shard_map/ppermute | solution.py:55
  298.4 26.1 %collective-permute-start.32 = (bf16[160,2048]{1,0:T(8,128)(2,1)S(1)}, bf16[160,2048]{1,0:T(8,128)(2,1)}, u32[]{:S(2)}, u32[]{:S(2)}) collective-permute-start(bf16[160,2048]{1,0:T(8,128)(2,1)S(1)} %get-tuple-element.280), channel_id=1, source_target_pairs={{0,2},{1,3},{2,4},{3,5},{4,6},{5,7},{6,0},{7,1},{8,10},{9,11},{10,... | collective-permute-start | bytes 1966088 | tf_op jit(solution)/shard_map/ppermute | solution.py:50
  300.0 30.2 %collective-permute-start.33 = (bf16[160,2048]{1,0:T(8,128)(2,1)S(1)}, bf16[160,2048]{1,0:T(8,128)(2,1)}, u32[]{:S(2)}, u32[]{:S(2)}) collective-permute-start(bf16[160,2048]{1,0:T(8,128)(2,1)S(1)} %get-tuple-element.281), channel_id=1, source_target_pairs={{2,0},{3,1},{4,2},{5,3},{6,4},{7,5},{0,6},{1,7},{10,8},{11,9},{12,... | collective-permute-start | bytes 1966088 | tf_op jit(solution)/shard_map/ppermute | solution.py:50
  339.2 57.8 %collective-permute-start.39 = (bf16[256,2560]{1,0:T(8,128)(2,1)S(1)}, bf16[256,2560]{1,0:T(8,128)(2,1)S(1)}, u32[]{:S(2)}, u32[]{:S(2)}) collective-permute-start(bf16[256,2560]{1,0:T(8,128)(2,1)S(1)} %add_convert_fusion.3), channel_id=1, source_target_pairs={{0,2},{1,3},{6,4},{7,5},{2,6},{3,7},{4,0},{5,1},{8,10},{9,11},{14,... | collective-permute-start | bytes 3932168 | tf_op jit(solution)/shard_map/ppermute | solution.py:50
  361.7 35.3 %collective-permute-start.38 = (bf16[160,2048]{1,0:T(8,128)(2,1)S(1)}, bf16[160,2048]{1,0:T(8,128)(2,1)}, u32[]{:S(2)}, u32[]{:S(2)}) collective-permute-start(bf16[160,2048]{1,0:T(8,128)(2,1)S(1)} %fusion.19.refs_0_), channel_id=1, source_target_pairs={{0,24},{8,16},{16,8},{24,0},{1,25},{9,17},{17,9},{25,1},{2,26},{10... | collective-permute-start | bytes 1966088 | tf_op jit(solution)/shard_map/ppermute | solution.py:55
  363.1 33.8 %collective-permute-start.37 = (bf16[160,2048]{1,0:T(8,128)(2,1)S(1)}, bf16[160,2048]{1,0:T(8,128)(2,1)S(1)}, u32[]{:S(2)}, u32[]{:S(2)}) collective-permute-start(bf16[160,2048]{1,0:T(8,128)(2,1)S(1)} %fusion.19.refs_0_), channel_id=1, source_target_pairs={{0,16},{8,24},{16,0},{24,8},{1,17},{9,25},{17,1},{25,9},{2,18},{10... | collective-permute-start | bytes 1966088 | tf_op jit(solution)/shard_map/ppermute | solution.py:55
  363.8 33.2 %collective-permute-start.36 = (bf16[160,2048]{1,0:T(8,128)(2,1)S(1)}, bf16[160,2048]{1,0:T(8,128)(2,1)S(1)}, u32[]{:S(2)}, u32[]{:S(2)}) collective-permute-start(bf16[160,2048]{1,0:T(8,128)(2,1)S(1)} %fusion.19.refs_0_), channel_id=1, source_target_pairs={{0,8},{8,0},{16,24},{24,16},{1,9},{9,1},{17,25},{25,17},{2,10},{10... | collective-permute-start | bytes 1966088 | tf_op jit(solution)/shard_map/ppermute | solution.py:55
  428.7 33.5 %collective-permute-start.40 = (bf16[256,2560]{1,0:T(8,128)(2,1)S(1)}, bf16[256,2560]{1,0:T(8,128)(2,1)S(1)}, u32[]{:S(2)}, u32[]{:S(2)}) collective-permute-start(bf16[256,2560]{1,0:T(8,128)(2,1)S(1)} %get-tuple-element.276), channel_id=1, source_target_pairs={{0,2},{1,3},{2,4},{3,5},{4,6},{5,7},{6,0},{7,1},{8,10},{9,11},{10,... | collective-permute-start | bytes 3932168 | tf_op jit(solution)/shard_map/ppermute | solution.py:50
  429.6 59.0 %collective-permute-start.41 = (bf16[256,2560]{1,0:T(8,128)(2,1)S(1)}, bf16[256,2560]{1,0:T(8,128)(2,1)S(1)}, u32[]{:S(2)}, u32[]{:S(2)}) collective-permute-start(bf16[256,2560]{1,0:T(8,128)(2,1)S(1)} %get-tuple-element.277), channel_id=1, source_target_pairs={{2,0},{3,1},{4,2},{5,3},{6,4},{7,5},{0,6},{1,7},{10,8},{11,9},{12,... | collective-permute-start | bytes 3932168 | tf_op jit(solution)/shard_map/ppermute | solution.py:50
  438.6 50.7 %collective-permute-start.46 = (bf16[128,2048]{1,0:T(8,128)(2,1)S(1)}, bf16[128,2048]{1,0:T(8,128)(2,1)S(1)}, u32[]{:S(2)}, u32[]{:S(2)}) collective-permute-start(bf16[128,2048]{1,0:T(8,128)(2,1)S(1)} %get-tuple-element.253), channel_id=1, source_target_pairs={{0,8},{8,0},{16,24},{24,16},{1,9},{9,1},{17,25},{25,17},{2,10},{10... | collective-permute-start | bytes 1572872 | tf_op jit(solution)/shard_map/ppermute | solution.py:55
  440.1 49.2 %collective-permute-start.47 = (bf16[128,2048]{1,0:T(8,128)(2,1)S(1)}, bf16[128,2048]{1,0:T(8,128)(2,1)S(1)}, u32[]{:S(2)}, u32[]{:S(2)}) collective-permute-start(bf16[128,2048]{1,0:T(8,128)(2,1)S(1)} %get-tuple-element.254), channel_id=1, source_target_pairs={{0,16},{8,24},{16,0},{24,8},{1,17},{9,25},{17,1},{25,9},{2,18},{10... | collective-permute-start | bytes 1572872 | tf_op jit(solution)/shard_map/ppermute | solution.py:55
  440.9 48.5 %collective-permute-start.48 = (bf16[128,2048]{1,0:T(8,128)(2,1)S(1)}, bf16[128,2048]{1,0:T(8,128)(2,1)S(1)}, u32[]{:S(2)}, u32[]{:S(2)}) collective-permute-start(bf16[128,2048]{1,0:T(8,128)(2,1)S(1)} %copy-done.53), channel_id=1, source_target_pairs={{0,24},{8,16},{16,8},{24,0},{1,25},{9,17},{17,9},{25,1},{2,26},{10... | collective-permute-start | bytes 1572872 | tf_op jit(solution)/shard_map/ppermute | solution.py:55
  516.7 28.3 %collective-permute-start.53 = (bf16[1040,512]{1,0:T(8,128)(2,1)S(1)}, bf16[1040,512]{1,0:T(8,128)(2,1)S(1)}, u32[]{:S(2)}, u32[]{:S(2)}) collective-permute-start(bf16[1040,512]{1,0:T(8,128)(2,1)S(1)} %get-tuple-element.278), channel_id=1, source_target_pairs={{0,2},{1,3},{2,4},{3,5},{4,6},{5,7},{6,0},{7,1},{8,10},{9,11},{10,... | collective-permute-start | bytes 3194888 | tf_op jit(solution)/shard_map/ppermute | solution.py:50
  516.8 46.5 %collective-permute-start.54 = (bf16[1040,512]{1,0:T(8,128)(2,1)S(1)}, bf16[1040,512]{1,0:T(8,128)(2,1)S(1)}, u32[]{:S(2)}, u32[]{:S(2)}) collective-permute-start(bf16[1040,512]{1,0:T(8,128)(2,1)S(1)} %get-tuple-element.279), channel_id=1, source_target_pairs={{2,0},{3,1},{4,2},{5,3},{6,4},{7,5},{0,6},{1,7},{10,8},{11,9},{12,... | collective-permute-start | bytes 3194888 | tf_op jit(solution)/shard_map/ppermute | solution.py:50
  520.6 43.4 %collective-permute-start.51 = (bf16[256,2560]{1,0:T(8,128)(2,1)S(1)}, bf16[256,2560]{1,0:T(8,128)(2,1)S(1)}, u32[]{:S(2)}, u32[]{:S(2)}) collective-permute-start(bf16[256,2560]{1,0:T(8,128)(2,1)S(1)} %fusion.3.refs_0_), channel_id=1, source_target_pairs={{0,24},{8,16},{16,8},{24,0},{1,25},{9,17},{17,9},{25,1},{2,26},{10... | collective-permute-start | bytes 3932168 | tf_op jit(solution)/shard_map/ppermute | solution.py:55
  522.2 55.7 %collective-permute-start.50 = (bf16[256,2560]{1,0:T(8,128)(2,1)S(1)}, bf16[256,2560]{1,0:T(8,128)(2,1)S(1)}, u32[]{:S(2)}, u32[]{:S(2)}) collective-permute-start(bf16[256,2560]{1,0:T(8,128)(2,1)S(1)} %fusion.3.refs_0_), channel_id=1, source_target_pairs={{0,16},{8,24},{16,0},{24,8},{1,17},{9,25},{17,1},{25,9},{2,18},{10... | collective-permute-start | bytes 3932168 | tf_op jit(solution)/shard_map/ppermute | solution.py:55
  523.5 54.5 %collective-permute-start.49 = (bf16[256,2560]{1,0:T(8,128)(2,1)S(1)}, bf16[256,2560]{1,0:T(8,128)(2,1)}, u32[]{:S(2)}, u32[]{:S(2)}) collective-permute-start(bf16[256,2560]{1,0:T(8,128)(2,1)S(1)} %fusion.3.refs_0_), channel_id=1, source_target_pairs={{0,8},{8,0},{16,24},{24,16},{1,9},{9,1},{17,25},{25,17},{2,10},{10... | collective-permute-start | bytes 3932168 | tf_op jit(solution)/shard_map/ppermute | solution.py:55
  578.0 27.3 %collective-permute-start.57 = (bf16[1040,512]{1,0:T(8,128)(2,1)S(1)}, bf16[1040,512]{1,0:T(8,128)(2,1)S(1)}, u32[]{:S(2)}, u32[]{:S(2)}) collective-permute-start(bf16[1040,512]{1,0:T(8,128)(2,1)S(1)} %fusion.11.refs_0_.refs_1_.refs_2_.refs_12_.refs_16_), channel_id=1, source_target_pairs={{0,24},{8,16},{16,8},{24,0},{1,25},{9,17},{17,9},{25,1},{2,26},{10... | collective-permute-start | bytes 3194888 | tf_op jit(solution)/shard_map/ppermute | solution.py:55
  579.6 47.6 %collective-permute-start.56 = (bf16[1040,512]{1,0:T(8,128)(2,1)S(1)}, bf16[1040,512]{1,0:T(8,128)(2,1)S(1)}, u32[]{:S(2)}, u32[]{:S(2)}) collective-permute-start(bf16[1040,512]{1,0:T(8,128)(2,1)S(1)} %fusion.11.refs_0_.refs_1_.refs_2_.refs_12_.refs_16_), channel_id=1, source_target_pairs={{0,16},{8,24},{16,0},{24,8},{1,17},{9,25},{17,1},{25,9},{2,18},{10... | collective-permute-start | bytes 3194888 | tf_op jit(solution)/shard_map/ppermute | solution.py:55
  580.8 46.3 %collective-permute-start.55 = (bf16[1040,512]{1,0:T(8,128)(2,1)S(1)}, bf16[1040,512]{1,0:T(8,128)(2,1)S(1)}, u32[]{:S(2)}, u32[]{:S(2)}) collective-permute-start(bf16[1040,512]{1,0:T(8,128)(2,1)S(1)} %fusion.11.refs_0_.refs_1_.refs_2_.refs_12_.refs_16_), channel_id=1, source_target_pairs={{0,8},{8,0},{16,24},{24,16},{1,9},{9,1},{17,25},{25,17},{2,10},{10... | collective-permute-start | bytes 3194888 | tf_op jit(solution)/shard_map/ppermute | solution.py:55
  (81 other events, 1209.8 us)

commit v3 on v2

--- a/solution.py
+++ b/solution.py
@@ -106,28 +106,60 @@
     return chip_send(far, [(0, 1), (3, 2), (1, 3), (2, 0)])
 
 
-def reduce_near(near, far, chip):
+def near_sends(near, far, chip, rows=None):
     chips = lax.axis_size("fsdp") // 2
     size = near.shape[0] // len(near_slots(chips))
-    near = near.astype(f32)
+    first, last = rows or (0, size)
+    parts = [
+        near[s * size + first : s * size + last].astype(f32) for s in range(len(near_slots(chips)))
+    ]
     if chips == 4:
-        far = far.astype(f32)
+        far = far[first:last].astype(f32)
         zero = jnp.zeros((), f32)
-        ends = near[:size] + jnp.where((chip == 0) | (chip == 3), far, zero)
-        up = (near[size : 2 * size] + jnp.where(chip == 1, far, zero)).astype(bf16)
-        down = (near[2 * size :] + jnp.where(chip == 2, far, zero)).astype(bf16)
-        from_below = chip_send(up, [(0, 1), (1, 2), (2, 3), (3, 0)])
-        from_above = chip_send(down, [(1, 0), (2, 1), (3, 2), (0, 3)])
-        return (ends + from_below.astype(f32) + from_above.astype(f32)).astype(bf16)
-    total = near[:size]
-    for t in range(1, chips):
-        part = near[t * size : (t + 1) * size].astype(bf16)
-        total = total + chip_send(part, [(z, (z + t) % chips) for z in range(chips)]).astype(f32)
+        ends = parts[0] + jnp.where((chip == 0) | (chip == 3), far, zero)
+        up = parts[1] + jnp.where(chip == 1, far, zero)
+        down = parts[2] + jnp.where(chip == 2, far, zero)
+        parts = [ends, up, down]
+    return [parts[0]] + [p.astype(bf16) for p in parts[1:]]
+
+
+def near_receive(sends):
+    chips = lax.axis_size("fsdp") // 2
+    if chips == 4:
+        from_below = chip_send(sends[1], [(0, 1), (1, 2), (2, 3), (3, 0)])
+        from_above = chip_send(sends[2], [(1, 0), (2, 1), (3, 2), (0, 3)])
+        return [sends[0], from_below, from_above]
+    return [sends[0]] + [
+        chip_send(sends[t], [(z, (z + t) % chips) for z in range(chips)]) for t in range(1, chips)
+    ]
+
+
+def near_total(received):
+    total = received[0]
+    for part in received[1:]:
+        total = total + part.astype(f32)
     return total.astype(bf16)
 
 
 def ctx_gather(a):
     return [a] + [ctx_send(a, t) for t in range(1, lax.axis_size("ctx"))]
+
+
+def ctx_gather_near(a):
+    if lax.axis_size("ctx") == 4:
+        return [ctx_send(a, 1), ctx_send(a, 2)]
+    return ctx_gather(a)[1:]
+
+
+def ctx_gather_far(near):
+    if lax.axis_size("ctx") == 4:
+        half = near[0].shape[0] // 2
+        return [ctx_send(near[1][:half], 1), ctx_send(near[0][half:], 2)]
+    return []
+
+
+def ctx_pieces(own, near, far):
+    return [own, *near] + ([jnp.concatenate(far, axis=0)] if far else [])
 
 
 def ctx_exchange(parts):
@@ -158,7 +190,7 @@
         out_shape=out_shape,
         scratch_shapes=scratch,
         compiler_params=pltpu.CompilerParams(vmem_limit_bytes=vmem_limit),
-        cost_estimate=pl.CostEstimate(flops=flops, bytes_accessed=moved, transcendentals=exps),
+        cost_estimate=pl.CostEstimate(flops=1, bytes_accessed=1, transcendentals=0),
     )(*args)
 
 
@@ -933,11 +965,23 @@
     return high, (a - high.astype(f32)).astype(bf16)
 
 
+def owner_counts(shards):
+    counts = []
+    for slots in (near_slots(shards // 2), far_slots(shards // 2)):
+        if slots:
+            counts += [len(slots)] * 2
+    return counts
+
+
+def shard_owners(outs, shards):
+    return [out for out, n in zip(outs, owner_counts(shards)) for _ in range(n)]
+
+
 def attn_grad_kernel(
     blocks, shards, each, with_out, scal, normed, att, gq, gk, gv, diag, gain_attn, gain_ffn, *refs
 ):
     low = refs[:blocks]
-    mine, other, joined, turned, table = refs[blocks:]
+    outs, (joined, turned, table) = refs[blocks:-3], refs[-3:]
     tokens, width = normed.shape
     wide = att.shape[1]
     size = width // shards
@@ -970,11 +1014,10 @@
         table[...] = value
 
     buckets = bucket_total // shards
-    for l, (side, at) in enumerate(side_of(shards)):
+    for l, out in enumerate(shard_owners(outs, shards)):
 
         @at_step(l)
         def _():
-            out = other if side else mine
             total = dot(normed[:, l * size : (l + 1) * size], joined[...], 0, 0).astype(bf16)
             for n in range(3):
                 out[n * size : (n + 1) * size, :] = total[:, n * wide : (n + 1) * wide]
@@ -1009,27 +1052,20 @@
     tokens, width = normed.shape
     wide = att.shape[1]
     blocks = len(low_all)
-    sides = side_of(shards)
-    half = shards // 2
-
-    def index(side):
-        steps = [l for l in range(shards) if sides[l][0] == side]
-
-        def at(l):
-            place = 0
-            for s in steps[1:]:
-                place = place + (l >= s).astype(i32)
-            return (place, 0)
-
-        return at
-
+    counts = owner_counts(shards)
+    specs, first = [], 0
+    for n in counts:
+        specs.append(
+            pl.BlockSpec((stride, wide), lambda l, f=first, n=n: (jnp.clip(l - f, 0, n - 1), 0))
+        )
+        first += n
     args = (scal, normed, att, *grads, diag, gain_attn, gain_ffn, *low_all)
     return call(
         functools.partial(attn_grad_kernel, blocks, shards, each, bool(each)),
         (shards,),
         [smem] + [whole(a) for a in args[1:]],
-        [pl.BlockSpec((stride, wide), index(0)), pl.BlockSpec((stride, wide), index(1))],
-        [struct((half * stride, wide), bf16)] * 2,
+        specs,
+        [struct((n * stride, wide), bf16) for n in counts],
         args,
         [
             pltpu.VMEM((tokens, 3 * wide), bf16),
@@ -1174,20 +1210,18 @@
     )[0]
 
 
-def attention_outputs_kernel(each, groups, head_width, scal, *refs):
-    blocks = groups
-    columns = refs[: 3 * blocks]
-    rest = refs[3 * blocks :]
-    with_out = bool(each)
+def attention_outputs_kernel(each, blocks, head_width, count, last, scal, *refs):
+    columns, rest = refs[: count * blocks], refs[count * blocks :]
+    with_out = last and bool(each)
     out_blocks = rest[:blocks] if with_out else ()
     rest = rest[blocks:] if with_out else rest
-    small, outs = rest[:blocks], rest[blocks:]
+    small, outs = (rest[:blocks], rest[blocks:]) if last else ((), rest)
     wide = columns[0].shape[1]
     step = pl.program_id(0)
 
     def body(order):
-        for n in range(3):
-            pieces = [columns[3 * t + n] for t in order]
+        for n in range(count):
+            pieces = [columns[count * t + n] for t in order]
             if each:
                 size = each * head_width
                 for g in range(wide // size):
@@ -1198,12 +1232,14 @@
                 for c, ref in enumerate(pieces):
                     outs[n][:, c * wide : (c + 1) * wide] = ref[...].astype(f32)
 
-        @at_step(0)
-        def _():
-            total = small[order[0]][...].astype(f32)
-            for t in order[1:]:
-                total = total + small[t][...].astype(f32)
-            outs[-1][...] = total
+        if last:
+
+            @at_step(0)
+            def _():
+                total = small[order[0]][...].astype(f32)
+                for t in order[1:]:
+                    total = total + small[t][...].astype(f32)
+                outs[-1][...] = total
 
     by_position(scal, blocks, body)
     if with_out:
@@ -1211,37 +1247,42 @@
 
             @pl.when((step ^ scal[0]) == t)
             def _():
-                size = outs[3].shape[0]
+                size = outs[count].shape[0]
                 for b in range(blocks):
-                    outs[3][:, b * wide : (b + 1) * wide] = out_blocks[t][
+                    outs[count][:, b * wide : (b + 1) * wide] = out_blocks[t][
                         b * size : (b + 1) * size, :
                     ].astype(f32)
 
 
-def attention_outputs(scal, pieces, rows, each, head_width):
-    stride, wide = pieces[0].shape
+def attention_outputs(scal, pieces, count, rows, each, head_width, last):
     blocks = len(pieces)
+    total, wide = pieces[0].shape
     tile = rows // blocks
-    width = wide * blocks
     per = rows // tile
     specs, args = [], []
     for a in pieces:
-        for n in range(3):
+        for n in range(count):
             specs.append(pl.BlockSpec((tile, wide), lambda i, n=n: (n * per + i, 0)))
             args.append(a)
-    if each:
-        specs += [pl.BlockSpec((rows, wide), lambda i: (3, 0))] * blocks
+    outputs = count
+    if last and each:
+        specs += [pl.BlockSpec((rows, wide), lambda i: (count, 0))] * blocks
         args += pieces
-    specs += [pl.BlockSpec((extra, wide), lambda i: (stride // extra - 1, 0))] * blocks
-    args += pieces
-    block = pl.BlockSpec((tile, width), lambda i: (i, 0))
-    count = 4 if each else 3
-    return call(
-        functools.partial(attention_outputs_kernel, each, blocks, head_width),
+        outputs += 1
+    if last:
+        specs += [pl.BlockSpec((extra, wide), lambda i: (total // extra - 1, 0))] * blocks
+        args += pieces
+    block = pl.BlockSpec((tile, wide * blocks), lambda i: (i, 0))
+    out_specs, out_shape = [block] * outputs, [struct((rows, wide * blocks), f32)] * outputs
+    if last:
+        out_specs.append(pl.BlockSpec((extra, wide), lambda i: (0, 0)))
+        out_shape.append(struct((extra, wide), f32))
+    return call(
+        functools.partial(attention_outputs_kernel, each, blocks, head_width, count, last),
         (blocks,),
         [smem] + specs,
-        [block] * count + [pl.BlockSpec((extra, wide), lambda i: (0, 0))],
-        [struct((rows, width), f32)] * count + [struct((extra, wide), f32)],
+        out_specs,
+        out_shape,
         (scal, *args),
     )
 
@@ -1346,8 +1387,9 @@
     joint = together([*near_attn, *all_tokens], own_gate_up)
     near_attn, all_tokens = joint[: len(near_attn)], joint[len(near_attn) :]
     far_attn = gather_far(near_attn, chip)
-    joint = together(with_other_core(near_attn) + far_attn)
-    weights_attn, far_attn = list(joint[:2]), joint[2:]
+    n = len(near_attn)
+    joint = together([core_swap(a) for a in near_attn] + far_attn)
+    weights_attn, far_attn = [*near_attn, *joint[:n]], joint[n:]
     near_gate_up = gather_near(after(own_gate_up, *far_attn))
     weights_attn += with_other_core(far_attn)
     if not strided:
@@ -1391,10 +1433,11 @@
             )
             for side in range(2)
         ]
+    joint = together([*near_down, *grads_down])
+    near_down, grads_down = joint[:-2], joint[-2:]
+    far_down = gather_far(near_down, chip)
     sums_down = core_sum(*grads_down)
-    near_down = together(near_down, *sums_down)
-    far_down = gather_far(near_down, chip)
-    joint = together(with_other_core(near_down) + far_down)
+    joint = together(with_other_core(near_down) + far_down, *sums_down)
     down_parts, far_down = list(joint[:2]), joint[2:]
     down_parts, down_shards = down_parts + with_other_core(far_down), shards
     if not aligned:
@@ -1407,52 +1450,56 @@
     if len(sums_down) == 2:
         far_sum = reduce_far(after(sums_down[0], *far_down))
     grad_units = units_back(scal, gate, up, all_tokens, down_parts, down_shards)
-    parts = ffn_transposed(grad_units, weights_gate_up, shard_rows, shards, blocks)
     if far_sum is not None:
-        *parts, far_sum = together([*parts, far_sum])
-    parts = list(parts)
-    share_down = reduce_near(after(sums_down[-1], *parts), far_sum, chip)
+        far_sum, grad_units = together([far_sum, grad_units])
+    sends = together(near_sends(sums_down[-1], far_sum, chip), grad_units)
+    received = near_receive(sends)
+    parts = ffn_transposed(after(grad_units, *sends), weights_gate_up, shard_rows, shards, blocks)
+    grads_gate_up = units_grad(normed_ffn, after(grad_units, *parts), shards)
     parts = ctx_exchange(parts)
-    grads_gate_up = units_grad(normed_ffn, after(grad_units, parts[0]), shards)
     result_parts = multiply_down(
         scal, after(mixed_units, *grads_gate_up), down_parts, down_shards, blocks
     )
-    parts = together(parts, *grads_gate_up, *result_parts)
+    joint = together([*parts, *received, *grads_gate_up], *result_parts)
+    parts, grads_gate_up = list(joint[:blocks]), joint[blocks + len(received) :]
+    share_down = near_total(joint[blocks : blocks + len(received)])
+    far_sum = []
+    if len(grads_gate_up) == 4:
+        far_add = add_low(grads_gate_up[2], core_swap(grads_gate_up[3]))
+        far_sum = [reduce_far(far_add)]
+        parts = together(parts, far_add)
     grad_hidden, low, grad_gain_ffn = ffn_norm_back(
         scal, hidden, gains, own_tokens, parts, shards
     )
 
     all_low = ctx_gather(low)
-    far_sum = None
-    if len(grads_gate_up) == 4:
-        swapped = core_swap(after(grads_gate_up[3], share_down, low))
-        far_sum = reduce_far(add_low(grads_gate_up[2], swapped))
-        swapped = core_swap(after(grads_gate_up[1], swapped))
-    else:
-        swapped = core_swap(after(grads_gate_up[1], share_down, low))
-    near_sum = add_low(grads_gate_up[0], swapped)
-    joint = together([*all_low, near_sum])
-    all_low, near_sum = joint[:-1], joint[-1]
-    pieces_down = ctx_gather(after(share_down, *all_low))
+    near_sum = add_low(grads_gate_up[0], core_swap(after(grads_gate_up[1], low)))
+    sends = near_sends(near_sum, far_sum[0] if far_sum else None, chip)
+    received = near_receive(sends)
+    result_parts = ctx_exchange(together(result_parts, *all_low))
     if strided:
-        grad_att = make_grad_attended(scal, all_low, weights_attn, shards)
+        grad_att = make_grad_attended(after(scal, *sends), all_low, weights_attn, shards)
     else:
         grad_att = dot(jnp.concatenate(all_low, axis=0), full_out, 1, 1).astype(bf16)
     *grads, diagonals = attention_backward(scal, qkv, probs, grad_att, rows, blocks)
+    joint = together([*grads, *result_parts])
+    grads, result_parts = joint[:3], joint[3:]
+    result = hidden
+    for part in result_parts:
+        result = result + part.astype(f32)
+    result = result.astype(bf16)
     parts, grad_gain_attn = attn_transposed(
         scales, grads, all_tokens, weights_attn, shard_rows, shards, blocks
     )
-    joint = together([*parts, *pieces_down, near_sum] + ([] if far_sum is None else [far_sum]))
-    parts, pieces_down = list(joint[:blocks]), joint[blocks : 2 * blocks]
-    near_sum = joint[2 * blocks]
-    far_sum = None if far_sum is None else joint[-1]
-    share_gate_up = reduce_near(near_sum, far_sum, chip)
+    near_down_share = ctx_gather_near(after(share_down, *result_parts))
+    joint = together([*parts, *near_down_share])
+    parts, near_down_share = list(joint[:blocks]), joint[blocks:]
     parts = ctx_exchange(parts)
     grads_attn = attn_grad(
         scal,
         normed,
         attended,
-        [after(grads[0], parts[0]), *grads[1:]],
+        [after(grads[0], *parts[:1]), *grads[1:]],
         diagonals,
         grad_gain_attn,
         grad_gain_ffn,
@@ -1461,22 +1508,32 @@
         each,
         stride,
     )
-    parts = together(parts, *grads_attn)
+    n = len(received)
+    joint = together([*parts, *received, *grads_attn])
+    parts, received, grads_attn = joint[:blocks], joint[blocks : blocks + n], joint[blocks + n :]
     input_grad = attn_norm_back(scal, grad_hidden, gains, own_tokens, parts, shards)
-    sums_attn = core_sum(grads_attn[0], after(grads_attn[1], input_grad))
-    result_parts = ctx_exchange(together(result_parts, *sums_attn))
-    result = hidden
-    for part in result_parts:
-        result = result + part.astype(f32)
-    result = result.astype(bf16)
-    share_gate_up, result = together([share_gate_up, result])
-    far_sum = None
-    if len(sums_attn) == 2:
-        far_sum = reduce_far(after(sums_attn[0], share_gate_up))
-    share_attn = reduce_near(after(sums_attn[-1], share_gate_up), far_sum, chip)
-    joint = together([*ctx_gather(share_gate_up), share_attn])
-    pieces_gate_up, share_attn = joint[:-1], joint[-1]
-    pieces_attn = ctx_gather(share_attn)
+    far_sum, far_add = [], grads_attn[0]
+    if len(grads_attn) == 4:
+        far_add = add_low(grads_attn[2], core_swap(grads_attn[3]))
+        far_sum = [reduce_far(far_add)]
+    near_sum = add_low(grads_attn[0], core_swap(after(grads_attn[1], far_add)))
+    share_gate_up = near_total(received)
+    near_units = ctx_gather_near(after(share_gate_up, far_add))
+    near_sum, *far_sum = together([near_sum, *far_sum])
+    far_sum = far_sum[0] if far_sum else None
+    cut = 2 * shard_rows
+    first = near_receive(near_sends(near_sum, far_sum, chip, (0, cut)))
+    sends = near_sends(near_sum, far_sum, chip, (cut, stride))
+    far_units = ctx_gather_far(together(near_units, *sends))
+    far_down_share = ctx_gather_far(together(near_down_share, *far_units))
+    joint = together([*first, *far_down_share, *sends])
+    first, far_down_share, sends = near_total(joint[:n]), joint[n:-n], joint[-n:]
+    second = near_receive(sends)
+    joint = together([*ctx_gather(first), *second])
+    pieces_first, second = joint[:blocks], near_total(joint[blocks:])
+    pieces_second = ctx_gather(second)
+    pieces_gate_up = ctx_pieces(share_gate_up, near_units, far_units)
+    pieces_down = ctx_pieces(share_down, near_down_share, far_down_share)
 
     g_down = assemble_rows(scal, pieces_down)
     if blocks * unit_rows % 128 == 0:
@@ -1497,7 +1554,13 @@
             ).astype(f32)
             for n in range(2)
         ]
-    *outs_attn, small = attention_outputs(scal, pieces_attn, shard_rows, each, head_width)
+    outs_attn = attention_outputs(
+        scal, list(pieces_first), 2, shard_rows, each, head_width, False
+    )
+    *rest, small = attention_outputs(
+        scal, list(pieces_second), 1, shard_rows, each, head_width, True
+    )
+    outs_attn = [*outs_attn, *rest]
     if not strided:
         spot = jnp.zeros((width, width), bf16)
         spot = lax.dynamic_update_slice_in_dim(

time: 647 us -> 552 us (0.85)
  waiting for transfers between devices: 351 us -> 243 us
  starting transfers between devices: 70.9 us -> 88.3 us
    ppermute x18 -> x20, waiting for transfers between devices: 180 us -> 79.5 us  [chip_send(): lax.ppermute(a, 'fsdp', [(2 * s + k, 2 * d + k) for s, d in pairs for k i...]
    ppermute x18 -> x20, starting transfers between devices: 35.1 us -> 45.6 us  [chip_send(): lax.ppermute(a, 'fsdp', [(2 * s + k, 2 * d + k) for s, d in pairs for k i...]
    ppermute x30 -> x35, waiting for transfers between devices: 160 us -> 152 us  [ctx_send(): return lax.ppermute(a, 'ctx', [(i, i ^ distance) for i in range(size)])]
    ppermute x30 -> x35, starting transfers between devices: 35.2 us -> 40.9 us  [ctx_send(): return lax.ppermute(a, 'ctx', [(i, i ^ distance) for i in range(size)])]
    pallas_call x22 -> x23, Pallas kernels: 164 us -> 167 us  [call(): pl.pallas_call(kernel, grid=grid, in_specs=in_specs, out_specs=out_specs,...]
    unnamed x113 -> x120, local copies, waits for them, and re-layouts: 20 us -> 17 us
  transfers between devices with their start and end apart: 58 -> 68, of which waited for: 32 -> 39; matrix products, arithmetic and copies ran while one was open for 3% -> 3% of each run, Pallas kernels for 21% -> 28%
where the time goes in v3:
time: 552 us; the launch traced here: 542 us
  waiting for transfers between devices  243 us (44%)
  Pallas kernels  167 us (30%)
  starting transfers between devices  88.3 us (16%)
  other arithmetic  21.4 us (4%)
  local copies, waits for them, and re-layouts  19.8 us (4%)
    pallas_call x23, Pallas kernels, call(): pl.pallas_call(kernel, grid=grid, in_specs=in_specs, out_specs=out_specs,...  167 us
    ppermute x35, waiting for transfers between devices, ctx_send(): return lax.ppermute(a, 'ctx', [(i, i ^ distance) for i in range(size)])  152 us
    ppermute x20, waiting for transfers between devices, chip_send(): lax.ppermute(a, 'fsdp', [(2 * s + k, 2 * d + k) for s, d in pairs for k i...  79.5 us
    ppermute x20, starting transfers between devices, chip_send(): lax.ppermute(a, 'fsdp', [(2 * s + k, 2 * d + k) for s, d in pairs for k i...  45.6 us
    ppermute x35, starting transfers between devices, ctx_send(): return lax.ppermute(a, 'ctx', [(i, i ^ distance) for i in range(size)])  40.9 us
    unnamed x120, local copies, waits for them, and re-layouts  17 us
    ppermute x13, waiting for transfers between devices, core_swap(): return lax.ppermute(a, 'fsdp', [(r, r ^ 1) for r in range(size)])  12.4 us
  transfers between devices with their start and end apart: 68, of which 39 were waited for; matrix products, arithmetic and copies ran while one was open for 3% of the time, Pallas kernels for 28%

profile of v3, /device:TPU:0, one launch (start us, length us, event | category | flops | bytes accessed | tf_op | source)
XLA Modules:
  0.0 542.5 jit_solution(320462691422745895)
XLA Ops:
  9.2 5.1 collective-permute-start
  22.2 18.4 %collective-permute-done.2.refs_1_ = bf16[256,2048]{1,0:T(8,128)(2,1)} collective-permute-done((bf16[256,2048]{1,0:T(8,128)(2,1)}, bf16[256,2048]{1,0:T(8,128)(2,1)}, u32[]{:S(2)}, u32[]{:S(2)}) %collective-permute-start.2) | collective-permute-done | bytes 1048608 | tf_op jit(solution)/shard_map/ppermute | solution.py:55
  40.6 22.2 %collective-permute-done.3.refs_2_ = bf16[256,2048]{1,0:T(8,128)(2,1)} collective-permute-done((bf16[256,2048]{1,0:T(8,128)(2,1)}, bf16[256,2048]{1,0:T(8,128)(2,1)}, u32[]{:S(2)}, u32[]{:S(2)}) %collective-permute-start.3) | collective-permute-done | bytes 1048608 | tf_op jit(solution)/shard_map/ppermute | solution.py:55
  68.9 21.9 %collective-permute-done.8.refs_10_.refs_6_ = bf16[1040,512]{1,0:T(8,128)(2,1)S(1)} collective-permute-done((bf16[1040,512]{1,0:T(8,128)(2,1)S(1)}, bf16[1040,512]{1,0:T(8,128)(2,1)S(1)}, u32[]{:S(2)}, u32[]{:S(2)}) %collective-permute-start.8) | collective-permute-done | bytes 1064992 | tf_op jit(solution)/shard_map/ppermute | solution.py:50
  95.4 10.0 %shard_map.241 = (bf16[512,2048]{1,0:T(8,128)(2,1)}, bf16[512,1536]{1,0:T(8,128)(2,1)}, f32[4,2,1024]{2,1,0:T(2,128)S(1)}, f32[2,2048]{1,0:T(2,128)S(1)}, f32[512,128]{1,0:T(8,128)S(1)}) custom-call(s32[10]{0:T(128)S(1)} %compare_select_fusion.3.scal, bf16[256,2048]{1,0:T(8,128)(2,1)} %shard_map.238.refs_0_.own, ...), custom_call_target="tpu_custom_call" | custom-call | flops 1 | bytes 1 | tf_op jit(solution)/shard_map/pallas_call | solution.py:185
  105.5 12.0 %shard_map.242 = (bf16[512,512]{1,0:T(8,128)(2,1)S(1)}, bf16[8,512,512]{2,1,0:T(8,128)(2,1)}) custom-call(s32[10]{0:T(128)S(1)} %compare_select_fusion.3.scal, bf16[512,1536]{1,0:T(8,128)(2,1)} %get-tuple-element.192.q_ref.k_ref.v_ref, bf16[512,1536]{1,0:T(8,128)(2,1)} %get-tuple-element.192.q_ref.k_ref.v_ref, ...), custom_call_target="tpu_custom_call" | custom-call | flops 1 | bytes 1 | tf_op jit(solution)/shard_map/pallas_call | solution.py:185
  118.3 5.0 shard_map.243
  126.9 11.3 %collective-permute-done.10.refs_1_ = bf16[128,2048]{1,0:T(8,128)(2,1)S(1)} collective-permute-done((bf16[128,2048]{1,0:T(8,128)(2,1)S(1)}, bf16[128,2048]{1,0:T(8,128)(2,1)S(1)}, u32[]{:S(2)}, u32[]{:S(2)}) %collective-permute-start.10) | collective-permute-done | bytes 524320 | tf_op jit(solution)/shard_map/ppermute | solution.py:55
  138.9 10.7 %collective-permute-done.12.refs_3_ = bf16[128,2048]{1,0:T(8,128)(2,1)S(1)} collective-permute-done((bf16[128,2048]{1,0:T(8,128)(2,1)}, bf16[128,2048]{1,0:T(8,128)(2,1)S(1)}, u32[]{:S(2)}, u32[]{:S(2)}) %collective-permute-start.12) | collective-permute-done | bytes 524320 | tf_op jit(solution)/shard_map/ppermute | solution.py:55
  162.2 11.3 %collective-permute-done.16.refs_1_ = bf16[128,2048]{1,0:T(8,128)(2,1)S(1)} collective-permute-done((bf16[128,2048]{1,0:T(8,128)(2,1)S(1)}, bf16[128,2048]{1,0:T(8,128)(2,1)S(1)}, u32[]{:S(2)}, u32[]{:S(2)}) %collective-permute-start.16) | collective-permute-done | bytes 524320 | tf_op jit(solution)/shard_map/ppermute | solution.py:55
  174.3 9.4 %collective-permute-done.17.refs_2_ = bf16[128,2048]{1,0:T(8,128)(2,1)S(1)} collective-permute-done((bf16[128,2048]{1,0:T(8,128)(2,1)S(1)}, bf16[128,2048]{1,0:T(8,128)(2,1)S(1)}, u32[]{:S(2)}, u32[]{:S(2)}) %collective-permute-start.17) | collective-permute-done | bytes 524320 | tf_op jit(solution)/shard_map/ppermute | solution.py:55
  193.6 12.3 %collective-permute-start.21 = (bf16[160,2048]{1,0:T(8,128)(2,1)S(1)}, bf16[160,2048]{1,0:T(8,128)(2,1)S(1)}, u32[]{:S(2)}, u32[]{:S(2)}) collective-permute-start(bf16[160,2048]{1,0:T(8,128)(2,1)S(1)} %constant_dynamic-slice_fusion), channel_id=1, source_target_pairs={{0,2},{1,3},{2,4},{3,5},{4,6},{5,7},{6,0},{7,1},{8,10},{9,11},{10,... | collective-permute-start | bytes 1966088 | tf_op jit(solution)/shard_map/ppermute | solution.py:50
  205.9 11.0 %shard_map.245 = (bf16[512,2048]{1,0:T(8,128)(2,1)}, f32[512,1280]{1,0:T(8,128)}, f32[512,1280]{1,0:T(8,128)}, bf16[512,1280]{1,0:T(8,128)(2,1)}) custom-call(bf16[128,2048]{1,0:T(8,128)(2,1)S(1)} %get-tuple-element.206.refs_0_, bf16[128,2048]{1,0:T(8,128)(2,1)S(1)} %copy-done.21, bf16[128,2048]{1,0:T(8,128)(2,1)S(1)} %copy-done.23, ...), custom_call_target="tpu_custom_call" | custom-call | flops 1 | bytes 1 | tf_op jit(solution)/shard_map/pallas_call | solution.py:185
  216.9 7.5 %shard_map.246 = (bf16[640,2048]{1,0:T(8,128)(2,1)}, bf16[640,2048]{1,0:T(8,128)(2,1)}) custom-call(s32[10]{0:T(128)S(1)} %compare_select_fusion.3.scal, bf16[512,1280]{1,0:T(8,128)(2,1)} %get-tuple-element.244.mixed, bf16[256,2048]{1,0:T(8,128)(2,1)} %shard_map.238.refs_0_.own, bf16[256,2048]{1,0:T(8,128)(2,1)} %collective-permute-done.2.refs_1_, ...), custom_call_target="tpu_custom_call" | custom-call | flops 1 | bytes 1 | tf_op jit(solution)/shard_map/pallas_call | solution.py:185
  231.8 10.5 %collective-permute-done.25.refs_6_.refs_2_ = bf16[160,2048]{1,0:T(8,128)(2,1)S(1)} collective-permute-done((bf16[160,2048]{1,0:T(8,128)(2,1)S(1)}, bf16[160,2048]{1,0:T(8,128)(2,1)S(1)}, u32[]{:S(2)}, u32[]{:S(2)}) %collective-permute-start.25) | collective-permute-done | bytes 655392 | tf_op jit(solution)/shard_map/ppermute | solution.py:50
  246.1 11.3 %shard_map.247.g = bf16[512,2560]{1,0:T(8,128)(2,1)} custom-call(s32[10]{0:T(128)S(1)} %compare_select_fusion.3.scal, f32[512,1280]{1,0:T(8,128)} %get-tuple-element.224.gate, f32[512,1280]{1,0:T(8,128)} %get-tuple-element.225.up, bf16[256,2048]{1,0:T(8,128)(2,1)} %shard_map.238.refs_0_.own, bf16[256,2048]{1,0:T(8,128)(2,1)} %collective-permute-done.2.refs_1_, ...), custom_call_target="tpu_custom_call" | custom-call | flops 1 | bytes 1 | tf_op jit(solution)/shard_map/pallas_call | solution.py:185
  267.4 12.5 %shard_map.248 = (bf16[128,2048]{1,0:T(8,128)(2,1)S(1)}, bf16[128,2048]{1,0:T(8,128)(2,1)S(1)}, bf16[128,2048]{1,0:T(8,128)(2,1)S(1)}, bf16[128,2048]{1,0:T(8,128)(2,1)}) custom-call(bf16[512,2560]{1,0:T(8,128)(2,1)} %shard_map.247.g, bf16[768,2560]{1,0:T(8,128)(2,1)} %copy-done.25, bf16[768,2560]{1,0:T(8,128)(2,1)} %copy-done.31, ...), custom_call_target="tpu_custom_call" | custom-call | flops 1 | bytes 1 | tf_op jit(solution)/shard_map/pallas_call | solution.py:185
  283.4 9.7 %shard_map.249 = (bf16[768,2560]{1,0:T(8,128)(2,1)}, bf16[768,2560]{1,0:T(8,128)(2,1)}, bf16[256,2560]{1,0:T(8,128)(2,1)S(1)}, bf16[256,2560]{1,0:T(8,128)(2,1)}) custom-call(bf16[512,2048]{1,0:T(8,128)(2,1)} %get-tuple-element.238.normed, bf16[512,2560]{1,0:T(8,128)(2,1)} %shard_map.247.g), custom_call_target="tpu_custom_call" | custom-call | flops 1 | bytes 1 | tf_op jit(solution)/shard_map/pallas_call | solution.py:185
  293.1 7.5 %shard_map.250 = (bf16[128,2048]{1,0:T(8,128)(2,1)S(1)}, bf16[128,2048]{1,0:T(8,128)(2,1)S(1)}, bf16[128,2048]{1,0:T(8,128)(2,1)S(1)}, bf16[128,2048]{1,0:T(8,128)(2,1)}) custom-call(s32[10]{0:T(128)S(1)} %compare_select_fusion.3.scal, bf16[512,1280]{1,0:T(8,128)(2,1)} %get-tuple-element.244.mixed, bf16[480,2048]{1,0:T(8,128)(2,1)} %copy-done.32, ...), custom_call_target="tpu_custom_call" | custom-call | flops 1 | bytes 1 | tf_op jit(solution)/shard_map/pallas_call | solution.py:185
  316.0 11.3 %collective-permute-done.36.refs_1_ = bf16[128,2048]{1,0:T(8,128)(2,1)S(1)} collective-permute-done((bf16[128,2048]{1,0:T(8,128)(2,1)S(1)}, bf16[128,2048]{1,0:T(8,128)(2,1)S(1)}, u32[]{:S(2)}, u32[]{:S(2)}) %collective-permute-start.36) | collective-permute-done | bytes 524320 | tf_op jit(solution)/shard_map/ppermute | solution.py:55
  328.2 10.7 %collective-permute-done.38.refs_3_ = bf16[128,2048]{1,0:T(8,128)(2,1)S(1)} collective-permute-done((bf16[128,2048]{1,0:T(8,128)(2,1)S(1)}, bf16[128,2048]{1,0:T(8,128)(2,1)S(1)}, u32[]{:S(2)}, u32[]{:S(2)}) %collective-permute-start.38) | collective-permute-done | bytes 524320 | tf_op jit(solution)/shard_map/ppermute | solution.py:55
  353.7 5.9 %shard_map.252.gatt = bf16[512,512]{1,0:T(8,128)(2,1)S(1)} custom-call(s32[10]{0:T(128)S(1)} %compare_select_fusion.3.scal, bf16[128,2048]{1,0:T(8,128)(2,1)S(1)} %get-tuple-element.261.refs_0_, bf16[128,2048]{1,0:T(8,128)(2,1)S(1)} %collective-permute-done.36.refs_1_, bf16[128,2048]{1,0:T(8,128)(2,1)} %copy-done.42, bf16[128,2048]{1,0:T(8,128)(2,1)} %copy-done.43, ...), custom_call_target="tpu_custom_call" | custom-call | flops 1 | bytes 1 | tf_op jit(solution)/shard_map/pallas_call | solution.py:185
  360.4 11.9 %shard_map.253 = (bf16[512,512]{1,0:T(8,128)(2,1)S(1)}, bf16[512,512]{1,0:T(8,128)(2,1)S(1)}, bf16[512,512]{1,0:T(8,128)(2,1)S(1)}, f32[4,2,1024]{2,1,0:T(2,128)S(1)}) custom-call(s32[10]{0:T(128)S(1)} %compare_select_fusion.3.scal, bf16[512,1536]{1,0:T(8,128)(2,1)} %get-tuple-element.192.q_ref.k_ref.v_ref, ...), custom_call_target="tpu_custom_call" | custom-call | flops 1 | bytes 1 | tf_op jit(solution)/shard_map/pallas_call | solution.py:185
  376.9 11.3 %shard_map.254 = (bf16[128,2048]{1,0:T(8,128)(2,1)S(1)}, bf16[128,2048]{1,0:T(8,128)(2,1)S(1)}, bf16[128,2048]{1,0:T(8,128)(2,1)S(1)}, bf16[128,2048]{1,0:T(8,128)(2,1)}, f32[1,2048]{1,0:T(1,128)S(1)}) custom-call(f32[512,128]{1,0:T(8,128)S(1)} %get-tuple-element.276.scales, bf16[512,512]{1,0:T(8,128)(2,1)} %copy-done.6, bf16[512,512]{1,0:T(8,128)(2,1)} %copy-done.8, ...), custom_call_target="tpu_custom_call" | custom-call | flops 1 | bytes 1 | tf_op jit(solution)/shard_map/pallas_call | solution.py:185
  394.0 11.9 %shard_map.255 = (bf16[3120,512]{1,0:T(8,128)(2,1)}, bf16[3120,512]{1,0:T(8,128)(2,1)}, bf16[1040,512]{1,0:T(8,128)(2,1)}, bf16[1040,512]{1,0:T(8,128)(2,1)}) custom-call(s32[10]{0:T(128)S(1)} %compare_select_fusion.3.scal, bf16[512,2048]{1,0:T(8,128)(2,1)} %get-tuple-element.292.normed, bf16[512,512]{1,0:T(8,128)(2,1)S(1)} %copy-done.12, ...), custom_call_target="tpu_custom_call" | custom-call | flops 1 | bytes 1 | tf_op jit(solution)/shard_map/pallas_call | solution.py:185
  405.8 6.2 %collective-permute-done.45.refs_2_ = bf16[128,2048]{1,0:T(8,128)(2,1)S(1)} collective-permute-done((bf16[128,2048]{1,0:T(8,128)(2,1)S(1)}, bf16[128,2048]{1,0:T(8,128)(2,1)S(1)}, u32[]{:S(2)}, u32[]{:S(2)}) %collective-permute-start.45) | collective-permute-done | bytes 524320 | tf_op jit(solution)/shard_map/ppermute | solution.py:55
  424.3 22.4 %collective-permute-done.51 = bf16[1040,512]{1,0:T(8,128)(2,1)S(1)} collective-permute-done((bf16[1040,512]{1,0:T(8,128)(2,1)S(1)}, bf16[1040,512]{1,0:T(8,128)(2,1)S(1)}, u32[]{:S(2)}, u32[]{:S(2)}) %collective-permute-start.51) | collective-permute-done | bytes 1064992 | tf_op jit(solution)/shard_map/ppermute | solution.py:50
  458.9 9.2 %collective-permute-done.56 = bf16[128,2560]{1,0:T(8,128)(2,1)S(1)} collective-permute-done((bf16[128,2560]{1,0:T(8,128)(2,1)S(1)}, bf16[128,2560]{1,0:T(8,128)(2,1)S(1)}, u32[]{:S(2)}, u32[]{:S(2)}) %collective-permute-start.56) | collective-permute-done | bytes 655392 | tf_op jit(solution)/shard_map/ppermute | solution.py:55
  471.8 8.0 %collective-permute-done.53 = bf16[512,512]{1,0:T(8,128)(2,1)S(1)} collective-permute-done((bf16[512,512]{1,0:T(8,128)(2,1)S(1)}, bf16[512,512]{1,0:T(8,128)(2,1)S(1)}, u32[]{:S(2)}, u32[]{:S(2)}) %collective-permute-start.53) | collective-permute-done | bytes 524320 | tf_op jit(solution)/shard_map/ppermute | solution.py:50
  489.7 5.2 collective-permute-done.60.refs_2_.refs_3_
  494.9 9.8 %collective-permute-done.61.refs_4_.refs_5_ = bf16[512,512]{1,0:T(8,128)(2,1)S(1)} collective-permute-done((bf16[512,512]{1,0:T(8,128)(2,1)S(1)}, bf16[512,512]{1,0:T(8,128)(2,1)S(1)}, u32[]{:S(2)}, u32[]{:S(2)}) %collective-permute-start.61) | collective-permute-done | bytes 524320 | tf_op jit(solution)/shard_map/ppermute | solution.py:55
  518.2 8.8 %shard_map.259 = (f32[256,5120]{1,0:T(8,128)}, f32[256,5120]{1,0:T(8,128)}) custom-call(s32[10]{0:T(128)S(1)} %compare_select_fusion.3.scal, bf16[256,2560]{1,0:T(8,128)(2,1)S(1)} %add_convert_fusion.3.refs_0_, bf16[256,2560]{1,0:T(8,128)(2,1)} %copy-done.39, bf16[256,2560]{1,0:T(8,128)(2,1)} %copy-done.40, bf16[256,2560]{1,0:T(8,128)(2,1)} %pad_maximum_fusion.refs_3_), custom_call_target="tpu_custom_call" | custom-call | flops 1 | bytes 1 | tf_op jit(solution)/shard_map/pallas_call | solution.py:185
  (279 shorter events, 188.1 us)
Async XLA Ops:
  9.2 53.7 %collective-permute-start = (bf16[1040,512]{1,0:T(8,128)(2,1)}, bf16[1040,512]{1,0:T(8,128)(2,1)}, u32[]{:S(2)}, u32[]{:S(2)}) collective-permute-start(bf16[1040,512]{1,0:T(8,128)(2,1)} %shard_map.239.refs_4_.refs_0_), channel_id=1, source_target_pairs={{2,0},{3,1},{4,2},{5,3},{6,4},{7,5},{0,6},{1,7},{10,8},{11,9},{12,... | collective-permute-start | bytes 3194888 | tf_op jit(solution)/shard_map/ppermute | solution.py:50
  14.2 48.6 %collective-permute-start.1 = (bf16[1040,512]{1,0:T(8,128)(2,1)}, bf16[1040,512]{1,0:T(8,128)(2,1)}, u32[]{:S(2)}, u32[]{:S(2)}) collective-permute-start(bf16[1040,512]{1,0:T(8,128)(2,1)} %shard_map.239.refs_4_.refs_0_), channel_id=1, source_target_pairs={{0,2},{1,3},{2,4},{3,5},{4,6},{5,7},{6,0},{7,1},{8,10},{9,11},{10,... | collective-permute-start | bytes 3194888 | tf_op jit(solution)/shard_map/ppermute | solution.py:50
  14.2 26.4 %collective-permute-start.2 = (bf16[256,2048]{1,0:T(8,128)(2,1)}, bf16[256,2048]{1,0:T(8,128)(2,1)}, u32[]{:S(2)}, u32[]{:S(2)}) collective-permute-start(bf16[256,2048]{1,0:T(8,128)(2,1)} %shard_map.238.refs_0_.own), channel_id=1, source_target_pairs={{0,8},{8,0},{16,24},{24,16},{1,9},{9,1},{17,25},{25,17},{2,10},{10... | collective-permute-start | bytes 3145736 | tf_op jit(solution)/shard_map/ppermute | solution.py:55
  15.7 47.1 %collective-permute-start.3 = (bf16[256,2048]{1,0:T(8,128)(2,1)}, bf16[256,2048]{1,0:T(8,128)(2,1)}, u32[]{:S(2)}, u32[]{:S(2)}) collective-permute-start(bf16[256,2048]{1,0:T(8,128)(2,1)} %shard_map.238.refs_0_.own), channel_id=1, source_target_pairs={{0,16},{8,24},{16,0},{24,8},{1,17},{9,25},{17,1},{25,9},{2,18},{10... | collective-permute-start | bytes 3145736 | tf_op jit(solution)/shard_map/ppermute | solution.py:55
  17.2 45.6 %collective-permute-start.4 = (bf16[256,2048]{1,0:T(8,128)(2,1)}, bf16[256,2048]{1,0:T(8,128)(2,1)}, u32[]{:S(2)}, u32[]{:S(2)}) collective-permute-start(bf16[256,2048]{1,0:T(8,128)(2,1)} %shard_map.238.refs_0_.own), channel_id=1, source_target_pairs={{0,24},{8,16},{16,8},{24,0},{1,25},{9,17},{17,9},{25,1},{2,26},{10... | collective-permute-start | bytes 3145736 | tf_op jit(solution)/shard_map/ppermute | solution.py:55
  64.9 25.9 %collective-permute-start.8 = (bf16[1040,512]{1,0:T(8,128)(2,1)S(1)}, bf16[1040,512]{1,0:T(8,128)(2,1)S(1)}, u32[]{:S(2)}, u32[]{:S(2)}) collective-permute-start(bf16[1040,512]{1,0:T(8,128)(2,1)S(1)} %select_select_fusion.1), channel_id=1, source_target_pairs={{6,2},{7,3},{0,4},{1,5},{2,0},{3,1},{4,6},{5,7},{14,10},{15,11},{8... | collective-permute-start | bytes 3194888 | tf_op jit(solution)/shard_map/ppermute | solution.py:50
  90.8 62.3 %collective-permute-start.13 = (bf16[256,2560]{1,0:T(8,128)(2,1)S(1)}, bf16[256,2560]{1,0:T(8,128)(2,1)}, u32[]{:S(2)}, u32[]{:S(2)}) collective-permute-start(bf16[256,2560]{1,0:T(8,128)(2,1)S(1)} %copy-done.3), channel_id=1, source_target_pairs={{2,0},{3,1},{4,2},{5,3},{6,4},{7,5},{0,6},{1,7},{10,8},{11,9},{12,... | collective-permute-start | bytes 3932168 | tf_op jit(solution)/shard_map/ppermute | solution.py:50
  94.4 58.7 %collective-permute-start.14 = (bf16[256,2560]{1,0:T(8,128)(2,1)S(1)}, bf16[256,2560]{1,0:T(8,128)(2,1)}, u32[]{:S(2)}, u32[]{:S(2)}) collective-permute-start(bf16[256,2560]{1,0:T(8,128)(2,1)S(1)} %copy-done.3), channel_id=1, source_target_pairs={{0,2},{1,3},{2,4},{3,5},{4,6},{5,7},{6,0},{7,1},{8,10},{9,11},{10,... | collective-permute-start | bytes 3932168 | tf_op jit(solution)/shard_map/ppermute | solution.py:50
  125.4 24.2 %collective-permute-start.12 = (bf16[128,2048]{1,0:T(8,128)(2,1)}, bf16[128,2048]{1,0:T(8,128)(2,1)S(1)}, u32[]{:S(2)}, u32[]{:S(2)}) collective-permute-start(bf16[128,2048]{1,0:T(8,128)(2,1)} %get-tuple-element.198), channel_id=1, source_target_pairs={{0,24},{8,16},{16,8},{24,0},{1,25},{9,17},{17,9},{25,1},{2,26},{10... | collective-permute-start | bytes 1572872 | tf_op jit(solution)/shard_map/ppermute | solution.py:55
  156.6 32.3 %collective-permute-start.15 = (bf16[768,2560]{1,0:T(8,128)(2,1)S(1)}, bf16[768,2560]{1,0:T(8,128)(2,1)S(1)}, u32[]{:S(2)}, u32[]{:S(2)}) collective-permute-start(bf16[768,2560]{1,0:T(8,128)(2,1)S(1)} %constant_dynamic-update-slice_fusion.refs_4_.refs_0_), channel_id=1, source_target_pairs={{0,1},{1,0},{2,3},{3,2},{4,5},{5,4},{6,7},{7,6},{8,9},{9,8},{10,11... | collective-permute-start | bytes 11796488 | tf_op jit(solution)/shard_map/ppermute | solution.py:46
  156.7 32.2 %collective-permute-start.19 = (bf16[256,2560]{1,0:T(8,128)(2,1)S(1)}, bf16[256,2560]{1,0:T(8,128)(2,1)}, u32[]{:S(2)}, u32[]{:S(2)}) collective-permute-start(bf16[256,2560]{1,0:T(8,128)(2,1)S(1)} %get-tuple-element.356), channel_id=1, source_target_pairs={{6,2},{7,3},{0,4},{1,5},{2,0},{3,1},{4,6},{5,7},{14,10},{15,11},{8... | collective-permute-start | bytes 3932168 | tf_op jit(solution)/shard_map/ppermute | solution.py:50
  190.9 33.5 %collective-permute-start.20 = (bf16[160,2048]{1,0:T(8,128)(2,1)S(1)}, bf16[160,2048]{1,0:T(8,128)(2,1)S(1)}, u32[]{:S(2)}, u32[]{:S(2)}) collective-permute-start(bf16[160,2048]{1,0:T(8,128)(2,1)S(1)} %constant_dynamic-slice_fusion), channel_id=1, source_target_pairs={{2,0},{3,1},{4,2},{5,3},{6,4},{7,5},{0,6},{1,7},{10,8},{11,9},{12,... | collective-permute-start | bytes 1966088 | tf_op jit(solution)/shard_map/ppermute | solution.py:50
  193.6 30.8 %collective-permute-start.21 = (bf16[160,2048]{1,0:T(8,128)(2,1)S(1)}, bf16[160,2048]{1,0:T(8,128)(2,1)S(1)}, u32[]{:S(2)}, u32[]{:S(2)}) collective-permute-start(bf16[160,2048]{1,0:T(8,128)(2,1)S(1)} %constant_dynamic-slice_fusion), channel_id=1, source_target_pairs={{0,2},{1,3},{2,4},{3,5},{4,6},{5,7},{6,0},{7,1},{8,10},{9,11},{10,... | collective-permute-start | bytes 1966088 | tf_op jit(solution)/shard_map/ppermute | solution.py:50
  263.5 41.2 %collective-permute-start.31 = (bf16[160,2048]{1,0:T(8,128)(2,1)S(1)}, bf16[160,2048]{1,0:T(8,128)(2,1)S(1)}, u32[]{:S(2)}, u32[]{:S(2)}) collective-permute-start(bf16[160,2048]{1,0:T(8,128)(2,1)S(1)} %get-tuple-element.231), channel_id=1, source_target_pairs={{0,2},{1,3},{2,4},{3,5},{4,6},{5,7},{6,0},{7,1},{8,10},{9,11},{10,... | collective-permute-start | bytes 1966088 | tf_op jit(solution)/shard_map/ppermute | solution.py:50
  265.1 39.7 %collective-permute-start.32 = (bf16[160,2048]{1,0:T(8,128)(2,1)S(1)}, bf16[160,2048]{1,0:T(8,128)(2,1)S(1)}, u32[]{:S(2)}, u32[]{:S(2)}) collective-permute-start(bf16[160,2048]{1,0:T(8,128)(2,1)S(1)} %get-tuple-element.232), channel_id=1, source_target_pairs={{2,0},{3,1},{4,2},{5,3},{6,4},{7,5},{0,6},{1,7},{10,8},{11,9},{12,... | collective-permute-start | bytes 1966088 | tf_op jit(solution)/shard_map/ppermute | solution.py:50
  280.8 24.0 %collective-permute-start.29 = (bf16[128,2048]{1,0:T(8,128)(2,1)S(1)}, bf16[128,2048]{1,0:T(8,128)(2,1)S(1)}, u32[]{:S(2)}, u32[]{:S(2)}) collective-permute-start(bf16[128,2048]{1,0:T(8,128)(2,1)S(1)} %get-tuple-element.236), channel_id=1, source_target_pairs={{0,16},{8,24},{16,0},{24,8},{1,17},{9,25},{17,1},{25,9},{2,18},{10... | collective-permute-start | bytes 1572872 | tf_op jit(solution)/shard_map/ppermute | solution.py:55
  312.3 30.0 %collective-permute-start.34 = (bf16[768,2560]{1,0:T(8,128)(2,1)}, bf16[768,2560]{1,0:T(8,128)(2,1)S(1)}, u32[]{:S(2)}, u32[]{:S(2)}) collective-permute-start(bf16[768,2560]{1,0:T(8,128)(2,1)} %get-tuple-element.262), channel_id=1, source_target_pairs={{0,1},{1,0},{2,3},{3,2},{4,5},{5,4},{6,7},{7,6},{8,9},{9,8},{10,11... | collective-permute-start | bytes 11796488 | tf_op jit(solution)/shard_map/ppermute | solution.py:46
  314.5 24.4 %collective-permute-start.38 = (bf16[128,2048]{1,0:T(8,128)(2,1)S(1)}, bf16[128,2048]{1,0:T(8,128)(2,1)S(1)}, u32[]{:S(2)}, u32[]{:S(2)}) collective-permute-start(bf16[128,2048]{1,0:T(8,128)(2,1)S(1)} %get-tuple-element.261.refs_0_), channel_id=1, source_target_pairs={{0,24},{8,16},{16,8},{24,0},{1,25},{9,17},{17,9},{25,1},{2,26},{10... | collective-permute-start | bytes 1572872 | tf_op jit(solution)/shard_map/ppermute | solution.py:55
  316.0 31.1 %collective-permute-start.35 = (bf16[256,2560]{1,0:T(8,128)(2,1)S(1)}, bf16[256,2560]{1,0:T(8,128)(2,1)S(1)}, u32[]{:S(2)}, u32[]{:S(2)}) collective-permute-start(bf16[256,2560]{1,0:T(8,128)(2,1)S(1)} %add_convert_fusion.4), channel_id=1, source_target_pairs={{0,2},{1,3},{6,4},{7,5},{2,6},{3,7},{4,0},{5,1},{8,10},{9,11},{14,... | collective-permute-start | bytes 3932168 | tf_op jit(solution)/shard_map/ppermute | solution.py:50
  338.9 35.9 %collective-permute-start.39 = (bf16[128,2048]{1,0:T(8,128)(2,1)S(1)}, bf16[128,2048]{1,0:T(8,128)(2,1)S(1)}, u32[]{:S(2)}, u32[]{:S(2)}) collective-permute-start(bf16[128,2048]{1,0:T(8,128)(2,1)S(1)} %get-tuple-element.268), channel_id=1, source_target_pairs={{0,8},{8,0},{16,24},{24,16},{1,9},{9,1},{17,25},{25,17},{2,10},{10... | collective-permute-start | bytes 1572872 | tf_op jit(solution)/shard_map/ppermute | solution.py:55
  339.7 35.0 %collective-permute-start.40 = (bf16[128,2048]{1,0:T(8,128)(2,1)S(1)}, bf16[128,2048]{1,0:T(8,128)(2,1)}, u32[]{:S(2)}, u32[]{:S(2)}) collective-permute-start(bf16[128,2048]{1,0:T(8,128)(2,1)S(1)} %get-tuple-element.269), channel_id=1, source_target_pairs={{0,16},{8,24},{16,0},{24,8},{1,17},{9,25},{17,1},{25,9},{2,18},{10... | collective-permute-start | bytes 1572872 | tf_op jit(solution)/shard_map/ppermute | solution.py:55
  341.3 33.5 %collective-permute-start.41 = (bf16[128,2048]{1,0:T(8,128)(2,1)}, bf16[128,2048]{1,0:T(8,128)(2,1)}, u32[]{:S(2)}, u32[]{:S(2)}) collective-permute-start(bf16[128,2048]{1,0:T(8,128)(2,1)} %get-tuple-element.270), channel_id=1, source_target_pairs={{0,24},{8,16},{16,8},{24,0},{1,25},{9,17},{17,9},{25,1},{2,26},{10... | collective-permute-start | bytes 1572872 | tf_op jit(solution)/shard_map/ppermute | solution.py:55
  349.6 63.4 %collective-permute-start.47 = (bf16[256,2560]{1,0:T(8,128)(2,1)}, bf16[256,2560]{1,0:T(8,128)(2,1)S(1)}, u32[]{:S(2)}, u32[]{:S(2)}) collective-permute-start(bf16[256,2560]{1,0:T(8,128)(2,1)} %get-tuple-element.345), channel_id=1, source_target_pairs={{0,2},{1,3},{2,4},{3,5},{4,6},{5,7},{6,0},{7,1},{8,10},{9,11},{10,... | collective-permute-start | bytes 3932168 | tf_op jit(solution)/shard_map/ppermute | solution.py:50
  349.6 63.4 %collective-permute-start.48 = (bf16[256,2560]{1,0:T(8,128)(2,1)}, bf16[256,2560]{1,0:T(8,128)(2,1)}, u32[]{:S(2)}, u32[]{:S(2)}) collective-permute-start(bf16[256,2560]{1,0:T(8,128)(2,1)} %get-tuple-element.344), channel_id=1, source_target_pairs={{2,0},{3,1},{4,2},{5,3},{6,4},{7,5},{0,6},{1,7},{10,8},{11,9},{12,... | collective-permute-start | bytes 3932168 | tf_op jit(solution)/shard_map/ppermute | solution.py:50
  419.8 26.9 %collective-permute-start.51 = (bf16[1040,512]{1,0:T(8,128)(2,1)S(1)}, bf16[1040,512]{1,0:T(8,128)(2,1)S(1)}, u32[]{:S(2)}, u32[]{:S(2)}) collective-permute-start(bf16[1040,512]{1,0:T(8,128)(2,1)S(1)} %add_convert_fusion.5), channel_id=1, source_target_pairs={{0,2},{1,3},{6,4},{7,5},{2,6},{3,7},{4,0},{5,1},{8,10},{9,11},{14,... | collective-permute-start | bytes 3194888 | tf_op jit(solution)/shard_map/ppermute | solution.py:50
  420.0 31.1 %collective-permute-start.54 = (bf16[256,2560]{1,0:T(8,128)(2,1)S(1)}, bf16[256,2560]{1,0:T(8,128)(2,1)S(1)}, u32[]{:S(2)}, u32[]{:S(2)}) collective-permute-start(bf16[256,2560]{1,0:T(8,128)(2,1)S(1)} %add_convert_fusion.3.refs_0_), channel_id=1, source_target_pairs={{0,8},{8,0},{16,24},{24,16},{1,9},{9,1},{17,25},{25,17},{2,10},{10... | collective-permute-start | bytes 3932168 | tf_op jit(solution)/shard_map/ppermute | solution.py:55
  421.3 30.8 %collective-permute-start.55 = (bf16[256,2560]{1,0:T(8,128)(2,1)S(1)}, bf16[256,2560]{1,0:T(8,128)(2,1)S(1)}, u32[]{:S(2)}, u32[]{:S(2)}) collective-permute-start(bf16[256,2560]{1,0:T(8,128)(2,1)S(1)} %add_convert_fusion.3.refs_0_), channel_id=1, source_target_pairs={{0,16},{8,24},{16,0},{24,8},{1,17},{9,25},{17,1},{25,9},{2,18},{10... | collective-permute-start | bytes 3932168 | tf_op jit(solution)/shard_map/ppermute | solution.py:55
  455.9 23.9 %collective-permute-start.53 = (bf16[512,512]{1,0:T(8,128)(2,1)S(1)}, bf16[512,512]{1,0:T(8,128)(2,1)S(1)}, u32[]{:S(2)}, u32[]{:S(2)}) collective-permute-start(bf16[512,512]{1,0:T(8,128)(2,1)S(1)} %get-tuple-element.350), channel_id=1, source_target_pairs={{2,0},{3,1},{4,2},{5,3},{6,4},{7,5},{0,6},{1,7},{10,8},{11,9},{12,... | collective-permute-start | bytes 1572872 | tf_op jit(solution)/shard_map/ppermute | solution.py:50
  485.1 24.1 %collective-permute-start.64 = (bf16[528,512]{1,0:T(8,128)(2,1)S(1)}, bf16[528,512]{1,0:T(8,128)(2,1)S(1)}, u32[]{:S(2)}, u32[]{:S(2)}) collective-permute-start(bf16[528,512]{1,0:T(8,128)(2,1)S(1)} %get-tuple-element.327), channel_id=1, source_target_pairs={{2,0},{3,1},{4,2},{5,3},{6,4},{7,5},{0,6},{1,7},{10,8},{11,9},{12,... | collective-permute-start | bytes 1622024 | tf_op jit(solution)/shard_map/ppermute | solution.py:50
  509.4 26.0 %collective-permute-start.65 = (bf16[528,512]{1,0:T(8,128)(2,1)S(1)}, bf16[528,512]{1,0:T(8,128)(2,1)S(1)}, u32[]{:S(2)}, u32[]{:S(2)}) collective-permute-start(bf16[528,512]{1,0:T(8,128)(2,1)S(1)} %add_convert_fusion.8.refs_0_.refs_4_.refs_8_), channel_id=1, source_target_pairs={{0,8},{8,0},{16,24},{24,16},{1,9},{9,1},{17,25},{25,17},{2,10},{10... | collective-permute-start | bytes 1622024 | tf_op jit(solution)/shard_map/ppermute | solution.py:55
  510.5 25.5 %collective-permute-start.66 = (bf16[528,512]{1,0:T(8,128)(2,1)S(1)}, bf16[528,512]{1,0:T(8,128)(2,1)S(1)}, u32[]{:S(2)}, u32[]{:S(2)}) collective-permute-start(bf16[528,512]{1,0:T(8,128)(2,1)S(1)} %add_convert_fusion.8.refs_0_.refs_4_.refs_8_), channel_id=1, source_target_pairs={{0,16},{8,24},{16,0},{24,8},{1,17},{9,25},{17,1},{25,9},{2,18},{10... | collective-permute-start | bytes 1622024 | tf_op jit(solution)/shard_map/ppermute | solution.py:55
  511.2 24.7 %collective-permute-start.67 = (bf16[528,512]{1,0:T(8,128)(2,1)S(1)}, bf16[528,512]{1,0:T(8,128)(2,1)S(1)}, u32[]{:S(2)}, u32[]{:S(2)}) collective-permute-start(bf16[528,512]{1,0:T(8,128)(2,1)S(1)} %add_convert_fusion.8.refs_0_.refs_4_.refs_8_), channel_id=1, source_target_pairs={{0,24},{8,16},{16,8},{24,0},{1,25},{9,17},{17,9},{25,1},{2,26},{10... | collective-permute-start | bytes 1622024 | tf_op jit(solution)/shard_map/ppermute | solution.py:55
  (95 other events, 1289.8 us)

commit v4 on v3

--- a/solution.py
+++ b/solution.py
@@ -46,6 +46,11 @@
     return lax.ppermute(a, "fsdp", [(r, r ^ 1) for r in range(size)])
 
 
+def core_exchange(a):
+    groups = [[r, r + 1] for r in range(0, lax.axis_size("fsdp"), 2)]
+    return lax.all_to_all(a, "fsdp", 0, 0, axis_index_groups=groups, tiled=True)
+
+
 def chip_send(a, pairs):
     return lax.ppermute(a, "fsdp", [(2 * s + k, 2 * d + k) for s, d in pairs for k in range(2)])
 
@@ -110,33 +115,35 @@
     chips = lax.axis_size("fsdp") // 2
     size = near.shape[0] // len(near_slots(chips))
     first, last = rows or (0, size)
-    parts = [
-        near[s * size + first : s * size + last].astype(f32) for s in range(len(near_slots(chips)))
-    ]
-    if chips == 4:
-        far = far[first:last].astype(f32)
-        zero = jnp.zeros((), f32)
-        ends = parts[0] + jnp.where((chip == 0) | (chip == 3), far, zero)
-        up = parts[1] + jnp.where(chip == 1, far, zero)
-        down = parts[2] + jnp.where(chip == 2, far, zero)
-        parts = [ends, up, down]
-    return [parts[0]] + [p.astype(bf16) for p in parts[1:]]
+    parts = [near[s * size + first : s * size + last] for s in range(len(near_slots(chips)))]
+    if chips != 4:
+        return parts[1:], (parts[0], None)
+    far = far[first:last]
+    wide = far.astype(f32)
+    zero = jnp.zeros((), f32)
+    up = parts[1].astype(f32) + jnp.where(chip == 1, wide, zero)
+    down = parts[2].astype(f32) + jnp.where(chip == 2, wide, zero)
+    return [up.astype(bf16), down.astype(bf16)], (parts[0], far)
 
 
 def near_receive(sends):
     chips = lax.axis_size("fsdp") // 2
     if chips == 4:
-        from_below = chip_send(sends[1], [(0, 1), (1, 2), (2, 3), (3, 0)])
-        from_above = chip_send(sends[2], [(1, 0), (2, 1), (3, 2), (0, 3)])
-        return [sends[0], from_below, from_above]
-    return [sends[0]] + [
-        chip_send(sends[t], [(z, (z + t) % chips) for z in range(chips)]) for t in range(1, chips)
+        from_below = chip_send(sends[0], [(0, 1), (1, 2), (2, 3), (3, 0)])
+        from_above = chip_send(sends[1], [(1, 0), (2, 1), (3, 2), (0, 3)])
+        return [from_below, from_above]
+    return [
+        chip_send(sends[t - 1], [(z, (z + t) % chips) for z in range(chips)])
+        for t in range(1, chips)
     ]
 
 
-def near_total(received):
-    total = received[0]
-    for part in received[1:]:
+def near_total(received, kept, chip):
+    own, far = kept
+    total = own.astype(f32)
+    if far is not None:
+        total = total + jnp.where((chip == 0) | (chip == 3), far.astype(f32), jnp.zeros((), f32))
+    for part in received:
         total = total + part.astype(f32)
     return total.astype(bf16)
 
@@ -545,10 +552,14 @@
 
 def out_kernel(blocks, parts, shards, scal, att, *refs):
     weights, outs, joined, sems = refs[:parts], refs[parts:-2], refs[-2], refs[-1]
-    start_and_wait(out_copies(shards, scal, weights, joined, sems))
+    copies = out_copies(shards, scal, weights, joined, sems)
+    for c in copies:
+        c.start()
     rows = outs[0].shape[0]
     wide = joined.shape[2]
     for b in range(joined.shape[0]):
+        for c in copies[b * shards : (b + 1) * shards]:
+            c.wait()
         total = dot(att[...], joined[b]).astype(bf16)
         for t in range(blocks):
             outs[t][:, b * wide : (b + 1) * wide] = total[t * rows : (t + 1) * rows]
@@ -572,15 +583,18 @@
 def grad_attended_kernel(blocks, parts, shards, scal, *refs):
     low, weights = refs[:blocks], refs[blocks : blocks + parts]
     out, joined, sems = refs[blocks + parts :]
-    start_and_wait(out_copies(shards, scal, weights, joined, sems))
+    copies = out_copies(shards, scal, weights, joined, sems)
+    for c in copies:
+        c.start()
     wide = joined.shape[2]
-    for t, ref in enumerate(low):
-        rows = ref.shape[0]
-        total = None
-        for b in range(joined.shape[0]):
-            term = dot(ref[:, b * wide : (b + 1) * wide], joined[b], 1, 1)
-            total = term if total is None else total + term
-        out[t * rows : (t + 1) * rows, :] = total.astype(bf16)
+    total = None
+    for b in range(joined.shape[0]):
+        for c in copies[b * shards : (b + 1) * shards]:
+            c.wait()
+        part = jnp.concatenate([ref[:, b * wide : (b + 1) * wide] for ref in low], axis=0)
+        term = dot(part, joined[b], 1, 1)
+        total = term if total is None else total + term
+    out[...] = total.astype(bf16)
 
 
 def make_grad_attended(scal, low_all, weights, shards):
@@ -840,53 +854,42 @@
     )
 
 
-def shard_specs(weights, rows):
-    specs, ranges, first = [], [], 0
-    for w in weights:
-        count = w.shape[0] // rows
-        specs.append(
-            pl.BlockSpec(
-                (rows, w.shape[1]), lambda l, f=first, n=count: (jnp.clip(l - f, 0, n - 1), 0)
-            )
-        )
-        ranges.append((first, first + count))
-        first += count
-    return specs, ranges
-
-
-def within(bounds):
-    l = pl.program_id(0)
-    return pl.when((l >= bounds[0]) & (l < bounds[1]))
-
-
-def ffn_transposed_kernel(ranges, g, *refs):
-    weights, outs = refs[: len(ranges)], refs[len(ranges) :]
+def ffn_transposed_kernel(parts, blocks, g, *refs):
+    weights, outs = refs[:parts], refs[parts : parts + blocks]
+    held, sems = refs[parts + blocks : -1], refs[-1]
     rows = outs[0].shape[0]
-    for ref, bounds in zip(weights, ranges):
-
-        @within(bounds)
-        def _():
-            total = dot(g[...], ref[...], 1, 1).astype(bf16)
+    copies = [pltpu.make_async_copy(w, h, sems.at[i]) for i, (w, h) in enumerate(zip(weights, held))]
+    order = sorted(range(parts), key=lambda i: held[i].shape[0])
+    first = [sum(h.shape[0] for h in held[:i]) for i in range(parts)]
+    for i in order:
+        copies[i].start()
+    for i in order:
+        copies[i].wait()
+        tile = held[i].shape[0] if held[i].shape[0] <= 768 else tile_of(held[i].shape[0], 512)
+        for n in range(0, held[i].shape[0], tile):
+            total = dot(g[...], held[i][n : n + tile, :], 1, 1).astype(bf16)
+            at = first[i] + n
             for t, out in enumerate(outs):
-                out[...] = total[t * rows : (t + 1) * rows]
-
-
-def ffn_transposed(g, weights, size, shards, blocks):
+                out[:, at : at + tile] = total[t * rows : (t + 1) * rows]
+
+
+def ffn_transposed(g, weights, blocks):
     tokens, depth = g.shape
-    rows, width = tokens // blocks, size * shards
-    specs, ranges = shard_specs(weights, size)
-    return call(
-        functools.partial(ffn_transposed_kernel, ranges),
-        (shards,),
-        [whole(g)] + specs,
-        [pl.BlockSpec((rows, size), lambda l: (0, l))] * blocks,
+    rows, width = tokens // blocks, sum(w.shape[0] for w in weights)
+    return call(
+        functools.partial(ffn_transposed_kernel, len(weights), blocks),
+        (1,),
+        [whole(g)] + [pl.BlockSpec(memory_space=ANY)] * len(weights),
+        [pl.BlockSpec((rows, width), lambda i: (0, 0))] * blocks,
         [struct((rows, width), bf16)] * blocks,
         (g, *weights),
+        [pltpu.VMEM(w.shape, bf16) for w in weights]
+        + [pltpu.SemaphoreType.DMA((len(weights),))],
         flops=2 * tokens * depth * width,
     )
 
 
-def units_grad_kernel(shards, normed, g, *refs):
+def units_grad_kernel(shards, scal, normed, g, *refs):
     outs, turned = refs[:-1], refs[-1]
 
     @at_step(0)
@@ -895,66 +898,92 @@
 
     total = dot(turned[...], g[...]).astype(bf16)
     at = 0
-    for out in outs:
+    for out in outs[:2]:
         n = out.shape[0]
         out[...] = total[at : at + n]
         at += n
-
-
-def units_grad(normed, g, shards):
+    if len(outs) == 3:
+        size = outs[2].shape[0] // 2
+        core = scal[2] & 1
+        for n, place in enumerate((core, 1 - core)):
+            start = pl.multiple_of(place * size, size)
+            outs[2][pl.ds(start, size), :] = total[at + n * size : at + (n + 1) * size]
+
+
+def units_grad(scal, normed, g, shards):
     tokens, depth = normed.shape
     width = g.shape[1]
     tile = tile_of(width, 512)
-    sizes = []
-    for slots in (near_slots(shards // 2), far_slots(shards // 2)):
-        if slots:
-            sizes += [len(slots) * (depth // shards)] * 2
+    size = depth // shards
+    sizes = [len(near_slots(shards // 2)) * size] * 2
+    if far_slots(shards // 2):
+        sizes.append(2 * size)
     return call(
         functools.partial(units_grad_kernel, shards),
         (width // tile,),
-        [whole(normed), pl.BlockSpec((tokens, tile), lambda i: (0, i))],
+        [smem, whole(normed), pl.BlockSpec((tokens, tile), lambda i: (0, i))],
         [pl.BlockSpec((n, tile), lambda i: (0, i)) for n in sizes],
         [struct((n, width), bf16) for n in sizes],
-        (normed, g),
+        (scal, normed, g),
         [pltpu.VMEM((depth, tokens), bf16)],
         flops=2 * tokens * depth * width,
     )
 
 
-def attn_transposed_kernel(blocks, ranges, size, scales, gq, gk, gv, *refs):
-    tokens_refs, weights = refs[:blocks], refs[blocks : blocks + len(ranges)]
-    outs, gain = refs[blocks + len(ranges) : -1], refs[-1]
-    rows = outs[0].shape[0]
-    for ref, bounds in zip(weights, ranges):
-
-        @within(bounds)
+def attn_transposed_kernel(blocks, parts, shards, scales, gq, gk, gv, *refs):
+    tokens_refs, weights = refs[:blocks], refs[blocks : blocks + parts]
+    outs = refs[blocks + parts : 2 * blocks + parts]
+    gain, held, sems = refs[2 * blocks + parts :]
+    rows, size = outs[0].shape
+    stride = sum(w.shape[0] for w in weights) // shards
+    step = pl.program_id(0)
+
+    def copy(l):
+        ref, at = shard_places(weights, stride)[l]
+        return pltpu.make_async_copy(ref.at[pl.ds(at, 3 * size), :], held.at[l], sems.at[l])
+
+    @at_step(0)
+    def _():
+        for l in range(shards):
+            copy(l).start()
+
+    for l in range(shards):
+
+        @at_step(l)
         def _():
-            total = None
-            for n, g in enumerate((gq, gk, gv)):
-                term = dot(g[...], ref[n * size : (n + 1) * size, :], 1, 1)
-                total = term if total is None else total + term
-            summed = jnp.zeros((1, size), f32)
-            for t, out in enumerate(outs):
-                at = slice(t * rows, (t + 1) * rows)
-                out[...] = total[at].astype(bf16)
-                unit = tokens_refs[t][...].astype(f32) * scales[at, 0:1]
-                summed = summed + jnp.sum(total[at] * unit, axis=0, keepdims=True)
-            gain[...] = summed
+            copy(l).wait()
+
+    total = None
+    for n, g in enumerate((gq, gk, gv)):
+        term = dot(g[...], held[step, n * size : (n + 1) * size, :], 1, 1)
+        total = term if total is None else total + term
+    summed = jnp.zeros((1, size), f32)
+    for t, out in enumerate(outs):
+        at = slice(t * rows, (t + 1) * rows)
+        out[...] = total[at].astype(bf16)
+        unit = tokens_refs[t][...].astype(f32) * scales[at, 0:1]
+        summed = summed + jnp.sum(total[at] * unit, axis=0, keepdims=True)
+    gain[...] = summed
 
 
 def attn_transposed(scales, grads, tokens_all, weights, size, shards, blocks):
     tokens, wide = grads[0].shape
     rows, width = tokens // blocks, size * shards
-    stride = sum(w.shape[0] for w in weights) // shards
-    specs, ranges = shard_specs(weights, stride)
     tile = pl.BlockSpec((rows, size), lambda l: (0, l))
     results = call(
-        functools.partial(attn_transposed_kernel, blocks, ranges, size),
+        functools.partial(attn_transposed_kernel, blocks, len(weights), shards),
         (shards,),
-        [whole(scales)] + [whole(g) for g in grads] + [tile] * blocks + specs,
+        [whole(scales)]
+        + [whole(g) for g in grads]
+        + [tile] * blocks
+        + [pl.BlockSpec(memory_space=ANY)] * len(weights),
         [tile] * blocks + [pl.BlockSpec((1, size), lambda l: (0, l))],
         [struct((rows, width), bf16)] * blocks + [struct((1, width), f32)],
         (scales, *grads, *tokens_all, *weights),
+        [
+            pltpu.VMEM((shards, 3 * size, wide), bf16),
+            pltpu.SemaphoreType.DMA((shards,)),
+        ],
         flops=6 * tokens * wide * width,
     )
     return results[:-1], results[-1]
@@ -1344,17 +1373,8 @@
             ]
         return [c * my_heads + h for h in range(my_heads)]
 
-    own_tokens = call(
-        functools.partial(tokens_kernel, shards),
-        (1,),
-        [smem] + [pl.BlockSpec((rows, width), lambda i: (0, 0))] * 2,
-        [pl.BlockSpec((2 * rows, width), lambda i: (0, 0))],
-        [struct((2 * rows, width), bf16)],
-        (scal, inputs[0], cotangent[0]),
-    )[0]
-    all_tokens = ctx_gather(own_tokens)
     args = (
-        after(scal, own_tokens),
+        scal,
         w_query,
         w_key,
         w_value,
@@ -1375,6 +1395,15 @@
         args,
     )[0]
     near_attn = gather_near(own_attn)
+    own_tokens = call(
+        functools.partial(tokens_kernel, shards),
+        (1,),
+        [smem] + [pl.BlockSpec((rows, width), lambda i: (0, 0))] * 2,
+        [pl.BlockSpec((2 * rows, width), lambda i: (0, 0))],
+        [struct((2 * rows, width), bf16)],
+        (after(scal, own_attn), inputs[0], cotangent[0]),
+    )[0]
+    all_tokens = ctx_gather(own_tokens)
     tile = tile_of(shard_rows, 64)
     own_gate_up = call(
         functools.partial(choose_units_kernel, shards),
@@ -1382,7 +1411,7 @@
         [smem] + [pl.BlockSpec((tile, w_gate.shape[1]), lambda i: (i, 0))] * 2,
         [pl.BlockSpec((tile, 2 * units), lambda i: (i, 0))],
         [struct((shard_rows, 2 * units), bf16)],
-        (after(scal, own_attn), w_gate, w_up),
+        (after(scal, own_tokens), w_gate, w_up),
     )[0]
     joint = together([*near_attn, *all_tokens], own_gate_up)
     near_attn, all_tokens = joint[: len(near_attn)], joint[len(near_attn) :]
@@ -1452,29 +1481,32 @@
     grad_units = units_back(scal, gate, up, all_tokens, down_parts, down_shards)
     if far_sum is not None:
         far_sum, grad_units = together([far_sum, grad_units])
-    sends = together(near_sends(sums_down[-1], far_sum, chip), grad_units)
+    sends, kept = near_sends(sums_down[-1], far_sum, chip)
+    sends = together(sends, grad_units)
     received = near_receive(sends)
-    parts = ffn_transposed(after(grad_units, *sends), weights_gate_up, shard_rows, shards, blocks)
-    grads_gate_up = units_grad(normed_ffn, after(grad_units, *parts), shards)
+    parts = ffn_transposed(after(grad_units, *sends), weights_gate_up, blocks)
+    grads_gate_up = units_grad(scal, normed_ffn, after(grad_units, *parts), shards)
     parts = ctx_exchange(parts)
-    result_parts = multiply_down(
-        scal, after(mixed_units, *grads_gate_up), down_parts, down_shards, blocks
-    )
-    joint = together([*parts, *received, *grads_gate_up], *result_parts)
-    parts, grads_gate_up = list(joint[:blocks]), joint[blocks + len(received) :]
-    share_down = near_total(joint[blocks : blocks + len(received)])
-    far_sum = []
-    if len(grads_gate_up) == 4:
-        far_add = add_low(grads_gate_up[2], core_swap(grads_gate_up[3]))
+    n = len(received)
+    joint = together([*received, *grads_gate_up])
+    received, grads_gate_up = joint[:n], joint[n:]
+    far_sum, far_add = [], grads_gate_up[0]
+    if len(grads_gate_up) == 3:
+        both = core_exchange(grads_gate_up[2])
+        far_add = add_low(both[:shard_rows], both[shard_rows:])
         far_sum = [reduce_far(far_add)]
-        parts = together(parts, far_add)
+    share_down = near_total(received, kept, chip)
+    parts = together(parts, far_add)
     grad_hidden, low, grad_gain_ffn = ffn_norm_back(
         scal, hidden, gains, own_tokens, parts, shards
     )
 
     all_low = ctx_gather(low)
     near_sum = add_low(grads_gate_up[0], core_swap(after(grads_gate_up[1], low)))
-    sends = near_sends(near_sum, far_sum[0] if far_sum else None, chip)
+    result_parts = multiply_down(
+        scal, after(mixed_units, near_sum), down_parts, down_shards, blocks
+    )
+    sends, kept = near_sends(near_sum, far_sum[0] if far_sum else None, chip)
     received = near_receive(sends)
     result_parts = ctx_exchange(together(result_parts, *all_low))
     if strided:
@@ -1517,20 +1549,28 @@
         far_add = add_low(grads_attn[2], core_swap(grads_attn[3]))
         far_sum = [reduce_far(far_add)]
     near_sum = add_low(grads_attn[0], core_swap(after(grads_attn[1], far_add)))
-    share_gate_up = near_total(received)
+    share_gate_up = near_total(received, kept, chip)
     near_units = ctx_gather_near(after(share_gate_up, far_add))
     near_sum, *far_sum = together([near_sum, *far_sum])
     far_sum = far_sum[0] if far_sum else None
     cut = 2 * shard_rows
-    first = near_receive(near_sends(near_sum, far_sum, chip, (0, cut)))
-    sends = near_sends(near_sum, far_sum, chip, (cut, stride))
-    far_units = ctx_gather_far(together(near_units, *sends))
+    sends, kept = near_sends(near_sum, far_sum, chip, (0, cut))
+    first = near_receive(sends)
+    far_units = ctx_gather_far(near_units)
+    sends, later = near_sends(
+        after(near_sum, *far_units),
+        None if far_sum is None else after(far_sum, *far_units),
+        chip,
+        (cut, stride),
+    )
     far_down_share = ctx_gather_far(together(near_down_share, *far_units))
+    n = len(first)
     joint = together([*first, *far_down_share, *sends])
-    first, far_down_share, sends = near_total(joint[:n]), joint[n:-n], joint[-n:]
+    first, far_down_share, sends = joint[:n], joint[n:-n], joint[-n:]
+    first = near_total(first, kept, chip)
     second = near_receive(sends)
     joint = together([*ctx_gather(first), *second])
-    pieces_first, second = joint[:blocks], near_total(joint[blocks:])
+    pieces_first, second = joint[:blocks], near_total(joint[blocks:], later, chip)
     pieces_second = ctx_gather(second)
     pieces_gate_up = ctx_pieces(share_gate_up, near_units, far_units)
     pieces_down = ctx_pieces(share_down, near_down_share, far_down_share)

time: 552 us -> 546 us (0.989)
  starting transfers between devices: 88.3 us -> 77.6 us
  blocking collectives: 0 us -> 7.24 us
  waiting for transfers between devices: 243 us -> 237 us
    ppermute x20, waiting for transfers between devices: 79.5 us -> 61.7 us  [chip_send(): lax.ppermute(a, 'fsdp', [(2 * s + k, 2 * d + k) for s, d in pairs for k i...]
    ppermute x35, waiting for transfers between devices: 152 us -> 164 us  [ctx_send(): return lax.ppermute(a, 'ctx', [(i, i ^ distance) for i in range(size)])]
    ppermute x20, starting transfers between devices: 45.6 us -> 34.4 us  [chip_send(): lax.ppermute(a, 'fsdp', [(2 * s + k, 2 * d + k) for s, d in pairs for k i...]
    all_to_all x0 -> x1, blocking collectives: none -> 7.24 us  [core_exchange(): return lax.all_to_all(a, 'fsdp', 0, 0, axis_index_groups=groups, tiled=True)]
    ppermute x13 -> x12, waiting for transfers between devices: 12.4 us -> 11.9 us  [core_swap(): return lax.ppermute(a, 'fsdp', [(r, r ^ 1) for r in range(size)])]
    unnamed x120 -> x124, local copies, waits for them, and re-layouts: 17 us -> 16.7 us
  transfers between devices with their start and end apart: 68 -> 67, of which waited for: 39 -> 40; matrix products, arithmetic and copies ran while one was open for 3% -> 4% of each run, Pallas kernels for 28% -> 29%
where the time goes in v4:
time: 546 us; the launch traced here: 536 us
  waiting for transfers between devices  237 us (43%)
  Pallas kernels  164 us (30%)
  starting transfers between devices  77.6 us (14%)
  other arithmetic  26.5 us (5%)
  local copies, waits for them, and re-layouts  20.8 us (4%)
  blocking collectives  7.24 us (1%)
    pallas_call x23, Pallas kernels, call(): pl.pallas_call(kernel, grid=grid, in_specs=in_specs, out_specs=out_specs,...  164 us
    ppermute x35, waiting for transfers between devices, ctx_send(): return lax.ppermute(a, 'ctx', [(i, i ^ distance) for i in range(size)])  164 us
    ppermute x20, waiting for transfers between devices, chip_send(): lax.ppermute(a, 'fsdp', [(2 * s + k, 2 * d + k) for s, d in pairs for k i...  61.7 us
    ppermute x35, starting transfers between devices, ctx_send(): return lax.ppermute(a, 'ctx', [(i, i ^ distance) for i in range(size)])  41.6 us
    ppermute x20, starting transfers between devices, chip_send(): lax.ppermute(a, 'fsdp', [(2 * s + k, 2 * d + k) for s, d in pairs for k i...  34.4 us
    unnamed x124, local copies, waits for them, and re-layouts  16.7 us
    ppermute x12, waiting for transfers between devices, core_swap(): return lax.ppermute(a, 'fsdp', [(r, r ^ 1) for r in range(size)])  11.9 us
  transfers between devices with their start and end apart: 67, of which 40 were waited for; matrix products, arithmetic and copies ran while one was open for 4% of the time, Pallas kernels for 29%

profile of v4, /device:TPU:0, one launch (start us, length us, event | category | flops | bytes accessed | tf_op | source)
XLA Modules:
  0.0 536.1 jit_solution(14552091121862793439)
XLA Ops:
  8.6 5.0 collective-permute-start
  23.4 18.4 %collective-permute-done.2.refs_1_ = bf16[256,2048]{1,0:T(8,128)(2,1)} collective-permute-done((bf16[256,2048]{1,0:T(8,128)(2,1)}, bf16[256,2048]{1,0:T(8,128)(2,1)}, u32[]{:S(2)}, u32[]{:S(2)}) %collective-permute-start.2) | collective-permute-done | bytes 1048608 | tf_op jit(solution)/shard_map/ppermute | solution.py:60
  41.7 22.2 %collective-permute-done.3.refs_2_ = bf16[256,2048]{1,0:T(8,128)(2,1)} collective-permute-done((bf16[256,2048]{1,0:T(8,128)(2,1)}, bf16[256,2048]{1,0:T(8,128)(2,1)}, u32[]{:S(2)}, u32[]{:S(2)}) %collective-permute-start.3) | collective-permute-done | bytes 1048608 | tf_op jit(solution)/shard_map/ppermute | solution.py:60
  70.0 21.9 %collective-permute-done.8.refs_10_.refs_6_ = bf16[1040,512]{1,0:T(8,128)(2,1)S(1)} collective-permute-done((bf16[1040,512]{1,0:T(8,128)(2,1)S(1)}, bf16[1040,512]{1,0:T(8,128)(2,1)S(1)}, u32[]{:S(2)}, u32[]{:S(2)}) %collective-permute-start.8) | collective-permute-done | bytes 1064992 | tf_op jit(solution)/shard_map/ppermute | solution.py:55
  96.6 9.9 %shard_map.241 = (bf16[512,2048]{1,0:T(8,128)(2,1)}, bf16[512,1536]{1,0:T(8,128)(2,1)}, f32[4,2,1024]{2,1,0:T(2,128)S(1)}, f32[2,2048]{1,0:T(2,128)S(1)}, f32[512,128]{1,0:T(8,128)S(1)}) custom-call(s32[10]{0:T(128)S(1)} %compare_select_fusion.3.scal, bf16[256,2048]{1,0:T(8,128)(2,1)S(1)} %copy-done.2, bf16[256,2048]{1,0:T(8,128)(2,1)} %collective-permute-done.2.refs_1_, ...), custom_call_target="tpu_custom_call" | custom-call | flops 1 | bytes 1 | tf_op jit(solution)/shard_map/pallas_call | solution.py:192
  106.5 12.0 %shard_map.242 = (bf16[512,512]{1,0:T(8,128)(2,1)S(1)}, bf16[8,512,512]{2,1,0:T(8,128)(2,1)}) custom-call(s32[10]{0:T(128)S(1)} %compare_select_fusion.3.scal, bf16[512,1536]{1,0:T(8,128)(2,1)} %get-tuple-element.180.q_ref.k_ref.v_ref, bf16[512,1536]{1,0:T(8,128)(2,1)} %get-tuple-element.180.q_ref.k_ref.v_ref, ...), custom_call_target="tpu_custom_call" | custom-call | flops 1 | bytes 1 | tf_op jit(solution)/shard_map/pallas_call | solution.py:192
  119.3 5.0 shard_map.243
  127.9 11.3 %collective-permute-done.10.refs_1_ = bf16[128,2048]{1,0:T(8,128)(2,1)S(1)} collective-permute-done((bf16[128,2048]{1,0:T(8,128)(2,1)S(1)}, bf16[128,2048]{1,0:T(8,128)(2,1)S(1)}, u32[]{:S(2)}, u32[]{:S(2)}) %collective-permute-start.10) | collective-permute-done | bytes 524320 | tf_op jit(solution)/shard_map/ppermute | solution.py:60
  139.9 10.7 %collective-permute-done.12.refs_3_ = bf16[128,2048]{1,0:T(8,128)(2,1)S(1)} collective-permute-done((bf16[128,2048]{1,0:T(8,128)(2,1)}, bf16[128,2048]{1,0:T(8,128)(2,1)S(1)}, u32[]{:S(2)}, u32[]{:S(2)}) %collective-permute-start.12) | collective-permute-done | bytes 524320 | tf_op jit(solution)/shard_map/ppermute | solution.py:60
  163.4 11.3 %collective-permute-done.16.refs_1_ = bf16[128,2048]{1,0:T(8,128)(2,1)S(1)} collective-permute-done((bf16[128,2048]{1,0:T(8,128)(2,1)S(1)}, bf16[128,2048]{1,0:T(8,128)(2,1)S(1)}, u32[]{:S(2)}, u32[]{:S(2)}) %collective-permute-start.16) | collective-permute-done | bytes 524320 | tf_op jit(solution)/shard_map/ppermute | solution.py:60
  174.7 10.2 %collective-permute-done.17.refs_2_ = bf16[128,2048]{1,0:T(8,128)(2,1)S(1)} collective-permute-done((bf16[128,2048]{1,0:T(8,128)(2,1)S(1)}, bf16[128,2048]{1,0:T(8,128)(2,1)S(1)}, u32[]{:S(2)}, u32[]{:S(2)}) %collective-permute-start.17) | collective-permute-done | bytes 524320 | tf_op jit(solution)/shard_map/ppermute | solution.py:60
  197.5 10.9 %shard_map.245 = (bf16[512,2048]{1,0:T(8,128)(2,1)}, f32[512,1280]{1,0:T(8,128)}, f32[512,1280]{1,0:T(8,128)}, bf16[512,1280]{1,0:T(8,128)(2,1)}) custom-call(bf16[128,2048]{1,0:T(8,128)(2,1)S(1)} %copy-done.22, bf16[128,2048]{1,0:T(8,128)(2,1)S(1)} %collective-permute-done.16.refs_1_, bf16[128,2048]{1,0:T(8,128)(2,1)S(1)} %copy-done.24, ...), custom_call_target="tpu_custom_call" | custom-call | flops 1 | bytes 1 | tf_op jit(solution)/shard_map/pallas_call | solution.py:192
  208.4 7.4 %shard_map.246 = (bf16[640,2048]{1,0:T(8,128)(2,1)}, bf16[640,2048]{1,0:T(8,128)(2,1)}) custom-call(s32[10]{0:T(128)S(1)} %compare_select_fusion.3.scal, bf16[512,1280]{1,0:T(8,128)(2,1)} %get-tuple-element.243.mixed, bf16[256,2048]{1,0:T(8,128)(2,1)S(1)} %copy-done.3, bf16[256,2048]{1,0:T(8,128)(2,1)} %collective-permute-done.2.refs_1_, ...), custom_call_target="tpu_custom_call" | custom-call | flops 1 | bytes 1 | tf_op jit(solution)/shard_map/pallas_call | solution.py:192
  215.9 9.0 %collective-permute-done.21 = bf16[160,2048]{1,0:T(8,128)(2,1)S(1)} collective-permute-done((bf16[160,2048]{1,0:T(8,128)(2,1)S(1)}, bf16[160,2048]{1,0:T(8,128)(2,1)S(1)}, u32[]{:S(2)}, u32[]{:S(2)}) %collective-permute-start.21) | collective-permute-done | bytes 655392 | tf_op jit(solution)/shard_map/ppermute | solution.py:55
  230.9 11.7 %collective-permute-done.25.refs_6_.refs_2_ = bf16[160,2048]{1,0:T(8,128)(2,1)S(1)} collective-permute-done((bf16[160,2048]{1,0:T(8,128)(2,1)S(1)}, bf16[160,2048]{1,0:T(8,128)(2,1)S(1)}, u32[]{:S(2)}, u32[]{:S(2)}) %collective-permute-start.25) | collective-permute-done | bytes 655392 | tf_op jit(solution)/shard_map/ppermute | solution.py:55
  244.9 11.2 %shard_map.247.g = bf16[512,2560]{1,0:T(8,128)(2,1)} custom-call(s32[10]{0:T(128)S(1)} %compare_select_fusion.3.scal, f32[512,1280]{1,0:T(8,128)} %get-tuple-element.212.gate, f32[512,1280]{1,0:T(8,128)} %get-tuple-element.213.up, bf16[256,2048]{1,0:T(8,128)(2,1)} %shard_map.239.refs_0_.own, bf16[256,2048]{1,0:T(8,128)(2,1)} %collective-permute-done.2.refs_1_, ...), custom_call_target="tpu_custom_call" | custom-call | flops 1 | bytes 1 | tf_op jit(solution)/shard_map/pallas_call | solution.py:192
  256.1 4.8 collective-permute-done.26
  265.2 12.7 %shard_map.248 = (bf16[128,2048]{1,0:T(8,128)(2,1)S(1)}, bf16[128,2048]{1,0:T(8,128)(2,1)S(1)}, bf16[128,2048]{1,0:T(8,128)(2,1)S(1)}, bf16[128,2048]{1,0:T(8,128)(2,1)}) custom-call(bf16[512,2560]{1,0:T(8,128)(2,1)} %shard_map.247.g, bf16[768,2560]{1,0:T(8,128)(2,1)} %copy-done.28, bf16[768,2560]{1,0:T(8,128)(2,1)} %copy-done.34, ...), custom_call_target="tpu_custom_call" | custom-call | flops 1 | bytes 1 | tf_op jit(solution)/shard_map/pallas_call | solution.py:192
  281.5 10.3 %shard_map.249 = (bf16[768,2560]{1,0:T(8,128)(2,1)}, bf16[768,2560]{1,0:T(8,128)(2,1)}, bf16[512,2560]{1,0:T(8,128)(2,1)}) custom-call(s32[10]{0:T(128)S(1)} %compare_select_fusion.3.scal, bf16[512,2048]{1,0:T(8,128)(2,1)} %get-tuple-element.220.normed, bf16[512,2560]{1,0:T(8,128)(2,1)} %shard_map.247.g), custom_call_target="tpu_custom_call" | custom-call | flops 1 | bytes 1 | tf_op jit(solution)/shard_map/pallas_call | solution.py:192
  292.5 7.2 %all_to_all.9 = bf16[2,256,2560]{2,1,0:T(8,128)(2,1)S(1)} all-to-all(bf16[2,256,2560]{2,1,0:T(8,128)(2,1)} %bitcast.15), channel_id=1, replica_groups={{0,1},{2,3},{4,5},{6,7},{8,9},{10,11},{12,13},{14,15},{16,17},{18,19},{..., dimensions={0} | all-to-all | bytes 5242880 | tf_op jit(solution)/shard_map/all_to_all | solution.py:51
  318.9 7.5 %shard_map.253 = (bf16[128,2048]{1,0:T(8,128)(2,1)S(1)}, bf16[128,2048]{1,0:T(8,128)(2,1)S(1)}, bf16[128,2048]{1,0:T(8,128)(2,1)S(1)}, bf16[128,2048]{1,0:T(8,128)(2,1)}) custom-call(s32[10]{0:T(128)S(1)} %compare_select_fusion.3.scal, bf16[512,1280]{1,0:T(8,128)(2,1)} %get-tuple-element.243.mixed, bf16[480,2048]{1,0:T(8,128)(2,1)} %copy-done.35, ...), custom_call_target="tpu_custom_call" | custom-call | flops 1 | bytes 1 | tf_op jit(solution)/shard_map/pallas_call | solution.py:192
  326.5 6.3 %collective-permute-done.36.refs_2_ = bf16[128,2048]{1,0:T(8,128)(2,1)S(1)} collective-permute-done((bf16[128,2048]{1,0:T(8,128)(2,1)S(1)}, bf16[128,2048]{1,0:T(8,128)(2,1)S(1)}, u32[]{:S(2)}, u32[]{:S(2)}) %collective-permute-start.36) | collective-permute-done | bytes 524320 | tf_op jit(solution)/shard_map/ppermute | solution.py:60
  353.9 11.6 %shard_map.252 = (bf16[512,512]{1,0:T(8,128)(2,1)S(1)}, bf16[512,512]{1,0:T(8,128)(2,1)S(1)}, bf16[512,512]{1,0:T(8,128)(2,1)S(1)}, f32[4,2,1024]{2,1,0:T(2,128)S(1)}) custom-call(s32[10]{0:T(128)S(1)} %compare_select_fusion.3.scal, bf16[512,1536]{1,0:T(8,128)(2,1)} %get-tuple-element.180.q_ref.k_ref.v_ref, ...), custom_call_target="tpu_custom_call" | custom-call | flops 1 | bytes 1 | tf_op jit(solution)/shard_map/pallas_call | solution.py:192
  370.4 10.0 %shard_map.254 = (bf16[128,2048]{1,0:T(8,128)(2,1)S(1)}, bf16[128,2048]{1,0:T(8,128)(2,1)S(1)}, bf16[128,2048]{1,0:T(8,128)(2,1)S(1)}, bf16[128,2048]{1,0:T(8,128)(2,1)}, f32[1,2048]{1,0:T(1,128)S(1)}) custom-call(f32[512,128]{1,0:T(8,128)S(1)} %get-tuple-element.257.scales, bf16[512,512]{1,0:T(8,128)(2,1)} %copy-done.8, bf16[512,512]{1,0:T(8,128)(2,1)} %copy-done.10, ...), custom_call_target="tpu_custom_call" | custom-call | flops 1 | bytes 1 | tf_op jit(solution)/shard_map/pallas_call | solution.py:192
  388.2 11.9 %shard_map.255 = (bf16[3120,512]{1,0:T(8,128)(2,1)}, bf16[3120,512]{1,0:T(8,128)(2,1)}, bf16[1040,512]{1,0:T(8,128)(2,1)}, bf16[1040,512]{1,0:T(8,128)(2,1)}) custom-call(s32[10]{0:T(128)S(1)} %compare_select_fusion.3.scal, bf16[512,2048]{1,0:T(8,128)(2,1)} %get-tuple-element.272.normed, bf16[512,512]{1,0:T(8,128)(2,1)S(1)} %copy-done.14, ...), custom_call_target="tpu_custom_call" | custom-call | flops 1 | bytes 1 | tf_op jit(solution)/shard_map/pallas_call | solution.py:192
  402.3 5.2 collective-permute-done.44.refs_2_
  418.9 28.5 %collective-permute-done.53.refs_2_ = bf16[256,2560]{1,0:T(8,128)(2,1)S(1)} collective-permute-done((bf16[256,2560]{1,0:T(8,128)(2,1)S(1)}, bf16[256,2560]{1,0:T(8,128)(2,1)S(1)}, u32[]{:S(2)}, u32[]{:S(2)}) %collective-permute-start.53) | collective-permute-done | bytes 1310752 | tf_op jit(solution)/shard_map/ppermute | solution.py:60
  455.1 8.6 %collective-permute-done.54 = bf16[128,2560]{1,0:T(8,128)(2,1)S(1)} collective-permute-done((bf16[128,2560]{1,0:T(8,128)(2,1)S(1)}, bf16[128,2560]{1,0:T(8,128)(2,1)S(1)}, u32[]{:S(2)}, u32[]{:S(2)}) %collective-permute-start.54) | collective-permute-done | bytes 655392 | tf_op jit(solution)/shard_map/ppermute | solution.py:60
  467.6 5.3 collective-permute-done.57
  485.4 5.2 collective-permute-done.59.refs_2_.refs_3_
  490.6 9.4 %collective-permute-done.60.refs_4_.refs_5_ = bf16[512,512]{1,0:T(8,128)(2,1)S(1)} collective-permute-done((bf16[512,512]{1,0:T(8,128)(2,1)S(1)}, bf16[512,512]{1,0:T(8,128)(2,1)S(1)}, u32[]{:S(2)}, u32[]{:S(2)}) %collective-permute-start.60) | collective-permute-done | bytes 524320 | tf_op jit(solution)/shard_map/ppermute | solution.py:60
  512.3 8.8 %shard_map.259 = (f32[256,5120]{1,0:T(8,128)}, f32[256,5120]{1,0:T(8,128)}) custom-call(s32[10]{0:T(128)S(1)} %compare_select_fusion.3.scal, bf16[256,2560]{1,0:T(8,128)(2,1)S(1)} %fusion.7.refs_0_, bf16[256,2560]{1,0:T(8,128)(2,1)} %copy-done.42, bf16[256,2560]{1,0:T(8,128)(2,1)} %copy-done.41, bf16[256,2560]{1,0:T(8,128)(2,1)} %pad_maximum_fusion.refs_3_), custom_call_target="tpu_custom_call" | custom-call | flops 1 | bytes 1 | tf_op jit(solution)/shard_map/pallas_call | solution.py:192
  (282 shorter events, 192.1 us)
Async XLA Ops:
  8.6 55.3 %collective-permute-start = (bf16[1040,512]{1,0:T(8,128)(2,1)}, bf16[1040,512]{1,0:T(8,128)(2,1)}, u32[]{:S(2)}, u32[]{:S(2)}) collective-permute-start(bf16[1040,512]{1,0:T(8,128)(2,1)} %shard_map.238.refs_4_.refs_0_), channel_id=1, source_target_pairs={{2,0},{3,1},{4,2},{5,3},{6,4},{7,5},{0,6},{1,7},{10,8},{11,9},{12,... | collective-permute-start | bytes 3194888 | tf_op jit(solution)/shard_map/ppermute | solution.py:55
  13.7 50.3 %collective-permute-start.1 = (bf16[1040,512]{1,0:T(8,128)(2,1)}, bf16[1040,512]{1,0:T(8,128)(2,1)}, u32[]{:S(2)}, u32[]{:S(2)}) collective-permute-start(bf16[1040,512]{1,0:T(8,128)(2,1)} %shard_map.238.refs_4_.refs_0_), channel_id=1, source_target_pairs={{0,2},{1,3},{2,4},{3,5},{4,6},{5,7},{6,0},{7,1},{8,10},{9,11},{10,... | collective-permute-start | bytes 3194888 | tf_op jit(solution)/shard_map/ppermute | solution.py:55
  15.3 26.4 %collective-permute-start.2 = (bf16[256,2048]{1,0:T(8,128)(2,1)}, bf16[256,2048]{1,0:T(8,128)(2,1)}, u32[]{:S(2)}, u32[]{:S(2)}) collective-permute-start(bf16[256,2048]{1,0:T(8,128)(2,1)} %shard_map.239.refs_0_.own), channel_id=1, source_target_pairs={{0,8},{8,0},{16,24},{24,16},{1,9},{9,1},{17,25},{25,17},{2,10},{10... | collective-permute-start | bytes 3145736 | tf_op jit(solution)/shard_map/ppermute | solution.py:60
  16.8 47.1 %collective-permute-start.3 = (bf16[256,2048]{1,0:T(8,128)(2,1)}, bf16[256,2048]{1,0:T(8,128)(2,1)}, u32[]{:S(2)}, u32[]{:S(2)}) collective-permute-start(bf16[256,2048]{1,0:T(8,128)(2,1)} %shard_map.239.refs_0_.own), channel_id=1, source_target_pairs={{0,16},{8,24},{16,0},{24,8},{1,17},{9,25},{17,1},{25,9},{2,18},{10... | collective-permute-start | bytes 3145736 | tf_op jit(solution)/shard_map/ppermute | solution.py:60
  18.4 45.6 %collective-permute-start.4 = (bf16[256,2048]{1,0:T(8,128)(2,1)}, bf16[256,2048]{1,0:T(8,128)(2,1)}, u32[]{:S(2)}, u32[]{:S(2)}) collective-permute-start(bf16[256,2048]{1,0:T(8,128)(2,1)} %shard_map.239.refs_0_.own), channel_id=1, source_target_pairs={{0,24},{8,16},{16,8},{24,0},{1,25},{9,17},{17,9},{25,1},{2,26},{10... | collective-permute-start | bytes 3145736 | tf_op jit(solution)/shard_map/ppermute | solution.py:60
  66.0 25.9 %collective-permute-start.8 = (bf16[1040,512]{1,0:T(8,128)(2,1)S(1)}, bf16[1040,512]{1,0:T(8,128)(2,1)S(1)}, u32[]{:S(2)}, u32[]{:S(2)}) collective-permute-start(bf16[1040,512]{1,0:T(8,128)(2,1)S(1)} %select_select_fusion.1), channel_id=1, source_target_pairs={{6,2},{7,3},{0,4},{1,5},{2,0},{3,1},{4,6},{5,7},{14,10},{15,11},{8... | collective-permute-start | bytes 3194888 | tf_op jit(solution)/shard_map/ppermute | solution.py:55
  91.9 62.2 %collective-permute-start.13 = (bf16[256,2560]{1,0:T(8,128)(2,1)S(1)}, bf16[256,2560]{1,0:T(8,128)(2,1)}, u32[]{:S(2)}, u32[]{:S(2)}) collective-permute-start(bf16[256,2560]{1,0:T(8,128)(2,1)S(1)} %copy-done.5), channel_id=1, source_target_pairs={{2,0},{3,1},{4,2},{5,3},{6,4},{7,5},{0,6},{1,7},{10,8},{11,9},{12,... | collective-permute-start | bytes 3932168 | tf_op jit(solution)/shard_map/ppermute | solution.py:55
  95.5 58.6 %collective-permute-start.14 = (bf16[256,2560]{1,0:T(8,128)(2,1)S(1)}, bf16[256,2560]{1,0:T(8,128)(2,1)}, u32[]{:S(2)}, u32[]{:S(2)}) collective-permute-start(bf16[256,2560]{1,0:T(8,128)(2,1)S(1)} %copy-done.5), channel_id=1, source_target_pairs={{0,2},{1,3},{2,4},{3,5},{4,6},{5,7},{6,0},{7,1},{8,10},{9,11},{10,... | collective-permute-start | bytes 3932168 | tf_op jit(solution)/shard_map/ppermute | solution.py:55
  126.4 24.2 %collective-permute-start.12 = (bf16[128,2048]{1,0:T(8,128)(2,1)}, bf16[128,2048]{1,0:T(8,128)(2,1)S(1)}, u32[]{:S(2)}, u32[]{:S(2)}) collective-permute-start(bf16[128,2048]{1,0:T(8,128)(2,1)} %get-tuple-element.186), channel_id=1, source_target_pairs={{0,24},{8,16},{16,8},{24,0},{1,25},{9,17},{17,9},{25,1},{2,26},{10... | collective-permute-start | bytes 1572872 | tf_op jit(solution)/shard_map/ppermute | solution.py:60
  157.7 32.5 %collective-permute-start.15 = (bf16[768,2560]{1,0:T(8,128)(2,1)S(1)}, bf16[768,2560]{1,0:T(8,128)(2,1)S(1)}, u32[]{:S(2)}, u32[]{:S(2)}) collective-permute-start(bf16[768,2560]{1,0:T(8,128)(2,1)S(1)} %constant_dynamic-update-slice_fusion.refs_4_.refs_0_), channel_id=1, source_target_pairs={{0,1},{1,0},{2,3},{3,2},{4,5},{5,4},{6,7},{7,6},{8,9},{9,8},{10,11... | collective-permute-start | bytes 11796488 | tf_op jit(solution)/shard_map/ppermute | solution.py:46
  157.7 32.4 %collective-permute-start.19 = (bf16[256,2560]{1,0:T(8,128)(2,1)S(1)}, bf16[256,2560]{1,0:T(8,128)(2,1)}, u32[]{:S(2)}, u32[]{:S(2)}) collective-permute-start(bf16[256,2560]{1,0:T(8,128)(2,1)S(1)} %get-tuple-element.328), channel_id=1, source_target_pairs={{6,2},{7,3},{0,4},{1,5},{2,0},{3,1},{4,6},{5,7},{14,10},{15,11},{8... | collective-permute-start | bytes 3932168 | tf_op jit(solution)/shard_map/ppermute | solution.py:55
  161.0 23.9 %collective-permute-start.17 = (bf16[128,2048]{1,0:T(8,128)(2,1)S(1)}, bf16[128,2048]{1,0:T(8,128)(2,1)S(1)}, u32[]{:S(2)}, u32[]{:S(2)}) collective-permute-start(bf16[128,2048]{1,0:T(8,128)(2,1)S(1)} %get-tuple-element.194.refs_0_), channel_id=1, source_target_pairs={{0,16},{8,24},{16,0},{24,8},{1,17},{9,25},{17,1},{25,9},{2,18},{10... | collective-permute-start | bytes 1572872 | tf_op jit(solution)/shard_map/ppermute | solution.py:60
  194.6 30.2 %collective-permute-start.21 = (bf16[160,2048]{1,0:T(8,128)(2,1)S(1)}, bf16[160,2048]{1,0:T(8,128)(2,1)S(1)}, u32[]{:S(2)}, u32[]{:S(2)}) collective-permute-start(bf16[160,2048]{1,0:T(8,128)(2,1)S(1)} %constant_dynamic-slice_fusion), channel_id=1, source_target_pairs={{0,2},{1,3},{2,4},{3,5},{4,6},{5,7},{6,0},{7,1},{8,10},{9,11},{10,... | collective-permute-start | bytes 1966088 | tf_op jit(solution)/shard_map/ppermute | solution.py:55
  261.3 30.5 %collective-permute-start.28 = (bf16[160,2048]{1,0:T(8,128)(2,1)S(1)}, bf16[160,2048]{1,0:T(8,128)(2,1)S(1)}, u32[]{:S(2)}, u32[]{:S(2)}) collective-permute-start(bf16[160,2048]{1,0:T(8,128)(2,1)S(1)} %get-tuple-element.218), channel_id=1, source_target_pairs={{0,2},{1,3},{2,4},{3,5},{4,6},{5,7},{6,0},{7,1},{8,10},{9,11},{10,... | collective-permute-start | bytes 1966088 | tf_op jit(solution)/shard_map/ppermute | solution.py:55
  262.5 30.1 %collective-permute-start.29 = (bf16[160,2048]{1,0:T(8,128)(2,1)S(1)}, bf16[160,2048]{1,0:T(8,128)(2,1)S(1)}, u32[]{:S(2)}, u32[]{:S(2)}) collective-permute-start(bf16[160,2048]{1,0:T(8,128)(2,1)S(1)} %get-tuple-element.219), channel_id=1, source_target_pairs={{2,0},{3,1},{4,2},{5,3},{6,4},{7,5},{0,6},{1,7},{10,8},{11,9},{12,... | collective-permute-start | bytes 1966088 | tf_op jit(solution)/shard_map/ppermute | solution.py:55
  307.4 32.4 %collective-permute-start.34 = (bf16[256,2560]{1,0:T(8,128)(2,1)}, bf16[256,2560]{1,0:T(8,128)(2,1)}, u32[]{:S(2)}, u32[]{:S(2)}) collective-permute-start(bf16[256,2560]{1,0:T(8,128)(2,1)} %fusion.16), channel_id=1, source_target_pairs={{0,2},{1,3},{6,4},{7,5},{2,6},{3,7},{4,0},{5,1},{8,10},{9,11},{14,... | collective-permute-start | bytes 3932168 | tf_op jit(solution)/shard_map/ppermute | solution.py:55
  308.8 23.9 %collective-permute-start.36 = (bf16[128,2048]{1,0:T(8,128)(2,1)S(1)}, bf16[128,2048]{1,0:T(8,128)(2,1)S(1)}, u32[]{:S(2)}, u32[]{:S(2)}) collective-permute-start(bf16[128,2048]{1,0:T(8,128)(2,1)S(1)} %get-tuple-element.237.refs_0_), channel_id=1, source_target_pairs={{0,16},{8,24},{16,0},{24,8},{1,17},{9,25},{17,1},{25,9},{2,18},{10... | collective-permute-start | bytes 1572872 | tf_op jit(solution)/shard_map/ppermute | solution.py:60
  310.0 24.2 %collective-permute-start.37 = (bf16[128,2048]{1,0:T(8,128)(2,1)S(1)}, bf16[128,2048]{1,0:T(8,128)(2,1)S(1)}, u32[]{:S(2)}, u32[]{:S(2)}) collective-permute-start(bf16[128,2048]{1,0:T(8,128)(2,1)S(1)} %get-tuple-element.237.refs_0_), channel_id=1, source_target_pairs={{0,24},{8,16},{16,8},{24,0},{1,25},{9,17},{17,9},{25,1},{2,26},{10... | collective-permute-start | bytes 1572872 | tf_op jit(solution)/shard_map/ppermute | solution.py:60
  334.2 33.6 %collective-permute-start.38 = (bf16[128,2048]{1,0:T(8,128)(2,1)S(1)}, bf16[128,2048]{1,0:T(8,128)(2,1)S(1)}, u32[]{:S(2)}, u32[]{:S(2)}) collective-permute-start(bf16[128,2048]{1,0:T(8,128)(2,1)S(1)} %get-tuple-element.249), channel_id=1, source_target_pairs={{0,8},{8,0},{16,24},{24,16},{1,9},{9,1},{17,25},{25,17},{2,10},{10... | collective-permute-start | bytes 1572872 | tf_op jit(solution)/shard_map/ppermute | solution.py:60
  335.0 32.8 %collective-permute-start.39 = (bf16[128,2048]{1,0:T(8,128)(2,1)S(1)}, bf16[128,2048]{1,0:T(8,128)(2,1)}, u32[]{:S(2)}, u32[]{:S(2)}) collective-permute-start(bf16[128,2048]{1,0:T(8,128)(2,1)S(1)} %get-tuple-element.250), channel_id=1, source_target_pairs={{0,16},{8,24},{16,0},{24,8},{1,17},{9,25},{17,1},{25,9},{2,18},{10... | collective-permute-start | bytes 1572872 | tf_op jit(solution)/shard_map/ppermute | solution.py:60
  336.6 31.2 %collective-permute-start.40 = (bf16[128,2048]{1,0:T(8,128)(2,1)}, bf16[128,2048]{1,0:T(8,128)(2,1)}, u32[]{:S(2)}, u32[]{:S(2)}) collective-permute-start(bf16[128,2048]{1,0:T(8,128)(2,1)} %get-tuple-element.251), channel_id=1, source_target_pairs={{0,24},{8,16},{16,8},{24,0},{1,25},{9,17},{17,9},{25,1},{2,26},{10... | collective-permute-start | bytes 1572872 | tf_op jit(solution)/shard_map/ppermute | solution.py:60
  343.4 56.6 %collective-permute-start.46 = (bf16[256,2560]{1,0:T(8,128)(2,1)}, bf16[256,2560]{1,0:T(8,128)(2,1)}, u32[]{:S(2)}, u32[]{:S(2)}) collective-permute-start(bf16[256,2560]{1,0:T(8,128)(2,1)} %get-tuple-element.321), channel_id=1, source_target_pairs={{0,2},{1,3},{2,4},{3,5},{4,6},{5,7},{6,0},{7,1},{8,10},{9,11},{10,... | collective-permute-start | bytes 3932168 | tf_op jit(solution)/shard_map/ppermute | solution.py:55
  343.4 58.9 %collective-permute-start.47 = (bf16[256,2560]{1,0:T(8,128)(2,1)}, bf16[256,2560]{1,0:T(8,128)(2,1)}, u32[]{:S(2)}, u32[]{:S(2)}) collective-permute-start(bf16[256,2560]{1,0:T(8,128)(2,1)} %get-tuple-element.320), channel_id=1, source_target_pairs={{2,0},{3,1},{4,2},{5,3},{6,4},{7,5},{0,6},{1,7},{10,8},{11,9},{12,... | collective-permute-start | bytes 3932168 | tf_op jit(solution)/shard_map/ppermute | solution.py:55
  412.9 37.0 %collective-permute-start.49 = (bf16[3120,512]{1,0:T(8,128)(2,1)S(1)}, bf16[3120,512]{1,0:T(8,128)(2,1)S(1)}, u32[]{:S(2)}, u32[]{:S(2)}) collective-permute-start(bf16[3120,512]{1,0:T(8,128)(2,1)S(1)} %copy-done.60), channel_id=1, source_target_pairs={{0,1},{1,0},{2,3},{3,2},{4,5},{5,4},{6,7},{7,6},{8,9},{9,8},{10,11... | collective-permute-start | bytes 9584648 | tf_op jit(solution)/shard_map/ppermute | solution.py:46
  416.3 31.1 %collective-permute-start.53 = (bf16[256,2560]{1,0:T(8,128)(2,1)S(1)}, bf16[256,2560]{1,0:T(8,128)(2,1)S(1)}, u32[]{:S(2)}, u32[]{:S(2)}) collective-permute-start(bf16[256,2560]{1,0:T(8,128)(2,1)S(1)} %fusion.7.refs_0_), channel_id=1, source_target_pairs={{0,16},{8,24},{16,0},{24,8},{1,17},{9,25},{17,1},{25,9},{2,18},{10... | collective-permute-start | bytes 3932168 | tf_op jit(solution)/shard_map/ppermute | solution.py:60
  417.9 30.9 %collective-permute-start.55 = (bf16[256,2560]{1,0:T(8,128)(2,1)S(1)}, bf16[256,2560]{1,0:T(8,128)(2,1)S(1)}, u32[]{:S(2)}, u32[]{:S(2)}) collective-permute-start(bf16[256,2560]{1,0:T(8,128)(2,1)S(1)} %fusion.7.refs_0_), channel_id=1, source_target_pairs={{0,8},{8,0},{16,24},{24,16},{1,9},{9,1},{17,25},{25,17},{2,10},{10... | collective-permute-start | bytes 3932168 | tf_op jit(solution)/shard_map/ppermute | solution.py:60
  418.7 32.2 %collective-permute-start.50 = (bf16[1040,512]{1,0:T(8,128)(2,1)S(1)}, bf16[1040,512]{1,0:T(8,128)(2,1)S(1)}, u32[]{:S(2)}, u32[]{:S(2)}) collective-permute-start(bf16[1040,512]{1,0:T(8,128)(2,1)S(1)} %add_convert_fusion.4), channel_id=1, source_target_pairs={{0,2},{1,3},{6,4},{7,5},{2,6},{3,7},{4,0},{5,1},{8,10},{9,11},{14,... | collective-permute-start | bytes 3194888 | tf_op jit(solution)/shard_map/ppermute | solution.py:55
  451.3 24.1 %collective-permute-start.52 = (bf16[512,512]{1,0:T(8,128)(2,1)S(1)}, bf16[512,512]{1,0:T(8,128)(2,1)S(1)}, u32[]{:S(2)}, u32[]{:S(2)}) collective-permute-start(bf16[512,512]{1,0:T(8,128)(2,1)S(1)} %get-tuple-element.324), channel_id=1, source_target_pairs={{2,0},{3,1},{4,2},{5,3},{6,4},{7,5},{0,6},{1,7},{10,8},{11,9},{12,... | collective-permute-start | bytes 1572872 | tf_op jit(solution)/shard_map/ppermute | solution.py:55
  479.2 23.9 %collective-permute-start.63 = (bf16[528,512]{1,0:T(8,128)(2,1)S(1)}, bf16[528,512]{1,0:T(8,128)(2,1)S(1)}, u32[]{:S(2)}, u32[]{:S(2)}) collective-permute-start(bf16[528,512]{1,0:T(8,128)(2,1)S(1)} %get-tuple-element.304), channel_id=1, source_target_pairs={{2,0},{3,1},{4,2},{5,3},{6,4},{7,5},{0,6},{1,7},{10,8},{11,9},{12,... | collective-permute-start | bytes 1622024 | tf_op jit(solution)/shard_map/ppermute | solution.py:55
  503.5 26.2 %collective-permute-start.64 = (bf16[528,512]{1,0:T(8,128)(2,1)S(1)}, bf16[528,512]{1,0:T(8,128)(2,1)S(1)}, u32[]{:S(2)}, u32[]{:S(2)}) collective-permute-start(bf16[528,512]{1,0:T(8,128)(2,1)S(1)} %fusion.24.refs_0_.refs_4_.refs_8_), channel_id=1, source_target_pairs={{0,8},{8,0},{16,24},{24,16},{1,9},{9,1},{17,25},{25,17},{2,10},{10... | collective-permute-start | bytes 1622024 | tf_op jit(solution)/shard_map/ppermute | solution.py:60
  504.8 24.9 %collective-permute-start.65 = (bf16[528,512]{1,0:T(8,128)(2,1)S(1)}, bf16[528,512]{1,0:T(8,128)(2,1)S(1)}, u32[]{:S(2)}, u32[]{:S(2)}) collective-permute-start(bf16[528,512]{1,0:T(8,128)(2,1)S(1)} %fusion.24.refs_0_.refs_4_.refs_8_), channel_id=1, source_target_pairs={{0,16},{8,24},{16,0},{24,8},{1,17},{9,25},{17,1},{25,9},{2,18},{10... | collective-permute-start | bytes 1622024 | tf_op jit(solution)/shard_map/ppermute | solution.py:60
  505.3 24.4 %collective-permute-start.66 = (bf16[528,512]{1,0:T(8,128)(2,1)S(1)}, bf16[528,512]{1,0:T(8,128)(2,1)S(1)}, u32[]{:S(2)}, u32[]{:S(2)}) collective-permute-start(bf16[528,512]{1,0:T(8,128)(2,1)S(1)} %fusion.24.refs_0_.refs_4_.refs_8_), channel_id=1, source_target_pairs={{0,24},{8,16},{16,8},{24,0},{1,25},{9,17},{17,9},{25,1},{2,26},{10... | collective-permute-start | bytes 1622024 | tf_op jit(solution)/shard_map/ppermute | solution.py:60
  (96 other events, 1451.0 us)

commit v5 on v4

--- a/solution.py
+++ b/solution.py
@@ -1504,8 +1504,9 @@
     all_low = ctx_gather(low)
     near_sum = add_low(grads_gate_up[0], core_swap(after(grads_gate_up[1], low)))
     result_parts = multiply_down(
-        scal, after(mixed_units, near_sum), down_parts, down_shards, blocks
-    )
+        scal, after(mixed_units, near_sum, share_down), down_parts, down_shards, blocks
+    )
+    near_sum, *result_parts = together([near_sum, *result_parts])
     sends, kept = near_sends(near_sum, far_sum[0] if far_sum else None, chip)
     received = near_receive(sends)
     result_parts = ctx_exchange(together(result_parts, *all_low))
@@ -1541,15 +1542,17 @@
         stride,
     )
     n = len(received)
-    joint = together([*parts, *received, *grads_attn])
-    parts, received, grads_attn = joint[:blocks], joint[blocks : blocks + n], joint[blocks + n :]
+    joint = together([*received, *grads_attn])
+    received, grads_attn = joint[:n], joint[n:]
+    share_gate_up = near_total(received, kept, chip)
+    joint = together([*parts, share_gate_up, *grads_attn])
+    parts, share_gate_up, grads_attn = joint[:blocks], joint[blocks], joint[blocks + 1 :]
     input_grad = attn_norm_back(scal, grad_hidden, gains, own_tokens, parts, shards)
     far_sum, far_add = [], grads_attn[0]
     if len(grads_attn) == 4:
         far_add = add_low(grads_attn[2], core_swap(grads_attn[3]))
         far_sum = [reduce_far(far_add)]
     near_sum = add_low(grads_attn[0], core_swap(after(grads_attn[1], far_add)))
-    share_gate_up = near_total(received, kept, chip)
     near_units = ctx_gather_near(after(share_gate_up, far_add))
     near_sum, *far_sum = together([near_sum, *far_sum])
     far_sum = far_sum[0] if far_sum else None

time: 546 us -> 542 us (level)
    ppermute x20, waiting for transfers between devices: 61.7 us -> 70.4 us  [chip_send(): lax.ppermute(a, 'fsdp', [(2 * s + k, 2 * d + k) for s, d in pairs for k i...]
    unnamed x124 -> x130, local copies, waits for them, and re-layouts: 16.7 us -> 16.7 us
  transfers between devices with their start and end apart: 67 -> 67, of which waited for: 40 -> 38; matrix products, arithmetic and copies ran while one was open for 4% -> 4% of each run, Pallas kernels for 29% -> 29%
where the time goes in v5:
time: 542 us; the launch traced here: 533 us
  waiting for transfers between devices  239 us (44%)
  Pallas kernels  164 us (30%)
  starting transfers between devices  76 us (14%)
  other arithmetic  23.2 us (4%)
  local copies, waits for them, and re-layouts  20.8 us (4%)
  blocking collectives  7.24 us (1%)
    pallas_call x23, Pallas kernels, call(): pl.pallas_call(kernel, grid=grid, in_specs=in_specs, out_specs=out_specs,...  164 us
    ppermute x35, waiting for transfers between devices, ctx_send(): return lax.ppermute(a, 'ctx', [(i, i ^ distance) for i in range(size)])  158 us
    ppermute x20, waiting for transfers between devices, chip_send(): lax.ppermute(a, 'fsdp', [(2 * s + k, 2 * d + k) for s, d in pairs for k i...  70.4 us
    ppermute x35, starting transfers between devices, ctx_send(): return lax.ppermute(a, 'ctx', [(i, i ^ distance) for i in range(size)])  40 us
    ppermute x20, starting transfers between devices, chip_send(): lax.ppermute(a, 'fsdp', [(2 * s + k, 2 * d + k) for s, d in pairs for k i...  34.4 us
    unnamed x130, local copies, waits for them, and re-layouts  16.7 us
  transfers between devices with their start and end apart: 67, of which 38 were waited for; matrix products, arithmetic and copies ran while one was open for 4% of the time, Pallas kernels for 29%

profile of v5, /device:TPU:0, one launch (start us, length us, event | category | flops | bytes accessed | tf_op | source)
XLA Modules:
  0.0 532.5 jit_solution(389256606807240246)
XLA Ops:
  8.6 5.0 collective-permute-start
  23.4 18.4 %collective-permute-done.2.refs_1_ = bf16[256,2048]{1,0:T(8,128)(2,1)} collective-permute-done((bf16[256,2048]{1,0:T(8,128)(2,1)}, bf16[256,2048]{1,0:T(8,128)(2,1)}, u32[]{:S(2)}, u32[]{:S(2)}) %collective-permute-start.2) | collective-permute-done | bytes 1048608 | tf_op jit(solution)/shard_map/ppermute | solution.py:60
  41.7 22.2 %collective-permute-done.3.refs_2_ = bf16[256,2048]{1,0:T(8,128)(2,1)} collective-permute-done((bf16[256,2048]{1,0:T(8,128)(2,1)}, bf16[256,2048]{1,0:T(8,128)(2,1)}, u32[]{:S(2)}, u32[]{:S(2)}) %collective-permute-start.3) | collective-permute-done | bytes 1048608 | tf_op jit(solution)/shard_map/ppermute | solution.py:60
  70.0 21.9 %collective-permute-done.8.refs_10_.refs_6_ = bf16[1040,512]{1,0:T(8,128)(2,1)S(1)} collective-permute-done((bf16[1040,512]{1,0:T(8,128)(2,1)S(1)}, bf16[1040,512]{1,0:T(8,128)(2,1)S(1)}, u32[]{:S(2)}, u32[]{:S(2)}) %collective-permute-start.8) | collective-permute-done | bytes 1064992 | tf_op jit(solution)/shard_map/ppermute | solution.py:55
  96.6 9.9 %shard_map.241 = (bf16[512,2048]{1,0:T(8,128)(2,1)}, bf16[512,1536]{1,0:T(8,128)(2,1)}, f32[4,2,1024]{2,1,0:T(2,128)S(1)}, f32[2,2048]{1,0:T(2,128)S(1)}, f32[512,128]{1,0:T(8,128)S(1)}) custom-call(s32[10]{0:T(128)S(1)} %compare_select_fusion.3.scal, bf16[256,2048]{1,0:T(8,128)(2,1)S(1)} %copy-done.2, bf16[256,2048]{1,0:T(8,128)(2,1)} %collective-permute-done.2.refs_1_, ...), custom_call_target="tpu_custom_call" | custom-call | flops 1 | bytes 1 | tf_op jit(solution)/shard_map/pallas_call | solution.py:192
  106.5 12.0 %shard_map.242 = (bf16[512,512]{1,0:T(8,128)(2,1)S(1)}, bf16[8,512,512]{2,1,0:T(8,128)(2,1)}) custom-call(s32[10]{0:T(128)S(1)} %compare_select_fusion.3.scal, bf16[512,1536]{1,0:T(8,128)(2,1)} %get-tuple-element.190.q_ref.k_ref.v_ref, bf16[512,1536]{1,0:T(8,128)(2,1)} %get-tuple-element.190.q_ref.k_ref.v_ref, ...), custom_call_target="tpu_custom_call" | custom-call | flops 1 | bytes 1 | tf_op jit(solution)/shard_map/pallas_call | solution.py:192
  119.3 5.0 shard_map.243
  127.8 11.3 %collective-permute-done.10.refs_1_ = bf16[128,2048]{1,0:T(8,128)(2,1)S(1)} collective-permute-done((bf16[128,2048]{1,0:T(8,128)(2,1)S(1)}, bf16[128,2048]{1,0:T(8,128)(2,1)S(1)}, u32[]{:S(2)}, u32[]{:S(2)}) %collective-permute-start.10) | collective-permute-done | bytes 524320 | tf_op jit(solution)/shard_map/ppermute | solution.py:60
  139.8 10.7 %collective-permute-done.12.refs_3_ = bf16[128,2048]{1,0:T(8,128)(2,1)S(1)} collective-permute-done((bf16[128,2048]{1,0:T(8,128)(2,1)}, bf16[128,2048]{1,0:T(8,128)(2,1)S(1)}, u32[]{:S(2)}, u32[]{:S(2)}) %collective-permute-start.12) | collective-permute-done | bytes 524320 | tf_op jit(solution)/shard_map/ppermute | solution.py:60
  163.4 11.3 %collective-permute-done.16.refs_1_ = bf16[128,2048]{1,0:T(8,128)(2,1)S(1)} collective-permute-done((bf16[128,2048]{1,0:T(8,128)(2,1)S(1)}, bf16[128,2048]{1,0:T(8,128)(2,1)S(1)}, u32[]{:S(2)}, u32[]{:S(2)}) %collective-permute-start.16) | collective-permute-done | bytes 524320 | tf_op jit(solution)/shard_map/ppermute | solution.py:60
  174.6 10.2 %collective-permute-done.17.refs_2_ = bf16[128,2048]{1,0:T(8,128)(2,1)S(1)} collective-permute-done((bf16[128,2048]{1,0:T(8,128)(2,1)S(1)}, bf16[128,2048]{1,0:T(8,128)(2,1)S(1)}, u32[]{:S(2)}, u32[]{:S(2)}) %collective-permute-start.17) | collective-permute-done | bytes 524320 | tf_op jit(solution)/shard_map/ppermute | solution.py:60
  197.5 10.9 %shard_map.245 = (bf16[512,2048]{1,0:T(8,128)(2,1)}, f32[512,1280]{1,0:T(8,128)}, f32[512,1280]{1,0:T(8,128)}, bf16[512,1280]{1,0:T(8,128)(2,1)}) custom-call(bf16[128,2048]{1,0:T(8,128)(2,1)S(1)} %copy-done.22, bf16[128,2048]{1,0:T(8,128)(2,1)S(1)} %collective-permute-done.16.refs_1_, bf16[128,2048]{1,0:T(8,128)(2,1)S(1)} %copy-done.24, ...), custom_call_target="tpu_custom_call" | custom-call | flops 1 | bytes 1 | tf_op jit(solution)/shard_map/pallas_call | solution.py:192
  208.5 7.4 %shard_map.246 = (bf16[640,2048]{1,0:T(8,128)(2,1)}, bf16[640,2048]{1,0:T(8,128)(2,1)}) custom-call(s32[10]{0:T(128)S(1)} %compare_select_fusion.3.scal, bf16[512,1280]{1,0:T(8,128)(2,1)} %get-tuple-element.251.mixed, bf16[256,2048]{1,0:T(8,128)(2,1)S(1)} %copy-done.3, bf16[256,2048]{1,0:T(8,128)(2,1)} %collective-permute-done.2.refs_1_, ...), custom_call_target="tpu_custom_call" | custom-call | flops 1 | bytes 1 | tf_op jit(solution)/shard_map/pallas_call | solution.py:192
  215.8 9.0 %collective-permute-done.21 = bf16[160,2048]{1,0:T(8,128)(2,1)S(1)} collective-permute-done((bf16[160,2048]{1,0:T(8,128)(2,1)S(1)}, bf16[160,2048]{1,0:T(8,128)(2,1)S(1)}, u32[]{:S(2)}, u32[]{:S(2)}) %collective-permute-start.21) | collective-permute-done | bytes 655392 | tf_op jit(solution)/shard_map/ppermute | solution.py:55
  231.0 11.7 %collective-permute-done.25.refs_6_.refs_2_ = bf16[160,2048]{1,0:T(8,128)(2,1)S(1)} collective-permute-done((bf16[160,2048]{1,0:T(8,128)(2,1)S(1)}, bf16[160,2048]{1,0:T(8,128)(2,1)S(1)}, u32[]{:S(2)}, u32[]{:S(2)}) %collective-permute-start.25) | collective-permute-done | bytes 655392 | tf_op jit(solution)/shard_map/ppermute | solution.py:55
  244.9 11.2 %shard_map.247.g = bf16[512,2560]{1,0:T(8,128)(2,1)} custom-call(s32[10]{0:T(128)S(1)} %compare_select_fusion.3.scal, f32[512,1280]{1,0:T(8,128)} %get-tuple-element.222.gate, f32[512,1280]{1,0:T(8,128)} %get-tuple-element.223.up, bf16[256,2048]{1,0:T(8,128)(2,1)} %shard_map.239.refs_0_.own, bf16[256,2048]{1,0:T(8,128)(2,1)} %collective-permute-done.2.refs_1_, ...), custom_call_target="tpu_custom_call" | custom-call | flops 1 | bytes 1 | tf_op jit(solution)/shard_map/pallas_call | solution.py:192
  256.1 4.8 collective-permute-done.26
  265.2 12.7 %shard_map.248 = (bf16[128,2048]{1,0:T(8,128)(2,1)S(1)}, bf16[128,2048]{1,0:T(8,128)(2,1)S(1)}, bf16[128,2048]{1,0:T(8,128)(2,1)S(1)}, bf16[128,2048]{1,0:T(8,128)(2,1)}) custom-call(bf16[512,2560]{1,0:T(8,128)(2,1)} %shard_map.247.g, bf16[768,2560]{1,0:T(8,128)(2,1)} %copy-done.28, bf16[768,2560]{1,0:T(8,128)(2,1)} %copy-done.34, ...), custom_call_target="tpu_custom_call" | custom-call | flops 1 | bytes 1 | tf_op jit(solution)/shard_map/pallas_call | solution.py:192
  281.5 10.4 %shard_map.249 = (bf16[768,2560]{1,0:T(8,128)(2,1)}, bf16[768,2560]{1,0:T(8,128)(2,1)}, bf16[512,2560]{1,0:T(8,128)(2,1)}) custom-call(s32[10]{0:T(128)S(1)} %compare_select_fusion.3.scal, bf16[512,2048]{1,0:T(8,128)(2,1)} %get-tuple-element.230.normed, bf16[512,2560]{1,0:T(8,128)(2,1)} %shard_map.247.g), custom_call_target="tpu_custom_call" | custom-call | flops 1 | bytes 1 | tf_op jit(solution)/shard_map/pallas_call | solution.py:192
  292.5 7.2 %all_to_all.9 = bf16[2,256,2560]{2,1,0:T(8,128)(2,1)S(1)} all-to-all(bf16[2,256,2560]{2,1,0:T(8,128)(2,1)} %bitcast.15), channel_id=1, replica_groups={{0,1},{2,3},{4,5},{6,7},{8,9},{10,11},{12,13},{14,15},{16,17},{18,19},{..., dimensions={0} | all-to-all | bytes 5242880 | tf_op jit(solution)/shard_map/all_to_all | solution.py:51
  318.9 7.5 %shard_map.251 = (bf16[128,2048]{1,0:T(8,128)(2,1)S(1)}, bf16[128,2048]{1,0:T(8,128)(2,1)S(1)}, bf16[128,2048]{1,0:T(8,128)(2,1)S(1)}, bf16[128,2048]{1,0:T(8,128)(2,1)}) custom-call(s32[10]{0:T(128)S(1)} %compare_select_fusion.3.scal, bf16[512,1280]{1,0:T(8,128)(2,1)} %get-tuple-element.251.mixed, bf16[480,2048]{1,0:T(8,128)(2,1)} %copy-done.35, ...), custom_call_target="tpu_custom_call" | custom-call | flops 1 | bytes 1 | tf_op jit(solution)/shard_map/pallas_call | solution.py:192
  326.5 13.3 %collective-permute-done.34 = bf16[256,2560]{1,0:T(8,128)(2,1)S(1)} collective-permute-done((bf16[256,2560]{1,0:T(8,128)(2,1)}, bf16[256,2560]{1,0:T(8,128)(2,1)S(1)}, u32[]{:S(2)}, u32[]{:S(2)}) %collective-permute-start.34) | collective-permute-done | bytes 1310752 | tf_op jit(solution)/shard_map/ppermute | solution.py:55
  354.4 11.6 %shard_map.253 = (bf16[512,512]{1,0:T(8,128)(2,1)S(1)}, bf16[512,512]{1,0:T(8,128)(2,1)S(1)}, bf16[512,512]{1,0:T(8,128)(2,1)S(1)}, f32[4,2,1024]{2,1,0:T(2,128)S(1)}) custom-call(s32[10]{0:T(128)S(1)} %compare_select_fusion.3.scal, bf16[512,1536]{1,0:T(8,128)(2,1)} %get-tuple-element.190.q_ref.k_ref.v_ref, ...), custom_call_target="tpu_custom_call" | custom-call | flops 1 | bytes 1 | tf_op jit(solution)/shard_map/pallas_call | solution.py:192
  373.6 10.0 %shard_map.254 = (bf16[128,2048]{1,0:T(8,128)(2,1)S(1)}, bf16[128,2048]{1,0:T(8,128)(2,1)S(1)}, bf16[128,2048]{1,0:T(8,128)(2,1)S(1)}, bf16[128,2048]{1,0:T(8,128)(2,1)}, f32[1,2048]{1,0:T(1,128)S(1)}) custom-call(f32[512,128]{1,0:T(8,128)S(1)} %get-tuple-element.274.scales, bf16[512,512]{1,0:T(8,128)(2,1)} %copy-done.8, bf16[512,512]{1,0:T(8,128)(2,1)} %copy-done.10, ...), custom_call_target="tpu_custom_call" | custom-call | flops 1 | bytes 1 | tf_op jit(solution)/shard_map/pallas_call | solution.py:192
  390.2 11.9 %shard_map.255 = (bf16[3120,512]{1,0:T(8,128)(2,1)}, bf16[3120,512]{1,0:T(8,128)(2,1)}, bf16[1040,512]{1,0:T(8,128)(2,1)}, bf16[1040,512]{1,0:T(8,128)(2,1)}) custom-call(s32[10]{0:T(128)S(1)} %compare_select_fusion.3.scal, bf16[512,2048]{1,0:T(8,128)(2,1)} %get-tuple-element.287.normed, bf16[512,512]{1,0:T(8,128)(2,1)S(1)} %copy-done.14, ...), custom_call_target="tpu_custom_call" | custom-call | flops 1 | bytes 1 | tf_op jit(solution)/shard_map/pallas_call | solution.py:192
  405.3 4.7 collective-permute-done.44.refs_2_
  415.3 29.0 %collective-permute-done.53.refs_2_ = bf16[256,2560]{1,0:T(8,128)(2,1)S(1)} collective-permute-done((bf16[256,2560]{1,0:T(8,128)(2,1)S(1)}, bf16[256,2560]{1,0:T(8,128)(2,1)S(1)}, u32[]{:S(2)}, u32[]{:S(2)}) %collective-permute-start.53) | collective-permute-done | bytes 1310752 | tf_op jit(solution)/shard_map/ppermute | solution.py:60
  451.5 9.1 %collective-permute-done.54 = bf16[128,2560]{1,0:T(8,128)(2,1)S(1)} collective-permute-done((bf16[128,2560]{1,0:T(8,128)(2,1)S(1)}, bf16[128,2560]{1,0:T(8,128)(2,1)S(1)}, u32[]{:S(2)}, u32[]{:S(2)}) %collective-permute-start.54) | collective-permute-done | bytes 655392 | tf_op jit(solution)/shard_map/ppermute | solution.py:60
  463.6 5.7 %collective-permute-done.57 = bf16[80,2048]{1,0:T(8,128)(2,1)S(1)} collective-permute-done((bf16[80,2048]{1,0:T(8,128)(2,1)S(1)}, bf16[80,2048]{1,0:T(8,128)(2,1)S(1)}, u32[]{:S(2)}, u32[]{:S(2)}) %collective-permute-start.57) | collective-permute-done | bytes 327712 | tf_op jit(solution)/shard_map/ppermute | solution.py:60
  480.7 6.3 %collective-permute-done.59.refs_2_.refs_3_ = bf16[512,512]{1,0:T(8,128)(2,1)S(1)} collective-permute-done((bf16[512,512]{1,0:T(8,128)(2,1)S(1)}, bf16[512,512]{1,0:T(8,128)(2,1)S(1)}, u32[]{:S(2)}, u32[]{:S(2)}) %collective-permute-start.59) | collective-permute-done | bytes 524320 | tf_op jit(solution)/shard_map/ppermute | solution.py:60
  487.0 8.9 %collective-permute-done.60.refs_4_.refs_5_ = bf16[512,512]{1,0:T(8,128)(2,1)S(1)} collective-permute-done((bf16[512,512]{1,0:T(8,128)(2,1)S(1)}, bf16[512,512]{1,0:T(8,128)(2,1)S(1)}, u32[]{:S(2)}, u32[]{:S(2)}) %collective-permute-start.60) | collective-permute-done | bytes 524320 | tf_op jit(solution)/shard_map/ppermute | solution.py:60
  508.7 8.8 %shard_map.259 = (f32[256,5120]{1,0:T(8,128)}, f32[256,5120]{1,0:T(8,128)}) custom-call(s32[10]{0:T(128)S(1)} %compare_select_fusion.3.scal, bf16[256,2560]{1,0:T(8,128)(2,1)S(1)} %fusion.7.refs_0_, bf16[256,2560]{1,0:T(8,128)(2,1)} %copy-done.43, bf16[256,2560]{1,0:T(8,128)(2,1)} %copy-done.42, bf16[256,2560]{1,0:T(8,128)(2,1)} %pad_maximum_fusion.refs_3_), custom_call_target="tpu_custom_call" | custom-call | flops 1 | bytes 1 | tf_op jit(solution)/shard_map/pallas_call | solution.py:192
  (288 shorter events, 180.1 us)
Async XLA Ops:
  8.6 55.3 %collective-permute-start = (bf16[1040,512]{1,0:T(8,128)(2,1)}, bf16[1040,512]{1,0:T(8,128)(2,1)}, u32[]{:S(2)}, u32[]{:S(2)}) collective-permute-start(bf16[1040,512]{1,0:T(8,128)(2,1)} %shard_map.238.refs_4_.refs_0_), channel_id=1, source_target_pairs={{2,0},{3,1},{4,2},{5,3},{6,4},{7,5},{0,6},{1,7},{10,8},{11,9},{12,... | collective-permute-start | bytes 3194888 | tf_op jit(solution)/shard_map/ppermute | solution.py:55
  13.7 50.3 %collective-permute-start.1 = (bf16[1040,512]{1,0:T(8,128)(2,1)}, bf16[1040,512]{1,0:T(8,128)(2,1)}, u32[]{:S(2)}, u32[]{:S(2)}) collective-permute-start(bf16[1040,512]{1,0:T(8,128)(2,1)} %shard_map.238.refs_4_.refs_0_), channel_id=1, source_target_pairs={{0,2},{1,3},{2,4},{3,5},{4,6},{5,7},{6,0},{7,1},{8,10},{9,11},{10,... | collective-permute-start | bytes 3194888 | tf_op jit(solution)/shard_map/ppermute | solution.py:55
  15.3 26.4 %collective-permute-start.2 = (bf16[256,2048]{1,0:T(8,128)(2,1)}, bf16[256,2048]{1,0:T(8,128)(2,1)}, u32[]{:S(2)}, u32[]{:S(2)}) collective-permute-start(bf16[256,2048]{1,0:T(8,128)(2,1)} %shard_map.239.refs_0_.own), channel_id=1, source_target_pairs={{0,8},{8,0},{16,24},{24,16},{1,9},{9,1},{17,25},{25,17},{2,10},{10... | collective-permute-start | bytes 3145736 | tf_op jit(solution)/shard_map/ppermute | solution.py:60
  16.8 47.1 %collective-permute-start.3 = (bf16[256,2048]{1,0:T(8,128)(2,1)}, bf16[256,2048]{1,0:T(8,128)(2,1)}, u32[]{:S(2)}, u32[]{:S(2)}) collective-permute-start(bf16[256,2048]{1,0:T(8,128)(2,1)} %shard_map.239.refs_0_.own), channel_id=1, source_target_pairs={{0,16},{8,24},{16,0},{24,8},{1,17},{9,25},{17,1},{25,9},{2,18},{10... | collective-permute-start | bytes 3145736 | tf_op jit(solution)/shard_map/ppermute | solution.py:60
  18.4 45.6 %collective-permute-start.4 = (bf16[256,2048]{1,0:T(8,128)(2,1)}, bf16[256,2048]{1,0:T(8,128)(2,1)}, u32[]{:S(2)}, u32[]{:S(2)}) collective-permute-start(bf16[256,2048]{1,0:T(8,128)(2,1)} %shard_map.239.refs_0_.own), channel_id=1, source_target_pairs={{0,24},{8,16},{16,8},{24,0},{1,25},{9,17},{17,9},{25,1},{2,26},{10... | collective-permute-start | bytes 3145736 | tf_op jit(solution)/shard_map/ppermute | solution.py:60
  66.0 25.9 %collective-permute-start.8 = (bf16[1040,512]{1,0:T(8,128)(2,1)S(1)}, bf16[1040,512]{1,0:T(8,128)(2,1)S(1)}, u32[]{:S(2)}, u32[]{:S(2)}) collective-permute-start(bf16[1040,512]{1,0:T(8,128)(2,1)S(1)} %select_select_fusion.1), channel_id=1, source_target_pairs={{6,2},{7,3},{0,4},{1,5},{2,0},{3,1},{4,6},{5,7},{14,10},{15,11},{8... | collective-permute-start | bytes 3194888 | tf_op jit(solution)/shard_map/ppermute | solution.py:55
  91.9 62.1 %collective-permute-start.13 = (bf16[256,2560]{1,0:T(8,128)(2,1)S(1)}, bf16[256,2560]{1,0:T(8,128)(2,1)}, u32[]{:S(2)}, u32[]{:S(2)}) collective-permute-start(bf16[256,2560]{1,0:T(8,128)(2,1)S(1)} %copy-done.5), channel_id=1, source_target_pairs={{2,0},{3,1},{4,2},{5,3},{6,4},{7,5},{0,6},{1,7},{10,8},{11,9},{12,... | collective-permute-start | bytes 3932168 | tf_op jit(solution)/shard_map/ppermute | solution.py:55
  95.5 58.5 %collective-permute-start.14 = (bf16[256,2560]{1,0:T(8,128)(2,1)S(1)}, bf16[256,2560]{1,0:T(8,128)(2,1)}, u32[]{:S(2)}, u32[]{:S(2)}) collective-permute-start(bf16[256,2560]{1,0:T(8,128)(2,1)S(1)} %copy-done.5), channel_id=1, source_target_pairs={{0,2},{1,3},{2,4},{3,5},{4,6},{5,7},{6,0},{7,1},{8,10},{9,11},{10,... | collective-permute-start | bytes 3932168 | tf_op jit(solution)/shard_map/ppermute | solution.py:55
  126.4 24.2 %collective-permute-start.12 = (bf16[128,2048]{1,0:T(8,128)(2,1)}, bf16[128,2048]{1,0:T(8,128)(2,1)S(1)}, u32[]{:S(2)}, u32[]{:S(2)}) collective-permute-start(bf16[128,2048]{1,0:T(8,128)(2,1)} %get-tuple-element.196), channel_id=1, source_target_pairs={{0,24},{8,16},{16,8},{24,0},{1,25},{9,17},{17,9},{25,1},{2,26},{10... | collective-permute-start | bytes 1572872 | tf_op jit(solution)/shard_map/ppermute | solution.py:60
  157.6 32.5 %collective-permute-start.15 = (bf16[768,2560]{1,0:T(8,128)(2,1)S(1)}, bf16[768,2560]{1,0:T(8,128)(2,1)S(1)}, u32[]{:S(2)}, u32[]{:S(2)}) collective-permute-start(bf16[768,2560]{1,0:T(8,128)(2,1)S(1)} %constant_dynamic-update-slice_fusion.refs_4_.refs_0_), channel_id=1, source_target_pairs={{0,1},{1,0},{2,3},{3,2},{4,5},{5,4},{6,7},{7,6},{8,9},{9,8},{10,11... | collective-permute-start | bytes 11796488 | tf_op jit(solution)/shard_map/ppermute | solution.py:46
  157.7 32.4 %collective-permute-start.19 = (bf16[256,2560]{1,0:T(8,128)(2,1)S(1)}, bf16[256,2560]{1,0:T(8,128)(2,1)}, u32[]{:S(2)}, u32[]{:S(2)}) collective-permute-start(bf16[256,2560]{1,0:T(8,128)(2,1)S(1)} %get-tuple-element.348), channel_id=1, source_target_pairs={{6,2},{7,3},{0,4},{1,5},{2,0},{3,1},{4,6},{5,7},{14,10},{15,11},{8... | collective-permute-start | bytes 3932168 | tf_op jit(solution)/shard_map/ppermute | solution.py:55
  161.0 23.8 %collective-permute-start.17 = (bf16[128,2048]{1,0:T(8,128)(2,1)S(1)}, bf16[128,2048]{1,0:T(8,128)(2,1)S(1)}, u32[]{:S(2)}, u32[]{:S(2)}) collective-permute-start(bf16[128,2048]{1,0:T(8,128)(2,1)S(1)} %get-tuple-element.204.refs_0_), channel_id=1, source_target_pairs={{0,16},{8,24},{16,0},{24,8},{1,17},{9,25},{17,1},{25,9},{2,18},{10... | collective-permute-start | bytes 1572872 | tf_op jit(solution)/shard_map/ppermute | solution.py:60
  162.4 23.7 %collective-permute-start.18 = (bf16[128,2048]{1,0:T(8,128)(2,1)S(1)}, bf16[128,2048]{1,0:T(8,128)(2,1)S(1)}, u32[]{:S(2)}, u32[]{:S(2)}) collective-permute-start(bf16[128,2048]{1,0:T(8,128)(2,1)S(1)} %get-tuple-element.204.refs_0_), channel_id=1, source_target_pairs={{0,24},{8,16},{16,8},{24,0},{1,25},{9,17},{17,9},{25,1},{2,26},{10... | collective-permute-start | bytes 1572872 | tf_op jit(solution)/shard_map/ppermute | solution.py:60
  192.1 23.7 %collective-permute-start.20 = (bf16[160,2048]{1,0:T(8,128)(2,1)S(1)}, bf16[160,2048]{1,0:T(8,128)(2,1)S(1)}, u32[]{:S(2)}, u32[]{:S(2)}) collective-permute-start(bf16[160,2048]{1,0:T(8,128)(2,1)S(1)} %constant_dynamic-slice_fusion), channel_id=1, source_target_pairs={{2,0},{3,1},{4,2},{5,3},{6,4},{7,5},{0,6},{1,7},{10,8},{11,9},{12,... | collective-permute-start | bytes 1966088 | tf_op jit(solution)/shard_map/ppermute | solution.py:55
  194.6 30.2 %collective-permute-start.21 = (bf16[160,2048]{1,0:T(8,128)(2,1)S(1)}, bf16[160,2048]{1,0:T(8,128)(2,1)S(1)}, u32[]{:S(2)}, u32[]{:S(2)}) collective-permute-start(bf16[160,2048]{1,0:T(8,128)(2,1)S(1)} %constant_dynamic-slice_fusion), channel_id=1, source_target_pairs={{0,2},{1,3},{2,4},{3,5},{4,6},{5,7},{6,0},{7,1},{8,10},{9,11},{10,... | collective-permute-start | bytes 1966088 | tf_op jit(solution)/shard_map/ppermute | solution.py:55
  261.3 30.5 %collective-permute-start.28 = (bf16[160,2048]{1,0:T(8,128)(2,1)S(1)}, bf16[160,2048]{1,0:T(8,128)(2,1)S(1)}, u32[]{:S(2)}, u32[]{:S(2)}) collective-permute-start(bf16[160,2048]{1,0:T(8,128)(2,1)S(1)} %get-tuple-element.228), channel_id=1, source_target_pairs={{0,2},{1,3},{2,4},{3,5},{4,6},{5,7},{6,0},{7,1},{8,10},{9,11},{10,... | collective-permute-start | bytes 1966088 | tf_op jit(solution)/shard_map/ppermute | solution.py:55
  262.5 30.1 %collective-permute-start.29 = (bf16[160,2048]{1,0:T(8,128)(2,1)S(1)}, bf16[160,2048]{1,0:T(8,128)(2,1)S(1)}, u32[]{:S(2)}, u32[]{:S(2)}) collective-permute-start(bf16[160,2048]{1,0:T(8,128)(2,1)S(1)} %get-tuple-element.229), channel_id=1, source_target_pairs={{2,0},{3,1},{4,2},{5,3},{6,4},{7,5},{0,6},{1,7},{10,8},{11,9},{12,... | collective-permute-start | bytes 1966088 | tf_op jit(solution)/shard_map/ppermute | solution.py:55
  307.5 32.3 %collective-permute-start.34 = (bf16[256,2560]{1,0:T(8,128)(2,1)}, bf16[256,2560]{1,0:T(8,128)(2,1)S(1)}, u32[]{:S(2)}, u32[]{:S(2)}) collective-permute-start(bf16[256,2560]{1,0:T(8,128)(2,1)} %fusion.16), channel_id=1, source_target_pairs={{0,2},{1,3},{6,4},{7,5},{2,6},{3,7},{4,0},{5,1},{8,10},{9,11},{14,... | collective-permute-start | bytes 3932168 | tf_op jit(solution)/shard_map/ppermute | solution.py:55
  307.5 38.3 %collective-permute-start.35 = (bf16[128,2048]{1,0:T(8,128)(2,1)S(1)}, bf16[128,2048]{1,0:T(8,128)(2,1)S(1)}, u32[]{:S(2)}, u32[]{:S(2)}) collective-permute-start(bf16[128,2048]{1,0:T(8,128)(2,1)S(1)} %get-tuple-element.247.refs_0_), channel_id=1, source_target_pairs={{0,8},{8,0},{16,24},{24,16},{1,9},{9,1},{17,25},{25,17},{2,10},{10... | collective-permute-start | bytes 1572872 | tf_op jit(solution)/shard_map/ppermute | solution.py:60
  308.8 37.0 %collective-permute-start.36 = (bf16[128,2048]{1,0:T(8,128)(2,1)S(1)}, bf16[128,2048]{1,0:T(8,128)(2,1)S(1)}, u32[]{:S(2)}, u32[]{:S(2)}) collective-permute-start(bf16[128,2048]{1,0:T(8,128)(2,1)S(1)} %get-tuple-element.247.refs_0_), channel_id=1, source_target_pairs={{0,16},{8,24},{16,0},{24,8},{1,17},{9,25},{17,1},{25,9},{2,18},{10... | collective-permute-start | bytes 1572872 | tf_op jit(solution)/shard_map/ppermute | solution.py:60
  310.0 35.8 %collective-permute-start.37 = (bf16[128,2048]{1,0:T(8,128)(2,1)S(1)}, bf16[128,2048]{1,0:T(8,128)(2,1)S(1)}, u32[]{:S(2)}, u32[]{:S(2)}) collective-permute-start(bf16[128,2048]{1,0:T(8,128)(2,1)S(1)} %get-tuple-element.247.refs_0_), channel_id=1, source_target_pairs={{0,24},{8,16},{16,8},{24,0},{1,25},{9,17},{17,9},{25,1},{2,26},{10... | collective-permute-start | bytes 1572872 | tf_op jit(solution)/shard_map/ppermute | solution.py:60
  342.0 60.2 %collective-permute-start.46 = (bf16[256,2560]{1,0:T(8,128)(2,1)}, bf16[256,2560]{1,0:T(8,128)(2,1)}, u32[]{:S(2)}, u32[]{:S(2)}) collective-permute-start(bf16[256,2560]{1,0:T(8,128)(2,1)} %get-tuple-element.341), channel_id=1, source_target_pairs={{0,2},{1,3},{2,4},{3,5},{4,6},{5,7},{6,0},{7,1},{8,10},{9,11},{10,... | collective-permute-start | bytes 3932168 | tf_op jit(solution)/shard_map/ppermute | solution.py:55
  342.0 60.2 %collective-permute-start.47 = (bf16[256,2560]{1,0:T(8,128)(2,1)}, bf16[256,2560]{1,0:T(8,128)(2,1)}, u32[]{:S(2)}, u32[]{:S(2)}) collective-permute-start(bf16[256,2560]{1,0:T(8,128)(2,1)} %get-tuple-element.340), channel_id=1, source_target_pairs={{2,0},{3,1},{4,2},{5,3},{6,4},{7,5},{0,6},{1,7},{10,8},{11,9},{12,... | collective-permute-start | bytes 3932168 | tf_op jit(solution)/shard_map/ppermute | solution.py:55
  413.0 33.3 %collective-permute-start.49 = (bf16[3120,512]{1,0:T(8,128)(2,1)S(1)}, bf16[3120,512]{1,0:T(8,128)(2,1)S(1)}, u32[]{:S(2)}, u32[]{:S(2)}) collective-permute-start(bf16[3120,512]{1,0:T(8,128)(2,1)S(1)} %copy-done.61), channel_id=1, source_target_pairs={{0,1},{1,0},{2,3},{3,2},{4,5},{5,4},{6,7},{7,6},{8,9},{9,8},{10,11... | collective-permute-start | bytes 9584648 | tf_op jit(solution)/shard_map/ppermute | solution.py:46
  413.2 31.1 %collective-permute-start.53 = (bf16[256,2560]{1,0:T(8,128)(2,1)S(1)}, bf16[256,2560]{1,0:T(8,128)(2,1)S(1)}, u32[]{:S(2)}, u32[]{:S(2)}) collective-permute-start(bf16[256,2560]{1,0:T(8,128)(2,1)S(1)} %fusion.7.refs_0_), channel_id=1, source_target_pairs={{0,16},{8,24},{16,0},{24,8},{1,17},{9,25},{17,1},{25,9},{2,18},{10... | collective-permute-start | bytes 3932168 | tf_op jit(solution)/shard_map/ppermute | solution.py:60
  413.8 31.3 %collective-permute-start.55 = (bf16[256,2560]{1,0:T(8,128)(2,1)S(1)}, bf16[256,2560]{1,0:T(8,128)(2,1)S(1)}, u32[]{:S(2)}, u32[]{:S(2)}) collective-permute-start(bf16[256,2560]{1,0:T(8,128)(2,1)S(1)} %fusion.7.refs_0_), channel_id=1, source_target_pairs={{0,8},{8,0},{16,24},{24,16},{1,9},{9,1},{17,25},{25,17},{2,10},{10... | collective-permute-start | bytes 3932168 | tf_op jit(solution)/shard_map/ppermute | solution.py:60
  415.1 32.2 %collective-permute-start.50 = (bf16[1040,512]{1,0:T(8,128)(2,1)S(1)}, bf16[1040,512]{1,0:T(8,128)(2,1)S(1)}, u32[]{:S(2)}, u32[]{:S(2)}) collective-permute-start(bf16[1040,512]{1,0:T(8,128)(2,1)S(1)} %add_convert_fusion.4), channel_id=1, source_target_pairs={{0,2},{1,3},{6,4},{7,5},{2,6},{3,7},{4,0},{5,1},{8,10},{9,11},{14,... | collective-permute-start | bytes 3194888 | tf_op jit(solution)/shard_map/ppermute | solution.py:55
  447.7 24.1 %collective-permute-start.52 = (bf16[512,512]{1,0:T(8,128)(2,1)S(1)}, bf16[512,512]{1,0:T(8,128)(2,1)S(1)}, u32[]{:S(2)}, u32[]{:S(2)}) collective-permute-start(bf16[512,512]{1,0:T(8,128)(2,1)S(1)} %get-tuple-element.344), channel_id=1, source_target_pairs={{2,0},{3,1},{4,2},{5,3},{6,4},{7,5},{0,6},{1,7},{10,8},{11,9},{12,... | collective-permute-start | bytes 1572872 | tf_op jit(solution)/shard_map/ppermute | solution.py:55
  475.7 23.9 %collective-permute-start.63 = (bf16[528,512]{1,0:T(8,128)(2,1)S(1)}, bf16[528,512]{1,0:T(8,128)(2,1)S(1)}, u32[]{:S(2)}, u32[]{:S(2)}) collective-permute-start(bf16[528,512]{1,0:T(8,128)(2,1)S(1)} %get-tuple-element.324), channel_id=1, source_target_pairs={{2,0},{3,1},{4,2},{5,3},{6,4},{7,5},{0,6},{1,7},{10,8},{11,9},{12,... | collective-permute-start | bytes 1622024 | tf_op jit(solution)/shard_map/ppermute | solution.py:55
  499.9 26.2 %collective-permute-start.64 = (bf16[528,512]{1,0:T(8,128)(2,1)S(1)}, bf16[528,512]{1,0:T(8,128)(2,1)S(1)}, u32[]{:S(2)}, u32[]{:S(2)}) collective-permute-start(bf16[528,512]{1,0:T(8,128)(2,1)S(1)} %fusion.24.refs_0_.refs_4_.refs_8_), channel_id=1, source_target_pairs={{0,8},{8,0},{16,24},{24,16},{1,9},{9,1},{17,25},{25,17},{2,10},{10... | collective-permute-start | bytes 1622024 | tf_op jit(solution)/shard_map/ppermute | solution.py:60
  500.8 25.3 %collective-permute-start.65 = (bf16[528,512]{1,0:T(8,128)(2,1)S(1)}, bf16[528,512]{1,0:T(8,128)(2,1)S(1)}, u32[]{:S(2)}, u32[]{:S(2)}) collective-permute-start(bf16[528,512]{1,0:T(8,128)(2,1)S(1)} %fusion.24.refs_0_.refs_4_.refs_8_), channel_id=1, source_target_pairs={{0,16},{8,24},{16,0},{24,8},{1,17},{9,25},{17,1},{25,9},{2,18},{10... | collective-permute-start | bytes 1622024 | tf_op jit(solution)/shard_map/ppermute | solution.py:60
  502.2 23.9 %collective-permute-start.66 = (bf16[528,512]{1,0:T(8,128)(2,1)S(1)}, bf16[528,512]{1,0:T(8,128)(2,1)S(1)}, u32[]{:S(2)}, u32[]{:S(2)}) collective-permute-start(bf16[528,512]{1,0:T(8,128)(2,1)S(1)} %fusion.24.refs_0_.refs_4_.refs_8_), channel_id=1, source_target_pairs={{0,24},{8,16},{16,8},{24,0},{1,25},{9,17},{17,9},{25,1},{2,26},{10... | collective-permute-start | bytes 1622024 | tf_op jit(solution)/shard_map/ppermute | solution.py:60
  (99 other events, 1455.0 us)

commit v6 on v5

--- a/solution.py
+++ b/solution.py
@@ -861,14 +861,16 @@
     copies = [pltpu.make_async_copy(w, h, sems.at[i]) for i, (w, h) in enumerate(zip(weights, held))]
     order = sorted(range(parts), key=lambda i: held[i].shape[0])
     first = [sum(h.shape[0] for h in held[:i]) for i in range(parts)]
-    for i in order:
+    for i in order[:2]:
         copies[i].start()
-    for i in order:
+    for n, i in enumerate(order):
         copies[i].wait()
+        if n + 2 < parts:
+            copies[order[n + 2]].start()
         tile = held[i].shape[0] if held[i].shape[0] <= 768 else tile_of(held[i].shape[0], 512)
-        for n in range(0, held[i].shape[0], tile):
-            total = dot(g[...], held[i][n : n + tile, :], 1, 1).astype(bf16)
-            at = first[i] + n
+        for row in range(0, held[i].shape[0], tile):
+            total = dot(g[...], held[i][row : row + tile, :], 1, 1).astype(bf16)
+            at = first[i] + row
             for t, out in enumerate(outs):
                 out[:, at : at + tile] = total[t * rows : (t + 1) * rows]
 

time: 542 us -> 542 us (level)
  no operation moved by 1% of the time
where the time goes in v6:
time: 542 us; the launch traced here: 533 us
  waiting for transfers between devices  239 us (44%)
  Pallas kernels  164 us (30%)
  starting transfers between devices  76 us (14%)
  other arithmetic  23.2 us (4%)
  local copies, waits for them, and re-layouts  20.8 us (4%)
  blocking collectives  7.24 us (1%)
    pallas_call x23, Pallas kernels, call(): pl.pallas_call(kernel, grid=grid, in_specs=in_specs, out_specs=out_specs,...  164 us
    ppermute x35, waiting for transfers between devices, ctx_send(): return lax.ppermute(a, 'ctx', [(i, i ^ distance) for i in range(size)])  158 us
    ppermute x20, waiting for transfers between devices, chip_send(): lax.ppermute(a, 'fsdp', [(2 * s + k, 2 * d + k) for s, d in pairs for k i...  70.4 us
    ppermute x35, starting transfers between devices, ctx_send(): return lax.ppermute(a, 'ctx', [(i, i ^ distance) for i in range(size)])  40 us
    ppermute x20, starting transfers between devices, chip_send(): lax.ppermute(a, 'fsdp', [(2 * s + k, 2 * d + k) for s, d in pairs for k i...  34.4 us
    unnamed x130, local copies, waits for them, and re-layouts  16.7 us
  transfers between devices with their start and end apart: 67, of which 38 were waited for; matrix products, arithmetic and copies ran while one was open for 4% of the time, Pallas kernels for 29%

profile of v6, /device:TPU:0, one launch (start us, length us, event | category | flops | bytes accessed | tf_op | source)
XLA Modules:
  0.0 532.5 jit_solution(9947460650087606996)
XLA Ops:
  8.6 5.0 collective-permute-start
  23.4 18.4 %collective-permute-done.2.refs_1_ = bf16[256,2048]{1,0:T(8,128)(2,1)} collective-permute-done((bf16[256,2048]{1,0:T(8,128)(2,1)}, bf16[256,2048]{1,0:T(8,128)(2,1)}, u32[]{:S(2)}, u32[]{:S(2)}) %collective-permute-start.2) | collective-permute-done | bytes 1048608 | tf_op jit(solution)/shard_map/ppermute | solution.py:60
  41.7 22.2 %collective-permute-done.3.refs_2_ = bf16[256,2048]{1,0:T(8,128)(2,1)} collective-permute-done((bf16[256,2048]{1,0:T(8,128)(2,1)}, bf16[256,2048]{1,0:T(8,128)(2,1)}, u32[]{:S(2)}, u32[]{:S(2)}) %collective-permute-start.3) | collective-permute-done | bytes 1048608 | tf_op jit(solution)/shard_map/ppermute | solution.py:60
  70.0 21.9 %collective-permute-done.8.refs_10_.refs_6_ = bf16[1040,512]{1,0:T(8,128)(2,1)S(1)} collective-permute-done((bf16[1040,512]{1,0:T(8,128)(2,1)S(1)}, bf16[1040,512]{1,0:T(8,128)(2,1)S(1)}, u32[]{:S(2)}, u32[]{:S(2)}) %collective-permute-start.8) | collective-permute-done | bytes 1064992 | tf_op jit(solution)/shard_map/ppermute | solution.py:55
  96.6 9.9 %shard_map.241 = (bf16[512,2048]{1,0:T(8,128)(2,1)}, bf16[512,1536]{1,0:T(8,128)(2,1)}, f32[4,2,1024]{2,1,0:T(2,128)S(1)}, f32[2,2048]{1,0:T(2,128)S(1)}, f32[512,128]{1,0:T(8,128)S(1)}) custom-call(s32[10]{0:T(128)S(1)} %compare_select_fusion.3.scal, bf16[256,2048]{1,0:T(8,128)(2,1)S(1)} %copy-done.2, bf16[256,2048]{1,0:T(8,128)(2,1)} %collective-permute-done.2.refs_1_, ...), custom_call_target="tpu_custom_call" | custom-call | flops 1 | bytes 1 | tf_op jit(solution)/shard_map/pallas_call | solution.py:192
  106.5 12.0 %shard_map.242 = (bf16[512,512]{1,0:T(8,128)(2,1)S(1)}, bf16[8,512,512]{2,1,0:T(8,128)(2,1)}) custom-call(s32[10]{0:T(128)S(1)} %compare_select_fusion.3.scal, bf16[512,1536]{1,0:T(8,128)(2,1)} %get-tuple-element.190.q_ref.k_ref.v_ref, bf16[512,1536]{1,0:T(8,128)(2,1)} %get-tuple-element.190.q_ref.k_ref.v_ref, ...), custom_call_target="tpu_custom_call" | custom-call | flops 1 | bytes 1 | tf_op jit(solution)/shard_map/pallas_call | solution.py:192
  119.3 5.0 shard_map.243
  127.8 11.3 %collective-permute-done.10.refs_1_ = bf16[128,2048]{1,0:T(8,128)(2,1)S(1)} collective-permute-done((bf16[128,2048]{1,0:T(8,128)(2,1)S(1)}, bf16[128,2048]{1,0:T(8,128)(2,1)S(1)}, u32[]{:S(2)}, u32[]{:S(2)}) %collective-permute-start.10) | collective-permute-done | bytes 524320 | tf_op jit(solution)/shard_map/ppermute | solution.py:60
  139.8 10.7 %collective-permute-done.12.refs_3_ = bf16[128,2048]{1,0:T(8,128)(2,1)S(1)} collective-permute-done((bf16[128,2048]{1,0:T(8,128)(2,1)}, bf16[128,2048]{1,0:T(8,128)(2,1)S(1)}, u32[]{:S(2)}, u32[]{:S(2)}) %collective-permute-start.12) | collective-permute-done | bytes 524320 | tf_op jit(solution)/shard_map/ppermute | solution.py:60
  163.4 11.3 %collective-permute-done.16.refs_1_ = bf16[128,2048]{1,0:T(8,128)(2,1)S(1)} collective-permute-done((bf16[128,2048]{1,0:T(8,128)(2,1)S(1)}, bf16[128,2048]{1,0:T(8,128)(2,1)S(1)}, u32[]{:S(2)}, u32[]{:S(2)}) %collective-permute-start.16) | collective-permute-done | bytes 524320 | tf_op jit(solution)/shard_map/ppermute | solution.py:60
  174.6 10.2 %collective-permute-done.17.refs_2_ = bf16[128,2048]{1,0:T(8,128)(2,1)S(1)} collective-permute-done((bf16[128,2048]{1,0:T(8,128)(2,1)S(1)}, bf16[128,2048]{1,0:T(8,128)(2,1)S(1)}, u32[]{:S(2)}, u32[]{:S(2)}) %collective-permute-start.17) | collective-permute-done | bytes 524320 | tf_op jit(solution)/shard_map/ppermute | solution.py:60
  197.5 10.9 %shard_map.245 = (bf16[512,2048]{1,0:T(8,128)(2,1)}, f32[512,1280]{1,0:T(8,128)}, f32[512,1280]{1,0:T(8,128)}, bf16[512,1280]{1,0:T(8,128)(2,1)}) custom-call(bf16[128,2048]{1,0:T(8,128)(2,1)S(1)} %copy-done.22, bf16[128,2048]{1,0:T(8,128)(2,1)S(1)} %collective-permute-done.16.refs_1_, bf16[128,2048]{1,0:T(8,128)(2,1)S(1)} %copy-done.24, ...), custom_call_target="tpu_custom_call" | custom-call | flops 1 | bytes 1 | tf_op jit(solution)/shard_map/pallas_call | solution.py:192
  208.5 7.4 %shard_map.246 = (bf16[640,2048]{1,0:T(8,128)(2,1)}, bf16[640,2048]{1,0:T(8,128)(2,1)}) custom-call(s32[10]{0:T(128)S(1)} %compare_select_fusion.3.scal, bf16[512,1280]{1,0:T(8,128)(2,1)} %get-tuple-element.251.mixed, bf16[256,2048]{1,0:T(8,128)(2,1)S(1)} %copy-done.3, bf16[256,2048]{1,0:T(8,128)(2,1)} %collective-permute-done.2.refs_1_, ...), custom_call_target="tpu_custom_call" | custom-call | flops 1 | bytes 1 | tf_op jit(solution)/shard_map/pallas_call | solution.py:192
  215.8 9.0 %collective-permute-done.21 = bf16[160,2048]{1,0:T(8,128)(2,1)S(1)} collective-permute-done((bf16[160,2048]{1,0:T(8,128)(2,1)S(1)}, bf16[160,2048]{1,0:T(8,128)(2,1)S(1)}, u32[]{:S(2)}, u32[]{:S(2)}) %collective-permute-start.21) | collective-permute-done | bytes 655392 | tf_op jit(solution)/shard_map/ppermute | solution.py:55
  231.0 11.7 %collective-permute-done.25.refs_6_.refs_2_ = bf16[160,2048]{1,0:T(8,128)(2,1)S(1)} collective-permute-done((bf16[160,2048]{1,0:T(8,128)(2,1)S(1)}, bf16[160,2048]{1,0:T(8,128)(2,1)S(1)}, u32[]{:S(2)}, u32[]{:S(2)}) %collective-permute-start.25) | collective-permute-done | bytes 655392 | tf_op jit(solution)/shard_map/ppermute | solution.py:55
  244.9 11.2 %shard_map.247.g = bf16[512,2560]{1,0:T(8,128)(2,1)} custom-call(s32[10]{0:T(128)S(1)} %compare_select_fusion.3.scal, f32[512,1280]{1,0:T(8,128)} %get-tuple-element.222.gate, f32[512,1280]{1,0:T(8,128)} %get-tuple-element.223.up, bf16[256,2048]{1,0:T(8,128)(2,1)} %shard_map.239.refs_0_.own, bf16[256,2048]{1,0:T(8,128)(2,1)} %collective-permute-done.2.refs_1_, ...), custom_call_target="tpu_custom_call" | custom-call | flops 1 | bytes 1 | tf_op jit(solution)/shard_map/pallas_call | solution.py:192
  256.1 4.8 collective-permute-done.26
  265.2 12.7 %shard_map.248 = (bf16[128,2048]{1,0:T(8,128)(2,1)S(1)}, bf16[128,2048]{1,0:T(8,128)(2,1)S(1)}, bf16[128,2048]{1,0:T(8,128)(2,1)S(1)}, bf16[128,2048]{1,0:T(8,128)(2,1)}) custom-call(bf16[512,2560]{1,0:T(8,128)(2,1)} %shard_map.247.g, bf16[768,2560]{1,0:T(8,128)(2,1)} %copy-done.28, bf16[768,2560]{1,0:T(8,128)(2,1)} %copy-done.34, ...), custom_call_target="tpu_custom_call" | custom-call | flops 1 | bytes 1 | tf_op jit(solution)/shard_map/pallas_call | solution.py:192
  281.5 10.4 %shard_map.249 = (bf16[768,2560]{1,0:T(8,128)(2,1)}, bf16[768,2560]{1,0:T(8,128)(2,1)}, bf16[512,2560]{1,0:T(8,128)(2,1)}) custom-call(s32[10]{0:T(128)S(1)} %compare_select_fusion.3.scal, bf16[512,2048]{1,0:T(8,128)(2,1)} %get-tuple-element.230.normed, bf16[512,2560]{1,0:T(8,128)(2,1)} %shard_map.247.g), custom_call_target="tpu_custom_call" | custom-call | flops 1 | bytes 1 | tf_op jit(solution)/shard_map/pallas_call | solution.py:192
  292.5 7.2 %all_to_all.9 = bf16[2,256,2560]{2,1,0:T(8,128)(2,1)S(1)} all-to-all(bf16[2,256,2560]{2,1,0:T(8,128)(2,1)} %bitcast.15), channel_id=1, replica_groups={{0,1},{2,3},{4,5},{6,7},{8,9},{10,11},{12,13},{14,15},{16,17},{18,19},{..., dimensions={0} | all-to-all | bytes 5242880 | tf_op jit(solution)/shard_map/all_to_all | solution.py:51
  318.9 7.5 %shard_map.251 = (bf16[128,2048]{1,0:T(8,128)(2,1)S(1)}, bf16[128,2048]{1,0:T(8,128)(2,1)S(1)}, bf16[128,2048]{1,0:T(8,128)(2,1)S(1)}, bf16[128,2048]{1,0:T(8,128)(2,1)}) custom-call(s32[10]{0:T(128)S(1)} %compare_select_fusion.3.scal, bf16[512,1280]{1,0:T(8,128)(2,1)} %get-tuple-element.251.mixed, bf16[480,2048]{1,0:T(8,128)(2,1)} %copy-done.35, ...), custom_call_target="tpu_custom_call" | custom-call | flops 1 | bytes 1 | tf_op jit(solution)/shard_map/pallas_call | solution.py:192
  326.5 13.3 %collective-permute-done.34 = bf16[256,2560]{1,0:T(8,128)(2,1)S(1)} collective-permute-done((bf16[256,2560]{1,0:T(8,128)(2,1)}, bf16[256,2560]{1,0:T(8,128)(2,1)S(1)}, u32[]{:S(2)}, u32[]{:S(2)}) %collective-permute-start.34) | collective-permute-done | bytes 1310752 | tf_op jit(solution)/shard_map/ppermute | solution.py:55
  354.4 11.6 %shard_map.253 = (bf16[512,512]{1,0:T(8,128)(2,1)S(1)}, bf16[512,512]{1,0:T(8,128)(2,1)S(1)}, bf16[512,512]{1,0:T(8,128)(2,1)S(1)}, f32[4,2,1024]{2,1,0:T(2,128)S(1)}) custom-call(s32[10]{0:T(128)S(1)} %compare_select_fusion.3.scal, bf16[512,1536]{1,0:T(8,128)(2,1)} %get-tuple-element.190.q_ref.k_ref.v_ref, ...), custom_call_target="tpu_custom_call" | custom-call | flops 1 | bytes 1 | tf_op jit(solution)/shard_map/pallas_call | solution.py:192
  373.6 10.0 %shard_map.254 = (bf16[128,2048]{1,0:T(8,128)(2,1)S(1)}, bf16[128,2048]{1,0:T(8,128)(2,1)S(1)}, bf16[128,2048]{1,0:T(8,128)(2,1)S(1)}, bf16[128,2048]{1,0:T(8,128)(2,1)}, f32[1,2048]{1,0:T(1,128)S(1)}) custom-call(f32[512,128]{1,0:T(8,128)S(1)} %get-tuple-element.274.scales, bf16[512,512]{1,0:T(8,128)(2,1)} %copy-done.8, bf16[512,512]{1,0:T(8,128)(2,1)} %copy-done.10, ...), custom_call_target="tpu_custom_call" | custom-call | flops 1 | bytes 1 | tf_op jit(solution)/shard_map/pallas_call | solution.py:192
  390.2 11.9 %shard_map.255 = (bf16[3120,512]{1,0:T(8,128)(2,1)}, bf16[3120,512]{1,0:T(8,128)(2,1)}, bf16[1040,512]{1,0:T(8,128)(2,1)}, bf16[1040,512]{1,0:T(8,128)(2,1)}) custom-call(s32[10]{0:T(128)S(1)} %compare_select_fusion.3.scal, bf16[512,2048]{1,0:T(8,128)(2,1)} %get-tuple-element.287.normed, bf16[512,512]{1,0:T(8,128)(2,1)S(1)} %copy-done.14, ...), custom_call_target="tpu_custom_call" | custom-call | flops 1 | bytes 1 | tf_op jit(solution)/shard_map/pallas_call | solution.py:192
  405.3 4.7 collective-permute-done.44.refs_2_
  415.3 29.0 %collective-permute-done.53.refs_2_ = bf16[256,2560]{1,0:T(8,128)(2,1)S(1)} collective-permute-done((bf16[256,2560]{1,0:T(8,128)(2,1)S(1)}, bf16[256,2560]{1,0:T(8,128)(2,1)S(1)}, u32[]{:S(2)}, u32[]{:S(2)}) %collective-permute-start.53) | collective-permute-done | bytes 1310752 | tf_op jit(solution)/shard_map/ppermute | solution.py:60
  451.5 9.1 %collective-permute-done.54 = bf16[128,2560]{1,0:T(8,128)(2,1)S(1)} collective-permute-done((bf16[128,2560]{1,0:T(8,128)(2,1)S(1)}, bf16[128,2560]{1,0:T(8,128)(2,1)S(1)}, u32[]{:S(2)}, u32[]{:S(2)}) %collective-permute-start.54) | collective-permute-done | bytes 655392 | tf_op jit(solution)/shard_map/ppermute | solution.py:60
  463.6 5.7 %collective-permute-done.57 = bf16[80,2048]{1,0:T(8,128)(2,1)S(1)} collective-permute-done((bf16[80,2048]{1,0:T(8,128)(2,1)S(1)}, bf16[80,2048]{1,0:T(8,128)(2,1)S(1)}, u32[]{:S(2)}, u32[]{:S(2)}) %collective-permute-start.57) | collective-permute-done | bytes 327712 | tf_op jit(solution)/shard_map/ppermute | solution.py:60
  480.7 6.3 %collective-permute-done.59.refs_2_.refs_3_ = bf16[512,512]{1,0:T(8,128)(2,1)S(1)} collective-permute-done((bf16[512,512]{1,0:T(8,128)(2,1)S(1)}, bf16[512,512]{1,0:T(8,128)(2,1)S(1)}, u32[]{:S(2)}, u32[]{:S(2)}) %collective-permute-start.59) | collective-permute-done | bytes 524320 | tf_op jit(solution)/shard_map/ppermute | solution.py:60
  487.0 8.9 %collective-permute-done.60.refs_4_.refs_5_ = bf16[512,512]{1,0:T(8,128)(2,1)S(1)} collective-permute-done((bf16[512,512]{1,0:T(8,128)(2,1)S(1)}, bf16[512,512]{1,0:T(8,128)(2,1)S(1)}, u32[]{:S(2)}, u32[]{:S(2)}) %collective-permute-start.60) | collective-permute-done | bytes 524320 | tf_op jit(solution)/shard_map/ppermute | solution.py:60
  508.7 8.8 %shard_map.259 = (f32[256,5120]{1,0:T(8,128)}, f32[256,5120]{1,0:T(8,128)}) custom-call(s32[10]{0:T(128)S(1)} %compare_select_fusion.3.scal, bf16[256,2560]{1,0:T(8,128)(2,1)S(1)} %fusion.7.refs_0_, bf16[256,2560]{1,0:T(8,128)(2,1)} %copy-done.43, bf16[256,2560]{1,0:T(8,128)(2,1)} %copy-done.42, bf16[256,2560]{1,0:T(8,128)(2,1)} %pad_maximum_fusion.refs_3_), custom_call_target="tpu_custom_call" | custom-call | flops 1 | bytes 1 | tf_op jit(solution)/shard_map/pallas_call | solution.py:192
  (288 shorter events, 180.1 us)
Async XLA Ops:
  8.6 55.3 %collective-permute-start = (bf16[1040,512]{1,0:T(8,128)(2,1)}, bf16[1040,512]{1,0:T(8,128)(2,1)}, u32[]{:S(2)}, u32[]{:S(2)}) collective-permute-start(bf16[1040,512]{1,0:T(8,128)(2,1)} %shard_map.238.refs_4_.refs_0_), channel_id=1, source_target_pairs={{2,0},{3,1},{4,2},{5,3},{6,4},{7,5},{0,6},{1,7},{10,8},{11,9},{12,... | collective-permute-start | bytes 3194888 | tf_op jit(solution)/shard_map/ppermute | solution.py:55
  13.7 50.3 %collective-permute-start.1 = (bf16[1040,512]{1,0:T(8,128)(2,1)}, bf16[1040,512]{1,0:T(8,128)(2,1)}, u32[]{:S(2)}, u32[]{:S(2)}) collective-permute-start(bf16[1040,512]{1,0:T(8,128)(2,1)} %shard_map.238.refs_4_.refs_0_), channel_id=1, source_target_pairs={{0,2},{1,3},{2,4},{3,5},{4,6},{5,7},{6,0},{7,1},{8,10},{9,11},{10,... | collective-permute-start | bytes 3194888 | tf_op jit(solution)/shard_map/ppermute | solution.py:55
  15.3 26.4 %collective-permute-start.2 = (bf16[256,2048]{1,0:T(8,128)(2,1)}, bf16[256,2048]{1,0:T(8,128)(2,1)}, u32[]{:S(2)}, u32[]{:S(2)}) collective-permute-start(bf16[256,2048]{1,0:T(8,128)(2,1)} %shard_map.239.refs_0_.own), channel_id=1, source_target_pairs={{0,8},{8,0},{16,24},{24,16},{1,9},{9,1},{17,25},{25,17},{2,10},{10... | collective-permute-start | bytes 3145736 | tf_op jit(solution)/shard_map/ppermute | solution.py:60
  16.8 47.1 %collective-permute-start.3 = (bf16[256,2048]{1,0:T(8,128)(2,1)}, bf16[256,2048]{1,0:T(8,128)(2,1)}, u32[]{:S(2)}, u32[]{:S(2)}) collective-permute-start(bf16[256,2048]{1,0:T(8,128)(2,1)} %shard_map.239.refs_0_.own), channel_id=1, source_target_pairs={{0,16},{8,24},{16,0},{24,8},{1,17},{9,25},{17,1},{25,9},{2,18},{10... | collective-permute-start | bytes 3145736 | tf_op jit(solution)/shard_map/ppermute | solution.py:60
  18.4 45.6 %collective-permute-start.4 = (bf16[256,2048]{1,0:T(8,128)(2,1)}, bf16[256,2048]{1,0:T(8,128)(2,1)}, u32[]{:S(2)}, u32[]{:S(2)}) collective-permute-start(bf16[256,2048]{1,0:T(8,128)(2,1)} %shard_map.239.refs_0_.own), channel_id=1, source_target_pairs={{0,24},{8,16},{16,8},{24,0},{1,25},{9,17},{17,9},{25,1},{2,26},{10... | collective-permute-start | bytes 3145736 | tf_op jit(solution)/shard_map/ppermute | solution.py:60
  66.0 25.9 %collective-permute-start.8 = (bf16[1040,512]{1,0:T(8,128)(2,1)S(1)}, bf16[1040,512]{1,0:T(8,128)(2,1)S(1)}, u32[]{:S(2)}, u32[]{:S(2)}) collective-permute-start(bf16[1040,512]{1,0:T(8,128)(2,1)S(1)} %select_select_fusion.1), channel_id=1, source_target_pairs={{6,2},{7,3},{0,4},{1,5},{2,0},{3,1},{4,6},{5,7},{14,10},{15,11},{8... | collective-permute-start | bytes 3194888 | tf_op jit(solution)/shard_map/ppermute | solution.py:55
  91.9 62.1 %collective-permute-start.13 = (bf16[256,2560]{1,0:T(8,128)(2,1)S(1)}, bf16[256,2560]{1,0:T(8,128)(2,1)}, u32[]{:S(2)}, u32[]{:S(2)}) collective-permute-start(bf16[256,2560]{1,0:T(8,128)(2,1)S(1)} %copy-done.5), channel_id=1, source_target_pairs={{2,0},{3,1},{4,2},{5,3},{6,4},{7,5},{0,6},{1,7},{10,8},{11,9},{12,... | collective-permute-start | bytes 3932168 | tf_op jit(solution)/shard_map/ppermute | solution.py:55
  95.5 58.5 %collective-permute-start.14 = (bf16[256,2560]{1,0:T(8,128)(2,1)S(1)}, bf16[256,2560]{1,0:T(8,128)(2,1)}, u32[]{:S(2)}, u32[]{:S(2)}) collective-permute-start(bf16[256,2560]{1,0:T(8,128)(2,1)S(1)} %copy-done.5), channel_id=1, source_target_pairs={{0,2},{1,3},{2,4},{3,5},{4,6},{5,7},{6,0},{7,1},{8,10},{9,11},{10,... | collective-permute-start | bytes 3932168 | tf_op jit(solution)/shard_map/ppermute | solution.py:55
  126.4 24.2 %collective-permute-start.12 = (bf16[128,2048]{1,0:T(8,128)(2,1)}, bf16[128,2048]{1,0:T(8,128)(2,1)S(1)}, u32[]{:S(2)}, u32[]{:S(2)}) collective-permute-start(bf16[128,2048]{1,0:T(8,128)(2,1)} %get-tuple-element.196), channel_id=1, source_target_pairs={{0,24},{8,16},{16,8},{24,0},{1,25},{9,17},{17,9},{25,1},{2,26},{10... | collective-permute-start | bytes 1572872 | tf_op jit(solution)/shard_map/ppermute | solution.py:60
  157.6 32.5 %collective-permute-start.15 = (bf16[768,2560]{1,0:T(8,128)(2,1)S(1)}, bf16[768,2560]{1,0:T(8,128)(2,1)S(1)}, u32[]{:S(2)}, u32[]{:S(2)}) collective-permute-start(bf16[768,2560]{1,0:T(8,128)(2,1)S(1)} %constant_dynamic-update-slice_fusion.refs_4_.refs_0_), channel_id=1, source_target_pairs={{0,1},{1,0},{2,3},{3,2},{4,5},{5,4},{6,7},{7,6},{8,9},{9,8},{10,11... | collective-permute-start | bytes 11796488 | tf_op jit(solution)/shard_map/ppermute | solution.py:46
  157.7 32.4 %collective-permute-start.19 = (bf16[256,2560]{1,0:T(8,128)(2,1)S(1)}, bf16[256,2560]{1,0:T(8,128)(2,1)}, u32[]{:S(2)}, u32[]{:S(2)}) collective-permute-start(bf16[256,2560]{1,0:T(8,128)(2,1)S(1)} %get-tuple-element.348), channel_id=1, source_target_pairs={{6,2},{7,3},{0,4},{1,5},{2,0},{3,1},{4,6},{5,7},{14,10},{15,11},{8... | collective-permute-start | bytes 3932168 | tf_op jit(solution)/shard_map/ppermute | solution.py:55
  161.0 23.8 %collective-permute-start.17 = (bf16[128,2048]{1,0:T(8,128)(2,1)S(1)}, bf16[128,2048]{1,0:T(8,128)(2,1)S(1)}, u32[]{:S(2)}, u32[]{:S(2)}) collective-permute-start(bf16[128,2048]{1,0:T(8,128)(2,1)S(1)} %get-tuple-element.204.refs_0_), channel_id=1, source_target_pairs={{0,16},{8,24},{16,0},{24,8},{1,17},{9,25},{17,1},{25,9},{2,18},{10... | collective-permute-start | bytes 1572872 | tf_op jit(solution)/shard_map/ppermute | solution.py:60
  162.4 23.7 %collective-permute-start.18 = (bf16[128,2048]{1,0:T(8,128)(2,1)S(1)}, bf16[128,2048]{1,0:T(8,128)(2,1)S(1)}, u32[]{:S(2)}, u32[]{:S(2)}) collective-permute-start(bf16[128,2048]{1,0:T(8,128)(2,1)S(1)} %get-tuple-element.204.refs_0_), channel_id=1, source_target_pairs={{0,24},{8,16},{16,8},{24,0},{1,25},{9,17},{17,9},{25,1},{2,26},{10... | collective-permute-start | bytes 1572872 | tf_op jit(solution)/shard_map/ppermute | solution.py:60
  192.1 23.7 %collective-permute-start.20 = (bf16[160,2048]{1,0:T(8,128)(2,1)S(1)}, bf16[160,2048]{1,0:T(8,128)(2,1)S(1)}, u32[]{:S(2)}, u32[]{:S(2)}) collective-permute-start(bf16[160,2048]{1,0:T(8,128)(2,1)S(1)} %constant_dynamic-slice_fusion), channel_id=1, source_target_pairs={{2,0},{3,1},{4,2},{5,3},{6,4},{7,5},{0,6},{1,7},{10,8},{11,9},{12,... | collective-permute-start | bytes 1966088 | tf_op jit(solution)/shard_map/ppermute | solution.py:55
  194.6 30.2 %collective-permute-start.21 = (bf16[160,2048]{1,0:T(8,128)(2,1)S(1)}, bf16[160,2048]{1,0:T(8,128)(2,1)S(1)}, u32[]{:S(2)}, u32[]{:S(2)}) collective-permute-start(bf16[160,2048]{1,0:T(8,128)(2,1)S(1)} %constant_dynamic-slice_fusion), channel_id=1, source_target_pairs={{0,2},{1,3},{2,4},{3,5},{4,6},{5,7},{6,0},{7,1},{8,10},{9,11},{10,... | collective-permute-start | bytes 1966088 | tf_op jit(solution)/shard_map/ppermute | solution.py:55
  261.3 30.5 %collective-permute-start.28 = (bf16[160,2048]{1,0:T(8,128)(2,1)S(1)}, bf16[160,2048]{1,0:T(8,128)(2,1)S(1)}, u32[]{:S(2)}, u32[]{:S(2)}) collective-permute-start(bf16[160,2048]{1,0:T(8,128)(2,1)S(1)} %get-tuple-element.228), channel_id=1, source_target_pairs={{0,2},{1,3},{2,4},{3,5},{4,6},{5,7},{6,0},{7,1},{8,10},{9,11},{10,... | collective-permute-start | bytes 1966088 | tf_op jit(solution)/shard_map/ppermute | solution.py:55
  262.5 30.1 %collective-permute-start.29 = (bf16[160,2048]{1,0:T(8,128)(2,1)S(1)}, bf16[160,2048]{1,0:T(8,128)(2,1)S(1)}, u32[]{:S(2)}, u32[]{:S(2)}) collective-permute-start(bf16[160,2048]{1,0:T(8,128)(2,1)S(1)} %get-tuple-element.229), channel_id=1, source_target_pairs={{2,0},{3,1},{4,2},{5,3},{6,4},{7,5},{0,6},{1,7},{10,8},{11,9},{12,... | collective-permute-start | bytes 1966088 | tf_op jit(solution)/shard_map/ppermute | solution.py:55
  307.5 32.3 %collective-permute-start.34 = (bf16[256,2560]{1,0:T(8,128)(2,1)}, bf16[256,2560]{1,0:T(8,128)(2,1)S(1)}, u32[]{:S(2)}, u32[]{:S(2)}) collective-permute-start(bf16[256,2560]{1,0:T(8,128)(2,1)} %fusion.16), channel_id=1, source_target_pairs={{0,2},{1,3},{6,4},{7,5},{2,6},{3,7},{4,0},{5,1},{8,10},{9,11},{14,... | collective-permute-start | bytes 3932168 | tf_op jit(solution)/shard_map/ppermute | solution.py:55
  307.5 38.3 %collective-permute-start.35 = (bf16[128,2048]{1,0:T(8,128)(2,1)S(1)}, bf16[128,2048]{1,0:T(8,128)(2,1)S(1)}, u32[]{:S(2)}, u32[]{:S(2)}) collective-permute-start(bf16[128,2048]{1,0:T(8,128)(2,1)S(1)} %get-tuple-element.247.refs_0_), channel_id=1, source_target_pairs={{0,8},{8,0},{16,24},{24,16},{1,9},{9,1},{17,25},{25,17},{2,10},{10... | collective-permute-start | bytes 1572872 | tf_op jit(solution)/shard_map/ppermute | solution.py:60
  308.8 37.0 %collective-permute-start.36 = (bf16[128,2048]{1,0:T(8,128)(2,1)S(1)}, bf16[128,2048]{1,0:T(8,128)(2,1)S(1)}, u32[]{:S(2)}, u32[]{:S(2)}) collective-permute-start(bf16[128,2048]{1,0:T(8,128)(2,1)S(1)} %get-tuple-element.247.refs_0_), channel_id=1, source_target_pairs={{0,16},{8,24},{16,0},{24,8},{1,17},{9,25},{17,1},{25,9},{2,18},{10... | collective-permute-start | bytes 1572872 | tf_op jit(solution)/shard_map/ppermute | solution.py:60
  310.0 35.8 %collective-permute-start.37 = (bf16[128,2048]{1,0:T(8,128)(2,1)S(1)}, bf16[128,2048]{1,0:T(8,128)(2,1)S(1)}, u32[]{:S(2)}, u32[]{:S(2)}) collective-permute-start(bf16[128,2048]{1,0:T(8,128)(2,1)S(1)} %get-tuple-element.247.refs_0_), channel_id=1, source_target_pairs={{0,24},{8,16},{16,8},{24,0},{1,25},{9,17},{17,9},{25,1},{2,26},{10... | collective-permute-start | bytes 1572872 | tf_op jit(solution)/shard_map/ppermute | solution.py:60
  342.0 60.2 %collective-permute-start.46 = (bf16[256,2560]{1,0:T(8,128)(2,1)}, bf16[256,2560]{1,0:T(8,128)(2,1)}, u32[]{:S(2)}, u32[]{:S(2)}) collective-permute-start(bf16[256,2560]{1,0:T(8,128)(2,1)} %get-tuple-element.341), channel_id=1, source_target_pairs={{0,2},{1,3},{2,4},{3,5},{4,6},{5,7},{6,0},{7,1},{8,10},{9,11},{10,... | collective-permute-start | bytes 3932168 | tf_op jit(solution)/shard_map/ppermute | solution.py:55
  342.0 60.2 %collective-permute-start.47 = (bf16[256,2560]{1,0:T(8,128)(2,1)}, bf16[256,2560]{1,0:T(8,128)(2,1)}, u32[]{:S(2)}, u32[]{:S(2)}) collective-permute-start(bf16[256,2560]{1,0:T(8,128)(2,1)} %get-tuple-element.340), channel_id=1, source_target_pairs={{2,0},{3,1},{4,2},{5,3},{6,4},{7,5},{0,6},{1,7},{10,8},{11,9},{12,... | collective-permute-start | bytes 3932168 | tf_op jit(solution)/shard_map/ppermute | solution.py:55
  413.0 33.3 %collective-permute-start.49 = (bf16[3120,512]{1,0:T(8,128)(2,1)S(1)}, bf16[3120,512]{1,0:T(8,128)(2,1)S(1)}, u32[]{:S(2)}, u32[]{:S(2)}) collective-permute-start(bf16[3120,512]{1,0:T(8,128)(2,1)S(1)} %copy-done.61), channel_id=1, source_target_pairs={{0,1},{1,0},{2,3},{3,2},{4,5},{5,4},{6,7},{7,6},{8,9},{9,8},{10,11... | collective-permute-start | bytes 9584648 | tf_op jit(solution)/shard_map/ppermute | solution.py:46
  413.2 31.1 %collective-permute-start.53 = (bf16[256,2560]{1,0:T(8,128)(2,1)S(1)}, bf16[256,2560]{1,0:T(8,128)(2,1)S(1)}, u32[]{:S(2)}, u32[]{:S(2)}) collective-permute-start(bf16[256,2560]{1,0:T(8,128)(2,1)S(1)} %fusion.7.refs_0_), channel_id=1, source_target_pairs={{0,16},{8,24},{16,0},{24,8},{1,17},{9,25},{17,1},{25,9},{2,18},{10... | collective-permute-start | bytes 3932168 | tf_op jit(solution)/shard_map/ppermute | solution.py:60
  413.8 31.3 %collective-permute-start.55 = (bf16[256,2560]{1,0:T(8,128)(2,1)S(1)}, bf16[256,2560]{1,0:T(8,128)(2,1)S(1)}, u32[]{:S(2)}, u32[]{:S(2)}) collective-permute-start(bf16[256,2560]{1,0:T(8,128)(2,1)S(1)} %fusion.7.refs_0_), channel_id=1, source_target_pairs={{0,8},{8,0},{16,24},{24,16},{1,9},{9,1},{17,25},{25,17},{2,10},{10... | collective-permute-start | bytes 3932168 | tf_op jit(solution)/shard_map/ppermute | solution.py:60
  415.1 32.2 %collective-permute-start.50 = (bf16[1040,512]{1,0:T(8,128)(2,1)S(1)}, bf16[1040,512]{1,0:T(8,128)(2,1)S(1)}, u32[]{:S(2)}, u32[]{:S(2)}) collective-permute-start(bf16[1040,512]{1,0:T(8,128)(2,1)S(1)} %add_convert_fusion.4), channel_id=1, source_target_pairs={{0,2},{1,3},{6,4},{7,5},{2,6},{3,7},{4,0},{5,1},{8,10},{9,11},{14,... | collective-permute-start | bytes 3194888 | tf_op jit(solution)/shard_map/ppermute | solution.py:55
  447.7 24.1 %collective-permute-start.52 = (bf16[512,512]{1,0:T(8,128)(2,1)S(1)}, bf16[512,512]{1,0:T(8,128)(2,1)S(1)}, u32[]{:S(2)}, u32[]{:S(2)}) collective-permute-start(bf16[512,512]{1,0:T(8,128)(2,1)S(1)} %get-tuple-element.344), channel_id=1, source_target_pairs={{2,0},{3,1},{4,2},{5,3},{6,4},{7,5},{0,6},{1,7},{10,8},{11,9},{12,... | collective-permute-start | bytes 1572872 | tf_op jit(solution)/shard_map/ppermute | solution.py:55
  475.7 23.9 %collective-permute-start.63 = (bf16[528,512]{1,0:T(8,128)(2,1)S(1)}, bf16[528,512]{1,0:T(8,128)(2,1)S(1)}, u32[]{:S(2)}, u32[]{:S(2)}) collective-permute-start(bf16[528,512]{1,0:T(8,128)(2,1)S(1)} %get-tuple-element.324), channel_id=1, source_target_pairs={{2,0},{3,1},{4,2},{5,3},{6,4},{7,5},{0,6},{1,7},{10,8},{11,9},{12,... | collective-permute-start | bytes 1622024 | tf_op jit(solution)/shard_map/ppermute | solution.py:55
  499.9 26.2 %collective-permute-start.64 = (bf16[528,512]{1,0:T(8,128)(2,1)S(1)}, bf16[528,512]{1,0:T(8,128)(2,1)S(1)}, u32[]{:S(2)}, u32[]{:S(2)}) collective-permute-start(bf16[528,512]{1,0:T(8,128)(2,1)S(1)} %fusion.24.refs_0_.refs_4_.refs_8_), channel_id=1, source_target_pairs={{0,8},{8,0},{16,24},{24,16},{1,9},{9,1},{17,25},{25,17},{2,10},{10... | collective-permute-start | bytes 1622024 | tf_op jit(solution)/shard_map/ppermute | solution.py:60
  500.8 25.3 %collective-permute-start.65 = (bf16[528,512]{1,0:T(8,128)(2,1)S(1)}, bf16[528,512]{1,0:T(8,128)(2,1)S(1)}, u32[]{:S(2)}, u32[]{:S(2)}) collective-permute-start(bf16[528,512]{1,0:T(8,128)(2,1)S(1)} %fusion.24.refs_0_.refs_4_.refs_8_), channel_id=1, source_target_pairs={{0,16},{8,24},{16,0},{24,8},{1,17},{9,25},{17,1},{25,9},{2,18},{10... | collective-permute-start | bytes 1622024 | tf_op jit(solution)/shard_map/ppermute | solution.py:60
  502.2 23.9 %collective-permute-start.66 = (bf16[528,512]{1,0:T(8,128)(2,1)S(1)}, bf16[528,512]{1,0:T(8,128)(2,1)S(1)}, u32[]{:S(2)}, u32[]{:S(2)}) collective-permute-start(bf16[528,512]{1,0:T(8,128)(2,1)S(1)} %fusion.24.refs_0_.refs_4_.refs_8_), channel_id=1, source_target_pairs={{0,24},{8,16},{16,8},{24,0},{1,25},{9,17},{17,9},{25,1},{2,26},{10... | collective-permute-start | bytes 1622024 | tf_op jit(solution)/shard_map/ppermute | solution.py:60
  (99 other events, 1455.0 us)
